TPU v7x, 32 devices: a whole 2x2x4 slice. The times are simulated.
32 devices in a mesh: parts: 2 (over y), patch: 4 (over z), sub: 2 (over x), lvl: 2 (over core).
Axes of the slice: x: 2, y: 2, z: 4, core: 2. Of those that a mesh axis runs over, the one named last changes fastest.
Arguments:
- node_states: float32 [8192, 512], P(('parts', 'patch', 'lvl')), parts along dimension 0, may hold values from -6 to 6
- coarse_states: float32 [1024, 512], P(('parts', 'patch', 'lvl')), parts along dimension 0, may hold values from -6 to 6
- children: int32 [512, 7], P(('patch', 'lvl')), may hold values from 0 to 511
- down_sources: int32 [4096, 3], P(('patch', 'lvl')), may hold values from 0 to 63
- bottom_links: int32 [4096, 6], P(('patch', 'lvl')), may hold values from 0 to 767, as said below
- coarse_links: int32 [512, 6], P(('patch', 'lvl')), may hold values from 0 to 511
- upward_sender: float32 [512, 512], P(None, 'sub'), may hold values from -0.25 to 0.25
- upward_receiver: float32 [512, 512], P(None, 'sub'), may hold values from -0.25 to 0.25
- upward_bias: float32 [512], P('sub'), may hold values from -4 to 4
- upward_output: float32 [512, 512], P('sub'), may hold values from -0.25 to 0.25
- upward_gain: float32 [512], replicated, may hold values from 0.1 to 1.9
- coarse_sender: float32 [512, 512], P(None, 'sub'), may hold values from -0.25 to 0.25
- coarse_receiver: float32 [512, 512], P(None, 'sub'), may hold values from -0.25 to 0.25
- coarse_bias: float32 [512], P('sub'), may hold values from -4 to 4
- coarse_output: float32 [512, 512], P('sub'), may hold values from -0.25 to 0.25
- coarse_gain: float32 [512], replicated, may hold values from 0.1 to 1.9
- downward_sender: float32 [512, 512], P(None, 'sub'), may hold values from -0.25 to 0.25
- downward_receiver: float32 [512, 512], P(None, 'sub'), may hold values from -0.25 to 0.25
- downward_bias: float32 [512], P('sub'), may hold values from -4 to 4
- downward_output: float32 [512, 512], P('sub'), may hold values from -0.25 to 0.25
- downward_gain: float32 [512], replicated, may hold values from 0.1 to 1.9
- bottom_sender: float32 [512, 512], P(None, 'sub'), may hold values from -0.25 to 0.25
- bottom_receiver: float32 [512, 512], P(None, 'sub'), may hold values from -0.25 to 0.25
- bottom_bias: float32 [512], P('sub'), may hold values from -4 to 4
- bottom_output: float32 [512, 512], P('sub'), may hold values from -0.25 to 0.25
- bottom_gain: float32 [512], replicated, may hold values from 0.1 to 1.9
Outputs:
- new_nodes: float32 [8192, 512], P(('parts', 'patch', 'lvl')), parts along dimension 0
- new_coarse: float32 [1024, 512], P(('parts', 'patch', 'lvl')), parts along dimension 0
There are 2 independent parts, one for each index of `parts`. A program takes and returns all parts, laid end to end along the dimension named above; an argument that names none is the same for every part. Nothing has to cross between parts.
Inputs may be any that keep to these rules, and one draw needn't show every extreme that they name: bottom_links[n, k] - 128 differs from n's row within its block by at most 128.
All inputs are finite; a program needn't handle non-finite values.
Results may differ from a plain program's by a relative error of at most 0.00011.
Values sent between devices are 32-bit elements; how exact they have to be, the bound alone decides.
No kernel may reach another device: no remote copies, remote signals or barrier semaphores. Data moves between devices by JAX's collectives and lax.ppermute only.
A program may use at most 64 MiB of HBM per device.

v0:
```python
import jax
import jax.numpy as jnp
from jax import lax
from jax.sharding import PartitionSpec as P

epsilon = 1e-05
highest = lax.Precision.HIGHEST


def extended(cells, sides, width):
    for axis, dim in sides:
        count = lax.axis_size(axis)
        head = lax.slice_in_dim(cells, 0, width, axis=dim)
        tail = lax.slice_in_dim(cells, cells.shape[dim] - width, cells.shape[dim], axis=dim)
        cells = jnp.concatenate(
            [
                lax.ppermute(tail, axis, [(i, (i + 1) % count) for i in range(count)]),
                cells,
                lax.ppermute(head, axis, [((i + 1) % count, i) for i in range(count)]),
            ],
            axis=dim,
        )
    return cells


def project(states, weights):
    return jnp.dot(states, weights, precision=highest, preferred_element_type=jnp.float32)


def layer_norm(values):
    center = values - jnp.mean(values, axis=-1, keepdims=True)
    spread = jnp.mean(center * center, axis=-1, keepdims=True)
    return center * lax.rsqrt(spread + epsilon)


def hidden_total(picked, receiver_rows):
    return jnp.sum(jax.nn.silu(picked + receiver_rows[:, None, :]), axis=1)


def finish(receivers, hidden, output_weights, gain_vector):
    partial_value = project(hidden, output_weights)
    summed = lax.psum(partial_value, "sub")
    return receivers + gain_vector * layer_norm(summed)


def pick_rows(source_rows, wanted):
    inside = (wanted >= 0) & (wanted < source_rows.shape[0])
    picked = jnp.take(source_rows, jnp.clip(wanted, 0, source_rows.shape[0] - 1), axis=0)
    return jnp.where(inside[:, None], picked, 0.0)


def body(
    node_states,
    coarse_states,
    children,
    down_sources,
    bottom_links,
    coarse_links,
    upward_sender,
    upward_receiver,
    upward_bias,
    upward_output,
    upward_gain,
    coarse_sender,
    coarse_receiver,
    coarse_bias,
    coarse_output,
    coarse_gain,
    downward_sender,
    downward_receiver,
    downward_bias,
    downward_output,
    downward_gain,
    bottom_sender,
    bottom_receiver,
    bottom_bias,
    bottom_output,
    bottom_gain,
):
    sender_rows = project(node_states, upward_sender)
    receiver_rows = project(coarse_states, upward_receiver) + upward_bias
    picked = jnp.take(sender_rows, children, axis=0)
    coarse_up = finish(
        coarse_states, hidden_total(picked, receiver_rows), upward_output, upward_gain
    )
    receiver_rows = project(coarse_up, coarse_receiver) + coarse_bias
    flat_links = coarse_links.reshape(-1)
    own_projection = project(coarse_up, coarse_sender)
    gathered = pick_rows(
        lax.all_gather(own_projection, ("patch", "lvl"), axis=0, tiled=True), flat_links
    )
    picked = gathered.reshape(coarse_links.shape[0], coarse_links.shape[1], receiver_rows.shape[1])
    new_coarse = finish(coarse_up, hidden_total(picked, receiver_rows), coarse_output, coarse_gain)
    sender_rows = project(new_coarse, downward_sender)
    receiver_rows = project(node_states, downward_receiver) + downward_bias
    picked = jnp.take(sender_rows, down_sources, axis=0)
    nodes_down = finish(
        node_states, hidden_total(picked, receiver_rows), downward_output, downward_gain
    )
    rim_rows = node_states.shape[0] // 4
    receiver_rows = project(nodes_down, bottom_receiver) + bottom_bias
    own_projection = project(nodes_down, bottom_sender)
    sender_rows = extended(own_projection, ((("patch", "lvl"), 0),), rim_rows)
    picked = jnp.take(sender_rows, bottom_links, axis=0)
    new_nodes = finish(nodes_down, hidden_total(picked, receiver_rows), bottom_output, bottom_gain)
    return (new_nodes, new_coarse)


def solution(mesh):
    in_specs = (
        P(("parts", "patch", "lvl"), None),
        P(("parts", "patch", "lvl"), None),
        P(("patch", "lvl"), None),
        P(("patch", "lvl"), None),
        P(("patch", "lvl"), None),
        P(("patch", "lvl"), None),
        P(None, "sub"),
        P(None, "sub"),
        P("sub"),
        P("sub", None),
        P(),
        P(None, "sub"),
        P(None, "sub"),
        P("sub"),
        P("sub", None),
        P(),
        P(None, "sub"),
        P(None, "sub"),
        P("sub"),
        P("sub", None),
        P(),
        P(None, "sub"),
        P(None, "sub"),
        P("sub"),
        P("sub", None),
        P(),
    )
    out_specs = (P(("parts", "patch", "lvl"), None), P(("parts", "patch", "lvl"), None))
    return jax.shard_map(body, mesh=mesh, in_specs=in_specs, out_specs=out_specs, check_vma=False)
```

profile of v0, /device:TPU:0, one launch (start us, length us, event | category | flops | bytes accessed | tf_op | source)
XLA Modules:
  0.0 235.0 jit_solution(15321210769861987477)
XLA Ops:
  7.2 0.0 all-reduce.5.cloned.1.call-start
  7.2 0.7 compare_select_fusion.3
  8.0 0.7 compare_and_fusion.4
  8.7 0.1 copy.35
  8.8 0.1 reshape.129
  8.9 2.3 fusion.3
  11.3 1.7 gather_fusion
  13.1 0.1 reshape.128
  13.1 0.1 copy.34
  13.3 0.4 convolution_add_fusion.3
  13.7 0.3 multiply_reduce_fusion.4
  14.0 2.1 fusion.4
  16.2 0.0 all-reduce.7.cloned.1.call-start
  16.3 0.1 copy.38
  16.4 0.1 min.12
  16.6 2.0 convolution_add_fusion.1
  18.6 0.1 copy.36
  18.7 0.1 copy.37
  18.9 21.6 %all-reduce.5.cloned.1.call-done = f32[64,512]{1,0:T(8,128)} async-done(((f32[64,512]{1,0:T(8,128)}), f32[64,512]{1,0:T(8,128)}) %all-reduce.5.cloned.1.call-update) | async-done | bytes 131088 | tf_op jit(solution)/shard_map/psum | solution.py:42
  40.5 1.0 reduce_sum.109
  41.5 1.1 multiply_reduce_fusion.6
  42.6 1.0 multiply_add_fusion.3
  43.7 0.4 fusion.5
  44.0 14.7 %all_gather.3 = f32[512,256]{1,0:T(8,128)S(1)} all-gather(f32[64,256]{1,0:T(8,128)S(1)} %fusion.5), channel_id=1, replica_groups=mesh['parts'=2,'patch'=4,'sub'=2,'lvl'=2] {'patch','lvl'}, dimensions={0}, use_global_device_ids=true | all-gather | bytes 589824 | tf_op jit(solution)/shard_map/all_gather | solution.py:90
  58.8 1.7 gather_fusion.1
  60.5 0.1 gather.20
  60.5 1.5 convolution_add_fusion.2
  62.0 0.5 multiply_reduce_fusion.3
  62.5 2.1 fusion.6
  64.7 0.0 all-reduce.9.cloned.1.call-start
  64.7 0.1 copy.39
  64.9 0.2 reshape.145
  65.1 0.2 copy.33
  65.3 21.1 %all-reduce.7.cloned.1.call-done = f32[64,512]{1,0:T(8,128)} async-done(((f32[64,512]{1,0:T(8,128)}), f32[64,512]{1,0:T(8,128)}) %all-reduce.7.cloned.1.call-update) | async-done | bytes 131088 | tf_op jit(solution)/shard_map/psum | solution.py:42
  86.4 1.0 reduce_sum.112
  87.5 1.1 multiply_reduce_fusion.5
  88.6 1.0 multiply_add_fusion.2
  89.6 0.4 fusion.7
  90.0 4.7 %gather_fusion.2 = f32[1536,256]{1,0:T(8,128)} fusion(f32[64,256]{1,0:T(8,128)S(1)} %fusion.7, s32[2048]{0:T(1024)S(1)} %pad_clamp_fusion), kind=kCustom, calls=%fused_computation.2 | custom fusion | bytes 3151872 | tf_op jit(solution)/shard_map/jit(_take)/gather | solution.py:96
  94.7 3.6 %reshape.144 = f32[512,3,256]{2,1,0:T(4,128)} reshape(f32[1536,256]{1,0:T(8,128)} %gather_fusion.2) | data formatting | bytes 3145728 | tf_op jit(solution)/shard_map/jit(_take)/gather | solution.py:96
  98.3 4.4 %fusion = f32[512,256]{1,0:T(8,128)S(1)} fusion(f32[512,3,256]{2,1,0:T(4,128)} %reshape.144, f32[512,256]{1,0:T(8,128)S(1)} %convolution_add_fusion.1, pred[512,3]{1,0:T(8,128)(4,1)S(1)} %copy.33), kind=kLoop, calls=%fused_computation.6 | loop fusion | flops 2621440 | bytes 2622976 | tf_op jit(solution)/shard_map/reduce_sum | solution.py:37
  102.8 2.0 fusion.8
  104.8 0.2 all-reduce.11.cloned.1.call-start
  105.0 0.1 copy.41
  105.2 0.2 reshape.153
  105.4 0.2 copy.40
  105.6 39.4 %all-reduce.9.cloned.1.call-done = f32[512,512]{1,0:T(8,128)} async-done(((f32[512,512]{1,0:T(8,128)}), f32[512,512]{1,0:T(8,128)}) %all-reduce.9.cloned.1.call-update) | async-done | bytes 1048592 | tf_op jit(solution)/shard_map/psum | solution.py:42
  145.0 1.4 reduce_sum.115
  146.4 1.5 multiply_reduce_fusion.2
  147.9 1.5 multiply_add_fusion.1
  149.4 1.0 fusion.9
  150.4 0.1 collective-permute-start
  150.5 3.5 %collective-permute-start.1 = (f32[128,256]{1,0:T(8,128)S(1)}, f32[128,256]{1,0:T(8,128)S(1)}, u32[]{:S(2)}, u32[]{:S(2)}) collective-permute-start(f32[128,256]{1,0:T(8,128)S(1)} %get-tuple-element.3), channel_id=1, source_target_pairs={{1,0},{4,1},{5,4},{8,5},{9,8},{12,9},{13,12},{0,13},{3,2},{6,3},{7... | collective-permute-start | bytes 393224 | tf_op jit(solution)/shard_map/ppermute | solution.py:19
  154.0 1.0 convolution_add_fusion
  155.0 1.8 collective-permute-done
  156.8 0.1 pad_maximum_fusion
  156.9 12.3 %gather_fusion.3 = f32[3072,256]{1,0:T(8,128)} fusion(f32[768,256]{1,0:T(8,128)S(1)} %pad_maximum_fusion, s32[3072]{0:T(1024)S(1)} %broadcast_clamp_fusion), kind=kCustom, calls=%fused_computation.3 | custom fusion | bytes 6303744 | tf_op jit(solution)/shard_map/jit(_take)/gather | solution.py:104
  169.2 4.5 %reshape.152 = f32[512,6,256]{2,1,0:T(8,128)} reshape(f32[3072,256]{1,0:T(8,128)} %gather_fusion.3) | data formatting | bytes 6291456 | tf_op jit(solution)/shard_map/jit(_take)/gather | solution.py:104
  173.7 7.1 %multiply_reduce_fusion = f32[512,256]{1,0:T(8,128)S(1)} fusion(f32[512,6,256]{2,1,0:T(8,128)} %reshape.152, f32[512,256]{1,0:T(8,128)S(1)} %convolution_add_fusion, pred[512,6]{1,0:T(8,128)(4,1)S(1)} %copy.40), kind=kLoop, calls=%fused_computation.4 | loop fusion | flops 5373952 | bytes 4197376 | tf_op jit(solution)/shard_map/reduce_sum | solution.py:37
  180.9 2.0 fusion.10
  182.9 40.3 %all-reduce.11.cloned.1.call-done = f32[512,512]{1,0:T(8,128)} async-done(((f32[512,512]{1,0:T(8,128)}), f32[512,512]{1,0:T(8,128)}) %all-reduce.11.cloned.1.call-update) | async-done | bytes 1048592 | tf_op jit(solution)/shard_map/psum | solution.py:42
  223.2 1.4 reduce_sum.118
  224.6 1.5 multiply_reduce_fusion.1
  226.1 2.4 %multiply_add_fusion = f32[512,512]{1,0:T(8,128)} fusion(f32[512,512]{1,0:T(8,128)S(1)} %multiply_add_fusion.1, f32[512,512]{1,0:T(8,128)} %all-reduce.11.cloned.1.call-done, f32[512]{0:T(512)S(1)} %add_rsqrt_fusion, f32[512]{0:T(512)S(1)} %broadcast_multiply_fusion, f32[512]{0:T(512)S(1)} %copy-done.16), kind=kLoop, calls=%fused_computation.11 | loop fusion | flops 1048576 | bytes 3151872 | tf_op jit(solution)/shard_map/add | solution.py:43
  (67 shorter events, 0.3 us)
Async XLA Ops:
  7.2 95.6 %copy-start = (f32[256,512]{1,0:T(8,128)S(1)}, f32[256,512]{1,0:T(8,128)}, u32[]{:S(2)}) copy-start(f32[256,512]{1,0:T(8,128)} %param.45) | copy-start | bytes 1572868
  7.2 33.3 %all-reduce.5.cloned.1.call-start = ((), (), s32[]{:S(2)}) async-start(), calls=%async_computation | async-start | bytes 262144 | tf_op jit(solution)/shard_map/psum | solution.py:42
  11.3 2.0 copy-start.2
  11.3 2.0 copy-start.5
  11.3 2.0 copy-start.17
  11.3 4.9 %copy-start.12 = (s32[64,6]{0,1:T(8,128)S(1)}, s32[64,6]{0,1:T(8,128)}, u32[]{:S(2)}) copy-start(s32[64,6]{0,1:T(8,128)} %param.31) | copy-start | bytes 4612
  11.3 5.2 %copy-start.11 = (s32[512,3]{0,1:T(4,128)S(1)}, s32[512,3]{0,1:T(4,128)}, u32[]{:S(2)}) copy-start(s32[512,3]{0,1:T(4,128)} %param.29) | copy-start | bytes 18436
  11.3 5.2 %copy-start.1 = (f32[512,512]{1,0:T(8,128)S(1)}, f32[512,512]{1,0:T(8,128)}, u32[]{:S(2)}) copy-start(f32[512,512]{1,0:T(8,128)} %param.26) | copy-start | bytes 3145732
  11.3 5.2 %copy-start.18 = (f32[256]{0:T(256)S(1)}, f32[256]{0:T(256)}, u32[]{:S(2)}) copy-start(f32[256]{0:T(256)} %param.44) | copy-start | bytes 3076
  13.1 29.6 %copy-start.13 = (f32[512]{0:T(512)S(1)}, f32[512]{0:T(512)}, u32[]{:S(2)}) copy-start(f32[512]{0:T(512)} %param.36) | copy-start | bytes 6148
  13.7 30.0 %copy-start.3 = (f32[512,256]{1,0:T(8,128)S(1)}, f32[512,256]{1,0:T(8,128)}, u32[]{:S(2)}) copy-start(f32[512,256]{1,0:T(8,128)} %param.37) | copy-start | bytes 1572868
  16.2 70.2 %all-reduce.7.cloned.1.call-start = ((), (), s32[]{:S(2)}) async-start(), calls=%async_computation.1 | async-start | bytes 262144 | tf_op jit(solution)/shard_map/psum | solution.py:42
  41.5 19.0 %copy-start.19 = (f32[256]{0:T(256)S(1)}, f32[256]{0:T(256)}, u32[]{:S(2)}) copy-start(f32[256]{0:T(256)} %param.39) | copy-start | bytes 3076
  58.8 29.8 %copy-start.14 = (f32[512]{0:T(512)S(1)}, f32[512]{0:T(512)}, u32[]{:S(2)}) copy-start(f32[512]{0:T(512)} %param.41) | copy-start | bytes 6148
  60.5 29.1 %copy-start.4 = (f32[512,256]{1,0:T(8,128)S(1)}, f32[512,256]{1,0:T(8,128)}, u32[]{:S(2)}) copy-start(f32[512,256]{1,0:T(8,128)} %param.42) | copy-start | bytes 1572868
  64.7 80.3 %all-reduce.9.cloned.1.call-start = ((), (), s32[]{:S(2)}) async-start(), calls=%async_computation.2 | async-start | bytes 2097152 | tf_op jit(solution)/shard_map/psum | solution.py:42
  89.6 5.1 %copy-start.6 = (f32[64,512]{1,0:T(8,128)}, f32[64,512]{1,0:T(8,128)S(1)}, u32[]{:S(2)}) copy-start(f32[64,512]{1,0:T(8,128)S(1)} %multiply_add_fusion.2) | copy-start | bytes 393220
  98.3 6.7 %copy-start.10 = (s32[512,6]{0,1:T(8,128)S(1)}, s32[512,6]{0,1:T(8,128)}, u32[]{:S(2)}) copy-start(s32[512,6]{0,1:T(8,128)} %param.30) | copy-start | bytes 36868
  102.7 45.1 %copy-start.15 = (f32[512]{0:T(512)S(1)}, f32[512]{0:T(512)}, u32[]{:S(2)}) copy-start(f32[512]{0:T(512)} %param.46) | copy-start | bytes 6148
  104.8 44.6 %copy-start.7 = (f32[512,256]{1,0:T(8,128)S(1)}, f32[512,256]{1,0:T(8,128)}, u32[]{:S(2)}) copy-start(f32[512,256]{1,0:T(8,128)} %param.47) | copy-start | bytes 1572868
  104.8 118.4 %all-reduce.11.cloned.1.call-start = ((), (), s32[]{:S(2)}) async-start(), calls=%async_computation.3 | async-start | bytes 2097152 | tf_op jit(solution)/shard_map/psum | solution.py:42
  147.8 6.2 %copy-start.8 = (f32[512,256]{1,0:T(8,128)S(1)}, f32[512,256]{1,0:T(8,128)}, u32[]{:S(2)}) copy-start(f32[512,256]{1,0:T(8,128)} %param.48) | copy-start | bytes 1572868
  147.9 6.2 %copy-start.20 = (f32[256]{0:T(256)S(1)}, f32[256]{0:T(256)}, u32[]{:S(2)}) copy-start(f32[256]{0:T(256)} %param.49) | copy-start | bytes 3076
  150.4 6.4 %collective-permute-start = (f32[128,256]{1,0:T(8,128)S(1)}, f32[128,256]{1,0:T(8,128)S(1)}, u32[]{:S(2)}, u32[]{:S(2)}) collective-permute-start(f32[128,256]{1,0:T(8,128)S(1)} %get-tuple-element.2), channel_id=1, source_target_pairs={{0,1},{1,4},{4,5},{5,8},{8,9},{9,12},{12,13},{13,0},{2,3},{3,6},{6... | collective-permute-start | bytes 393224 | tf_op jit(solution)/shard_map/ppermute | solution.py:17
  150.5 6.3 %collective-permute-start.1 = (f32[128,256]{1,0:T(8,128)S(1)}, f32[128,256]{1,0:T(8,128)S(1)}, u32[]{:S(2)}, u32[]{:S(2)}) collective-permute-start(f32[128,256]{1,0:T(8,128)S(1)} %get-tuple-element.3), channel_id=1, source_target_pairs={{1,0},{4,1},{5,4},{8,5},{9,8},{12,9},{13,12},{0,13},{3,2},{6,3},{7... | collective-permute-start | bytes 393224 | tf_op jit(solution)/shard_map/ppermute | solution.py:19
  173.7 7.1 %copy-start.9 = (f32[256,512]{1,0:T(8,128)S(1)}, f32[256,512]{1,0:T(8,128)}, u32[]{:S(2)}) copy-start(f32[256,512]{1,0:T(8,128)} %param.50) | copy-start | bytes 1572868
  180.9 45.2 %copy-start.16 = (f32[512]{0:T(512)S(1)}, f32[512]{0:T(512)}, u32[]{:S(2)}) copy-start(f32[512]{0:T(512)} %param.51) | copy-start | bytes 6148
Sparse Core Ops, SparseCore 0:
  16.3 24.1 all-reduce.4
  64.8 21.5 all-reduce.6
  104.9 40.0 all-reduce.8
  183.0 40.1 all-reduce.10
where the time goes:
time: 236 us; the launch traced here: 235 us
  waiting for transfers between devices  124 us (53%)
  local copies, waits for them, and re-layouts  30.7 us (13%)
  other arithmetic  29.8 us (13%)
  matrix products  17.2 us (7%)
  blocking collectives  14.7 us (6%)
  between operations  14.4 us (6%)
  starting transfers between devices  3.93 us (2%)
    psum x4, waiting for transfers between devices, finish(): summed = lax.psum(partial_value, 'sub')  122 us
    dot_general x12, matrix products, project(): jnp.dot(states, weights, precision=highest, preferred_element_type=jnp.fl...  17.2 us
    gather x2, local copies, waits for them, and re-layouts, body(): picked = jnp.take(sender_rows, bottom_links, axis=0)  16.9 us
    all_gather x1, blocking collectives, body(): lax.all_gather(own_projection, ('patch', 'lvl'), axis=0, tiled=True)  14.7 us
    reduce_sum x4, other arithmetic, hidden_total(): return jnp.sum(jax.nn.silu(picked + receiver_rows[:, None, :]), axis=1)  12.4 us
    gather x2, local copies, waits for them, and re-layouts, body(): picked = jnp.take(sender_rows, down_sources, axis=0)  8.31 us
    add x4, other arithmetic, finish(): return receivers + gain_vector * layer_norm(summed)  5.93 us
    reduce_sum x4, other arithmetic, layer_norm(): spread = jnp.mean(center * center, axis=-1, keepdims=True)  5.13 us
  transfers between devices with their start and end apart: 6, of which 5 were waited for; matrix products, arithmetic and copies ran while one was open for 2% of the time, Pallas kernels for 0%

commit v1 on v0

v1 whole, which is shorter than its diff:
```python
import functools

import jax
import jax.numpy as jnp
from jax import lax
from jax.experimental import pallas as pl
from jax.experimental.pallas import tpu as pltpu
from jax.sharding import PartitionSpec as P

epsilon = 1e-05
f32 = jnp.float32
bf16 = jnp.bfloat16
limit_bytes = 40 * 1024 * 1024
most_direct = 4


def split(values):
    high = values.astype(bf16)
    return high, (values - high.astype(f32)).astype(bf16)


def dot(a, b):
    return jnp.dot(a, b, preferred_element_type=f32)


def dot3(a, b_high, b_low):
    a_high, a_low = split(a)
    return dot(a_high, b_high) + (dot(a_high, b_low) + dot(a_low, b_high))


def normed(values):
    center = values - jnp.mean(values, axis=-1, keepdims=True)
    spread = jnp.mean(center * center, axis=-1, keepdims=True)
    return center * lax.rsqrt(spread + epsilon)


def one_hot(wanted, names):
    return jnp.concatenate(
        [
            jnp.where(wanted[:, k : k + 1] == names, 1.0, 0.0).astype(bf16)
            for k in range(wanted.shape[1])
        ],
        axis=0,
    )


def silu_sum(picked, halves, count):
    rows = halves.shape[0]
    total = None
    for k in range(count):
        u = picked[k * rows : (k + 1) * rows] + halves
        term = u + u * jnp.tanh(u)
        total = term if total is None else total + term
    return total


def added(refs):
    total = refs[0][...]
    for ref in refs[1:]:
        total = total + ref[...]
    return total


def upward_kernel(nodes, coarse, children, ws, wr, bias, wo, part):
    sender_high, sender_low = split(0.5 * dot3(nodes[...], *split(ws[...])))
    receivers = 0.5 * (dot3(coarse[...], *split(wr[...])) + bias[...])
    wanted = children[...]
    names = lax.broadcasted_iota(jnp.int32, (wanted.shape[0], nodes.shape[0]), 1)
    picks = one_hot(wanted, names)
    picked = dot(picks, sender_high) + dot(picks, sender_low)
    hidden = silu_sum(picked, receivers, wanted.shape[1])
    part[...] = dot3(hidden, *split(wo[...]))


def coarse_project_kernel(count, *refs):
    parts, (coarse, gain, ws, wr, bias, updated, senders, receivers) = refs[:count], refs[count:]
    rows = coarse[...] + gain[...] * normed(added(parts))
    updated[...] = rows
    senders[...] = 0.5 * dot3(rows, *split(ws[...]))
    receivers[...] = 0.5 * (dot3(rows, *split(wr[...])) + bias[...])


def coarse_kernel(count, *refs):
    pieces, (links, names, receivers, wo, part) = refs[:count], refs[count:]
    senders = jnp.concatenate([piece[...] for piece in pieces], axis=0)
    sender_high, sender_low = split(senders)
    wanted = links[...]
    picks = one_hot(wanted, jnp.broadcast_to(names[...], (wanted.shape[0], names.shape[1])))
    picked = dot(picks, sender_high) + dot(picks, sender_low)
    hidden = silu_sum(picked, receivers[...], wanted.shape[1])
    part[...] = dot3(hidden, *split(wo[...]))


def collect(own, packs, outs):
    ws, wr, bias, wo = own
    ws_high, ws_low, wr_high, wr_low, wo_high, wo_low, bias_all = outs
    subs, lvls = lax.axis_size("sub"), lax.axis_size("lvl")
    sub, lvl = lax.axis_index("sub"), lax.axis_index("lvl")
    depth, width = ws.shape
    ws_high[sub], ws_low[sub] = split(ws[...])
    wr_high[sub], wr_low[sub] = split(wr[...])
    rows = pl.ds(pl.multiple_of(sub * width, width), width)
    wo_high[rows, :], wo_low[rows, :] = split(wo[...])
    bias_all[sub] = jnp.broadcast_to(bias[...], (8, width))
    share, thin = depth // lvls, width // lvls
    for s in range(1, subs):
        block = lax.rem(sub + subs - s, subs)
        for t in range(lvls):
            pack = packs[(s - 1) * lvls + t]
            level = lax.rem(lvl + lvls - t, lvls)
            rows = pl.ds(pl.multiple_of(level * share, share), share)
            ws_high[block, rows, :], ws_low[block, rows, :] = split(pack[0:share, :])
            wr_high[block, rows, :], wr_low[block, rows, :] = split(pack[share : 2 * share, :])
            rows = pl.ds(pl.multiple_of(block * width + level * thin, thin), thin)
            for j in range(wo.shape[1] // width):
                high, low = split(pack[2 * share + j * thin : 2 * share + (j + 1) * thin, :])
                wo_high[rows, j * width : (j + 1) * width] = high
                wo_low[rows, j * width : (j + 1) * width] = low
            if t == 0:
                bias_all[block] = pack[pack.shape[0] - 8 :, :]


def down_ready_kernel(count, nodes, ws, wr, bias, wo, *refs):
    packs = refs[:count]
    receivers, ws_high, ws_low, wo_high, wo_low, wr_high, wr_low, bias_all = refs[count:]
    collect(
        (ws, wr, bias, wo), packs, (ws_high, ws_low, wr_high, wr_low, wo_high, wo_low, bias_all)
    )
    width = ws.shape[1]
    for g in range(ws_high.shape[0]):
        product = dot3(nodes[...], wr_high[g], wr_low[g])
        receivers[:, g * width : (g + 1) * width] = 0.5 * (product + bias_all[g][0:1])


def bottom_ready_kernel(count, ws, wr, bias, wo, *refs):
    collect((ws, wr, bias, wo), refs[:count], refs[count:])


def down_rows(nodes, receivers, sources, senders, wo_high, wo_low, gain):
    blocks = senders.shape[0] // 2
    column = lax.broadcasted_iota(jnp.int32, (nodes.shape[0], 2 * blocks), 1)
    names = jnp.where(column < blocks, column, column - blocks)
    picked = dot(one_hot(sources, names), senders)
    hidden = silu_sum(picked, receivers, sources.shape[1])
    return nodes + gain * normed(dot3(hidden, wo_high, wo_low))


def down_edge_kernel(count, rim, *refs):
    parts, refs = refs[:count], refs[count:]
    (coarse_up, coarse_gain, nodes, receivers, sources, ws_high, ws_low, wo_high, wo_low, gain) = refs[:10]
    new_coarse, senders, head, tail = refs[10:]
    rows = coarse_up[...] + coarse_gain[...] * normed(added(parts))
    new_coarse[...] = rows
    blocks = rows.shape[0]
    width = ws_high.shape[2]
    for g in range(ws_high.shape[0]):
        columns = slice(g * width, (g + 1) * width)
        high, low = split(0.5 * dot3(rows, ws_high[g], ws_low[g]))
        senders[0:blocks, columns] = high
        senders[blocks : 2 * blocks, columns] = low
    total = nodes.shape[0]
    for out, place in ((head, slice(0, rim)), (tail, slice(total - rim, total))):
        out[...] = down_rows(
            nodes[place], receivers[place], sources[place], senders[...], wo_high[...], wo_low[...], gain[...]
        )


def down_middle_kernel(rim, nodes, receivers, sources, senders, wo_high, wo_low, gain, middle):
    place = slice(rim, nodes.shape[0] - rim)
    middle[...] = down_rows(
        nodes[place], receivers[place], sources[place], senders[...], wo_high[...], wo_low[...], gain[...]
    )


def bottom_rows(nodes, receivers, links, start, sender_high, sender_low, wo_high, wo_low, gain):
    rows, reach = nodes.shape[0], sender_high.shape[0]
    names = start + lax.broadcasted_iota(jnp.int32, (rows, reach), 1)
    picks = one_hot(links, names)
    half = wo_high.shape[0] // 2
    hidden = []
    for place in (slice(0, half), slice(half, 2 * half)):
        picked = dot(picks, sender_high[:, place]) + dot(picks, sender_low[:, place])
        hidden.append(silu_sum(picked, receivers[:, place], links.shape[1]))
    return nodes + gain * normed(dot3(jnp.concatenate(hidden, axis=1), wo_high, wo_low))


def bottom_middle_kernel(rim, head, middle, tail, links, ws_high, ws_low, wr_high, wr_low, wo_high, wo_low, bias, gain, senders_high, senders_low, receivers, out):
    nodes = jnp.concatenate([head[...], middle[...], tail[...]], axis=0)
    nodes_high, nodes_low = split(nodes)
    width = ws_high.shape[2]
    for g in range(ws_high.shape[0]):
        columns = slice(g * width, (g + 1) * width)
        product = dot(nodes_high, ws_high[g]) + (dot(nodes_high, ws_low[g]) + dot(nodes_low, ws_high[g]))
        senders_high[:, columns], senders_low[:, columns] = split(0.5 * product)
        product = dot(nodes_high, wr_high[g]) + (dot(nodes_high, wr_low[g]) + dot(nodes_low, wr_high[g]))
        receivers[:, columns] = 0.5 * (product + bias[g][0:1])
    total = nodes.shape[0]
    for first in range(rim, total - rim, rim):
        place = slice(first, first + rim)
        reach = slice(first - rim, first + 2 * rim)
        out[first - rim : first, :] = bottom_rows(
            middle[first - rim : first], receivers[place], links[place], first,
            senders_high[reach], senders_low[reach], wo_high[...], wo_low[...], gain[...],
        )


def bottom_edge_kernel(rim, before, after, head, tail, inner, links, senders_high, senders_low, receivers, ws_high, ws_low, wo_high, wo_low, gain, out):
    total = links.shape[0]
    out[rim : total - rim, :] = inner[...]
    edges = ((before, head, slice(0, rim), slice(0, 2 * rim)), (after, tail, slice(total - rim, total), slice(total - 2 * rim, total)))
    outer = split(jnp.concatenate([before[...], after[...]], axis=0))
    projected = jnp.concatenate(
        [
            dot(outer[0], ws_high[g]) + (dot(outer[0], ws_low[g]) + dot(outer[1], ws_high[g]))
            for g in range(ws_high.shape[0])
        ],
        axis=1,
    )
    outer_high, outer_low = split(0.5 * projected)
    for side, (nodes, place, reach) in enumerate(
        ((head, slice(0, rim), slice(0, 2 * rim)), (tail, slice(total - rim, total), slice(total - 2 * rim, total)))
    ):
        strip = slice(side * rim, (side + 1) * rim)
        order = (lambda a, b: [a, b]) if side == 0 else (lambda a, b: [b, a])
        high = jnp.concatenate(order(outer_high[strip], senders_high[reach]), axis=0)
        low = jnp.concatenate(order(outer_low[strip], senders_low[reach]), axis=0)
        out[place, :] = bottom_rows(
            nodes[...], receivers[place], links[place], 0 if side == 0 else total - rim,
            high, low, wo_high[...], wo_low[...], gain[...],
        )


def call(kernel, outs, operands, flops, scratch=()):
    moved = sum(x.size * x.dtype.itemsize for x in (*outs, *operands))
    whole = pl.BlockSpec(memory_space=pltpu.VMEM)
    return pl.pallas_call(
        kernel,
        out_shape=tuple(outs),
        in_specs=[whole] * len(operands),
        out_specs=tuple([whole] * len(outs)),
        scratch_shapes=list(scratch),
        compiler_params=pltpu.CompilerParams(vmem_limit_bytes=limit_bytes),
        cost_estimate=pl.CostEstimate(flops=int(flops), bytes_accessed=moved, transcendentals=0),
    )(*operands)


def like(shape, kind=f32):
    return jax.ShapeDtypeStruct(tuple(shape), kind)


def shifted(values, axis, step):
    count = lax.axis_size(axis)
    return lax.ppermute(values, axis, [(i, (i + step) % count) for i in range(count)])


def sub_parts(part):
    if lax.axis_size("sub") == 2:
        return [part, shifted(part, "sub", 1)]
    return [lax.psum(part, "sub")]


def coarse_pieces(senders):
    patches, lvls = lax.axis_size("patch"), lax.axis_size("lvl")
    rows = senders.shape[0]
    if patches > most_direct:
        return (
            [lax.all_gather(senders, ("patch", "lvl"), axis=0, tiled=True)],
            jnp.arange(rows * patches * lvls, dtype=jnp.int32)[None],
        )
    pieces = [senders] + [shifted(senders, "patch", s) for s in range(1, patches)]
    everything = list(pieces)
    for t in range(1, lvls):
        everything += [shifted(piece, "lvl", t) for piece in pieces]
    place = jnp.arange(rows * patches * lvls, dtype=jnp.int32)
    step, away = (place // rows) % patches, place // (rows * patches)
    patch = (lax.axis_index("patch") - step) % patches
    lvl = (lax.axis_index("lvl") - away) % lvls
    return everything, ((patch * lvls + lvl) * rows + place % rows)[None].astype(jnp.int32)


def packed(ws, wr, bias, wo):
    lvls, lvl = lax.axis_size("lvl"), lax.axis_index("lvl")
    depth, width = ws.shape
    share, thin = depth // lvls, width // lvls
    strip = lax.dynamic_slice_in_dim(wo, lvl * thin, thin, axis=0)
    return jnp.concatenate(
        [
            lax.dynamic_slice_in_dim(ws, lvl * share, share, axis=0),
            lax.dynamic_slice_in_dim(wr, lvl * share, share, axis=0),
            *(strip[:, j * width : (j + 1) * width] for j in range(wo.shape[1] // width)),
            jnp.broadcast_to(bias[None], (8, width)),
        ],
        axis=0,
    )


def fetched(pack):
    packs = []
    for s in range(1, lax.axis_size("sub")):
        share = shifted(pack, "sub", s)
        packs += [share] + [shifted(share, "lvl", t) for t in range(1, lax.axis_size("lvl"))]
    return packs


def body(
    node_states,
    coarse_states,
    children,
    down_sources,
    bottom_links,
    coarse_links,
    upward_sender,
    upward_receiver,
    upward_bias,
    upward_output,
    upward_gain,
    coarse_sender,
    coarse_receiver,
    coarse_bias,
    coarse_output,
    coarse_gain,
    downward_sender,
    downward_receiver,
    downward_bias,
    downward_output,
    downward_gain,
    bottom_sender,
    bottom_receiver,
    bottom_bias,
    bottom_output,
    bottom_gain,
):
    rows, latent = node_states.shape
    blocks = coarse_states.shape[0]
    width = upward_sender.shape[1]
    subs = lax.axis_size("sub")
    hidden = width * subs
    rim = rows // 4
    weights = [like((subs, latent, width), bf16)] * 2
    outputs = [like((hidden, latent), bf16)] * 2
    biases = like((subs, 8, width))

    down_packs = fetched(packed(downward_sender, downward_receiver, downward_bias, downward_output))
    bottom_packs = fetched(packed(bottom_sender, bottom_receiver, bottom_bias, bottom_output))

    (part,) = call(
        upward_kernel,
        [like((blocks, latent))],
        [node_states, coarse_states, children, upward_sender, upward_receiver, upward_bias[None], upward_output],
        6 * rows * latent * width + 4 * children.size * rows * width,
    )
    parts = sub_parts(part)
    coarse_up, senders, receivers = call(
        functools.partial(coarse_project_kernel, len(parts)),
        [like((blocks, latent)), like((blocks, width)), like((blocks, width))],
        [*parts, coarse_states, upward_gain[None], coarse_sender, coarse_receiver, coarse_bias[None]],
        12 * blocks * latent * width,
    )
    pieces, names = coarse_pieces(senders)
    (part,) = call(
        functools.partial(coarse_kernel, len(pieces)),
        [like((blocks, latent))],
        [*pieces, coarse_links, names, receivers, coarse_output],
        4 * coarse_links.size * names.size * width,
    )
    parts = sub_parts(part)

    receivers, ws_high, ws_low, wo_high, wo_low = call(
        functools.partial(down_ready_kernel, len(down_packs)),
        [like((rows, hidden)), *weights, *outputs],
        [node_states, downward_sender, downward_receiver, downward_bias[None], downward_output, *down_packs],
        6 * rows * latent * hidden,
        [pltpu.VMEM((subs, latent, width), bf16)] * 2 + [pltpu.VMEM((subs, 8, width), f32)],
    )
    new_coarse, senders, head, tail = call(
        functools.partial(down_edge_kernel, len(parts), rim),
        [like((blocks, latent)), like((2 * blocks, hidden), bf16), like((rim, latent)), like((rim, latent))],
        [*parts, coarse_up, coarse_gain[None], node_states, receivers, down_sources, ws_high, ws_low, wo_high, wo_low, downward_gain[None]],
        6 * 2 * rim * latent * hidden,
    )
    ring = ("patch", "lvl")
    before, after = shifted(tail, ring, 1), shifted(head, ring, -1)
    (middle,) = call(
        functools.partial(down_middle_kernel, rim),
        [like((rows - 2 * rim, latent))],
        [node_states, receivers, down_sources, senders, wo_high, wo_low, downward_gain[None]],
        6 * (rows - 2 * rim) * latent * hidden,
    )

    ws_high, ws_low, wr_high, wr_low, wo_high, wo_low, bias = call(
        functools.partial(bottom_ready_kernel, len(bottom_packs)),
        [*weights, *weights, *outputs, biases],
        [bottom_sender, bottom_receiver, bottom_bias[None], bottom_output, *bottom_packs],
        latent * hidden,
    )
    senders_high, senders_low, receivers, inner = call(
        functools.partial(bottom_middle_kernel, rim),
        [like((rows, hidden), bf16), like((rows, hidden), bf16), like((rows, hidden)), like((rows - 2 * rim, latent))],
        [head, middle, tail, bottom_links, ws_high, ws_low, wr_high, wr_low, wo_high, wo_low, bias, bottom_gain[None]],
        (12 * rows + 12 * rows) * latent * hidden,
    )
    (new_nodes,) = call(
        functools.partial(bottom_edge_kernel, rim),
        [like((rows, latent))],
        [before, after, head, tail, inner, bottom_links, senders_high, senders_low, receivers, ws_high, ws_low, wo_high, wo_low, bottom_gain[None]],
        24 * rim * latent * hidden,
    )
    return (new_nodes, new_coarse)


def solution(mesh):
    split_rows, level_rows = P(("parts", "patch", "lvl"), None), P(("patch", "lvl"), None)
    weights = (P(None, "sub"), P(None, "sub"), P("sub"), P("sub", None), P())
    in_specs = (split_rows, split_rows, *([level_rows] * 4), *(weights * 4))
    out_specs = (split_rows, split_rows)
    return jax.shard_map(body, mesh=mesh, in_specs=in_specs, out_specs=out_specs, check_vma=False)
```

time: 236 us -> 103 us (0.44)
  waiting for transfers between devices: 124 us -> 43.7 us
  other arithmetic: 29.8 us -> 0.03 us
  Pallas kernels: 0 us -> 22 us
  matrix products: 17.2 us -> 0 us
  blocking collectives: 14.7 us -> 0 us
  between operations: 14.4 us -> 0.9 us
  starting transfers between devices: 3.93 us -> 15.2 us
  local copies, waits for them, and re-layouts: 30.7 us -> 20.5 us
    psum x4 -> x0, waiting for transfers between devices: 122 us -> none  [finish(): summed = lax.psum(partial_value, 'sub')]
    ppermute x2 -> x15, waiting for transfers between devices: 1.79 us -> 43.7 us  [shifted(): lax.ppermute(values, axis, [(i, (i + step) % count) for i in range(count)])]
    gather x8 -> x0, local copies, waits for them, and re-layouts: 28.7 us -> none  [the longest x2 16.9 us: body(): picked = jnp.take(sender_rows, bottom_links, axis=0)]
    reduce_sum x12 -> x0, other arithmetic: 22.3 us -> none  [the longest x4 12.4 us: hidden_total(): return jnp.sum(jax.nn.silu(picked + receiver_rows[:, None, :]), axis=1)]
    pallas_call x0 -> x9, Pallas kernels: none -> 22 us  [call(): pl.pallas_call(kernel, out_shape=tuple(outs), in_specs=[whole] * len(oper...]
    unnamed x42 -> x79, local copies, waits for them, and re-layouts: 0.13 us -> 19.3 us
    dot_general x12 -> x0, matrix products: 17.2 us -> none  [project(): jnp.dot(states, weights, precision=highest, preferred_element_type=jnp.fl...]
    all_gather x1 -> x0, blocking collectives: 14.7 us -> none  [body(): lax.all_gather(own_projection, ('patch', 'lvl'), axis=0, tiled=True)]
  transfers between devices with their start and end apart: 6 -> 15, of which waited for: 5 -> 7; matrix products, arithmetic and copies ran while one was open for 2% -> 4% of each run, Pallas kernels for 0% -> 17%
where the time goes in v1:
time: 103 us; the launch traced here: 102 us
  waiting for transfers between devices  43.7 us (42%)
  Pallas kernels  22 us (21%)
  local copies, waits for them, and re-layouts  20.5 us (20%)
  starting transfers between devices  15.2 us (15%)
    ppermute x15, waiting for transfers between devices, shifted(): lax.ppermute(values, axis, [(i, (i + step) % count) for i in range(count)])  43.7 us
    pallas_call x9, Pallas kernels, call(): pl.pallas_call(kernel, out_shape=tuple(outs), in_specs=[whole] * len(oper...  22 us
    unnamed x79, local copies, waits for them, and re-layouts  19.3 us
    ppermute x15, starting transfers between devices, shifted(): lax.ppermute(values, axis, [(i, (i + step) % count) for i in range(count)])  15.2 us
  transfers between devices with their start and end apart: 15, of which 7 were waited for; matrix products, arithmetic and copies ran while one was open for 4% of the time, Pallas kernels for 17%

profile of v1, /device:TPU:0, one launch (start us, length us, event | category | flops | bytes accessed | tf_op | source)
XLA Modules:
  0.0 102.4 jit_solution(2838000243383567657)
XLA Ops:
  0.7 1.8 %dynamic-slice_dynamic-update-slice_fusion.3 = f32[776,256]{1,0:T(8,128)} fusion(f32[512,256]{1,0:T(8,128)} %ws.4, s32[]{:T(128)S(6)} %select_n.85), kind=kLoop, calls=%fused_computation.3 | loop fusion | bytes 524292
  2.4 0.7 dynamic-slice_dynamic-update-slice_fusion.1
  3.2 1.9 %dynamic-slice_dynamic-update-slice_fusion = (f32[776,256]{1,0:T(8,128)}, f32[776,256]{1,0:T(8,128)}) fusion(f32[776,256]{1,0:T(8,128)} %dynamic-slice_dynamic-update-slice_fusion.1, f32[512,256]{1,0:T(8,128)} %wr.5, s32[]{:T(128)S(6)} %select_n.85, f32[776,256]{1,0:T(8,128)} %dynamic-slice_dynamic-update-slice_fusion.3, f32[512,256]{1,0:T(8,128)S(1)} %copy-done.3), kind=kLoop, calls=%fused_computation | loop fusion | bytes 1048580
  5.0 0.7 dynamic-slice_dynamic-update-slice_fusion.7
  5.7 0.7 dynamic-slice_dynamic-update-slice_fusion.6
  6.4 0.6 constant_dynamic-update-slice_fusion
  7.0 2.9 %collective-permute-start.9 = (f32[776,256]{1,0:T(8,128)}, f32[776,256]{1,0:T(8,128)}, u32[]{:S(2)}, u32[]{:S(2)}) collective-permute-start(f32[776,256]{1,0:T(8,128)} %constant_dynamic-update-slice_fusion), channel_id=1, source_target_pairs={{0,2},{2,0},{1,3},{3,1},{4,6},{6,4},{5,7},{7,5},{8,10},{10,8},{9,1... | collective-permute-start | bytes 2383880 | tf_op jit(solution)/shard_map/ppermute | solution.py:253
  9.9 0.7 dynamic-slice_dynamic-update-slice_fusion.5
  10.6 0.7 dynamic-slice_dynamic-update-slice_fusion.4
  11.2 0.0 copy-done.25
  11.2 0.6 constant_dynamic-update-slice_fusion.1
  11.8 0.0 collective-permute-start.13
  11.8 16.9 %collective-permute-done.9.refs_0_ = f32[776,256]{1,0:T(8,128)} collective-permute-done((f32[776,256]{1,0:T(8,128)}, f32[776,256]{1,0:T(8,128)}, u32[]{:S(2)}, u32[]{:S(2)}) %collective-permute-start.9) | collective-permute-done | bytes 794656 | tf_op jit(solution)/shard_map/ppermute | solution.py:253
  28.8 16.2 %collective-permute-done.13.refs_0_ = f32[776,256]{1,0:T(8,128)} collective-permute-done((f32[776,256]{1,0:T(8,128)}, f32[776,256]{1,0:T(8,128)}, u32[]{:S(2)}, u32[]{:S(2)}) %collective-permute-start.13) | collective-permute-done | bytes 794656 | tf_op jit(solution)/shard_map/ppermute | solution.py:253
  45.0 0.1 copy.28.children
  45.1 0.7 copy-done.29
  45.7 1.0 %copy-done.12 = f32[512,256]{1,0:T(8,128)S(1)} copy-done((f32[512,256]{1,0:T(8,128)S(1)}, f32[512,256]{1,0:T(8,128)}, u32[]{:S(2)}) %copy-start.12) | copy-done | bytes 524312
  46.8 1.0 %copy-done.13 = f32[512,256]{1,0:T(8,128)S(1)} copy-done((f32[512,256]{1,0:T(8,128)S(1)}, f32[512,256]{1,0:T(8,128)}, u32[]{:S(2)}) %copy-start.13) | copy-done | bytes 524312
  47.8 1.0 %copy-done.14 = f32[256,512]{1,0:T(8,128)S(1)} copy-done((f32[256,512]{1,0:T(8,128)S(1)}, f32[256,512]{1,0:T(8,128)}, u32[]{:S(2)}) %copy-start.14) | copy-done | bytes 524312
  48.9 0.9 copy-done.15
  49.8 1.8 %shard_map.257.refs_0_ = f32[64,512]{1,0:T(8,128)S(1)} custom-call(f32[512,512]{1,0:T(8,128)S(1)} %copy-done, f32[64,512]{1,0:T(8,128)S(1)} %copy-done.15, s32[64,7]{1,0:T(8,128)S(1)} %copy.28.children, f32[512,256]{1,0:T(8,128)S(1)} %copy-done.12, f32[512,256]{1,0:T(8,128)S(1)} %copy-done.13, f32[1,256]{1,0:T(1,128)S(1)} %bitcast.16, f32[256,512]{1,0:T(8,128)S(1)} %copy-done.14), custom_call_target="tpu_custom_call" | custom-call | flops 637534208 | bytes 2886400 | tf_op jit(solution)/shard_map/pallas_call | solution.py:236
  51.6 0.0 copy-start.26
  51.6 1.8 %collective-permute-start = (f32[64,512]{1,0:T(8,128)S(1)}, f32[64,512]{1,0:T(8,128)S(1)}, u32[]{:S(2)}, u32[]{:S(2)}) collective-permute-start(f32[64,512]{1,0:T(8,128)S(1)} %shard_map.257.refs_0_), channel_id=1, source_target_pairs={{0,2},{2,0},{1,3},{3,1},{4,6},{6,4},{5,7},{7,5},{8,10},{10,8},{9,1... | collective-permute-start | bytes 393224 | tf_op jit(solution)/shard_map/ppermute | solution.py:253
  53.4 4.2 %collective-permute-done.refs_1_ = f32[64,512]{1,0:T(8,128)S(1)} collective-permute-done((f32[64,512]{1,0:T(8,128)S(1)}, f32[64,512]{1,0:T(8,128)S(1)}, u32[]{:S(2)}, u32[]{:S(2)}) %collective-permute-start) | collective-permute-done | bytes 131104 | tf_op jit(solution)/shard_map/ppermute | solution.py:253
  57.6 0.7 copy-done.30
  58.3 0.6 shard_map.258
  58.9 0.7 copy-done.17
  59.5 0.0 collective-permute-start.4
  59.5 3.8 %collective-permute-start.3 = (f32[64,256]{1,0:T(8,128)S(1)}, f32[64,256]{1,0:T(8,128)S(1)}, u32[]{:S(2)}, u32[]{:S(2)}) collective-permute-start(f32[64,256]{1,0:T(8,128)S(1)} %get-tuple-element.25.refs_0_), channel_id=1, source_target_pairs={{0,12},{4,0},{8,4},{12,8},{1,13},{5,1},{9,5},{13,9},{2,14},{6,2},{... | collective-permute-start | bytes 196616 | tf_op jit(solution)/shard_map/ppermute | solution.py:253
  63.4 0.0 collective-permute-start.2
  63.4 0.0 collective-permute-done.4.refs_4_
  63.4 1.0 collective-permute-start.1
  64.4 0.1 copy.29.refs_8_
  64.5 1.3 %collective-permute-done.3.refs_3_ = f32[64,256]{1,0:T(8,128)S(1)} collective-permute-done((f32[64,256]{1,0:T(8,128)S(1)}, f32[64,256]{1,0:T(8,128)S(1)}, u32[]{:S(2)}, u32[]{:S(2)}) %collective-permute-start.3) | collective-permute-done | bytes 65568 | tf_op jit(solution)/shard_map/ppermute | solution.py:253
  65.8 0.0 collective-permute-start.7
  65.8 0.6 copy-done.19
  66.5 4.1 %collective-permute-done.2.refs_2_ = f32[64,256]{1,0:T(8,128)S(1)} collective-permute-done((f32[64,256]{1,0:T(8,128)S(1)}, f32[64,256]{1,0:T(8,128)S(1)}, u32[]{:S(2)}, u32[]{:S(2)}) %collective-permute-start.2) | collective-permute-done | bytes 65568 | tf_op jit(solution)/shard_map/ppermute | solution.py:253
  70.5 0.6 copy-done.21
  71.2 0.5 collective-permute-start.5
  71.7 0.1 collective-permute-done.6.refs_6_
  71.8 1.0 collective-permute-done.5.refs_5_
  72.8 0.8 copy-done.20
  73.6 0.8 copy-done.22
  74.5 1.7 %shard_map.259.refs_0_ = f32[64,512]{1,0:T(8,128)S(1)} custom-call(f32[64,256]{1,0:T(8,128)S(1)} %get-tuple-element.25.refs_0_, f32[64,256]{1,0:T(8,128)} %collective-permute-done.1.refs_1_, f32[64,256]{1,0:T(8,128)S(1)} %copy-done.22, f32[64,256]{1,0:T(8,128)S(1)} %copy-done.20, f32[64,256]{1,0:T(8,128)S(1)} %collective-permute-done.4.refs_4_, ...), custom_call_target="tpu_custom_call" | custom-call | flops 201326592 | bytes 1248768 | tf_op jit(solution)/shard_map/pallas_call | solution.py:236
  76.2 0.0 copy-start.1
  76.2 1.6 %collective-permute-start.8 = (f32[64,512]{1,0:T(8,128)S(1)}, f32[64,512]{1,0:T(8,128)}, u32[]{:S(2)}, u32[]{:S(2)}) collective-permute-start(f32[64,512]{1,0:T(8,128)S(1)} %shard_map.259.refs_0_), channel_id=1, source_target_pairs={{0,2},{2,0},{1,3},{3,1},{4,6},{6,4},{5,7},{7,5},{8,10},{10,8},{9,1... | collective-permute-start | bytes 393224 | tf_op jit(solution)/shard_map/ppermute | solution.py:253
  77.7 0.1 copy.30.refs_6_.sources
  77.9 1.6 %copy.32.links = s32[512,6]{1,0:T(8,128)} copy(s32[512,6]{0,1:T(8,128)} %param.30) | data formatting | bytes 24576 | tf_op args[4]
  79.5 3.0 %shard_map.260 = (f32[512,512]{1,0:T(8,128)S(1)}, bf16[2,512,256]{2,1,0:T(8,128)(2,1)S(1)}, bf16[2,512,256]{2,1,0:T(8,128)(2,1)S(1)}, bf16[512,512]{1,0:T(8,128)(2,1)S(1)}, bf16[512,512]{1,0:T(8,128)(2,1)S(1)}) custom-call(f32[512,512]{1,0:T(8,128)S(1)} %copy-done, f32[512,256]{1,0:T(8,128)S(1)} %copy-done.1, f32[512,256]{1,0:T(8,128)S(1)} %copy-done.3, ...), custom_call_target="tpu_custom_call" | custom-call | flops 805306368 | bytes 7357440 | tf_op jit(solution)/shard_map/pallas_call | solution.py:236
  82.5 0.0 copy-start.27
  82.5 0.0 copy-start.23
  82.5 0.7 copy-done.27
  83.2 0.0 copy-done.23
  83.2 3.0 %shard_map.261 = (f32[64,512]{1,0:T(8,128)}, bf16[128,512]{1,0:T(8,128)(2,1)S(1)}, f32[128,512]{1,0:T(8,128)S(1)}, f32[128,512]{1,0:T(8,128)S(1)}) custom-call(f32[64,512]{1,0:T(8,128)S(1)} %shard_map.259.refs_0_, f32[64,512]{1,0:T(8,128)} %collective-permute-done.8.refs_1_, f32[64,512]{1,0:T(8,128)S(1)} %copy-done.18, f32[1,512]{1,0:T(1,128)S(1)} %bitcast.13, ...), custom_call_target="tpu_custom_call" | custom-call | flops 402653184 | bytes 5384192 | tf_op jit(solution)/shard_map/pallas_call | solution.py:236
  86.2 0.1 collective-permute-start.11
  86.3 3.5 %collective-permute-start.12 = (f32[128,512]{1,0:T(8,128)S(1)}, f32[128,512]{1,0:T(8,128)S(1)}, u32[]{:S(2)}, u32[]{:S(2)}) collective-permute-start(f32[128,512]{1,0:T(8,128)S(1)} %get-tuple-element.34.head), channel_id=1, source_target_pairs={{0,13},{1,0},{4,1},{5,4},{8,5},{9,8},{12,9},{13,12},{2,15},{3,2},{... | collective-permute-start | bytes 786440 | tf_op jit(solution)/shard_map/ppermute | solution.py:253
  89.7 1.2 %shard_map.262.middle = f32[256,512]{1,0:T(8,128)S(1)} custom-call(f32[512,512]{1,0:T(8,128)S(1)} %copy-done, f32[512,512]{1,0:T(8,128)S(1)} %get-tuple-element.28.refs_5_.receivers, s32[512,3]{1,0:T(8,128)S(1)} %copy.30.refs_6_.sources, bf16[128,512]{1,0:T(8,128)(2,1)S(1)} %get-tuple-element.35.senders, ...), custom_call_target="tpu_custom_call" | custom-call | flops 402653184 | bytes 3809280 | tf_op jit(solution)/shard_map/pallas_call | solution.py:236
  90.9 0.0 copy-done.7
  90.9 0.0 copy-start.8
  90.9 1.9 %shard_map.263 = (bf16[2,512,256]{2,1,0:T(8,128)(2,1)S(1)}, bf16[2,512,256]{2,1,0:T(8,128)(2,1)S(1)}, bf16[2,512,256]{2,1,0:T(8,128)(2,1)S(1)}, bf16[2,512,256]{...) custom-call(f32[512,256]{1,0:T(8,128)S(1)} %copy-done.4, ...), custom_call_target="tpu_custom_call" | custom-call | flops 262144 | bytes 6325248 | tf_op jit(solution)/shard_map/pallas_call | solution.py:236
  92.9 0.0 copy-start.28
  92.9 0.7 copy-done.28
  93.5 4.5 %shard_map.264 = (bf16[512,512]{1,0:T(8,128)(2,1)S(1)}, bf16[512,512]{1,0:T(8,128)(2,1)S(1)}, f32[512,512]{1,0:T(8,128)S(1)}, f32[256,512]{1,0:T(8,128)S(1)}) custom-call(f32[128,512]{1,0:T(8,128)S(1)} %get-tuple-element.34.head, f32[256,512]{1,0:T(8,128)S(1)} %shard_map.262.middle, f32[128,512]{1,0:T(8,128)S(1)} %get-tuple-element.33.tail, ...), custom_call_target="tpu_custom_call" | custom-call | flops 3221225472 | bytes 6846464 | tf_op jit(solution)/shard_map/pallas_call | solution.py:236
  98.1 4.4 %shard_map.265 = f32[512,512]{1,0:T(8,128)} custom-call(f32[128,512]{1,0:T(8,128)S(1)} %collective-permute-done.11.before, f32[128,512]{1,0:T(8,128)S(1)} %collective-permute-done.12.after, f32[128,512]{1,0:T(8,128)S(1)} %get-tuple-element.34.head, f32[128,512]{1,0:T(8,128)S(1)} %get-tuple-element.33.tail, f32[256,512]{1,0:T(8,128)S(1)} %get-tuple-element.43.inner, ...), custom_call_target="tpu_custom_call" | custom-call | flops 805306368 | bytes 6830080 | tf_op jit(solution)/shard_map/pallas_call | solution.py:236
  (57 shorter events, 0.1 us)
Async XLA Ops:
  0.6 1.8 %copy-start.4 = (f32[512,256]{1,0:T(8,128)S(1)}, f32[512,256]{1,0:T(8,128)}, u32[]{:S(2)}) copy-start(f32[512,256]{1,0:T(8,128)} %ws.5) | copy-start | bytes 1572868
  0.6 2.5 %copy-start.3 = (f32[512,256]{1,0:T(8,128)S(1)}, f32[512,256]{1,0:T(8,128)}, u32[]{:S(2)}) copy-start(f32[512,256]{1,0:T(8,128)} %wr.4) | copy-start | bytes 1572868
  2.4 2.6 %copy-start.2 = (f32[256,512]{1,0:T(8,128)S(1)}, f32[256,512]{1,0:T(8,128)}, u32[]{:S(2)}) copy-start(f32[256,512]{1,0:T(8,128)} %wo.4) | copy-start | bytes 1572868
  2.4 3.9 %copy-start.24 = (f32[256]{0:T(256)S(1)}, f32[256]{0:T(256)}, u32[]{:S(2)}) copy-start(f32[256]{0:T(256)} %param.44) | copy-start | bytes 3076
  2.4 7.5 %copy-start.5 = (f32[256,512]{1,0:T(8,128)S(1)}, f32[256,512]{1,0:T(8,128)}, u32[]{:S(2)}) copy-start(f32[256,512]{1,0:T(8,128)} %wo.5) | copy-start | bytes 1572868
  3.2 41.9 %copy-start = (f32[512,512]{1,0:T(8,128)S(1)}, f32[512,512]{1,0:T(8,128)}, u32[]{:S(2)}) copy-start(f32[512,512]{1,0:T(8,128)} %nodes.5) | copy-start | bytes 3145732
  7.0 21.8 %collective-permute-start.9 = (f32[776,256]{1,0:T(8,128)}, f32[776,256]{1,0:T(8,128)}, u32[]{:S(2)}, u32[]{:S(2)}) collective-permute-start(f32[776,256]{1,0:T(8,128)} %constant_dynamic-update-slice_fusion), channel_id=1, source_target_pairs={{0,2},{2,0},{1,3},{3,1},{4,6},{6,4},{5,7},{7,5},{8,10},{10,8},{9,1... | collective-permute-start | bytes 2383880 | tf_op jit(solution)/shard_map/ppermute | solution.py:253
  10.6 0.7 copy-start.25
  11.2 33.7 %copy-start.32 = (s32[64,7]{0,1:T(8,128)S(1)}, s32[64,7]{0,1:T(8,128)}, u32[]{:S(2)}) copy-start(s32[64,7]{0,1:T(8,128)} %param.28) | copy-start | bytes 5380
  11.8 33.1 %collective-permute-start.13 = (f32[776,256]{1,0:T(8,128)}, f32[776,256]{1,0:T(8,128)}, u32[]{:S(2)}, u32[]{:S(2)}) collective-permute-start(f32[776,256]{1,0:T(8,128)} %constant_dynamic-update-slice_fusion.1), channel_id=1, source_target_pairs={{0,2},{2,0},{1,3},{3,1},{4,6},{6,4},{5,7},{7,5},{8,10},{10,8},{9,1... | collective-permute-start | bytes 2383880 | tf_op jit(solution)/shard_map/ppermute | solution.py:253
  28.8 50.7 %collective-permute-start.10 = (f32[776,256]{1,0:T(8,128)}, f32[776,256]{1,0:T(8,128)}, u32[]{:S(2)}, u32[]{:S(2)}) collective-permute-start(f32[776,256]{1,0:T(8,128)} %collective-permute-done.9.refs_0_), channel_id=1, source_target_pairs={{0,1},{1,0},{2,3},{3,2},{4,5},{5,4},{6,7},{7,6},{8,9},{9,8},{10,11... | collective-permute-start | bytes 2383880 | tf_op jit(solution)/shard_map/ppermute | solution.py:253
  45.0 45.9 %collective-permute-start.14 = (f32[776,256]{1,0:T(8,128)}, f32[776,256]{1,0:T(8,128)}, u32[]{:S(2)}, u32[]{:S(2)}) collective-permute-start(f32[776,256]{1,0:T(8,128)} %collective-permute-done.13.refs_0_), channel_id=1, source_target_pairs={{0,1},{1,0},{2,3},{3,2},{4,5},{5,4},{6,7},{7,6},{8,9},{9,8},{10,11... | collective-permute-start | bytes 2383880 | tf_op jit(solution)/shard_map/ppermute | solution.py:253
  45.1 0.7 copy-start.29
  45.7 1.0 %copy-start.12 = (f32[512,256]{1,0:T(8,128)S(1)}, f32[512,256]{1,0:T(8,128)}, u32[]{:S(2)}) copy-start(f32[512,256]{1,0:T(8,128)} %ws.3) | copy-start | bytes 1572868
  46.8 1.0 %copy-start.13 = (f32[512,256]{1,0:T(8,128)S(1)}, f32[512,256]{1,0:T(8,128)}, u32[]{:S(2)}) copy-start(f32[512,256]{1,0:T(8,128)} %wr.3) | copy-start | bytes 1572868
  47.8 1.0 %copy-start.14 = (f32[256,512]{1,0:T(8,128)S(1)}, f32[256,512]{1,0:T(8,128)}, u32[]{:S(2)}) copy-start(f32[256,512]{1,0:T(8,128)} %wo.3) | copy-start | bytes 1572868
  48.9 0.9 copy-start.15
  49.8 7.8 %copy-start.9 = (f32[512,256]{1,0:T(8,128)S(1)}, f32[512,256]{1,0:T(8,128)}, u32[]{:S(2)}) copy-start(f32[512,256]{1,0:T(8,128)} %refs_4_.2) | copy-start | bytes 1572868
  49.8 7.8 %copy-start.10 = (f32[512,256]{1,0:T(8,128)S(1)}, f32[512,256]{1,0:T(8,128)}, u32[]{:S(2)}) copy-start(f32[512,256]{1,0:T(8,128)} %refs_5_.1) | copy-start | bytes 1572868
  49.8 7.8 %copy-start.16 = (f32[64,512]{1,0:T(8,128)S(1)}, f32[64,512]{1,0:T(8,128)}, u32[]{:S(2)}) copy-start(f32[64,512]{1,0:T(8,128)} %refs_2_.1) | copy-start | bytes 393220
  51.6 6.0 %copy-start.26 = (f32[512]{0:T(512)S(1)}, f32[512]{0:T(512)}, u32[]{:S(2)}) copy-start(f32[512]{0:T(512)} %param.36) | copy-start | bytes 6148
  51.6 6.0 %collective-permute-start = (f32[64,512]{1,0:T(8,128)S(1)}, f32[64,512]{1,0:T(8,128)S(1)}, u32[]{:S(2)}, u32[]{:S(2)}) collective-permute-start(f32[64,512]{1,0:T(8,128)S(1)} %shard_map.257.refs_0_), channel_id=1, source_target_pairs={{0,2},{2,0},{1,3},{3,1},{4,6},{6,4},{5,7},{7,5},{8,10},{10,8},{9,1... | collective-permute-start | bytes 393224 | tf_op jit(solution)/shard_map/ppermute | solution.py:253
  57.6 0.7 copy-start.30
  58.3 14.5 %copy-start.11 = (f32[256,512]{1,0:T(8,128)S(1)}, f32[256,512]{1,0:T(8,128)}, u32[]{:S(2)}) copy-start(f32[256,512]{1,0:T(8,128)} %refs_11_.1) | copy-start | bytes 1572868
  58.9 0.7 copy-start.17
  59.5 4.9 %copy-start.33 = (s32[64,6]{0,1:T(8,128)S(1)}, s32[64,6]{0,1:T(8,128)}, u32[]{:S(2)}) copy-start(s32[64,6]{0,1:T(8,128)} %param.31) | copy-start | bytes 4612
  59.5 3.9 %collective-permute-start.4 = (f32[64,256]{1,0:T(8,128)S(1)}, f32[64,256]{1,0:T(8,128)S(1)}, u32[]{:S(2)}, u32[]{:S(2)}) collective-permute-start(f32[64,256]{1,0:T(8,128)S(1)} %get-tuple-element.25.refs_0_), channel_id=1, source_target_pairs={{0,1},{1,0},{2,3},{3,2},{4,5},{5,4},{6,7},{7,6},{8,9},{9,8},{10,11... | collective-permute-start | bytes 196616 | tf_op jit(solution)/shard_map/ppermute | solution.py:253
  59.5 6.3 %collective-permute-start.3 = (f32[64,256]{1,0:T(8,128)S(1)}, f32[64,256]{1,0:T(8,128)S(1)}, u32[]{:S(2)}, u32[]{:S(2)}) collective-permute-start(f32[64,256]{1,0:T(8,128)S(1)} %get-tuple-element.25.refs_0_), channel_id=1, source_target_pairs={{0,12},{4,0},{8,4},{12,8},{1,13},{5,1},{9,5},{13,9},{2,14},{6,2},{... | collective-permute-start | bytes 196616 | tf_op jit(solution)/shard_map/ppermute | solution.py:253
  63.4 7.1 %collective-permute-start.2 = (f32[64,256]{1,0:T(8,128)S(1)}, f32[64,256]{1,0:T(8,128)S(1)}, u32[]{:S(2)}, u32[]{:S(2)}) collective-permute-start(f32[64,256]{1,0:T(8,128)S(1)} %get-tuple-element.25.refs_0_), channel_id=1, source_target_pairs={{0,8},{4,12},{8,0},{12,4},{1,9},{5,13},{9,1},{13,5},{2,10},{6,14},... | collective-permute-start | bytes 196616 | tf_op jit(solution)/shard_map/ppermute | solution.py:253
  63.4 7.8 %collective-permute-start.1 = (f32[64,256]{1,0:T(8,128)S(1)}, f32[64,256]{1,0:T(8,128)}, u32[]{:S(2)}, u32[]{:S(2)}) collective-permute-start(f32[64,256]{1,0:T(8,128)S(1)} %get-tuple-element.25.refs_0_), channel_id=1, source_target_pairs={{0,4},{4,8},{8,12},{12,0},{1,5},{5,9},{9,13},{13,1},{2,6},{6,10},{... | collective-permute-start | bytes 196616 | tf_op jit(solution)/shard_map/ppermute | solution.py:253
  65.8 5.9 %collective-permute-start.7 = (f32[64,256]{1,0:T(8,128)S(1)}, f32[64,256]{1,0:T(8,128)S(1)}, u32[]{:S(2)}, u32[]{:S(2)}) collective-permute-start(f32[64,256]{1,0:T(8,128)S(1)} %collective-permute-done.3.refs_3_), channel_id=1, source_target_pairs={{0,1},{1,0},{2,3},{3,2},{4,5},{5,4},{6,7},{7,6},{8,9},{9,8},{10,11... | collective-permute-start | bytes 196616 | tf_op jit(solution)/shard_map/ppermute | solution.py:253
  65.8 0.6 copy-start.19
  70.5 1.3 %collective-permute-start.6 = (f32[64,256]{1,0:T(8,128)S(1)}, f32[64,256]{1,0:T(8,128)S(1)}, u32[]{:S(2)}, u32[]{:S(2)}) collective-permute-start(f32[64,256]{1,0:T(8,128)S(1)} %collective-permute-done.2.refs_2_), channel_id=1, source_target_pairs={{0,1},{1,0},{2,3},{3,2},{4,5},{5,4},{6,7},{7,6},{8,9},{9,8},{10,11... | collective-permute-start | bytes 196616 | tf_op jit(solution)/shard_map/ppermute | solution.py:253
  70.5 0.6 copy-start.21
  71.2 1.6 %collective-permute-start.5 = (f32[64,256]{1,0:T(8,128)}, f32[64,256]{1,0:T(8,128)S(1)}, u32[]{:S(2)}, u32[]{:S(2)}) collective-permute-start(f32[64,256]{1,0:T(8,128)} %collective-permute-done.1.refs_1_), channel_id=1, source_target_pairs={{0,1},{1,0},{2,3},{3,2},{4,5},{5,4},{6,7},{7,6},{8,9},{9,8},{10,11... | collective-permute-start | bytes 196616 | tf_op jit(solution)/shard_map/ppermute | solution.py:253
  72.8 0.8 copy-start.20
  73.6 0.8 copy-start.22
  74.5 3.3 %copy-start.31 = (s32[512,3]{0,1:T(4,128)S(1)}, s32[512,3]{0,1:T(4,128)}, u32[]{:S(2)}) copy-start(s32[512,3]{0,1:T(4,128)} %param.29) | copy-start | bytes 18436
  76.2 3.3 %copy-start.1 = (f32[512,256]{1,0:T(8,128)S(1)}, f32[512,256]{1,0:T(8,128)}, u32[]{:S(2)}) copy-start(f32[512,256]{1,0:T(8,128)} %ws.4) | copy-start | bytes 1572868
  76.2 6.3 %collective-permute-start.8 = (f32[64,512]{1,0:T(8,128)S(1)}, f32[64,512]{1,0:T(8,128)}, u32[]{:S(2)}, u32[]{:S(2)}) collective-permute-start(f32[64,512]{1,0:T(8,128)S(1)} %shard_map.259.refs_0_), channel_id=1, source_target_pairs={{0,2},{2,0},{1,3},{3,1},{4,6},{6,4},{5,7},{7,5},{8,10},{10,8},{9,1... | collective-permute-start | bytes 393224 | tf_op jit(solution)/shard_map/ppermute | solution.py:253
  79.5 3.0 %copy-start.18 = (f32[64,512]{1,0:T(8,128)S(1)}, f32[64,512]{1,0:T(8,128)}, u32[]{:S(2)}) copy-start(f32[64,512]{1,0:T(8,128)} %copy-done.17) | copy-start | bytes 393220
  82.5 0.7 copy-start.27
  82.5 0.7 copy-start.23
  86.2 11.9 %collective-permute-start.11 = (f32[128,512]{1,0:T(8,128)S(1)}, f32[128,512]{1,0:T(8,128)S(1)}, u32[]{:S(2)}, u32[]{:S(2)}) collective-permute-start(f32[128,512]{1,0:T(8,128)S(1)} %get-tuple-element.33.tail), channel_id=1, source_target_pairs={{0,1},{1,4},{4,5},{5,8},{8,9},{9,12},{12,13},{13,0},{2,3},{3,6},{6... | collective-permute-start | bytes 786440 | tf_op jit(solution)/shard_map/ppermute | solution.py:253
  86.3 11.8 %collective-permute-start.12 = (f32[128,512]{1,0:T(8,128)S(1)}, f32[128,512]{1,0:T(8,128)S(1)}, u32[]{:S(2)}, u32[]{:S(2)}) collective-permute-start(f32[128,512]{1,0:T(8,128)S(1)} %get-tuple-element.34.head), channel_id=1, source_target_pairs={{0,13},{1,0},{4,1},{5,4},{8,5},{9,8},{12,9},{13,12},{2,15},{3,2},{... | collective-permute-start | bytes 786440 | tf_op jit(solution)/shard_map/ppermute | solution.py:253
  89.7 1.2 %copy-start.6 = (f32[256,512]{1,0:T(8,128)S(1)}, f32[256,512]{1,0:T(8,128)}, u32[]{:S(2)}) copy-start(f32[256,512]{1,0:T(8,128)} %wo.5) | copy-start | bytes 1572868
  89.7 1.2 %copy-start.7 = (f32[512,256]{1,0:T(8,128)S(1)}, f32[512,256]{1,0:T(8,128)}, u32[]{:S(2)}) copy-start(f32[512,256]{1,0:T(8,128)} %wr.5) | copy-start | bytes 1572868
  90.9 2.0 %copy-start.8 = (s32[512,6]{1,0:T(8,128)S(1)}, s32[512,6]{1,0:T(8,128)}, u32[]{:S(2)}) copy-start(s32[512,6]{1,0:T(8,128)} %copy.32.links) | copy-start | bytes 36868
  92.9 0.7 copy-start.28

commit v2 on v1

--- a/solution.py
+++ b/solution.py
@@ -11,6 +11,7 @@
 f32 = jnp.float32
 bf16 = jnp.bfloat16
 limit_bytes = 40 * 1024 * 1024
+large_limit = 60 * 1024 * 1024
 most_direct = 4
 
 
@@ -61,66 +62,136 @@
     return total
 
 
-def upward_kernel(nodes, coarse, children, ws, wr, bias, wo, part):
-    sender_high, sender_low = split(0.5 * dot3(nodes[...], *split(ws[...])))
-    receivers = 0.5 * (dot3(coarse[...], *split(wr[...])) + bias[...])
+def started(copies, sems):
+    moves = [pltpu.make_async_copy(a, b, sems.at[i]) for i, (a, b) in enumerate(copies)]
+    for move in moves:
+        move.start()
+    return moves
+
+
+def strips(source, target, count):
+    rows = source.shape[0] // count
+    return [
+        (source.at[pl.ds(i * rows, rows)], target.at[pl.ds(i * rows, rows)]) for i in range(count)
+    ]
+
+
+def upward_kernel(nodes_hbm, coarse, children, ws_hbm, wr_hbm, bias, wo_hbm, part, nodes, ws, wr, wo, sems):
+    moves = started(
+        strips(ws_hbm, ws, 2)
+        + strips(nodes_hbm, nodes, 4)
+        + strips(wr_hbm, wr, 2)
+        + strips(wo_hbm, wo, 2),
+        sems,
+    )
     wanted = children[...]
     names = lax.broadcasted_iota(jnp.int32, (wanted.shape[0], nodes.shape[0]), 1)
     picks = one_hot(wanted, names)
+    for move in moves[:6]:
+        move.wait()
+    sender_high, sender_low = split(0.5 * dot3(nodes[...], *split(ws[...])))
+    for move in moves[6:8]:
+        move.wait()
+    receivers = 0.5 * (dot3(coarse[...], *split(wr[...])) + bias[...])
     picked = dot(picks, sender_high) + dot(picks, sender_low)
     hidden = silu_sum(picked, receivers, wanted.shape[1])
+    for move in moves[8:]:
+        move.wait()
     part[...] = dot3(hidden, *split(wo[...]))
 
 
+def coarse_ready_kernel(after, ws, wr, wo, ws_high, ws_low, wr_high, wr_low, wo_high, wo_low):
+    del after
+    ws_high[...], ws_low[...] = split(ws[...])
+    wr_high[...], wr_low[...] = split(wr[...])
+    wo_high[...], wo_low[...] = split(wo[...])
+
+
+def share_copies(ws, wr, bias, wo, pack):
+    parts, lvls = lax.axis_size("parts"), lax.axis_size("lvl")
+    mine = lax.axis_index("parts") * lvls + lax.axis_index("lvl")
+    depth, width = ws.shape
+    share, thin = depth // (parts * lvls), width // (parts * lvls)
+    rows = pl.ds(pl.multiple_of(mine * share, share), share)
+    strip = pl.ds(pl.multiple_of(mine * thin, thin), thin)
+    columns = range(wo.shape[1] // width)
+    return [
+        (ws.at[rows], pack.at[pl.ds(0, share)]),
+        (wr.at[rows], pack.at[pl.ds(share, share)]),
+        *(
+            (wo.at[strip, pl.ds(j * width, width)], pack.at[pl.ds(2 * share + j * thin, thin)])
+            for j in columns
+        ),
+        (bias, pack.at[pl.ds(2 * share + len(columns) * thin, 1)]),
+    ]
+
+
+def share_kernel(*refs):
+    own, (down_pack, bottom_pack, sems) = refs[:8], refs[8:]
+    for move in started(share_copies(*own[:4], down_pack) + share_copies(*own[4:], bottom_pack), sems):
+        move.wait()
+
+
+def picks_kernel(after, links, names, picks):
+    del after
+    wanted = links[...]
+    picks[...] = one_hot(wanted, jnp.broadcast_to(names[...], (wanted.shape[0], names.shape[1])))
+
+
 def coarse_project_kernel(count, *refs):
-    parts, (coarse, gain, ws, wr, bias, updated, senders, receivers) = refs[:count], refs[count:]
+    parts, refs = refs[:count], refs[count:]
+    coarse, gain, ws_high, ws_low, wr_high, wr_low, bias, updated, senders, receivers = refs
     rows = coarse[...] + gain[...] * normed(added(parts))
     updated[...] = rows
-    senders[...] = 0.5 * dot3(rows, *split(ws[...]))
-    receivers[...] = 0.5 * (dot3(rows, *split(wr[...])) + bias[...])
+    senders[...] = 0.5 * dot3(rows, ws_high[...], ws_low[...])
+    receivers[...] = 0.5 * (dot3(rows, wr_high[...], wr_low[...]) + bias[...])
 
 
 def coarse_kernel(count, *refs):
-    pieces, (links, names, receivers, wo, part) = refs[:count], refs[count:]
+    pieces, (all_picks, receivers, wo_high, wo_low, part) = refs[:count], refs[count:]
     senders = jnp.concatenate([piece[...] for piece in pieces], axis=0)
     sender_high, sender_low = split(senders)
-    wanted = links[...]
-    picks = one_hot(wanted, jnp.broadcast_to(names[...], (wanted.shape[0], names.shape[1])))
+    picks = all_picks[...]
     picked = dot(picks, sender_high) + dot(picks, sender_low)
-    hidden = silu_sum(picked, receivers[...], wanted.shape[1])
-    part[...] = dot3(hidden, *split(wo[...]))
+    hidden = silu_sum(picked, receivers[...], picks.shape[0] // receivers.shape[0])
+    part[...] = dot3(hidden, wo_high[...], wo_low[...])
 
 
 def collect(own, packs, outs):
     ws, wr, bias, wo = own
     ws_high, ws_low, wr_high, wr_low, wo_high, wo_low, bias_all = outs
-    subs, lvls = lax.axis_size("sub"), lax.axis_size("lvl")
-    sub, lvl = lax.axis_index("sub"), lax.axis_index("lvl")
+    subs, parts, lvls = lax.axis_size("sub"), lax.axis_size("parts"), lax.axis_size("lvl")
+    sub, part, lvl = lax.axis_index("sub"), lax.axis_index("parts"), lax.axis_index("lvl")
     depth, width = ws.shape
     ws_high[sub], ws_low[sub] = split(ws[...])
     wr_high[sub], wr_low[sub] = split(wr[...])
     rows = pl.ds(pl.multiple_of(sub * width, width), width)
     wo_high[rows, :], wo_low[rows, :] = split(wo[...])
     bias_all[sub] = jnp.broadcast_to(bias[...], (8, width))
-    share, thin = depth // lvls, width // lvls
+    share, thin = depth // (parts * lvls), width // (parts * lvls)
+    columns = wo.shape[1] // width
+    place = iter(packs)
     for s in range(1, subs):
         block = lax.rem(sub + subs - s, subs)
-        for t in range(lvls):
-            pack = packs[(s - 1) * lvls + t]
-            level = lax.rem(lvl + lvls - t, lvls)
-            rows = pl.ds(pl.multiple_of(level * share, share), share)
-            ws_high[block, rows, :], ws_low[block, rows, :] = split(pack[0:share, :])
-            wr_high[block, rows, :], wr_low[block, rows, :] = split(pack[share : 2 * share, :])
-            rows = pl.ds(pl.multiple_of(block * width + level * thin, thin), thin)
-            for j in range(wo.shape[1] // width):
-                high, low = split(pack[2 * share + j * thin : 2 * share + (j + 1) * thin, :])
-                wo_high[rows, j * width : (j + 1) * width] = high
-                wo_low[rows, j * width : (j + 1) * width] = low
-            if t == 0:
-                bias_all[block] = pack[pack.shape[0] - 8 :, :]
-
-
-def down_ready_kernel(count, nodes, ws, wr, bias, wo, *refs):
+        for p in range(parts):
+            for t in range(lvls):
+                pack = next(place)
+                mine = lax.rem(part + parts - p, parts) * lvls + lax.rem(lvl + lvls - t, lvls)
+                rows = pl.ds(pl.multiple_of(mine * share, share), share)
+                ws_high[block, rows, :], ws_low[block, rows, :] = split(pack[0:share, :])
+                wr_high[block, rows, :], wr_low[block, rows, :] = split(pack[share : 2 * share, :])
+                rows = pl.ds(pl.multiple_of(block * width + mine * thin, thin), thin)
+                for j in range(columns):
+                    high, low = split(pack[2 * share + j * thin : 2 * share + (j + 1) * thin, :])
+                    wo_high[rows, j * width : (j + 1) * width] = high
+                    wo_low[rows, j * width : (j + 1) * width] = low
+                if p == 0 and t == 0:
+                    last = 2 * share + columns * thin
+                    bias_all[block] = jnp.broadcast_to(pack[last : last + 1, :], (8, width))
+
+
+def down_ready_kernel(count, after, nodes, ws, wr, bias, wo, *refs):
+    del after
     packs = refs[:count]
     receivers, ws_high, ws_low, wo_high, wo_low, wr_high, wr_low, bias_all = refs[count:]
     collect(
@@ -230,16 +301,19 @@
         )
 
 
-def call(kernel, outs, operands, flops, scratch=()):
+whole = pl.BlockSpec(memory_space=pltpu.VMEM)
+away = pl.BlockSpec(memory_space=pl.ANY)
+
+
+def call(kernel, outs, operands, flops, scratch=(), far=(), far_outs=(), limit=limit_bytes):
     moved = sum(x.size * x.dtype.itemsize for x in (*outs, *operands))
-    whole = pl.BlockSpec(memory_space=pltpu.VMEM)
     return pl.pallas_call(
         kernel,
         out_shape=tuple(outs),
-        in_specs=[whole] * len(operands),
-        out_specs=tuple([whole] * len(outs)),
+        in_specs=[away if i in far else whole for i in range(len(operands))],
+        out_specs=tuple(away if i in far_outs else whole for i in range(len(outs))),
         scratch_shapes=list(scratch),
-        compiler_params=pltpu.CompilerParams(vmem_limit_bytes=limit_bytes),
+        compiler_params=pltpu.CompilerParams(vmem_limit_bytes=limit),
         cost_estimate=pl.CostEstimate(flops=int(flops), bytes_accessed=moved, transcendentals=0),
     )(*operands)
 
@@ -261,45 +335,51 @@
 
 def coarse_pieces(senders):
     patches, lvls = lax.axis_size("patch"), lax.axis_size("lvl")
-    rows = senders.shape[0]
     if patches > most_direct:
-        return (
-            [lax.all_gather(senders, ("patch", "lvl"), axis=0, tiled=True)],
-            jnp.arange(rows * patches * lvls, dtype=jnp.int32)[None],
-        )
+        return [lax.all_gather(senders, ("patch", "lvl"), axis=0, tiled=True)]
     pieces = [senders] + [shifted(senders, "patch", s) for s in range(1, patches)]
     everything = list(pieces)
     for t in range(1, lvls):
         everything += [shifted(piece, "lvl", t) for piece in pieces]
+    return everything
+
+
+def coarse_names(rows):
+    patches, lvls = lax.axis_size("patch"), lax.axis_size("lvl")
     place = jnp.arange(rows * patches * lvls, dtype=jnp.int32)
+    if patches > most_direct:
+        return place[None]
     step, away = (place // rows) % patches, place // (rows * patches)
     patch = (lax.axis_index("patch") - step) % patches
     lvl = (lax.axis_index("lvl") - away) % lvls
-    return everything, ((patch * lvls + lvl) * rows + place % rows)[None].astype(jnp.int32)
-
-
-def packed(ws, wr, bias, wo):
-    lvls, lvl = lax.axis_size("lvl"), lax.axis_index("lvl")
-    depth, width = ws.shape
-    share, thin = depth // lvls, width // lvls
-    strip = lax.dynamic_slice_in_dim(wo, lvl * thin, thin, axis=0)
-    return jnp.concatenate(
-        [
-            lax.dynamic_slice_in_dim(ws, lvl * share, share, axis=0),
-            lax.dynamic_slice_in_dim(wr, lvl * share, share, axis=0),
-            *(strip[:, j * width : (j + 1) * width] for j in range(wo.shape[1] // width)),
-            jnp.broadcast_to(bias[None], (8, width)),
-        ],
-        axis=0,
-    )
-
-
-def fetched(pack):
-    packs = []
-    for s in range(1, lax.axis_size("sub")):
-        share = shifted(pack, "sub", s)
-        packs += [share] + [shifted(share, "lvl", t) for t in range(1, lax.axis_size("lvl"))]
-    return packs
+    return ((patch * lvls + lvl) * rows + place % rows)[None].astype(jnp.int32)
+
+
+def held(values, event):
+    return lax.optimization_barrier((values, event))[0]
+
+
+def over_sub(pack):
+    return [shifted(pack, "sub", s) for s in range(1, lax.axis_size("sub"))]
+
+
+def over_parts(shares):
+    return [
+        [shifted(share, "parts", p) for p in range(1, lax.axis_size("parts"))] for share in shares
+    ]
+
+
+def over_lvl(shares):
+    return [
+        [share] + [shifted(share, "lvl", t) for t in range(1, lax.axis_size("lvl"))]
+        for share in shares
+    ]
+
+
+def all_shares(shares, others):
+    near = over_lvl(shares)
+    far = [over_lvl(row) for row in others]
+    return [x for first, row in zip(near, far) for x in (first + [y for group in row for y in group])]
 
 
 def body(
@@ -340,27 +420,69 @@
     outputs = [like((hidden, latent), bf16)] * 2
     biases = like((subs, 8, width))
 
-    down_packs = fetched(packed(downward_sender, downward_receiver, downward_bias, downward_output))
-    bottom_packs = fetched(packed(bottom_sender, bottom_receiver, bottom_bias, bottom_output))
-
+    shares = lax.axis_size("parts") * lax.axis_size("lvl")
+    columns = latent // width
+    pack = like((2 * latent // shares + (width // shares) * columns + 8, width))
+    down_own = (downward_sender, downward_receiver, downward_bias[None], downward_output)
+    bottom_own = (bottom_sender, bottom_receiver, bottom_bias[None], bottom_output)
+
+    down_pack, bottom_pack = call(
+        share_kernel,
+        [pack, pack],
+        [*down_own, *bottom_own],
+        latent,
+        [pltpu.SemaphoreType.DMA((2 * (3 + columns),))],
+        far=range(8),
+        far_outs=(0, 1),
+        limit=large_limit,
+    )
+    down_near = over_sub(down_pack)
     (part,) = call(
         upward_kernel,
         [like((blocks, latent))],
         [node_states, coarse_states, children, upward_sender, upward_receiver, upward_bias[None], upward_output],
         6 * rows * latent * width + 4 * children.size * rows * width,
+        [
+            pltpu.VMEM((rows, latent), f32),
+            pltpu.VMEM((latent, width), f32),
+            pltpu.VMEM((latent, width), f32),
+            pltpu.VMEM((width, latent), f32),
+            pltpu.SemaphoreType.DMA((10,)),
+        ],
+        far=(0, 3, 4, 6),
+        limit=large_limit,
     )
     parts = sub_parts(part)
+    ws_high, ws_low, wr_high, wr_low, wo_high, wo_low = call(
+        coarse_ready_kernel,
+        [like((latent, width), bf16)] * 4 + [like((width, latent), bf16)] * 2,
+        [part, coarse_sender, coarse_receiver, coarse_output],
+        latent * hidden,
+        far=(0,),
+    )
     coarse_up, senders, receivers = call(
         functools.partial(coarse_project_kernel, len(parts)),
         [like((blocks, latent)), like((blocks, width)), like((blocks, width))],
-        [*parts, coarse_states, upward_gain[None], coarse_sender, coarse_receiver, coarse_bias[None]],
+        [*parts, coarse_states, upward_gain[None], ws_high, ws_low, wr_high, wr_low, coarse_bias[None]],
         12 * blocks * latent * width,
     )
-    pieces, names = coarse_pieces(senders)
+    pieces = coarse_pieces(senders)
+    names = coarse_names(blocks)
+    (picks,) = call(
+        picks_kernel,
+        [like((coarse_links.size, names.size), bf16)],
+        [senders, coarse_links, names],
+        coarse_links.size * names.size,
+        far=(0,),
+    )
+    down_near, bottom_pack = held((down_near, bottom_pack), picks)
+    down_far = over_parts(down_near)
+    bottom_near = over_sub(bottom_pack)
+    down_packs = all_shares(down_near, down_far)
     (part,) = call(
         functools.partial(coarse_kernel, len(pieces)),
         [like((blocks, latent))],
-        [*pieces, coarse_links, names, receivers, coarse_output],
+        [*pieces, picks, receivers, wo_high, wo_low],
         4 * coarse_links.size * names.size * width,
     )
     parts = sub_parts(part)
@@ -368,10 +490,13 @@
     receivers, ws_high, ws_low, wo_high, wo_low = call(
         functools.partial(down_ready_kernel, len(down_packs)),
         [like((rows, hidden)), *weights, *outputs],
-        [node_states, downward_sender, downward_receiver, downward_bias[None], downward_output, *down_packs],
+        [part, node_states, *down_own, *down_packs],
         6 * rows * latent * hidden,
         [pltpu.VMEM((subs, latent, width), bf16)] * 2 + [pltpu.VMEM((subs, 8, width), f32)],
-    )
+        far=(0,),
+    )
+    bottom_near = held(bottom_near, receivers)
+    bottom_far = over_parts(bottom_near)
     new_coarse, senders, head, tail = call(
         functools.partial(down_edge_kernel, len(parts), rim),
         [like((blocks, latent)), like((2 * blocks, hidden), bf16), like((rim, latent)), like((rim, latent))],
@@ -387,10 +512,12 @@
         6 * (rows - 2 * rim) * latent * hidden,
     )
 
+    bottom_near, bottom_far = held((bottom_near, bottom_far), head)
+    bottom_packs = all_shares(bottom_near, bottom_far)
     ws_high, ws_low, wr_high, wr_low, wo_high, wo_low, bias = call(
         functools.partial(bottom_ready_kernel, len(bottom_packs)),
         [*weights, *weights, *outputs, biases],
-        [bottom_sender, bottom_receiver, bottom_bias[None], bottom_output, *bottom_packs],
+        [*bottom_own, *bottom_packs],
         latent * hidden,
     )
     senders_high, senders_low, receivers, inner = call(

time: 103 us -> 108 us (1.049)
  Pallas kernels: 22 us -> 48.5 us
  waiting for transfers between devices: 43.7 us -> 27.7 us
  local copies, waits for them, and re-layouts: 20.5 us -> 14.8 us
    pallas_call x9 -> x12, Pallas kernels: 22 us -> 48.5 us  [call(): pl.pallas_call(kernel, out_shape=tuple(outs), in_specs=[away if i in far...]
    ppermute x15 -> x19, waiting for transfers between devices: 43.7 us -> 27.7 us  [shifted(): lax.ppermute(values, axis, [(i, (i + step) % count) for i in range(count)])]
    unnamed x79 -> x82, local copies, waits for them, and re-layouts: 19.3 us -> 14.8 us
    concatenate x2 -> x0, local copies, waits for them, and re-layouts: 1.19 us -> none  [packed(): jnp.concatenate([lax.dynamic_slice_in_dim(ws, lvl * share, share, axis=0)...]
    ppermute x15 -> x19, starting transfers between devices: 15.2 us -> 14.9 us  [shifted(): lax.ppermute(values, axis, [(i, (i + step) % count) for i in range(count)])]
  transfers between devices with their start and end apart: 15 -> 19, of which waited for: 7 -> 8; matrix products, arithmetic and copies ran while one was open for 4% -> 2% of each run, Pallas kernels for 17% -> 18%
where the time goes in v2:
time: 108 us; the launch traced here: 107 us
  Pallas kernels  48.5 us (45%)
  waiting for transfers between devices  27.7 us (26%)
  starting transfers between devices  14.9 us (14%)
  local copies, waits for them, and re-layouts  14.8 us (14%)
    pallas_call x12, Pallas kernels, call(): pl.pallas_call(kernel, out_shape=tuple(outs), in_specs=[away if i in far...  48.5 us
    ppermute x19, waiting for transfers between devices, shifted(): lax.ppermute(values, axis, [(i, (i + step) % count) for i in range(count)])  27.7 us
    ppermute x19, starting transfers between devices, shifted(): lax.ppermute(values, axis, [(i, (i + step) % count) for i in range(count)])  14.9 us
    unnamed x82, local copies, waits for them, and re-layouts  14.8 us
  transfers between devices with their start and end apart: 19, of which 8 were waited for; matrix products, arithmetic and copies ran while one was open for 2% of the time, Pallas kernels for 18%

profile of v2, /device:TPU:0, one launch (start us, length us, event | category | flops | bytes accessed | tf_op | source)
XLA Modules:
  0.0 107.1 jit_solution(147062504765030783)
XLA Ops:
  0.6 25.1 %shard_map.262 = (f32[392,256]{1,0:T(8,128)}, f32[392,256]{1,0:T(8,128)}) custom-call(f32[512,256]{1,0:T(8,128)} %ws.4, f32[512,256]{1,0:T(8,128)} %wr.4, f32[1,256]{1,0:T(1,128)} %bitcast.10, f32[256,512]{1,0:T(8,128)} %wo.4, f32[512,256]{1,0:T(8,128)} %ws.5, f32[512,256]{1,0:T(8,128)} %wr.5, f32[1,256]{1,0:T(1,128)} %bitcast.12, f32[256,512]{1,0:T(8,128)} %wo.5), custom_call_target="tpu_custom_call" | custom-call | flops 512 | bytes 3950592 | tf_op jit(solution)/shard_map/pallas_call | solution.py:310
  25.7 3.0 %collective-permute-start.9 = (f32[392,256]{1,0:T(8,128)}, f32[392,256]{1,0:T(8,128)S(1)}, u32[]{:S(2)}, u32[]{:S(2)}) collective-permute-start(f32[392,256]{1,0:T(8,128)} %get-tuple-element.47), channel_id=1, source_target_pairs={{0,2},{2,0},{1,3},{3,1},{4,6},{6,4},{5,7},{7,5},{8,10},{10,8},{9,1... | collective-permute-start | bytes 1204232 | tf_op jit(solution)/shard_map/ppermute | solution.py:327
  28.7 0.7 copy.28.children
  29.5 5.3 %shard_map.257.after.refs_0_ = f32[64,512]{1,0:T(8,128)} custom-call(f32[512,512]{1,0:T(8,128)} %nodes.3, f32[64,512]{1,0:T(8,128)} %refs_2_.1, s32[64,7]{1,0:T(8,128)} %copy.28.children, f32[512,256]{1,0:T(8,128)} %ws_hbm.1, f32[512,256]{1,0:T(8,128)} %wr_hbm.1, f32[1,256]{1,0:T(1,128)} %bitcast.19, f32[256,512]{1,0:T(8,128)} %wo_hbm.1), custom_call_target="tpu_custom_call" | custom-call | flops 637534208 | bytes 2886400 | tf_op jit(solution)/shard_map/pallas_call | solution.py:310
  34.7 0.1 collective-permute-start
  34.9 0.9 copy-done.7
  35.8 0.3 shard_map.258
  36.1 0.0 copy-start.37
  36.1 0.7 copy-done.37
  36.7 0.1 copy.29.links
  36.9 4.2 %collective-permute-done.refs_1_ = f32[64,512]{1,0:T(8,128)S(1)} collective-permute-done((f32[64,512]{1,0:T(8,128)}, f32[64,512]{1,0:T(8,128)S(1)}, u32[]{:S(2)}, u32[]{:S(2)}) %collective-permute-start) | collective-permute-done | bytes 131104 | tf_op jit(solution)/shard_map/ppermute | solution.py:327
  41.1 0.7 copy-done.31
  41.7 0.0 copy-done.34
  41.8 0.5 shard_map.259
  42.3 0.0 copy-start.24
  42.3 0.0 copy-start
  42.3 0.1 shard_map.260.refs_8_
  42.5 0.5 copy-done.24
  43.0 1.8 %collective-permute-start.11 = (f32[392,256]{1,0:T(8,128)S(1)}, f32[392,256]{1,0:T(8,128)S(1)}, u32[]{:S(2)}, u32[]{:S(2)}) collective-permute-start(f32[392,256]{1,0:T(8,128)S(1)} %collective-permute-done.9.refs_0_), channel_id=1, source_target_pairs={{0,16},{16,0},{1,17},{17,1},{2,18},{18,2},{3,19},{19,3},{4,20},{20... | collective-permute-start | bytes 1204232 | tf_op jit(solution)/shard_map/ppermute | solution.py:327
  44.7 8.7 %collective-permute-done.11.refs_2_ = f32[392,256]{1,0:T(8,128)S(1)} collective-permute-done((f32[392,256]{1,0:T(8,128)S(1)}, f32[392,256]{1,0:T(8,128)S(1)}, u32[]{:S(2)}, u32[]{:S(2)}) %collective-permute-start.11) | collective-permute-done | bytes 401440 | tf_op jit(solution)/shard_map/ppermute | solution.py:327
  53.4 1.4 %collective-permute-start.15 = (f32[392,256]{1,0:T(8,128)S(1)}, f32[392,256]{1,0:T(8,128)}, u32[]{:S(2)}, u32[]{:S(2)}) collective-permute-start(f32[392,256]{1,0:T(8,128)S(1)} %copy-done.38), channel_id=1, source_target_pairs={{0,2},{2,0},{1,3},{3,1},{4,6},{6,4},{5,7},{7,5},{8,10},{10,8},{9,1... | collective-permute-start | bytes 1204232 | tf_op jit(solution)/shard_map/ppermute | solution.py:327
  54.9 0.2 collective-permute-start.4
  55.1 3.6 %collective-permute-start.3 = (f32[64,256]{1,0:T(8,128)S(1)}, f32[64,256]{1,0:T(8,128)S(1)}, u32[]{:S(2)}, u32[]{:S(2)}) collective-permute-start(f32[64,256]{1,0:T(8,128)S(1)} %get-tuple-element.42.after.refs_0_), channel_id=1, source_target_pairs={{0,12},{4,0},{8,4},{12,8},{1,13},{5,1},{9,5},{13,9},{2,14},{6,2},{... | collective-permute-start | bytes 196616 | tf_op jit(solution)/shard_map/ppermute | solution.py:327
  58.7 0.0 collective-permute-start.2
  58.7 2.5 %collective-permute-done.3.refs_3_ = f32[64,256]{1,0:T(8,128)S(1)} collective-permute-done((f32[64,256]{1,0:T(8,128)S(1)}, f32[64,256]{1,0:T(8,128)S(1)}, u32[]{:S(2)}, u32[]{:S(2)}) %collective-permute-start.3) | collective-permute-done | bytes 65568 | tf_op jit(solution)/shard_map/ppermute | solution.py:327
  61.2 3.0 %collective-permute-done.2.refs_2_ = f32[64,256]{1,0:T(8,128)S(1)} collective-permute-done((f32[64,256]{1,0:T(8,128)S(1)}, f32[64,256]{1,0:T(8,128)S(1)}, u32[]{:S(2)}, u32[]{:S(2)}) %collective-permute-start.2) | collective-permute-done | bytes 65568 | tf_op jit(solution)/shard_map/ppermute | solution.py:327
  64.2 3.5 %collective-permute-done.1.refs_1_ = f32[64,256]{1,0:T(8,128)S(1)} collective-permute-done((f32[64,256]{1,0:T(8,128)S(1)}, f32[64,256]{1,0:T(8,128)S(1)}, u32[]{:S(2)}, u32[]{:S(2)}) %collective-permute-start.1) | collective-permute-done | bytes 65568 | tf_op jit(solution)/shard_map/ppermute | solution.py:327
  67.8 0.5 collective-permute-start.5
  68.3 0.7 collective-permute-done.6.refs_6_
  69.0 0.2 collective-permute-done.5.refs_5_
  69.2 0.8 shard_map.261.after.refs_0_
  70.0 0.2 copy-done.1
  70.2 0.2 copy-done.2
  70.4 1.0 copy-done.19
  71.4 1.6 %shard_map.263 = (f32[512,512]{1,0:T(8,128)S(1)}, bf16[2,512,256]{2,1,0:T(8,128)(2,1)S(1)}, bf16[2,512,256]{2,1,0:T(8,128)(2,1)S(1)}, bf16[512,512]{1,0:T(8,128)(2,1)S(1)}, bf16[512,512]{1,0:T(8,128)(2,1)S(1)}) custom-call(f32[64,512]{1,0:T(8,128)S(1)} %shard_map.261.after.refs_0_, f32[512,512]{1,0:T(8,128)S(1)} %copy-done, f32[512,256]{1,0:T(8,128)S(1)} %copy-done.1, ...), custom_call_target="tpu_custom_call" | custom-call | flops 805306368 | bytes 7504896 | tf_op jit(solution)/shard_map/pallas_call | solution.py:310
  73.0 0.0 copy-start.13
  73.0 0.8 copy-done.13
  73.8 0.8 copy-done.15
  74.6 1.5 %collective-permute-start.16 = (f32[392,256]{1,0:T(8,128)}, f32[392,256]{1,0:T(8,128)}, u32[]{:S(2)}, u32[]{:S(2)}) collective-permute-start(f32[392,256]{1,0:T(8,128)} %collective-permute-done.15.refs_0_), channel_id=1, source_target_pairs={{0,16},{16,0},{1,17},{17,1},{2,18},{18,2},{3,19},{19,3},{4,20},{20... | collective-permute-start | bytes 1204232 | tf_op jit(solution)/shard_map/ppermute | solution.py:327
  76.1 0.5 collective-permute-start.8
  76.6 0.1 copy.30.refs_6_.sources
  76.8 4.9 %collective-permute-done.8.refs_1_ = f32[64,512]{1,0:T(8,128)} collective-permute-done((f32[64,512]{1,0:T(8,128)S(1)}, f32[64,512]{1,0:T(8,128)}, u32[]{:S(2)}, u32[]{:S(2)}) %collective-permute-start.8) | collective-permute-done | bytes 131104 | tf_op jit(solution)/shard_map/ppermute | solution.py:327
  81.7 0.7 copy-done.32
  82.4 0.0 copy-done.28
  82.4 1.0 copy-done.14
  83.4 1.0 copy-done.16
  84.5 0.9 copy-done.25
  85.4 3.0 %shard_map.264 = (f32[64,512]{1,0:T(8,128)}, bf16[128,512]{1,0:T(8,128)(2,1)S(1)}, f32[128,512]{1,0:T(8,128)S(1)}, f32[128,512]{1,0:T(8,128)S(1)}) custom-call(f32[64,512]{1,0:T(8,128)S(1)} %shard_map.261.after.refs_0_, f32[64,512]{1,0:T(8,128)} %collective-permute-done.8.refs_1_, f32[64,512]{1,0:T(8,128)S(1)} %copy-done.25, f32[1,512]{1,0:T(1,128)S(1)} %bitcast.15, ...), custom_call_target="tpu_custom_call" | custom-call | flops 402653184 | bytes 5384192 | tf_op jit(solution)/shard_map/pallas_call | solution.py:310
  88.4 0.7 copy-done.20
  89.1 0.7 copy-done.22
  89.8 0.7 copy-done.26
  90.4 0.5 collective-permute-start.18
  90.9 1.6 %copy.32.links = s32[512,6]{1,0:T(8,128)} copy(s32[512,6]{0,1:T(8,128)} %param.30) | data formatting | bytes 24576 | tf_op args[4]
  92.5 1.7 %collective-permute-start.14 = (f32[128,512]{1,0:T(8,128)}, f32[128,512]{1,0:T(8,128)S(1)}, u32[]{:S(2)}, u32[]{:S(2)}) collective-permute-start(f32[128,512]{1,0:T(8,128)} %copy-done.20), channel_id=1, source_target_pairs={{0,13},{1,0},{4,1},{5,4},{8,5},{9,8},{12,9},{13,12},{2,15},{3,2},{... | collective-permute-start | bytes 786440 | tf_op jit(solution)/shard_map/ppermute | solution.py:327
  94.2 0.0 copy-start.5
  94.3 0.0 copy-start.6
  94.3 0.0 copy-start.30
  94.3 1.2 %shard_map.265.middle = f32[256,512]{1,0:T(8,128)S(1)} custom-call(f32[512,512]{1,0:T(8,128)S(1)} %copy-done, f32[512,512]{1,0:T(8,128)S(1)} %get-tuple-element.50.refs_5_.receivers, s32[512,3]{1,0:T(8,128)S(1)} %copy.30.refs_6_.sources, bf16[128,512]{1,0:T(8,128)(2,1)S(1)} %copy-done.27, bf16[512,512]{1,0:T(8,128)(2,1)S(1)} %get-tuple-element.53.refs_9_.wo_high, ...), custom_call_target="tpu_custom_call" | custom-call | flops 402653184 | bytes 3809280 | tf_op jit(solution)/shard_map/pallas_call | solution.py:310
  95.5 0.0 copy-start.23
  95.5 0.1 copy-done.6
  95.6 1.9 %shard_map.266 = (bf16[2,512,256]{2,1,0:T(8,128)(2,1)S(1)}, bf16[2,512,256]{2,1,0:T(8,128)(2,1)S(1)}, bf16[2,512,256]{2,1,0:T(8,128)(2,1)S(1)}, bf16[2,512,256]{...) custom-call(f32[512,256]{1,0:T(8,128)S(1)} %copy-done.4, ...), custom_call_target="tpu_custom_call" | custom-call | flops 262144 | bytes 6341632 | tf_op jit(solution)/shard_map/pallas_call | solution.py:310
  97.6 0.6 copy-done.33
  98.2 4.5 %shard_map.267 = (bf16[512,512]{1,0:T(8,128)(2,1)S(1)}, bf16[512,512]{1,0:T(8,128)(2,1)S(1)}, f32[512,512]{1,0:T(8,128)S(1)}, f32[256,512]{1,0:T(8,128)S(1)}) custom-call(f32[128,512]{1,0:T(8,128)S(1)} %copy-done.21, f32[256,512]{1,0:T(8,128)S(1)} %shard_map.265.middle, f32[128,512]{1,0:T(8,128)S(1)} %copy-done.23, s32[512,6]{1,0:T(8,128)S(1)} %copy-done.9, ...), custom_call_target="tpu_custom_call" | custom-call | flops 3221225472 | bytes 6846464 | tf_op jit(solution)/shard_map/pallas_call | solution.py:310
  102.7 4.3 %shard_map.268 = f32[512,512]{1,0:T(8,128)} custom-call(f32[128,512]{1,0:T(8,128)S(1)} %collective-permute-done.13.before, f32[128,512]{1,0:T(8,128)S(1)} %collective-permute-done.14.after, f32[128,512]{1,0:T(8,128)S(1)} %copy-done.21, f32[128,512]{1,0:T(8,128)S(1)} %copy-done.23, f32[256,512]{1,0:T(8,128)S(1)} %get-tuple-element.69.inner, ...), custom_call_target="tpu_custom_call" | custom-call | flops 805306368 | bytes 6830080 | tf_op jit(solution)/shard_map/pallas_call | solution.py:310
  (69 shorter events, 0.2 us)
Async XLA Ops:
  0.6 28.1 %copy-start.36 = (s32[64,7]{0,1:T(8,128)S(1)}, s32[64,7]{0,1:T(8,128)}, u32[]{:S(2)}) copy-start(s32[64,7]{0,1:T(8,128)} %param.28) | copy-start | bytes 5380
  25.7 17.2 %collective-permute-start.9 = (f32[392,256]{1,0:T(8,128)}, f32[392,256]{1,0:T(8,128)S(1)}, u32[]{:S(2)}, u32[]{:S(2)}) collective-permute-start(f32[392,256]{1,0:T(8,128)} %get-tuple-element.47), channel_id=1, source_target_pairs={{0,2},{2,0},{1,3},{3,1},{4,6},{6,4},{5,7},{7,5},{8,10},{10,8},{9,1... | collective-permute-start | bytes 1204232 | tf_op jit(solution)/shard_map/ppermute | solution.py:327
  29.4 5.4 %copy-start.10 = (f32[512,256]{1,0:T(8,128)S(1)}, f32[512,256]{1,0:T(8,128)}, u32[]{:S(2)}) copy-start(f32[512,256]{1,0:T(8,128)} %ws.3) | copy-start | bytes 1572868
  29.5 5.4 %copy-start.11 = (f32[512,256]{1,0:T(8,128)S(1)}, f32[512,256]{1,0:T(8,128)}, u32[]{:S(2)}) copy-start(f32[512,256]{1,0:T(8,128)} %wr.3) | copy-start | bytes 1572868
  29.5 5.4 %copy-start.12 = (f32[256,512]{1,0:T(8,128)S(1)}, f32[256,512]{1,0:T(8,128)}, u32[]{:S(2)}) copy-start(f32[256,512]{1,0:T(8,128)} %wo.3) | copy-start | bytes 1572868
  34.7 6.3 %collective-permute-start = (f32[64,512]{1,0:T(8,128)}, f32[64,512]{1,0:T(8,128)S(1)}, u32[]{:S(2)}, u32[]{:S(2)}) collective-permute-start(f32[64,512]{1,0:T(8,128)} %shard_map.257.after.refs_0_), channel_id=1, source_target_pairs={{0,2},{2,0},{1,3},{3,1},{4,6},{6,4},{5,7},{7,5},{8,10},{10,8},{9,1... | collective-permute-start | bytes 393224 | tf_op jit(solution)/shard_map/ppermute | solution.py:327
  34.8 0.9 copy-start.7
  35.8 5.3 %copy-start.8 = (f32[64,512]{1,0:T(8,128)S(1)}, f32[64,512]{1,0:T(8,128)}, u32[]{:S(2)}) copy-start(f32[64,512]{1,0:T(8,128)} %shard_map.257.after.refs_0_) | copy-start | bytes 393220
  35.8 5.3 %copy-start.17 = (f32[64,512]{1,0:T(8,128)S(1)}, f32[64,512]{1,0:T(8,128)}, u32[]{:S(2)}) copy-start(f32[64,512]{1,0:T(8,128)} %refs_2_.1) | copy-start | bytes 393220
  36.1 0.7 copy-start.37
  41.1 0.7 copy-start.31
  41.1 0.7 copy-start.34
  41.7 11.7 %copy-start.38 = (f32[392,256]{1,0:T(8,128)S(1)}, f32[392,256]{1,0:T(8,128)}, u32[]{:S(2)}) copy-start(f32[392,256]{1,0:T(8,128)} %get-tuple-element.58) | copy-start | bytes 1204228
  41.7 28.2 %copy-start.3 = (f32[256,512]{1,0:T(8,128)S(1)}, f32[256,512]{1,0:T(8,128)}, u32[]{:S(2)}) copy-start(f32[256,512]{1,0:T(8,128)} %wo.4) | copy-start | bytes 1572868
  42.3 0.7 copy-start.24
  42.3 27.7 %copy-start = (f32[512,512]{1,0:T(8,128)S(1)}, f32[512,512]{1,0:T(8,128)}, u32[]{:S(2)}) copy-start(f32[512,512]{1,0:T(8,128)} %nodes.3) | copy-start | bytes 3145732
  43.0 27.0 %copy-start.18 = (f32[392,256]{1,0:T(8,128)}, f32[392,256]{1,0:T(8,128)S(1)}, u32[]{:S(2)}) copy-start(f32[392,256]{1,0:T(8,128)S(1)} %collective-permute-done.9.refs_0_) | copy-start | bytes 1204228
  43.0 10.5 %collective-permute-start.11 = (f32[392,256]{1,0:T(8,128)S(1)}, f32[392,256]{1,0:T(8,128)S(1)}, u32[]{:S(2)}, u32[]{:S(2)}) collective-permute-start(f32[392,256]{1,0:T(8,128)S(1)} %collective-permute-done.9.refs_0_), channel_id=1, source_target_pairs={{0,16},{16,0},{1,17},{17,1},{2,18},{18,2},{3,19},{19,3},{4,20},{20... | collective-permute-start | bytes 1204232 | tf_op jit(solution)/shard_map/ppermute | solution.py:327
  44.7 25.2 %collective-permute-start.10 = (f32[392,256]{1,0:T(8,128)S(1)}, f32[392,256]{1,0:T(8,128)S(1)}, u32[]{:S(2)}, u32[]{:S(2)}) collective-permute-start(f32[392,256]{1,0:T(8,128)S(1)} %collective-permute-done.9.refs_0_), channel_id=1, source_target_pairs={{0,1},{1,0},{2,3},{3,2},{4,5},{5,4},{6,7},{7,6},{8,9},{9,8},{10,11... | collective-permute-start | bytes 1204232 | tf_op jit(solution)/shard_map/ppermute | solution.py:327
  53.4 16.5 %collective-permute-start.12 = (f32[392,256]{1,0:T(8,128)S(1)}, f32[392,256]{1,0:T(8,128)S(1)}, u32[]{:S(2)}, u32[]{:S(2)}) collective-permute-start(f32[392,256]{1,0:T(8,128)S(1)} %collective-permute-done.11.refs_2_), channel_id=1, source_target_pairs={{0,1},{1,0},{2,3},{3,2},{4,5},{5,4},{6,7},{7,6},{8,9},{9,8},{10,11... | collective-permute-start | bytes 1204232 | tf_op jit(solution)/shard_map/ppermute | solution.py:327
  53.4 21.1 %collective-permute-start.15 = (f32[392,256]{1,0:T(8,128)S(1)}, f32[392,256]{1,0:T(8,128)}, u32[]{:S(2)}, u32[]{:S(2)}) collective-permute-start(f32[392,256]{1,0:T(8,128)S(1)} %copy-done.38), channel_id=1, source_target_pairs={{0,2},{2,0},{1,3},{3,1},{4,6},{6,4},{5,7},{7,5},{8,10},{10,8},{9,1... | collective-permute-start | bytes 1204232 | tf_op jit(solution)/shard_map/ppermute | solution.py:327
  54.9 3.8 %collective-permute-start.4 = (f32[64,256]{1,0:T(8,128)S(1)}, f32[64,256]{1,0:T(8,128)S(1)}, u32[]{:S(2)}, u32[]{:S(2)}) collective-permute-start(f32[64,256]{1,0:T(8,128)S(1)} %get-tuple-element.42.after.refs_0_), channel_id=1, source_target_pairs={{0,1},{1,0},{2,3},{3,2},{4,5},{5,4},{6,7},{7,6},{8,9},{9,8},{10,11... | collective-permute-start | bytes 196616 | tf_op jit(solution)/shard_map/ppermute | solution.py:327
  55.1 6.1 %collective-permute-start.3 = (f32[64,256]{1,0:T(8,128)S(1)}, f32[64,256]{1,0:T(8,128)S(1)}, u32[]{:S(2)}, u32[]{:S(2)}) collective-permute-start(f32[64,256]{1,0:T(8,128)S(1)} %get-tuple-element.42.after.refs_0_), channel_id=1, source_target_pairs={{0,12},{4,0},{8,4},{12,8},{1,13},{5,1},{9,5},{13,9},{2,14},{6,2},{... | collective-permute-start | bytes 196616 | tf_op jit(solution)/shard_map/ppermute | solution.py:327
  58.7 5.5 %collective-permute-start.2 = (f32[64,256]{1,0:T(8,128)S(1)}, f32[64,256]{1,0:T(8,128)S(1)}, u32[]{:S(2)}, u32[]{:S(2)}) collective-permute-start(f32[64,256]{1,0:T(8,128)S(1)} %get-tuple-element.42.after.refs_0_), channel_id=1, source_target_pairs={{0,8},{4,12},{8,0},{12,4},{1,9},{5,13},{9,1},{13,5},{2,10},{6,14},... | collective-permute-start | bytes 196616 | tf_op jit(solution)/shard_map/ppermute | solution.py:327
  61.2 6.6 %collective-permute-start.1 = (f32[64,256]{1,0:T(8,128)S(1)}, f32[64,256]{1,0:T(8,128)S(1)}, u32[]{:S(2)}, u32[]{:S(2)}) collective-permute-start(f32[64,256]{1,0:T(8,128)S(1)} %get-tuple-element.42.after.refs_0_), channel_id=1, source_target_pairs={{0,4},{4,8},{8,12},{12,0},{1,5},{5,9},{9,13},{13,1},{2,6},{6,10},{... | collective-permute-start | bytes 196616 | tf_op jit(solution)/shard_map/ppermute | solution.py:327
  64.2 3.6 %collective-permute-start.7 = (f32[64,256]{1,0:T(8,128)S(1)}, f32[64,256]{1,0:T(8,128)S(1)}, u32[]{:S(2)}, u32[]{:S(2)}) collective-permute-start(f32[64,256]{1,0:T(8,128)S(1)} %collective-permute-done.3.refs_3_), channel_id=1, source_target_pairs={{0,1},{1,0},{2,3},{3,2},{4,5},{5,4},{6,7},{7,6},{8,9},{9,8},{10,11... | collective-permute-start | bytes 196616 | tf_op jit(solution)/shard_map/ppermute | solution.py:327
  67.8 1.3 %collective-permute-start.6 = (f32[64,256]{1,0:T(8,128)S(1)}, f32[64,256]{1,0:T(8,128)S(1)}, u32[]{:S(2)}, u32[]{:S(2)}) collective-permute-start(f32[64,256]{1,0:T(8,128)S(1)} %collective-permute-done.2.refs_2_), channel_id=1, source_target_pairs={{0,1},{1,0},{2,3},{3,2},{4,5},{5,4},{6,7},{7,6},{8,9},{9,8},{10,11... | collective-permute-start | bytes 196616 | tf_op jit(solution)/shard_map/ppermute | solution.py:327
  67.8 1.4 %collective-permute-start.5 = (f32[64,256]{1,0:T(8,128)S(1)}, f32[64,256]{1,0:T(8,128)S(1)}, u32[]{:S(2)}, u32[]{:S(2)}) collective-permute-start(f32[64,256]{1,0:T(8,128)S(1)} %collective-permute-done.1.refs_1_), channel_id=1, source_target_pairs={{0,1},{1,0},{2,3},{3,2},{4,5},{5,4},{6,7},{7,6},{8,9},{9,8},{10,11... | collective-permute-start | bytes 196616 | tf_op jit(solution)/shard_map/ppermute | solution.py:327
  69.2 1.0 copy-start.1
  69.2 1.2 %copy-start.2 = (f32[512,256]{1,0:T(8,128)S(1)}, f32[512,256]{1,0:T(8,128)}, u32[]{:S(2)}) copy-start(f32[512,256]{1,0:T(8,128)} %wr.4) | copy-start | bytes 1572868
  69.2 1.2 %copy-start.29 = (f32[256]{0:T(256)S(1)}, f32[256]{0:T(256)}, u32[]{:S(2)}) copy-start(f32[256]{0:T(256)} %param.44) | copy-start | bytes 3076
  69.2 7.5 %copy-start.35 = (s32[512,3]{0,1:T(4,128)S(1)}, s32[512,3]{0,1:T(4,128)}, u32[]{:S(2)}) copy-start(s32[512,3]{0,1:T(4,128)} %param.29) | copy-start | bytes 18436
  70.4 1.0 copy-start.19
  73.0 0.8 copy-start.13
  73.8 0.8 copy-start.15
  74.6 15.9 %collective-permute-start.16 = (f32[392,256]{1,0:T(8,128)}, f32[392,256]{1,0:T(8,128)}, u32[]{:S(2)}, u32[]{:S(2)}) collective-permute-start(f32[392,256]{1,0:T(8,128)} %collective-permute-done.15.refs_0_), channel_id=1, source_target_pairs={{0,16},{16,0},{1,17},{17,1},{2,18},{18,2},{3,19},{19,3},{4,20},{20... | collective-permute-start | bytes 1204232 | tf_op jit(solution)/shard_map/ppermute | solution.py:327
  76.1 5.6 %collective-permute-start.8 = (f32[64,512]{1,0:T(8,128)S(1)}, f32[64,512]{1,0:T(8,128)}, u32[]{:S(2)}, u32[]{:S(2)}) collective-permute-start(f32[64,512]{1,0:T(8,128)S(1)} %shard_map.261.after.refs_0_), channel_id=1, source_target_pairs={{0,2},{2,0},{1,3},{3,1},{4,6},{6,4},{5,7},{7,5},{8,10},{10,8},{9,1... | collective-permute-start | bytes 393224 | tf_op jit(solution)/shard_map/ppermute | solution.py:327
  81.7 0.7 copy-start.32
  81.7 0.7 copy-start.28
  82.4 1.0 copy-start.14
  83.4 1.0 copy-start.16
  84.5 0.9 copy-start.25
  88.4 0.7 copy-start.20
  89.1 0.7 copy-start.22
  89.8 0.7 copy-start.26
  90.4 3.8 %copy-start.27 = (bf16[128,512]{1,0:T(8,128)(2,1)S(1)}, bf16[128,512]{1,0:T(8,128)(2,1)}, u32[]{:S(2)}) copy-start(bf16[128,512]{1,0:T(8,128)(2,1)} %copy-done.26) | copy-start | bytes 393220
  90.4 5.1 %collective-permute-start.17 = (f32[392,256]{1,0:T(8,128)}, f32[392,256]{1,0:T(8,128)}, u32[]{:S(2)}, u32[]{:S(2)}) collective-permute-start(f32[392,256]{1,0:T(8,128)} %collective-permute-done.15.refs_0_), channel_id=1, source_target_pairs={{0,1},{1,0},{2,3},{3,2},{4,5},{5,4},{6,7},{7,6},{8,9},{9,8},{10,11... | collective-permute-start | bytes 1204232 | tf_op jit(solution)/shard_map/ppermute | solution.py:327
  90.4 5.1 %collective-permute-start.18 = (f32[392,256]{1,0:T(8,128)}, f32[392,256]{1,0:T(8,128)}, u32[]{:S(2)}, u32[]{:S(2)}) collective-permute-start(f32[392,256]{1,0:T(8,128)} %collective-permute-done.16.refs_2_), channel_id=1, source_target_pairs={{0,1},{1,0},{2,3},{3,2},{4,5},{5,4},{6,7},{7,6},{8,9},{9,8},{10,11... | collective-permute-start | bytes 1204232 | tf_op jit(solution)/shard_map/ppermute | solution.py:327
  92.5 10.2 %collective-permute-start.14 = (f32[128,512]{1,0:T(8,128)}, f32[128,512]{1,0:T(8,128)S(1)}, u32[]{:S(2)}, u32[]{:S(2)}) collective-permute-start(f32[128,512]{1,0:T(8,128)} %copy-done.20), channel_id=1, source_target_pairs={{0,13},{1,0},{4,1},{5,4},{8,5},{9,8},{12,9},{13,12},{2,15},{3,2},{... | collective-permute-start | bytes 786440 | tf_op jit(solution)/shard_map/ppermute | solution.py:327
  94.2 8.5 %collective-permute-start.13 = (f32[128,512]{1,0:T(8,128)}, f32[128,512]{1,0:T(8,128)S(1)}, u32[]{:S(2)}, u32[]{:S(2)}) collective-permute-start(f32[128,512]{1,0:T(8,128)} %copy-done.22), channel_id=1, source_target_pairs={{0,1},{1,4},{4,5},{5,8},{8,9},{9,12},{12,13},{13,0},{2,3},{3,6},{6... | collective-permute-start | bytes 786440 | tf_op jit(solution)/shard_map/ppermute | solution.py:327
  94.2 1.3 %copy-start.4 = (f32[512,256]{1,0:T(8,128)S(1)}, f32[512,256]{1,0:T(8,128)}, u32[]{:S(2)}) copy-start(f32[512,256]{1,0:T(8,128)} %ws.5) | copy-start | bytes 1572868
  94.2 1.3 %copy-start.5 = (f32[512,256]{1,0:T(8,128)S(1)}, f32[512,256]{1,0:T(8,128)}, u32[]{:S(2)}) copy-start(f32[512,256]{1,0:T(8,128)} %wr.5) | copy-start | bytes 1572868
  94.3 1.3 %copy-start.6 = (f32[256,512]{1,0:T(8,128)S(1)}, f32[256,512]{1,0:T(8,128)}, u32[]{:S(2)}) copy-start(f32[256,512]{1,0:T(8,128)} %wo.5) | copy-start | bytes 1572868
  94.3 1.3 %copy-start.30 = (f32[256]{0:T(256)S(1)}, f32[256]{0:T(256)}, u32[]{:S(2)}) copy-start(f32[256]{0:T(256)} %param.49) | copy-start | bytes 3076
  95.4 2.1 %copy-start.9 = (s32[512,6]{1,0:T(8,128)S(1)}, s32[512,6]{1,0:T(8,128)}, u32[]{:S(2)}) copy-start(s32[512,6]{1,0:T(8,128)} %copy.32.links) | copy-start | bytes 36868
  95.5 2.1 %copy-start.21 = (f32[128,512]{1,0:T(8,128)S(1)}, f32[128,512]{1,0:T(8,128)}, u32[]{:S(2)}) copy-start(f32[128,512]{1,0:T(8,128)} %copy-done.20) | copy-start | bytes 786436
  95.5 2.1 %copy-start.23 = (f32[128,512]{1,0:T(8,128)S(1)}, f32[128,512]{1,0:T(8,128)}, u32[]{:S(2)}) copy-start(f32[128,512]{1,0:T(8,128)} %copy-done.22) | copy-start | bytes 786436
  97.5 0.7 copy-start.33

commit v3 on v2

--- a/solution.py
+++ b/solution.py
@@ -10,7 +10,8 @@
 epsilon = 1e-05
 f32 = jnp.float32
 bf16 = jnp.bfloat16
-limit_bytes = 40 * 1024 * 1024
+limit_bytes = 16 * 1024 * 1024
+wide_limit = 50 * 1024 * 1024
 large_limit = 60 * 1024 * 1024
 most_direct = 4
 
@@ -33,6 +34,16 @@
     center = values - jnp.mean(values, axis=-1, keepdims=True)
     spread = jnp.mean(center * center, axis=-1, keepdims=True)
     return center * lax.rsqrt(spread + epsilon)
+
+
+def upright(rows):
+    count, size = rows.shape
+    tall, wide = -count % 8, -size % 128
+    if tall:
+        rows = jnp.concatenate([rows, jnp.zeros((tall, size), rows.dtype)], axis=0)
+    if wide:
+        rows = jnp.concatenate([rows, jnp.zeros((count + tall, wide), rows.dtype)], axis=1)
+    return jnp.transpose(rows)[:size, :count]
 
 
 def one_hot(wanted, names):
@@ -69,39 +80,24 @@
     return moves
 
 
-def strips(source, target, count):
-    rows = source.shape[0] // count
-    return [
-        (source.at[pl.ds(i * rows, rows)], target.at[pl.ds(i * rows, rows)]) for i in range(count)
-    ]
-
-
-def upward_kernel(nodes_hbm, coarse, children, ws_hbm, wr_hbm, bias, wo_hbm, part, nodes, ws, wr, wo, sems):
-    moves = started(
-        strips(ws_hbm, ws, 2)
-        + strips(nodes_hbm, nodes, 4)
-        + strips(wr_hbm, wr, 2)
-        + strips(wo_hbm, wo, 2),
-        sems,
-    )
-    wanted = children[...]
+def upward_kernel(nodes, coarse, children, ws, wr, bias, wo, part):
+    wanted = upright(children[...])
     names = lax.broadcasted_iota(jnp.int32, (wanted.shape[0], nodes.shape[0]), 1)
     picks = one_hot(wanted, names)
-    for move in moves[:6]:
-        move.wait()
     sender_high, sender_low = split(0.5 * dot3(nodes[...], *split(ws[...])))
-    for move in moves[6:8]:
-        move.wait()
     receivers = 0.5 * (dot3(coarse[...], *split(wr[...])) + bias[...])
     picked = dot(picks, sender_high) + dot(picks, sender_low)
     hidden = silu_sum(picked, receivers, wanted.shape[1])
-    for move in moves[8:]:
-        move.wait()
     part[...] = dot3(hidden, *split(wo[...]))
 
 
-def coarse_ready_kernel(after, ws, wr, wo, ws_high, ws_low, wr_high, wr_low, wo_high, wo_low):
+def coarse_ready_kernel(after, ws, wr, wo, *refs):
     del after
+    params, (ws_high, ws_low, wr_high, wr_low, wo_high, wo_low, gains, biases) = refs[:7], refs[7:]
+    for i in range(4):
+        gains[i : i + 1] = params[i][...]
+    for i in range(3):
+        biases[i : i + 1] = params[4 + i][...]
     ws_high[...], ws_low[...] = split(ws[...])
     wr_high[...], wr_low[...] = split(wr[...])
     wo_high[...], wo_low[...] = split(wo[...])
@@ -134,21 +130,22 @@
 
 def picks_kernel(after, links, names, picks):
     del after
-    wanted = links[...]
+    wanted = upright(links[...])
     picks[...] = one_hot(wanted, jnp.broadcast_to(names[...], (wanted.shape[0], names.shape[1])))
 
 
 def coarse_project_kernel(count, *refs):
     parts, refs = refs[:count], refs[count:]
-    coarse, gain, ws_high, ws_low, wr_high, wr_low, bias, updated, senders, receivers = refs
-    rows = coarse[...] + gain[...] * normed(added(parts))
+    coarse, gains, biases, ws_high, ws_low, wr_high, wr_low, updated, senders, receivers = refs
+    rows = coarse[...] + gains[0:1] * normed(added(parts))
     updated[...] = rows
     senders[...] = 0.5 * dot3(rows, ws_high[...], ws_low[...])
-    receivers[...] = 0.5 * (dot3(rows, wr_high[...], wr_low[...]) + bias[...])
+    receivers[...] = 0.5 * (dot3(rows, wr_high[...], wr_low[...]) + biases[0:1])
 
 
 def coarse_kernel(count, *refs):
-    pieces, (all_picks, receivers, wo_high, wo_low, part) = refs[:count], refs[count:]
+    pieces, (all_picks, receivers, wo_high, wo_low) = refs[:count], refs[count : count + 4]
+    part = refs[-1]
     senders = jnp.concatenate([piece[...] for piece in pieces], axis=0)
     sender_high, sender_low = split(senders)
     picks = all_picks[...]
@@ -167,7 +164,7 @@
     wr_high[sub], wr_low[sub] = split(wr[...])
     rows = pl.ds(pl.multiple_of(sub * width, width), width)
     wo_high[rows, :], wo_low[rows, :] = split(wo[...])
-    bias_all[sub] = jnp.broadcast_to(bias[...], (8, width))
+    bias_all[sub] = jnp.broadcast_to(bias, (8, width))
     share, thin = depth // (parts * lvls), width // (parts * lvls)
     columns = wo.shape[1] // width
     place = iter(packs)
@@ -190,12 +187,11 @@
                     bias_all[block] = jnp.broadcast_to(pack[last : last + 1, :], (8, width))
 
 
-def down_ready_kernel(count, after, nodes, ws, wr, bias, wo, *refs):
-    del after
+def down_ready_kernel(count, nodes, ws, wr, biases, wo, *refs):
     packs = refs[:count]
     receivers, ws_high, ws_low, wo_high, wo_low, wr_high, wr_low, bias_all = refs[count:]
     collect(
-        (ws, wr, bias, wo), packs, (ws_high, ws_low, wr_high, wr_low, wo_high, wo_low, bias_all)
+        (ws, wr, biases[1:2], wo), packs, (ws_high, ws_low, wr_high, wr_low, wo_high, wo_low, bias_all)
     )
     width = ws.shape[1]
     for g in range(ws_high.shape[0]):
@@ -203,8 +199,8 @@
         receivers[:, g * width : (g + 1) * width] = 0.5 * (product + bias_all[g][0:1])
 
 
-def bottom_ready_kernel(count, ws, wr, bias, wo, *refs):
-    collect((ws, wr, bias, wo), refs[:count], refs[count:])
+def bottom_ready_kernel(count, ws, wr, biases, wo, *refs):
+    collect((ws, wr, biases[2:3], wo), refs[:count], refs[count:])
 
 
 def down_rows(nodes, receivers, sources, senders, wo_high, wo_low, gain):
@@ -218,9 +214,9 @@
 
 def down_edge_kernel(count, rim, *refs):
     parts, refs = refs[:count], refs[count:]
-    (coarse_up, coarse_gain, nodes, receivers, sources, ws_high, ws_low, wo_high, wo_low, gain) = refs[:10]
-    new_coarse, senders, head, tail = refs[10:]
-    rows = coarse_up[...] + coarse_gain[...] * normed(added(parts))
+    (coarse_up, gains, nodes, receivers, sources, ws_high, ws_low, wo_high, wo_low) = refs[:9]
+    new_coarse, senders, head, tail = refs[9:]
+    rows = coarse_up[...] + gains[1:2] * normed(added(parts))
     new_coarse[...] = rows
     blocks = rows.shape[0]
     width = ws_high.shape[2]
@@ -230,16 +226,17 @@
         senders[0:blocks, columns] = high
         senders[blocks : 2 * blocks, columns] = low
     total = nodes.shape[0]
+    wanted = upright(sources[...])
     for out, place in ((head, slice(0, rim)), (tail, slice(total - rim, total))):
         out[...] = down_rows(
-            nodes[place], receivers[place], sources[place], senders[...], wo_high[...], wo_low[...], gain[...]
+            nodes[place], receivers[place], wanted[place], senders[...], wo_high[...], wo_low[...], gains[2:3]
         )
 
 
-def down_middle_kernel(rim, nodes, receivers, sources, senders, wo_high, wo_low, gain, middle):
+def down_middle_kernel(rim, nodes, receivers, sources, senders, wo_high, wo_low, gains, middle):
     place = slice(rim, nodes.shape[0] - rim)
     middle[...] = down_rows(
-        nodes[place], receivers[place], sources[place], senders[...], wo_high[...], wo_low[...], gain[...]
+        nodes[place], receivers[place], upright(sources[...])[place], senders[...], wo_high[...], wo_low[...], gains[2:3]
     )
 
 
@@ -255,7 +252,7 @@
     return nodes + gain * normed(dot3(jnp.concatenate(hidden, axis=1), wo_high, wo_low))
 
 
-def bottom_middle_kernel(rim, head, middle, tail, links, ws_high, ws_low, wr_high, wr_low, wo_high, wo_low, bias, gain, senders_high, senders_low, receivers, out):
+def bottom_middle_kernel(rim, head, middle, tail, links, ws_high, ws_low, wr_high, wr_low, wo_high, wo_low, bias, gains, senders_high, senders_low, receivers, out):
     nodes = jnp.concatenate([head[...], middle[...], tail[...]], axis=0)
     nodes_high, nodes_low = split(nodes)
     width = ws_high.shape[2]
@@ -266,19 +263,20 @@
         product = dot(nodes_high, wr_high[g]) + (dot(nodes_high, wr_low[g]) + dot(nodes_low, wr_high[g]))
         receivers[:, columns] = 0.5 * (product + bias[g][0:1])
     total = nodes.shape[0]
+    wanted = upright(links[...])
     for first in range(rim, total - rim, rim):
         place = slice(first, first + rim)
         reach = slice(first - rim, first + 2 * rim)
         out[first - rim : first, :] = bottom_rows(
-            middle[first - rim : first], receivers[place], links[place], first,
-            senders_high[reach], senders_low[reach], wo_high[...], wo_low[...], gain[...],
+            middle[first - rim : first], receivers[place], wanted[place], first,
+            senders_high[reach], senders_low[reach], wo_high[...], wo_low[...], gains[3:4],
         )
 
 
-def bottom_edge_kernel(rim, before, after, head, tail, inner, links, senders_high, senders_low, receivers, ws_high, ws_low, wo_high, wo_low, gain, out):
-    total = links.shape[0]
+def bottom_edge_kernel(rim, before, after, head, tail, inner, links, senders_high, senders_low, receivers, ws_high, ws_low, wo_high, wo_low, gains, out):
+    total = links.shape[1]
+    wanted = upright(links[...])
     out[rim : total - rim, :] = inner[...]
-    edges = ((before, head, slice(0, rim), slice(0, 2 * rim)), (after, tail, slice(total - rim, total), slice(total - 2 * rim, total)))
     outer = split(jnp.concatenate([before[...], after[...]], axis=0))
     projected = jnp.concatenate(
         [
@@ -296,8 +294,8 @@
         high = jnp.concatenate(order(outer_high[strip], senders_high[reach]), axis=0)
         low = jnp.concatenate(order(outer_low[strip], senders_low[reach]), axis=0)
         out[place, :] = bottom_rows(
-            nodes[...], receivers[place], links[place], 0 if side == 0 else total - rim,
-            high, low, wo_high[...], wo_low[...], gain[...],
+            nodes[...], receivers[place], wanted[place], 0 if side == 0 else total - rim,
+            high, low, wo_high[...], wo_low[...], gains[3:4],
         )
 
 
@@ -337,11 +335,10 @@
     patches, lvls = lax.axis_size("patch"), lax.axis_size("lvl")
     if patches > most_direct:
         return [lax.all_gather(senders, ("patch", "lvl"), axis=0, tiled=True)]
-    pieces = [senders] + [shifted(senders, "patch", s) for s in range(1, patches)]
-    everything = list(pieces)
-    for t in range(1, lvls):
-        everything += [shifted(piece, "lvl", t) for piece in pieces]
-    return everything
+    near = [[senders] + [shifted(senders, "lvl", t) for t in range(1, lvls)]]
+    pieces = lax.optimization_barrier([shifted(senders, "patch", s) for s in range(1, patches)])
+    near += [[piece] + [shifted(piece, "lvl", t) for t in range(1, lvls)] for piece in pieces]
+    return [row[t] for t in range(lvls) for row in near]
 
 
 def coarse_names(rows):
@@ -418,7 +415,7 @@
     rim = rows // 4
     weights = [like((subs, latent, width), bf16)] * 2
     outputs = [like((hidden, latent), bf16)] * 2
-    biases = like((subs, 8, width))
+    bias_rows = like((subs, 8, width))
 
     shares = lax.axis_size("parts") * lax.axis_size("lvl")
     columns = latent // width
@@ -433,37 +430,32 @@
         latent,
         [pltpu.SemaphoreType.DMA((2 * (3 + columns),))],
         far=range(8),
-        far_outs=(0, 1),
         limit=large_limit,
     )
     down_near = over_sub(down_pack)
     (part,) = call(
         upward_kernel,
         [like((blocks, latent))],
-        [node_states, coarse_states, children, upward_sender, upward_receiver, upward_bias[None], upward_output],
+        [node_states, coarse_states, children.T, upward_sender, upward_receiver, upward_bias[None], upward_output],
         6 * rows * latent * width + 4 * children.size * rows * width,
+        limit=wide_limit,
+    )
+    parts = sub_parts(part)
+    ws_high, ws_low, wr_high, wr_low, wo_high, wo_low, gains, biases = call(
+        coarse_ready_kernel,
+        [like((latent, width), bf16)] * 4 + [like((width, latent), bf16)] * 2 + [like((4, latent)), like((3, width))],
         [
-            pltpu.VMEM((rows, latent), f32),
-            pltpu.VMEM((latent, width), f32),
-            pltpu.VMEM((latent, width), f32),
-            pltpu.VMEM((width, latent), f32),
-            pltpu.SemaphoreType.DMA((10,)),
+            part, coarse_sender, coarse_receiver, coarse_output,
+            upward_gain[None], coarse_gain[None], downward_gain[None], bottom_gain[None],
+            coarse_bias[None], downward_bias[None], bottom_bias[None],
         ],
-        far=(0, 3, 4, 6),
-        limit=large_limit,
-    )
-    parts = sub_parts(part)
-    ws_high, ws_low, wr_high, wr_low, wo_high, wo_low = call(
-        coarse_ready_kernel,
-        [like((latent, width), bf16)] * 4 + [like((width, latent), bf16)] * 2,
-        [part, coarse_sender, coarse_receiver, coarse_output],
         latent * hidden,
         far=(0,),
     )
     coarse_up, senders, receivers = call(
         functools.partial(coarse_project_kernel, len(parts)),
         [like((blocks, latent)), like((blocks, width)), like((blocks, width))],
-        [*parts, coarse_states, upward_gain[None], ws_high, ws_low, wr_high, wr_low, coarse_bias[None]],
+        [*parts, coarse_states, gains, biases, ws_high, ws_low, wr_high, wr_low],
         12 * blocks * latent * width,
     )
     pieces = coarse_pieces(senders)
@@ -471,36 +463,40 @@
     (picks,) = call(
         picks_kernel,
         [like((coarse_links.size, names.size), bf16)],
-        [senders, coarse_links, names],
+        [senders, coarse_links.T, names],
         coarse_links.size * names.size,
         far=(0,),
     )
-    down_near, bottom_pack = held((down_near, bottom_pack), picks)
+    down_near, bottom_pack = held((down_near, bottom_pack), pieces[len(pieces) // 2])
     down_far = over_parts(down_near)
     bottom_near = over_sub(bottom_pack)
+    down_near, down_far, bottom_near = held(
+        (down_near, down_far, bottom_near), pieces[min(1, len(pieces) - 1)]
+    )
     down_packs = all_shares(down_near, down_far)
+    down_receivers, ws_high, ws_low, down_high, down_low = call(
+        functools.partial(down_ready_kernel, len(down_packs)),
+        [like((rows, hidden)), *weights, *outputs],
+        [node_states, downward_sender, downward_receiver, biases, downward_output, *down_packs],
+        6 * rows * latent * hidden,
+        [pltpu.VMEM((subs, latent, width), bf16)] * 2 + [pltpu.VMEM((subs, 8, width), f32)],
+    )
     (part,) = call(
         functools.partial(coarse_kernel, len(pieces)),
         [like((blocks, latent))],
-        [*pieces, picks, receivers, wo_high, wo_low],
+        [*pieces, picks, receivers, wo_high, wo_low, down_receivers],
         4 * coarse_links.size * names.size * width,
+        far=(len(pieces) + 4,),
     )
     parts = sub_parts(part)
-
-    receivers, ws_high, ws_low, wo_high, wo_low = call(
-        functools.partial(down_ready_kernel, len(down_packs)),
-        [like((rows, hidden)), *weights, *outputs],
-        [part, node_states, *down_own, *down_packs],
-        6 * rows * latent * hidden,
-        [pltpu.VMEM((subs, latent, width), bf16)] * 2 + [pltpu.VMEM((subs, 8, width), f32)],
-        far=(0,),
-    )
-    bottom_near = held(bottom_near, receivers)
+    receivers, wo_high, wo_low = down_receivers, down_high, down_low
+
+    bottom_near = held(bottom_near, part)
     bottom_far = over_parts(bottom_near)
     new_coarse, senders, head, tail = call(
         functools.partial(down_edge_kernel, len(parts), rim),
         [like((blocks, latent)), like((2 * blocks, hidden), bf16), like((rim, latent)), like((rim, latent))],
-        [*parts, coarse_up, coarse_gain[None], node_states, receivers, down_sources, ws_high, ws_low, wo_high, wo_low, downward_gain[None]],
+        [*parts, coarse_up, gains, node_states, receivers, down_sources.T, ws_high, ws_low, wo_high, wo_low],
         6 * 2 * rim * latent * hidden,
     )
     ring = ("patch", "lvl")
@@ -508,7 +504,7 @@
     (middle,) = call(
         functools.partial(down_middle_kernel, rim),
         [like((rows - 2 * rim, latent))],
-        [node_states, receivers, down_sources, senders, wo_high, wo_low, downward_gain[None]],
+        [node_states, receivers, down_sources.T, senders, wo_high, wo_low, gains],
         6 * (rows - 2 * rim) * latent * hidden,
     )
 
@@ -516,20 +512,20 @@
     bottom_packs = all_shares(bottom_near, bottom_far)
     ws_high, ws_low, wr_high, wr_low, wo_high, wo_low, bias = call(
         functools.partial(bottom_ready_kernel, len(bottom_packs)),
-        [*weights, *weights, *outputs, biases],
-        [*bottom_own, *bottom_packs],
+        [*weights, *weights, *outputs, bias_rows],
+        [bottom_sender, bottom_receiver, biases, bottom_output, *bottom_packs],
         latent * hidden,
     )
     senders_high, senders_low, receivers, inner = call(
         functools.partial(bottom_middle_kernel, rim),
         [like((rows, hidden), bf16), like((rows, hidden), bf16), like((rows, hidden)), like((rows - 2 * rim, latent))],
-        [head, middle, tail, bottom_links, ws_high, ws_low, wr_high, wr_low, wo_high, wo_low, bias, bottom_gain[None]],
+        [head, middle, tail, bottom_links.T, ws_high, ws_low, wr_high, wr_low, wo_high, wo_low, bias, gains],
         (12 * rows + 12 * rows) * latent * hidden,
     )
     (new_nodes,) = call(
         functools.partial(bottom_edge_kernel, rim),
         [like((rows, latent))],
-        [before, after, head, tail, inner, bottom_links, senders_high, senders_low, receivers, ws_high, ws_low, wo_high, wo_low, bottom_gain[None]],
+        [before, after, head, tail, inner, bottom_links.T, senders_high, senders_low, receivers, ws_high, ws_low, wo_high, wo_low, gains],
         24 * rim * latent * hidden,
     )
     return (new_nodes, new_coarse)

time: 108 us -> 68.8 us (0.64)
  Pallas kernels: 48.5 us -> 21.8 us
  local copies, waits for them, and re-layouts: 14.8 us -> 4.57 us
  waiting for transfers between devices: 27.7 us -> 23.6 us
  starting transfers between devices: 14.9 us -> 17.4 us
    pallas_call x12, Pallas kernels: 48.5 us -> 21.8 us  [call(): pl.pallas_call(kernel, out_shape=tuple(outs), in_specs=[away if i in far...]
    unnamed x82 -> x86, local copies, waits for them, and re-layouts: 14.8 us -> 4.57 us
    ppermute x19, waiting for transfers between devices: 27.7 us -> 23.6 us  [shifted(): lax.ppermute(values, axis, [(i, (i + step) % count) for i in range(count)])]
    ppermute x19, starting transfers between devices: 14.9 us -> 17.4 us  [shifted(): lax.ppermute(values, axis, [(i, (i + step) % count) for i in range(count)])]
  transfers between devices with their start and end apart: 19 -> 19, of which waited for: 8 -> 8; matrix products, arithmetic and copies ran while one was open for 2% -> 0% of each run, Pallas kernels for 18% -> 21%
where the time goes in v3:
time: 68.8 us; the launch traced here: 68.6 us
  waiting for transfers between devices  23.6 us (34%)
  Pallas kernels  21.8 us (32%)
  starting transfers between devices  17.4 us (25%)
  local copies, waits for them, and re-layouts  4.57 us (7%)
  between operations  1.15 us (2%)
    ppermute x19, waiting for transfers between devices, shifted(): lax.ppermute(values, axis, [(i, (i + step) % count) for i in range(count)])  23.6 us
    pallas_call x12, Pallas kernels, call(): pl.pallas_call(kernel, out_shape=tuple(outs), in_specs=[away if i in far...  21.8 us
    ppermute x19, starting transfers between devices, shifted(): lax.ppermute(values, axis, [(i, (i + step) % count) for i in range(count)])  17.4 us
    unnamed x86, local copies, waits for them, and re-layouts  4.57 us
  transfers between devices with their start and end apart: 19, of which 8 were waited for; matrix products, arithmetic and copies ran while one was open for 0% of the time, Pallas kernels for 21%

profile of v3, /device:TPU:0, one launch (start us, length us, event | category | flops | bytes accessed | tf_op | source)
XLA Modules:
  0.0 68.6 jit_solution(2157357719733069638)
XLA Ops:
  0.7 2.3 %shard_map.261 = (f32[392,256]{1,0:T(8,128)}, f32[392,256]{1,0:T(8,128)}) custom-call(f32[512,256]{1,0:T(8,128)} %ws.6, f32[512,256]{1,0:T(8,128)} %wr.6, f32[1,256]{1,0:T(1,128)} %bitcast.18, f32[256,512]{1,0:T(8,128)} %wo.6, f32[512,256]{1,0:T(8,128)} %ws.7, f32[512,256]{1,0:T(8,128)} %wr.7, f32[1,256]{1,0:T(1,128)} %bitcast.20, f32[256,512]{1,0:T(8,128)} %wo.7), custom_call_target="tpu_custom_call" | custom-call | flops 512 | bytes 3950592 | tf_op jit(solution)/shard_map/pallas_call | solution.py:308
  3.0 0.0 copy-start.32
  3.0 3.0 %collective-permute-start.8 = (f32[392,256]{1,0:T(8,128)}, f32[392,256]{1,0:T(8,128)S(1)}, u32[]{:S(2)}, u32[]{:S(2)}) collective-permute-start(f32[392,256]{1,0:T(8,128)} %get-tuple-element.59), channel_id=1, source_target_pairs={{0,2},{2,0},{1,3},{3,1},{4,6},{6,4},{5,7},{7,5},{8,10},{10,8},{9,1... | collective-permute-start | bytes 1204232 | tf_op jit(solution)/shard_map/ppermute | solution.py:325
  6.1 0.6 copy-done.40
  6.7 0.0 copy-start.38
  6.7 0.0 copy-start.39
  6.7 0.0 copy-start.41
  6.8 1.8 %shard_map.257.after.refs_0_ = f32[64,512]{1,0:T(8,128)S(1)} custom-call(f32[512,512]{1,0:T(8,128)S(1)} %copy-done, f32[64,512]{1,0:T(8,128)S(1)} %copy-done.13, s32[7,64]{1,0:T(8,128)S(1)} %bitcast.16, f32[512,256]{1,0:T(8,128)S(1)} %copy-done.10, f32[512,256]{1,0:T(8,128)S(1)} %copy-done.11, f32[1,256]{1,0:T(1,128)S(1)} %bitcast.26, f32[256,512]{1,0:T(8,128)S(1)} %copy-done.12), custom_call_target="tpu_custom_call" | custom-call | flops 637534208 | bytes 2886400 | tf_op jit(solution)/shard_map/pallas_call | solution.py:308
  8.6 0.1 collective-permute-start
  8.7 0.0 copy-start.36
  8.7 0.0 copy-start.34
  8.8 0.6 copy-done.37
  9.3 0.0 copy-done.36
  9.4 0.0 copy-done.34
  9.4 0.3 shard_map.258
  9.7 8.6 %collective-permute-done.refs_1_ = f32[64,512]{1,0:T(8,128)S(1)} collective-permute-done((f32[64,512]{1,0:T(8,128)S(1)}, f32[64,512]{1,0:T(8,128)S(1)}, u32[]{:S(2)}, u32[]{:S(2)}) %collective-permute-start) | collective-permute-done | bytes 131104 | tf_op jit(solution)/shard_map/ppermute | solution.py:325
  18.3 0.5 shard_map.259
  18.9 0.0 copy-start.18
  18.9 0.6 copy-done.18
  19.6 0.6 copy-done.20
  20.2 0.0 collective-permute-start.4
  20.2 1.3 %collective-permute-done.4.refs_4_ = f32[64,256]{1,0:T(8,128)S(1)} collective-permute-done((f32[64,256]{1,0:T(8,128)S(1)}, f32[64,256]{1,0:T(8,128)S(1)}, u32[]{:S(2)}, u32[]{:S(2)}) %collective-permute-start.4) | collective-permute-done | bytes 65568 | tf_op jit(solution)/shard_map/ppermute | solution.py:325
  21.4 0.6 copy-done.22
  22.1 1.7 %collective-permute-start.10 = (f32[392,256]{1,0:T(8,128)S(1)}, f32[392,256]{1,0:T(8,128)S(1)}, u32[]{:S(2)}, u32[]{:S(2)}) collective-permute-start(f32[392,256]{1,0:T(8,128)S(1)} %copy-done.42), channel_id=1, source_target_pairs={{0,2},{2,0},{1,3},{3,1},{4,6},{6,4},{5,7},{7,5},{8,10},{10,8},{9,1... | collective-permute-start | bytes 1204232 | tf_op jit(solution)/shard_map/ppermute | solution.py:325
  23.8 1.5 %collective-permute-start.9 = (f32[392,256]{1,0:T(8,128)S(1)}, f32[392,256]{1,0:T(8,128)}, u32[]{:S(2)}, u32[]{:S(2)}) collective-permute-start(f32[392,256]{1,0:T(8,128)S(1)} %collective-permute-done.8.refs_0_), channel_id=1, source_target_pairs={{0,16},{16,0},{1,17},{17,1},{2,18},{18,2},{3,19},{19,3},{4,20},{20... | collective-permute-start | bytes 1204232 | tf_op jit(solution)/shard_map/ppermute | solution.py:325
  25.3 3.6 %collective-permute-start.3 = (f32[64,256]{1,0:T(8,128)S(1)}, f32[64,256]{1,0:T(8,128)S(1)}, u32[]{:S(2)}, u32[]{:S(2)}) collective-permute-start(f32[64,256]{1,0:T(8,128)S(1)} %get-tuple-element.52.after.refs_0_), channel_id=1, source_target_pairs={{0,12},{4,0},{8,4},{12,8},{1,13},{5,1},{9,5},{13,9},{2,14},{6,2},{... | collective-permute-start | bytes 196616 | tf_op jit(solution)/shard_map/ppermute | solution.py:325
  28.9 0.0 collective-permute-start.2
  28.9 1.0 %collective-permute-start.1 = (f32[64,256]{1,0:T(8,128)S(1)}, f32[64,256]{1,0:T(8,128)S(1)}, u32[]{:S(2)}, u32[]{:S(2)}) collective-permute-start(f32[64,256]{1,0:T(8,128)S(1)} %get-tuple-element.52.after.refs_0_), channel_id=1, source_target_pairs={{0,4},{4,8},{8,12},{12,0},{1,5},{5,9},{9,13},{13,1},{2,6},{6,10},{... | collective-permute-start | bytes 196616 | tf_op jit(solution)/shard_map/ppermute | solution.py:325
  29.9 1.5 %collective-permute-done.3.refs_3_ = f32[64,256]{1,0:T(8,128)S(1)} collective-permute-done((f32[64,256]{1,0:T(8,128)S(1)}, f32[64,256]{1,0:T(8,128)S(1)}, u32[]{:S(2)}, u32[]{:S(2)}) %collective-permute-start.3) | collective-permute-done | bytes 65568 | tf_op jit(solution)/shard_map/ppermute | solution.py:325
  31.5 3.7 %collective-permute-done.2.refs_2_ = f32[64,256]{1,0:T(8,128)S(1)} collective-permute-done((f32[64,256]{1,0:T(8,128)S(1)}, f32[64,256]{1,0:T(8,128)S(1)}, u32[]{:S(2)}, u32[]{:S(2)}) %collective-permute-start.2) | collective-permute-done | bytes 65568 | tf_op jit(solution)/shard_map/ppermute | solution.py:325
  35.2 0.1 collective-permute-start.11
  35.3 0.5 copy-done.26
  35.8 0.0 collective-permute-start.12
  35.8 0.0 copy-done.28
  35.8 0.0 copy-start.29
  35.9 0.2 shard_map.260.refs_8_
  36.1 0.6 copy-done.29
  36.7 0.5 collective-permute-start.5
  37.2 0.1 collective-permute-start.6
  37.3 0.4 collective-permute-start.7
  37.8 0.0 collective-permute-done.11.refs_1_
  37.8 0.1 collective-permute-done.12.refs_3_
  37.9 2.9 %shard_map.262 = (f32[512,512]{1,0:T(8,128)S(1)}, bf16[2,512,256]{2,1,0:T(8,128)(2,1)S(1)}, bf16[2,512,256]{2,1,0:T(8,128)(2,1)S(1)}, bf16[512,512]{1,0:T(8,128)(2,1)S(1)}, bf16[512,512]{1,0:T(8,128)(2,1)S(1)}) custom-call(f32[512,512]{1,0:T(8,128)S(1)} %copy-done, f32[512,256]{1,0:T(8,128)S(1)} %copy-done.1, f32[512,256]{1,0:T(8,128)S(1)} %copy-done.2, ...), custom_call_target="tpu_custom_call" | custom-call | flops 805306368 | bytes 7375872 | tf_op jit(solution)/shard_map/pallas_call | solution.py:308
  40.8 0.0 collective-permute-done.7.refs_7_
  40.8 0.0 collective-permute-done.5.refs_5_
  40.9 0.0 copy-start.19
  40.9 0.8 %shard_map.263.refs_0_ = f32[64,512]{1,0:T(8,128)S(1)} custom-call(f32[64,256]{1,0:T(8,128)S(1)} %get-tuple-element.52.after.refs_0_, f32[64,256]{1,0:T(8,128)S(1)} %copy-done.29, f32[64,256]{1,0:T(8,128)S(1)} %copy-done.27, f32[64,256]{1,0:T(8,128)S(1)} %copy-done.25, f32[64,256]{1,0:T(8,128)S(1)} %copy-done.23, ...), custom_call_target="tpu_custom_call" | custom-call | flops 201326592 | bytes 2686976 | tf_op jit(solution)/shard_map/pallas_call | solution.py:308
  41.7 0.0 copy-start.30
  41.7 1.3 %collective-permute-start.16 = (f32[392,256]{1,0:T(8,128)S(1)}, f32[392,256]{1,0:T(8,128)S(1)}, u32[]{:S(2)}, u32[]{:S(2)}) collective-permute-start(f32[392,256]{1,0:T(8,128)S(1)} %collective-permute-done.10.refs_0_), channel_id=1, source_target_pairs={{0,16},{16,0},{1,17},{17,1},{2,18},{18,2},{3,19},{19,3},{4,20},{20... | collective-permute-start | bytes 1204232 | tf_op jit(solution)/shard_map/ppermute | solution.py:325
  43.0 0.5 collective-permute-start.13
  43.5 4.7 %collective-permute-done.13.refs_1_ = f32[64,512]{1,0:T(8,128)S(1)} collective-permute-done((f32[64,512]{1,0:T(8,128)S(1)}, f32[64,512]{1,0:T(8,128)S(1)}, u32[]{:S(2)}, u32[]{:S(2)}) %collective-permute-start.13) | collective-permute-done | bytes 131104 | tf_op jit(solution)/shard_map/ppermute | solution.py:325
  48.3 2.1 %shard_map.264 = (f32[64,512]{1,0:T(8,128)}, bf16[128,512]{1,0:T(8,128)(2,1)S(1)}, f32[128,512]{1,0:T(8,128)S(1)}, f32[128,512]{1,0:T(8,128)S(1)}) custom-call(f32[64,512]{1,0:T(8,128)S(1)} %shard_map.263.refs_0_, f32[64,512]{1,0:T(8,128)S(1)} %collective-permute-done.13.refs_1_, f32[64,512]{1,0:T(8,128)S(1)} %copy-done.19, ...), custom_call_target="tpu_custom_call" | custom-call | flops 402653184 | bytes 5388288 | tf_op jit(solution)/shard_map/pallas_call | solution.py:308
  50.4 2.7 %collective-permute-done.16.refs_2_ = f32[392,256]{1,0:T(8,128)S(1)} collective-permute-done((f32[392,256]{1,0:T(8,128)S(1)}, f32[392,256]{1,0:T(8,128)S(1)}, u32[]{:S(2)}, u32[]{:S(2)}) %collective-permute-start.16) | collective-permute-done | bytes 401440 | tf_op jit(solution)/shard_map/ppermute | solution.py:325
  53.1 0.5 collective-permute-start.18
  53.6 3.0 %collective-permute-start.15 = (f32[128,512]{1,0:T(8,128)S(1)}, f32[128,512]{1,0:T(8,128)S(1)}, u32[]{:S(2)}, u32[]{:S(2)}) collective-permute-start(f32[128,512]{1,0:T(8,128)S(1)} %get-tuple-element.72.head), channel_id=1, source_target_pairs={{0,13},{1,0},{4,1},{5,4},{8,5},{9,8},{12,9},{13,12},{2,15},{3,2},{... | collective-permute-start | bytes 786440 | tf_op jit(solution)/shard_map/ppermute | solution.py:325
  56.5 0.0 collective-permute-start.14
  56.6 1.4 %shard_map.265.middle = f32[256,512]{1,0:T(8,128)S(1)} custom-call(f32[512,512]{1,0:T(8,128)S(1)} %copy-done, f32[512,512]{1,0:T(8,128)S(1)} %get-tuple-element.65.refs_12_.refs_5_.receivers, s32[3,512]{1,0:T(4,128)S(1)} %bitcast.13, bf16[128,512]{1,0:T(8,128)(2,1)S(1)} %get-tuple-element.73.senders, bf16[512,512]{1,0:T(8,128)(2,1)S(1)} %get-tuple-element.69.refs_9_.wo_high, ...), custom_call_target="tpu_custom_call" | custom-call | flops 402653184 | bytes 3815424 | tf_op jit(solution)/shard_map/pallas_call | solution.py:308
  57.9 0.0 copy-start.31
  57.9 0.0 collective-permute-done.17.refs_1_
  58.0 0.5 shard_map.266
  58.5 0.2 copy-done.31
  58.6 4.6 %shard_map.267 = (bf16[512,512]{1,0:T(8,128)(2,1)S(1)}, bf16[512,512]{1,0:T(8,128)(2,1)S(1)}, f32[512,512]{1,0:T(8,128)S(1)}, f32[256,512]{1,0:T(8,128)S(1)}) custom-call(f32[128,512]{1,0:T(8,128)S(1)} %get-tuple-element.72.head, f32[256,512]{1,0:T(8,128)S(1)} %shard_map.265.middle, f32[128,512]{1,0:T(8,128)S(1)} %get-tuple-element.71.tail, ...), custom_call_target="tpu_custom_call" | custom-call | flops 3221225472 | bytes 6852608 | tf_op jit(solution)/shard_map/pallas_call | solution.py:308
  63.3 0.9 %collective-permute-done.14.before = f32[128,512]{1,0:T(8,128)S(1)} collective-permute-done((f32[128,512]{1,0:T(8,128)S(1)}, f32[128,512]{1,0:T(8,128)S(1)}, u32[]{:S(2)}, u32[]{:S(2)}) %collective-permute-start.14) | collective-permute-done | bytes 262176 | tf_op jit(solution)/shard_map/ppermute | solution.py:325
  64.2 4.4 %shard_map.268 = f32[512,512]{1,0:T(8,128)} custom-call(f32[128,512]{1,0:T(8,128)S(1)} %collective-permute-done.14.before, f32[128,512]{1,0:T(8,128)S(1)} %collective-permute-done.15.after, f32[128,512]{1,0:T(8,128)S(1)} %get-tuple-element.72.head, f32[128,512]{1,0:T(8,128)S(1)} %get-tuple-element.71.tail, f32[256,512]{1,0:T(8,128)S(1)} %get-tuple-element.85.inner, ...), custom_call_target="tpu_custom_call" | custom-call | flops 805306368 | bytes 6836224 | tf_op jit(solution)/shard_map/pallas_call | solution.py:308
  (73 shorter events, 0.2 us)
Async XLA Ops:
  0.6 5.4 %copy-start = (f32[512,512]{1,0:T(8,128)S(1)}, f32[512,512]{1,0:T(8,128)}, u32[]{:S(2)}) copy-start(f32[512,512]{1,0:T(8,128)} %nodes.5) | copy-start | bytes 3145732
  0.6 5.4 %copy-start.10 = (f32[512,256]{1,0:T(8,128)S(1)}, f32[512,256]{1,0:T(8,128)}, u32[]{:S(2)}) copy-start(f32[512,256]{1,0:T(8,128)} %ws.4) | copy-start | bytes 1572868
  0.7 5.4 %copy-start.11 = (f32[512,256]{1,0:T(8,128)S(1)}, f32[512,256]{1,0:T(8,128)}, u32[]{:S(2)}) copy-start(f32[512,256]{1,0:T(8,128)} %wr.4) | copy-start | bytes 1572868
  0.7 5.4 %copy-start.12 = (f32[256,512]{1,0:T(8,128)S(1)}, f32[256,512]{1,0:T(8,128)}, u32[]{:S(2)}) copy-start(f32[256,512]{1,0:T(8,128)} %wo.4) | copy-start | bytes 1572868
  0.7 5.4 %copy-start.13 = (f32[64,512]{1,0:T(8,128)S(1)}, f32[64,512]{1,0:T(8,128)}, u32[]{:S(2)}) copy-start(f32[64,512]{1,0:T(8,128)} %refs_2_.1) | copy-start | bytes 393220
  3.0 3.1 %copy-start.32 = (s32[64,7]{0,1:T(8,128)S(1)}, s32[64,7]{0,1:T(8,128)}, u32[]{:S(2)}) copy-start(s32[64,7]{0,1:T(8,128)} %param.28) | copy-start | bytes 5380
  3.0 19.0 %collective-permute-start.8 = (f32[392,256]{1,0:T(8,128)}, f32[392,256]{1,0:T(8,128)S(1)}, u32[]{:S(2)}, u32[]{:S(2)}) collective-permute-start(f32[392,256]{1,0:T(8,128)} %get-tuple-element.59), channel_id=1, source_target_pairs={{0,2},{2,0},{1,3},{3,1},{4,6},{6,4},{5,7},{7,5},{8,10},{10,8},{9,1... | collective-permute-start | bytes 1204232 | tf_op jit(solution)/shard_map/ppermute | solution.py:325
  6.0 0.7 copy-start.40
  6.7 2.0 %copy-start.7 = (f32[512,256]{1,0:T(8,128)S(1)}, f32[512,256]{1,0:T(8,128)}, u32[]{:S(2)}) copy-start(f32[512,256]{1,0:T(8,128)} %ws.5) | copy-start | bytes 1572868
  6.7 2.0 %copy-start.8 = (f32[512,256]{1,0:T(8,128)S(1)}, f32[512,256]{1,0:T(8,128)}, u32[]{:S(2)}) copy-start(f32[512,256]{1,0:T(8,128)} %wr.5) | copy-start | bytes 1572868
  6.7 2.0 %copy-start.9 = (f32[256,512]{1,0:T(8,128)S(1)}, f32[256,512]{1,0:T(8,128)}, u32[]{:S(2)}) copy-start(f32[256,512]{1,0:T(8,128)} %wo.5) | copy-start | bytes 1572868
  6.7 2.0 %copy-start.35 = (f32[256]{0:T(256)S(1)}, f32[256]{0:T(256)}, u32[]{:S(2)}) copy-start(f32[256]{0:T(256)} %param.49) | copy-start | bytes 3076
  6.7 2.0 %copy-start.38 = (f32[512]{0:T(512)S(1)}, f32[512]{0:T(512)}, u32[]{:S(2)}) copy-start(f32[512]{0:T(512)} %param.46) | copy-start | bytes 6148
  6.7 2.0 %copy-start.39 = (f32[512]{0:T(512)S(1)}, f32[512]{0:T(512)}, u32[]{:S(2)}) copy-start(f32[512]{0:T(512)} %param.51) | copy-start | bytes 6148
  6.7 2.0 %copy-start.41 = (f32[256]{0:T(256)S(1)}, f32[256]{0:T(256)}, u32[]{:S(2)}) copy-start(f32[256]{0:T(256)} %param.39) | copy-start | bytes 3076
  8.6 9.8 %collective-permute-start = (f32[64,512]{1,0:T(8,128)S(1)}, f32[64,512]{1,0:T(8,128)S(1)}, u32[]{:S(2)}, u32[]{:S(2)}) collective-permute-start(f32[64,512]{1,0:T(8,128)S(1)} %shard_map.257.after.refs_0_), channel_id=1, source_target_pairs={{0,2},{2,0},{1,3},{3,1},{4,6},{6,4},{5,7},{7,5},{8,10},{10,8},{9,1... | collective-permute-start | bytes 393224 | tf_op jit(solution)/shard_map/ppermute | solution.py:325
  8.7 0.7 copy-start.37
  8.7 0.7 %copy-start.36 = (f32[512]{0:T(512)S(1)}, f32[512]{0:T(512)}, u32[]{:S(2)}) copy-start(f32[512]{0:T(512)} %param.36) | copy-start | bytes 6148
  8.7 0.7 %copy-start.34 = (f32[256]{0:T(256)S(1)}, f32[256]{0:T(256)}, u32[]{:S(2)}) copy-start(f32[256]{0:T(256)} %param.44) | copy-start | bytes 3076
  9.4 12.7 %copy-start.42 = (f32[392,256]{1,0:T(8,128)S(1)}, f32[392,256]{1,0:T(8,128)}, u32[]{:S(2)}) copy-start(f32[392,256]{1,0:T(8,128)} %get-tuple-element.62) | copy-start | bytes 1204228
  9.4 26.5 %copy-start.33 = (s32[64,6]{0,1:T(8,128)S(1)}, s32[64,6]{0,1:T(8,128)}, u32[]{:S(2)}) copy-start(s32[64,6]{0,1:T(8,128)} %param.31) | copy-start | bytes 4612
  9.7 9.2 %copy-start.14 = (bf16[256,512]{1,0:T(8,128)(2,1)}, bf16[256,512]{1,0:T(8,128)(2,1)S(1)}, u32[]{:S(2)}) copy-start(bf16[256,512]{1,0:T(8,128)(2,1)S(1)} %get-tuple-element.57.refs_10_) | copy-start | bytes 786436
  9.7 9.2 %copy-start.16 = (bf16[256,512]{1,0:T(8,128)(2,1)}, bf16[256,512]{1,0:T(8,128)(2,1)S(1)}, u32[]{:S(2)}) copy-start(bf16[256,512]{1,0:T(8,128)(2,1)S(1)} %get-tuple-element.58.refs_11_) | copy-start | bytes 786436
  18.3 19.6 %copy-start.1 = (f32[512,256]{1,0:T(8,128)S(1)}, f32[512,256]{1,0:T(8,128)}, u32[]{:S(2)}) copy-start(f32[512,256]{1,0:T(8,128)} %ws.6) | copy-start | bytes 1572868
  18.3 19.6 %copy-start.2 = (f32[512,256]{1,0:T(8,128)S(1)}, f32[512,256]{1,0:T(8,128)}, u32[]{:S(2)}) copy-start(f32[512,256]{1,0:T(8,128)} %wr.6) | copy-start | bytes 1572868
  18.3 19.6 %copy-start.3 = (f32[256,512]{1,0:T(8,128)S(1)}, f32[256,512]{1,0:T(8,128)}, u32[]{:S(2)}) copy-start(f32[256,512]{1,0:T(8,128)} %wo.6) | copy-start | bytes 1572868
  18.9 0.7 copy-start.18
  19.6 0.6 copy-start.20
  20.2 1.3 %collective-permute-start.4 = (f32[64,256]{1,0:T(8,128)S(1)}, f32[64,256]{1,0:T(8,128)S(1)}, u32[]{:S(2)}, u32[]{:S(2)}) collective-permute-start(f32[64,256]{1,0:T(8,128)S(1)} %get-tuple-element.52.after.refs_0_), channel_id=1, source_target_pairs={{0,1},{1,0},{2,3},{3,2},{4,5},{5,4},{6,7},{7,6},{8,9},{9,8},{10,11... | collective-permute-start | bytes 196616 | tf_op jit(solution)/shard_map/ppermute | solution.py:325
  21.4 0.6 copy-start.22
  22.1 13.1 %collective-permute-start.10 = (f32[392,256]{1,0:T(8,128)S(1)}, f32[392,256]{1,0:T(8,128)S(1)}, u32[]{:S(2)}, u32[]{:S(2)}) collective-permute-start(f32[392,256]{1,0:T(8,128)S(1)} %copy-done.42), channel_id=1, source_target_pairs={{0,2},{2,0},{1,3},{3,1},{4,6},{6,4},{5,7},{7,5},{8,10},{10,8},{9,1... | collective-permute-start | bytes 1204232 | tf_op jit(solution)/shard_map/ppermute | solution.py:325
  23.8 11.4 %collective-permute-start.9 = (f32[392,256]{1,0:T(8,128)S(1)}, f32[392,256]{1,0:T(8,128)}, u32[]{:S(2)}, u32[]{:S(2)}) collective-permute-start(f32[392,256]{1,0:T(8,128)S(1)} %collective-permute-done.8.refs_0_), channel_id=1, source_target_pairs={{0,16},{16,0},{1,17},{17,1},{2,18},{18,2},{3,19},{19,3},{4,20},{20... | collective-permute-start | bytes 1204232 | tf_op jit(solution)/shard_map/ppermute | solution.py:325
  25.3 6.1 %collective-permute-start.3 = (f32[64,256]{1,0:T(8,128)S(1)}, f32[64,256]{1,0:T(8,128)S(1)}, u32[]{:S(2)}, u32[]{:S(2)}) collective-permute-start(f32[64,256]{1,0:T(8,128)S(1)} %get-tuple-element.52.after.refs_0_), channel_id=1, source_target_pairs={{0,12},{4,0},{8,4},{12,8},{1,13},{5,1},{9,5},{13,9},{2,14},{6,2},{... | collective-permute-start | bytes 196616 | tf_op jit(solution)/shard_map/ppermute | solution.py:325
  28.9 6.2 %collective-permute-start.2 = (f32[64,256]{1,0:T(8,128)S(1)}, f32[64,256]{1,0:T(8,128)S(1)}, u32[]{:S(2)}, u32[]{:S(2)}) collective-permute-start(f32[64,256]{1,0:T(8,128)S(1)} %get-tuple-element.52.after.refs_0_), channel_id=1, source_target_pairs={{0,8},{4,12},{8,0},{12,4},{1,9},{5,13},{9,1},{13,5},{2,10},{6,14},... | collective-permute-start | bytes 196616 | tf_op jit(solution)/shard_map/ppermute | solution.py:325
  28.9 6.2 %collective-permute-start.1 = (f32[64,256]{1,0:T(8,128)S(1)}, f32[64,256]{1,0:T(8,128)S(1)}, u32[]{:S(2)}, u32[]{:S(2)}) collective-permute-start(f32[64,256]{1,0:T(8,128)S(1)} %get-tuple-element.52.after.refs_0_), channel_id=1, source_target_pairs={{0,4},{4,8},{8,12},{12,0},{1,5},{5,9},{9,13},{13,1},{2,6},{6,10},{... | collective-permute-start | bytes 196616 | tf_op jit(solution)/shard_map/ppermute | solution.py:325
  31.5 3.7 %copy-start.24 = (f32[64,256]{1,0:T(8,128)}, f32[64,256]{1,0:T(8,128)S(1)}, u32[]{:S(2)}) copy-start(f32[64,256]{1,0:T(8,128)S(1)} %collective-permute-done.3.refs_3_) | copy-start | bytes 196612
  35.2 0.6 copy-start.26
  35.2 0.6 copy-start.28
  35.2 2.6 %collective-permute-start.11 = (f32[392,256]{1,0:T(8,128)S(1)}, f32[392,256]{1,0:T(8,128)}, u32[]{:S(2)}, u32[]{:S(2)}) collective-permute-start(f32[392,256]{1,0:T(8,128)S(1)} %collective-permute-done.8.refs_0_), channel_id=1, source_target_pairs={{0,1},{1,0},{2,3},{3,2},{4,5},{5,4},{6,7},{7,6},{8,9},{9,8},{10,11... | collective-permute-start | bytes 1204232 | tf_op jit(solution)/shard_map/ppermute | solution.py:325
  35.8 2.1 %collective-permute-start.12 = (f32[392,256]{1,0:T(8,128)}, f32[392,256]{1,0:T(8,128)}, u32[]{:S(2)}, u32[]{:S(2)}) collective-permute-start(f32[392,256]{1,0:T(8,128)} %collective-permute-done.9.refs_2_), channel_id=1, source_target_pairs={{0,1},{1,0},{2,3},{3,2},{4,5},{5,4},{6,7},{7,6},{8,9},{9,8},{10,11... | collective-permute-start | bytes 1204232 | tf_op jit(solution)/shard_map/ppermute | solution.py:325
  35.8 0.8 %copy-start.29 = (f32[64,256]{1,0:T(8,128)S(1)}, f32[64,256]{1,0:T(8,128)}, u32[]{:S(2)}) copy-start(f32[64,256]{1,0:T(8,128)} %copy-done.28) | copy-start | bytes 196612
  35.9 1.4 %copy-start.27 = (f32[64,256]{1,0:T(8,128)S(1)}, f32[64,256]{1,0:T(8,128)}, u32[]{:S(2)}) copy-start(f32[64,256]{1,0:T(8,128)} %copy-done.26) | copy-start | bytes 196612
  35.9 1.5 %copy-start.25 = (f32[64,256]{1,0:T(8,128)S(1)}, f32[64,256]{1,0:T(8,128)}, u32[]{:S(2)}) copy-start(f32[64,256]{1,0:T(8,128)} %copy-done.24) | copy-start | bytes 196612
  36.7 4.2 %copy-start.15 = (bf16[256,512]{1,0:T(8,128)(2,1)S(1)}, bf16[256,512]{1,0:T(8,128)(2,1)}, u32[]{:S(2)}) copy-start(bf16[256,512]{1,0:T(8,128)(2,1)} %copy-done.14) | copy-start | bytes 786436
  36.7 4.2 %copy-start.17 = (bf16[256,512]{1,0:T(8,128)(2,1)S(1)}, bf16[256,512]{1,0:T(8,128)(2,1)}, u32[]{:S(2)}) copy-start(bf16[256,512]{1,0:T(8,128)(2,1)} %copy-done.16) | copy-start | bytes 786436
  36.7 4.2 %copy-start.21 = (f32[64,256]{1,0:T(8,128)S(1)}, f32[64,256]{1,0:T(8,128)}, u32[]{:S(2)}) copy-start(f32[64,256]{1,0:T(8,128)} %copy-done.20) | copy-start | bytes 196612
  36.7 4.2 %copy-start.23 = (f32[64,256]{1,0:T(8,128)S(1)}, f32[64,256]{1,0:T(8,128)}, u32[]{:S(2)}) copy-start(f32[64,256]{1,0:T(8,128)} %copy-done.22) | copy-start | bytes 196612
  36.7 4.1 %collective-permute-start.5 = (f32[64,256]{1,0:T(8,128)S(1)}, f32[64,256]{1,0:T(8,128)S(1)}, u32[]{:S(2)}, u32[]{:S(2)}) collective-permute-start(f32[64,256]{1,0:T(8,128)S(1)} %copy-done.29), channel_id=1, source_target_pairs={{0,1},{1,0},{2,3},{3,2},{4,5},{5,4},{6,7},{7,6},{8,9},{9,8},{10,11... | collective-permute-start | bytes 196616 | tf_op jit(solution)/shard_map/ppermute | solution.py:325
  37.2 3.6 %collective-permute-start.6 = (f32[64,256]{1,0:T(8,128)S(1)}, f32[64,256]{1,0:T(8,128)S(1)}, u32[]{:S(2)}, u32[]{:S(2)}) collective-permute-start(f32[64,256]{1,0:T(8,128)S(1)} %copy-done.27), channel_id=1, source_target_pairs={{0,1},{1,0},{2,3},{3,2},{4,5},{5,4},{6,7},{7,6},{8,9},{9,8},{10,11... | collective-permute-start | bytes 196616 | tf_op jit(solution)/shard_map/ppermute | solution.py:325
  37.3 3.5 %collective-permute-start.7 = (f32[64,256]{1,0:T(8,128)S(1)}, f32[64,256]{1,0:T(8,128)S(1)}, u32[]{:S(2)}, u32[]{:S(2)}) collective-permute-start(f32[64,256]{1,0:T(8,128)S(1)} %copy-done.25), channel_id=1, source_target_pairs={{0,1},{1,0},{2,3},{3,2},{4,5},{5,4},{6,7},{7,6},{8,9},{9,8},{10,11... | collective-permute-start | bytes 196616 | tf_op jit(solution)/shard_map/ppermute | solution.py:325
  40.9 7.4 %copy-start.19 = (f32[64,512]{1,0:T(8,128)S(1)}, f32[64,512]{1,0:T(8,128)}, u32[]{:S(2)}) copy-start(f32[64,512]{1,0:T(8,128)} %copy-done.18) | copy-start | bytes 393220
  41.7 6.6 %copy-start.30 = (s32[512,3]{0,1:T(4,128)S(1)}, s32[512,3]{0,1:T(4,128)}, u32[]{:S(2)}) copy-start(s32[512,3]{0,1:T(4,128)} %param.29) | copy-start | bytes 18436
  41.7 11.4 %collective-permute-start.16 = (f32[392,256]{1,0:T(8,128)S(1)}, f32[392,256]{1,0:T(8,128)S(1)}, u32[]{:S(2)}, u32[]{:S(2)}) collective-permute-start(f32[392,256]{1,0:T(8,128)S(1)} %collective-permute-done.10.refs_0_), channel_id=1, source_target_pairs={{0,16},{16,0},{1,17},{17,1},{2,18},{18,2},{3,19},{19,3},{4,20},{20... | collective-permute-start | bytes 1204232 | tf_op jit(solution)/shard_map/ppermute | solution.py:325
  43.0 5.3 %collective-permute-start.13 = (f32[64,512]{1,0:T(8,128)S(1)}, f32[64,512]{1,0:T(8,128)S(1)}, u32[]{:S(2)}, u32[]{:S(2)}) collective-permute-start(f32[64,512]{1,0:T(8,128)S(1)} %shard_map.263.refs_0_), channel_id=1, source_target_pairs={{0,2},{2,0},{1,3},{3,1},{4,6},{6,4},{5,7},{7,5},{8,10},{10,8},{9,1... | collective-permute-start | bytes 393224 | tf_op jit(solution)/shard_map/ppermute | solution.py:325
  53.1 4.9 %collective-permute-start.17 = (f32[392,256]{1,0:T(8,128)S(1)}, f32[392,256]{1,0:T(8,128)S(1)}, u32[]{:S(2)}, u32[]{:S(2)}) collective-permute-start(f32[392,256]{1,0:T(8,128)S(1)} %collective-permute-done.10.refs_0_), channel_id=1, source_target_pairs={{0,1},{1,0},{2,3},{3,2},{4,5},{5,4},{6,7},{7,6},{8,9},{9,8},{10,11... | collective-permute-start | bytes 1204232 | tf_op jit(solution)/shard_map/ppermute | solution.py:325
  53.1 4.9 %collective-permute-start.18 = (f32[392,256]{1,0:T(8,128)S(1)}, f32[392,256]{1,0:T(8,128)S(1)}, u32[]{:S(2)}, u32[]{:S(2)}) collective-permute-start(f32[392,256]{1,0:T(8,128)S(1)} %collective-permute-done.16.refs_2_), channel_id=1, source_target_pairs={{0,1},{1,0},{2,3},{3,2},{4,5},{5,4},{6,7},{7,6},{8,9},{9,8},{10,11... | collective-permute-start | bytes 1204232 | tf_op jit(solution)/shard_map/ppermute | solution.py:325
  53.6 10.6 %collective-permute-start.15 = (f32[128,512]{1,0:T(8,128)S(1)}, f32[128,512]{1,0:T(8,128)S(1)}, u32[]{:S(2)}, u32[]{:S(2)}) collective-permute-start(f32[128,512]{1,0:T(8,128)S(1)} %get-tuple-element.72.head), channel_id=1, source_target_pairs={{0,13},{1,0},{4,1},{5,4},{8,5},{9,8},{12,9},{13,12},{2,15},{3,2},{... | collective-permute-start | bytes 786440 | tf_op jit(solution)/shard_map/ppermute | solution.py:325
  56.5 7.6 %collective-permute-start.14 = (f32[128,512]{1,0:T(8,128)S(1)}, f32[128,512]{1,0:T(8,128)S(1)}, u32[]{:S(2)}, u32[]{:S(2)}) collective-permute-start(f32[128,512]{1,0:T(8,128)S(1)} %get-tuple-element.71.tail), channel_id=1, source_target_pairs={{0,1},{1,4},{4,5},{5,8},{8,9},{9,12},{12,13},{13,0},{2,3},{3,6},{6... | collective-permute-start | bytes 786440 | tf_op jit(solution)/shard_map/ppermute | solution.py:325
  56.6 1.4 %copy-start.4 = (f32[512,256]{1,0:T(8,128)S(1)}, f32[512,256]{1,0:T(8,128)}, u32[]{:S(2)}) copy-start(f32[512,256]{1,0:T(8,128)} %ws.7) | copy-start | bytes 1572868
  56.6 1.4 %copy-start.5 = (f32[512,256]{1,0:T(8,128)S(1)}, f32[512,256]{1,0:T(8,128)}, u32[]{:S(2)}) copy-start(f32[512,256]{1,0:T(8,128)} %wr.7) | copy-start | bytes 1572868
  56.6 1.4 %copy-start.6 = (f32[256,512]{1,0:T(8,128)S(1)}, f32[256,512]{1,0:T(8,128)}, u32[]{:S(2)}) copy-start(f32[256,512]{1,0:T(8,128)} %wo.7) | copy-start | bytes 1572868
  57.9 0.7 %copy-start.31 = (s32[512,6]{0,1:T(8,128)S(1)}, s32[512,6]{0,1:T(8,128)}, u32[]{:S(2)}) copy-start(s32[512,6]{0,1:T(8,128)} %param.30) | copy-start | bytes 36868

commit v4 on v3

--- a/solution.py
+++ b/solution.py
@@ -91,9 +91,11 @@
     part[...] = dot3(hidden, *split(wo[...]))
 
 
-def coarse_ready_kernel(after, ws, wr, wo, *refs):
+def coarse_ready_kernel(parts, after, ws, wr, wo, *refs):
     del after
-    params, (ws_high, ws_low, wr_high, wr_low, wo_high, wo_low, gains, biases) = refs[:7], refs[7:]
+    params, own, refs = refs[:7], refs[7:11], refs[11:]
+    ws_high, ws_low, wr_high, wr_low, wo_high, wo_low, gains, biases, pack, sems = refs
+    moves = started(share_copies(own, pack, parts), sems)
     for i in range(4):
         gains[i : i + 1] = params[i][...]
     for i in range(3):
@@ -101,30 +103,37 @@
     ws_high[...], ws_low[...] = split(ws[...])
     wr_high[...], wr_low[...] = split(wr[...])
     wo_high[...], wo_low[...] = split(wo[...])
-
-
-def share_copies(ws, wr, bias, wo, pack):
-    parts, lvls = lax.axis_size("parts"), lax.axis_size("lvl")
-    mine = lax.axis_index("parts") * lvls + lax.axis_index("lvl")
-    depth, width = ws.shape
-    share, thin = depth // (parts * lvls), width // (parts * lvls)
-    rows = pl.ds(pl.multiple_of(mine * share, share), share)
-    strip = pl.ds(pl.multiple_of(mine * thin, thin), thin)
-    columns = range(wo.shape[1] // width)
-    return [
-        (ws.at[rows], pack.at[pl.ds(0, share)]),
-        (wr.at[rows], pack.at[pl.ds(share, share)]),
-        *(
-            (wo.at[strip, pl.ds(j * width, width)], pack.at[pl.ds(2 * share + j * thin, thin)])
-            for j in columns
-        ),
-        (bias, pack.at[pl.ds(2 * share + len(columns) * thin, 1)]),
-    ]
-
-
-def share_kernel(*refs):
-    own, (down_pack, bottom_pack, sems) = refs[:8], refs[8:]
-    for move in started(share_copies(*own[:4], down_pack) + share_copies(*own[4:], bottom_pack), sems):
+    for move in moves:
+        move.wait()
+
+
+def shares(parts):
+    lvls = lax.axis_size("lvl")
+    mine = lax.axis_index("lvl")
+    if parts > 1:
+        mine = lax.axis_index("parts") * lvls + mine
+    return mine, parts * lvls
+
+
+def share_copies(sources, pack, parts):
+    mine, count = shares(parts)
+    width = pack.shape[1]
+    copies, at = [], 0
+    for source in sources:
+        rows = source.shape[0] // count
+        if source.shape[0] == 1:
+            copies.append((source, pack.at[pl.ds(at, 1)]))
+            at += 8
+            continue
+        strip = pl.ds(pl.multiple_of(mine * rows, rows), rows)
+        for j in range(source.shape[1] // width):
+            copies.append((source.at[strip, pl.ds(j * width, width)], pack.at[pl.ds(at, rows)]))
+            at += rows
+    return copies
+
+
+def share_kernel(parts, *refs):
+    for move in started(share_copies(refs[:-2], refs[-2], parts), refs[-1]):
         move.wait()
 
 
@@ -154,53 +163,86 @@
     part[...] = dot3(hidden, wo_high[...], wo_low[...])
 
 
-def collect(own, packs, outs):
-    ws, wr, bias, wo = own
-    ws_high, ws_low, wr_high, wr_low, wo_high, wo_low, bias_all = outs
-    subs, parts, lvls = lax.axis_size("sub"), lax.axis_size("parts"), lax.axis_size("lvl")
+def shared_among(packs):
+    return max(1, len(packs) // max(1, lax.axis_size("sub") - 1))
+
+
+def fetched_shares(packs):
+    subs, lvls = lax.axis_size("sub"), lax.axis_size("lvl")
+    parts = len(packs) // max(1, (subs - 1) * lvls)
     sub, part, lvl = lax.axis_index("sub"), lax.axis_index("parts"), lax.axis_index("lvl")
-    depth, width = ws.shape
-    ws_high[sub], ws_low[sub] = split(ws[...])
-    wr_high[sub], wr_low[sub] = split(wr[...])
-    rows = pl.ds(pl.multiple_of(sub * width, width), width)
-    wo_high[rows, :], wo_low[rows, :] = split(wo[...])
-    bias_all[sub] = jnp.broadcast_to(bias, (8, width))
-    share, thin = depth // (parts * lvls), width // (parts * lvls)
-    columns = wo.shape[1] // width
     place = iter(packs)
     for s in range(1, subs):
-        block = lax.rem(sub + subs - s, subs)
         for p in range(parts):
             for t in range(lvls):
-                pack = next(place)
                 mine = lax.rem(part + parts - p, parts) * lvls + lax.rem(lvl + lvls - t, lvls)
-                rows = pl.ds(pl.multiple_of(mine * share, share), share)
-                ws_high[block, rows, :], ws_low[block, rows, :] = split(pack[0:share, :])
-                wr_high[block, rows, :], wr_low[block, rows, :] = split(pack[share : 2 * share, :])
-                rows = pl.ds(pl.multiple_of(block * width + mine * thin, thin), thin)
-                for j in range(columns):
-                    high, low = split(pack[2 * share + j * thin : 2 * share + (j + 1) * thin, :])
-                    wo_high[rows, j * width : (j + 1) * width] = high
-                    wo_low[rows, j * width : (j + 1) * width] = low
-                if p == 0 and t == 0:
-                    last = 2 * share + columns * thin
-                    bias_all[block] = jnp.broadcast_to(pack[last : last + 1, :], (8, width))
-
-
-def down_ready_kernel(count, nodes, ws, wr, biases, wo, *refs):
-    packs = refs[:count]
-    receivers, ws_high, ws_low, wo_high, wo_low, wr_high, wr_low, bias_all = refs[count:]
-    collect(
-        (ws, wr, biases[1:2], wo), packs, (ws_high, ws_low, wr_high, wr_low, wo_high, wo_low, bias_all)
-    )
+                yield next(place), lax.rem(sub + subs - s, subs), mine, p == 0 and t == 0
+
+
+def collect_in(own, packs, at, high, low):
+    sub = lax.axis_index("sub")
+    count = shared_among(packs)
+    high[sub], low[sub] = split(own[...])
+    share = own.shape[0] // count
+    for pack, block, mine, _ in fetched_shares(packs):
+        rows = pl.ds(pl.multiple_of(mine * share, share), share)
+        high[block, rows, :], low[block, rows, :] = split(pack[at : at + share, :])
+
+
+def collect_out(own, packs, at, high, low):
+    sub = lax.axis_index("sub")
+    count = shared_among(packs)
+    width, latent = own.shape
+    rows = pl.ds(pl.multiple_of(sub * width, width), width)
+    high[rows, :], low[rows, :] = split(own[...])
+    thin = width // count
+    for pack, block, mine, _ in fetched_shares(packs):
+        rows = pl.ds(pl.multiple_of(block * width + mine * thin, thin), thin)
+        for j in range(latent // width):
+            first, second = split(pack[at + j * thin : at + (j + 1) * thin, :])
+            high[rows, j * width : (j + 1) * width] = first
+            low[rows, j * width : (j + 1) * width] = second
+
+
+def collect_bias(own, packs, at, out):
+    out[lax.axis_index("sub")] = jnp.broadcast_to(own, (8, own.shape[1]))
+    for pack, block, _, whole_row in fetched_shares(packs):
+        if whole_row:
+            out[block] = jnp.broadcast_to(pack[at : at + 1, :], (8, own.shape[1]))
+
+
+def down_weights_kernel(count, after, nodes, ws, wr, biases, wo, *refs):
+    del after
+    packs, refs = refs[:count], refs[count:]
+    receivers, ws_high, ws_low, wo_high, wo_low, wr_high, wr_low, bias_all = refs
     width = ws.shape[1]
-    for g in range(ws_high.shape[0]):
+    share = ws.shape[0] // shared_among(packs)
+    collect_in(ws, packs, 0, ws_high, ws_low)
+    collect_in(wr, packs, share, wr_high, wr_low)
+    collect_out(wo, packs, 2 * share, wo_high, wo_low)
+    collect_bias(biases[1:2], packs, 3 * share, bias_all)
+    for g in range(wr_high.shape[0]):
         product = dot3(nodes[...], wr_high[g], wr_low[g])
         receivers[:, g * width : (g + 1) * width] = 0.5 * (product + bias_all[g][0:1])
 
 
-def bottom_ready_kernel(count, ws, wr, biases, wo, *refs):
-    collect((ws, wr, biases[2:3], wo), refs[:count], refs[count:])
+def bottom_weights_kernel(count, ws, wr, biases, wo, *refs):
+    packs, (ws_high, ws_low, wr_high, wr_low, wo_high, wo_low, bias_all) = refs[:count], refs[count:]
+    share = ws.shape[0] // shared_among(packs)
+    collect_in(ws, packs, 0, ws_high, ws_low)
+    collect_in(wr, packs, share, wr_high, wr_low)
+    collect_out(wo, packs, 2 * share, wo_high, wo_low)
+    collect_bias(biases[2:3], packs, 3 * share, bias_all)
+
+
+def bottom_picks_kernel(rim, after, links, picks):
+    del after
+    wanted = upright(links[...])
+    size = rim * wanted.shape[1]
+    names = lax.broadcasted_iota(jnp.int32, (rim, 3 * rim), 1)
+    for i in range(wanted.shape[0] // rim):
+        strip = wanted[i * rim : (i + 1) * rim]
+        picks[i * size : (i + 1) * size, :] = one_hot(strip, names + i * rim)
 
 
 def down_rows(nodes, receivers, sources, senders, wo_high, wo_low, gain):
@@ -240,19 +282,16 @@
     )
 
 
-def bottom_rows(nodes, receivers, links, start, sender_high, sender_low, wo_high, wo_low, gain):
-    rows, reach = nodes.shape[0], sender_high.shape[0]
-    names = start + lax.broadcasted_iota(jnp.int32, (rows, reach), 1)
-    picks = one_hot(links, names)
+def bottom_rows(nodes, receivers, picks, sender_high, sender_low, wo_high, wo_low, gain):
     half = wo_high.shape[0] // 2
     hidden = []
     for place in (slice(0, half), slice(half, 2 * half)):
         picked = dot(picks, sender_high[:, place]) + dot(picks, sender_low[:, place])
-        hidden.append(silu_sum(picked, receivers[:, place], links.shape[1]))
+        hidden.append(silu_sum(picked, receivers[:, place], picks.shape[0] // nodes.shape[0]))
     return nodes + gain * normed(dot3(jnp.concatenate(hidden, axis=1), wo_high, wo_low))
 
 
-def bottom_middle_kernel(rim, head, middle, tail, links, ws_high, ws_low, wr_high, wr_low, wo_high, wo_low, bias, gains, senders_high, senders_low, receivers, out):
+def bottom_middle_kernel(rim, head, middle, tail, picks, ws_high, ws_low, wr_high, wr_low, wo_high, wo_low, bias, gains, senders_high, senders_low, receivers, out):
     nodes = jnp.concatenate([head[...], middle[...], tail[...]], axis=0)
     nodes_high, nodes_low = split(nodes)
     width = ws_high.shape[2]
@@ -263,19 +302,19 @@
         product = dot(nodes_high, wr_high[g]) + (dot(nodes_high, wr_low[g]) + dot(nodes_low, wr_high[g]))
         receivers[:, columns] = 0.5 * (product + bias[g][0:1])
     total = nodes.shape[0]
-    wanted = upright(links[...])
+    size = picks.shape[0] * rim // total
     for first in range(rim, total - rim, rim):
         place = slice(first, first + rim)
         reach = slice(first - rim, first + 2 * rim)
         out[first - rim : first, :] = bottom_rows(
-            middle[first - rim : first], receivers[place], wanted[place], first,
+            middle[first - rim : first], receivers[place], picks[first // rim * size : (first // rim + 1) * size],
             senders_high[reach], senders_low[reach], wo_high[...], wo_low[...], gains[3:4],
         )
 
 
-def bottom_edge_kernel(rim, before, after, head, tail, inner, links, senders_high, senders_low, receivers, ws_high, ws_low, wo_high, wo_low, gains, out):
-    total = links.shape[1]
-    wanted = upright(links[...])
+def bottom_edge_kernel(rim, before, after, head, tail, inner, picks, senders_high, senders_low, receivers, ws_high, ws_low, wo_high, wo_low, gains, out):
+    total = out.shape[0]
+    size = picks.shape[0] * rim // total
     out[rim : total - rim, :] = inner[...]
     outer = split(jnp.concatenate([before[...], after[...]], axis=0))
     projected = jnp.concatenate(
@@ -294,7 +333,7 @@
         high = jnp.concatenate(order(outer_high[strip], senders_high[reach]), axis=0)
         low = jnp.concatenate(order(outer_low[strip], senders_low[reach]), axis=0)
         out[place, :] = bottom_rows(
-            nodes[...], receivers[place], wanted[place], 0 if side == 0 else total - rim,
+            nodes[...], receivers[place], picks[place.start // rim * size : (place.start // rim + 1) * size],
             high, low, wo_high[...], wo_low[...], gains[3:4],
         )
 
@@ -331,14 +370,15 @@
     return [lax.psum(part, "sub")]
 
 
-def coarse_pieces(senders):
+def coarse_pieces(senders, others):
     patches, lvls = lax.axis_size("patch"), lax.axis_size("lvl")
     if patches > most_direct:
-        return [lax.all_gather(senders, ("patch", "lvl"), axis=0, tiled=True)]
+        return [lax.all_gather(senders, ("patch", "lvl"), axis=0, tiled=True)], others
     near = [[senders] + [shifted(senders, "lvl", t) for t in range(1, lvls)]]
-    pieces = lax.optimization_barrier([shifted(senders, "patch", s) for s in range(1, patches)])
+    pieces = [shifted(senders, "patch", s) for s in range(1, patches)]
+    pieces, others = lax.optimization_barrier((pieces, others))
     near += [[piece] + [shifted(piece, "lvl", t) for t in range(1, lvls)] for piece in pieces]
-    return [row[t] for t in range(lvls) for row in near]
+    return [row[t] for t in range(lvls) for row in near], others
 
 
 def coarse_names(rows):
@@ -417,19 +457,19 @@
     outputs = [like((hidden, latent), bf16)] * 2
     bias_rows = like((subs, 8, width))
 
-    shares = lax.axis_size("parts") * lax.axis_size("lvl")
     columns = latent // width
-    pack = like((2 * latent // shares + (width // shares) * columns + 8, width))
-    down_own = (downward_sender, downward_receiver, downward_bias[None], downward_output)
-    bottom_own = (bottom_sender, bottom_receiver, bottom_bias[None], bottom_output)
-
-    down_pack, bottom_pack = call(
-        share_kernel,
-        [pack, pack],
-        [*down_own, *bottom_own],
+    ensemble, lvls = lax.axis_size("parts"), lax.axis_size("lvl")
+    share = latent // (ensemble * lvls)
+    row = 8
+    pack = like((3 * share + row, width))
+    copying = [pltpu.SemaphoreType.DMA((3 + columns,))]
+    (down_pack,) = call(
+        functools.partial(share_kernel, ensemble),
+        [pack],
+        [downward_sender, downward_receiver, downward_output, downward_bias[None]],
         latent,
-        [pltpu.SemaphoreType.DMA((2 * (3 + columns),))],
-        far=range(8),
+        copying,
+        far=range(4),
         limit=large_limit,
     )
     down_near = over_sub(down_pack)
@@ -441,24 +481,29 @@
         limit=wide_limit,
     )
     parts = sub_parts(part)
-    ws_high, ws_low, wr_high, wr_low, wo_high, wo_low, gains, biases = call(
-        coarse_ready_kernel,
-        [like((latent, width), bf16)] * 4 + [like((width, latent), bf16)] * 2 + [like((4, latent)), like((3, width))],
+    ws_high, ws_low, wr_high, wr_low, wo_high, wo_low, gains, biases, bottom_pack = call(
+        functools.partial(coarse_ready_kernel, ensemble),
+        [like((latent, width), bf16)] * 4
+        + [like((width, latent), bf16)] * 2
+        + [like((4, latent)), like((3, width)), pack],
         [
             part, coarse_sender, coarse_receiver, coarse_output,
             upward_gain[None], coarse_gain[None], downward_gain[None], bottom_gain[None],
             coarse_bias[None], downward_bias[None], bottom_bias[None],
+            bottom_sender, bottom_receiver, bottom_output, bottom_bias[None],
         ],
         latent * hidden,
-        far=(0,),
-    )
+        copying,
+        far=(0, 11, 12, 13, 14),
+    )
+    bottom_near = over_sub(held(bottom_pack, parts[-1]))
+    down_far = over_parts(down_near)
     coarse_up, senders, receivers = call(
         functools.partial(coarse_project_kernel, len(parts)),
         [like((blocks, latent)), like((blocks, width)), like((blocks, width))],
         [*parts, coarse_states, gains, biases, ws_high, ws_low, wr_high, wr_low],
         12 * blocks * latent * width,
     )
-    pieces = coarse_pieces(senders)
     names = coarse_names(blocks)
     (picks,) = call(
         picks_kernel,
@@ -467,32 +512,35 @@
         coarse_links.size * names.size,
         far=(0,),
     )
-    down_near, bottom_pack = held((down_near, bottom_pack), pieces[len(pieces) // 2])
-    down_far = over_parts(down_near)
-    bottom_near = over_sub(bottom_pack)
-    down_near, down_far, bottom_near = held(
-        (down_near, down_far, bottom_near), pieces[min(1, len(pieces) - 1)]
+    (bottom_picks,) = call(
+        functools.partial(bottom_picks_kernel, rim),
+        [like((bottom_links.size, 3 * rim), bf16)],
+        [senders, bottom_links.T],
+        bottom_links.size * 3 * rim,
+        far=(0,),
+    )
+    pieces, (picks, bottom_picks, down_near, down_far, bottom_near) = coarse_pieces(
+        senders, (picks, bottom_picks, down_near, down_far, bottom_near)
     )
     down_packs = all_shares(down_near, down_far)
-    down_receivers, ws_high, ws_low, down_high, down_low = call(
-        functools.partial(down_ready_kernel, len(down_packs)),
-        [like((rows, hidden)), *weights, *outputs],
-        [node_states, downward_sender, downward_receiver, biases, downward_output, *down_packs],
-        6 * rows * latent * hidden,
-        [pltpu.VMEM((subs, latent, width), bf16)] * 2 + [pltpu.VMEM((subs, 8, width), f32)],
-    )
+    bottom_far = over_parts(bottom_near)
     (part,) = call(
         functools.partial(coarse_kernel, len(pieces)),
         [like((blocks, latent))],
-        [*pieces, picks, receivers, wo_high, wo_low, down_receivers],
+        [*pieces, picks, receivers, wo_high, wo_low, *down_packs],
         4 * coarse_links.size * names.size * width,
-        far=(len(pieces) + 4,),
+        far=range(len(pieces) + 4, len(pieces) + 4 + len(down_packs)),
     )
     parts = sub_parts(part)
-    receivers, wo_high, wo_low = down_receivers, down_high, down_low
-
-    bottom_near = held(bottom_near, part)
-    bottom_far = over_parts(bottom_near)
+    receivers, ws_high, ws_low, wo_high, wo_low = call(
+        functools.partial(down_weights_kernel, len(down_packs)),
+        [like((rows, hidden)), *weights, *outputs],
+        [part, node_states, downward_sender, downward_receiver, biases, downward_output, *down_packs],
+        6 * rows * latent * hidden,
+        [pltpu.VMEM((subs, latent, width), bf16)] * 2 + [pltpu.VMEM((subs, 8, width), f32)],
+        far=(0,),
+    )
+    parts, bottom_far = lax.optimization_barrier((parts, bottom_far))
     new_coarse, senders, head, tail = call(
         functools.partial(down_edge_kernel, len(parts), rim),
         [like((blocks, latent)), like((2 * blocks, hidden), bf16), like((rim, latent)), like((rim, latent))],
@@ -511,7 +559,7 @@
     bottom_near, bottom_far = held((bottom_near, bottom_far), head)
     bottom_packs = all_shares(bottom_near, bottom_far)
     ws_high, ws_low, wr_high, wr_low, wo_high, wo_low, bias = call(
-        functools.partial(bottom_ready_kernel, len(bottom_packs)),
+        functools.partial(bottom_weights_kernel, len(bottom_packs)),
         [*weights, *weights, *outputs, bias_rows],
         [bottom_sender, bottom_receiver, biases, bottom_output, *bottom_packs],
         latent * hidden,
@@ -519,13 +567,13 @@
     senders_high, senders_low, receivers, inner = call(
         functools.partial(bottom_middle_kernel, rim),
         [like((rows, hidden), bf16), like((rows, hidden), bf16), like((rows, hidden)), like((rows - 2 * rim, latent))],
-        [head, middle, tail, bottom_links.T, ws_high, ws_low, wr_high, wr_low, wo_high, wo_low, bias, gains],
+        [head, middle, tail, bottom_picks, ws_high, ws_low, wr_high, wr_low, wo_high, wo_low, bias, gains],
         (12 * rows + 12 * rows) * latent * hidden,
     )
     (new_nodes,) = call(
         functools.partial(bottom_edge_kernel, rim),
         [like((rows, latent))],
-        [before, after, head, tail, inner, bottom_links.T, senders_high, senders_low, receivers, ws_high, ws_low, wo_high, wo_low, gains],
+        [before, after, head, tail, inner, bottom_picks, senders_high, senders_low, receivers, ws_high, ws_low, wo_high, wo_low, gains],
         24 * rim * latent * hidden,
     )
     return (new_nodes, new_coarse)

time: 68.8 us -> 70.4 us (1.023)
  local copies, waits for them, and re-layouts: 4.57 us -> 19.9 us
  waiting for transfers between devices: 23.6 us -> 10.7 us
  starting transfers between devices: 17.4 us -> 15.4 us
  Pallas kernels: 21.8 us -> 22.7 us
    unnamed x86 -> x94, local copies, waits for them, and re-layouts: 4.57 us -> 19.9 us
    ppermute x19, waiting for transfers between devices: 23.6 us -> 10.7 us  [shifted(): lax.ppermute(values, axis, [(i, (i + step) % count) for i in range(count)])]
    ppermute x19, starting transfers between devices: 17.4 us -> 15.4 us  [shifted(): lax.ppermute(values, axis, [(i, (i + step) % count) for i in range(count)])]
    pallas_call x12 -> x13, Pallas kernels: 21.8 us -> 22.7 us  [call(): pl.pallas_call(kernel, out_shape=tuple(outs), in_specs=[away if i in far...]
  transfers between devices with their start and end apart: 19 -> 19, of which waited for: 8 -> 7; matrix products, arithmetic and copies ran while one was open for 0% -> 0% of each run, Pallas kernels for 21% -> 21%
where the time goes in v4:
time: 70.4 us; the launch traced here: 69.8 us
  Pallas kernels  22.7 us (32%)
  local copies, waits for them, and re-layouts  19.9 us (28%)
  starting transfers between devices  15.4 us (22%)
  waiting for transfers between devices  10.7 us (15%)
  between operations  1.01 us (1%)
    pallas_call x13, Pallas kernels, call(): pl.pallas_call(kernel, out_shape=tuple(outs), in_specs=[away if i in far...  22.7 us
    unnamed x94, local copies, waits for them, and re-layouts  19.9 us
    ppermute x19, starting transfers between devices, shifted(): lax.ppermute(values, axis, [(i, (i + step) % count) for i in range(count)])  15.4 us
    ppermute x19, waiting for transfers between devices, shifted(): lax.ppermute(values, axis, [(i, (i + step) % count) for i in range(count)])  10.7 us
  transfers between devices with their start and end apart: 19, of which 7 were waited for; matrix products, arithmetic and copies ran while one was open for 0% of the time, Pallas kernels for 21%

profile of v4, /device:TPU:0, one launch (start us, length us, event | category | flops | bytes accessed | tf_op | source)
XLA Modules:
  0.0 69.8 jit_solution(14486000603438298242)
XLA Ops:
  0.7 2.0 %shard_map.262 = f32[392,256]{1,0:T(8,128)} custom-call(f32[512,256]{1,0:T(8,128)} %ws.6, f32[512,256]{1,0:T(8,128)} %wr.6, f32[256,512]{1,0:T(8,128)} %wo.6, f32[1,256]{1,0:T(1,128)} %bitcast.15), custom_call_target="tpu_custom_call" | custom-call | flops 512 | bytes 1975296 | tf_op jit(solution)/shard_map/pallas_call | solution.py:347
  2.7 0.0 copy-start.8
  2.7 3.0 %collective-permute-start.4 = (f32[392,256]{1,0:T(8,128)}, f32[392,256]{1,0:T(8,128)S(1)}, u32[]{:S(2)}, u32[]{:S(2)}) collective-permute-start(f32[392,256]{1,0:T(8,128)} %shard_map.262), channel_id=1, source_target_pairs={{0,2},{2,0},{1,3},{3,1},{4,6},{6,4},{5,7},{7,5},{8,10},{10,8},{9,1... | collective-permute-start | bytes 1204232 | tf_op jit(solution)/shard_map/ppermute | solution.py:364
  5.7 1.0 %copy-done.10 = f32[512,256]{1,0:T(8,128)S(1)} copy-done((f32[512,256]{1,0:T(8,128)S(1)}, f32[512,256]{1,0:T(8,128)}, u32[]{:S(2)}) %copy-start.10) | copy-done | bytes 524312
  6.7 1.0 %copy-done.11 = f32[512,256]{1,0:T(8,128)S(1)} copy-done((f32[512,256]{1,0:T(8,128)S(1)}, f32[512,256]{1,0:T(8,128)}, u32[]{:S(2)}) %copy-start.11) | copy-done | bytes 524312
  7.8 1.0 %copy-done.12 = f32[256,512]{1,0:T(8,128)S(1)} copy-done((f32[256,512]{1,0:T(8,128)S(1)}, f32[256,512]{1,0:T(8,128)}, u32[]{:S(2)}) %copy-start.12) | copy-done | bytes 524312
  8.8 0.9 %copy-done.13 = f32[64,512]{1,0:T(8,128)S(1)} copy-done((f32[64,512]{1,0:T(8,128)S(1)}, f32[64,512]{1,0:T(8,128)}, u32[]{:S(2)}) %copy-start.13) | copy-done | bytes 131096
  9.7 0.7 copy-done.39
  10.4 0.7 copy-done.46
  11.1 0.0 copy-start.44
  11.1 0.0 copy-start.45
  11.1 1.8 %shard_map.257.after.refs_0_ = f32[64,512]{1,0:T(8,128)S(1)} custom-call(f32[512,512]{1,0:T(8,128)S(1)} %copy-done, f32[64,512]{1,0:T(8,128)S(1)} %copy-done.13, s32[7,64]{1,0:T(8,128)S(1)} %bitcast.19, f32[512,256]{1,0:T(8,128)S(1)} %copy-done.10, f32[512,256]{1,0:T(8,128)S(1)} %copy-done.11, f32[1,256]{1,0:T(1,128)S(1)} %bitcast.26, f32[256,512]{1,0:T(8,128)S(1)} %copy-done.12), custom_call_target="tpu_custom_call" | custom-call | flops 637534208 | bytes 2886400 | tf_op jit(solution)/shard_map/pallas_call | solution.py:347
  13.0 0.2 collective-permute-start
  13.2 1.5 %shard_map.258 = (bf16[512,256]{1,0:T(8,128)(2,1)S(1)}, bf16[512,256]{1,0:T(8,128)(2,1)S(1)}, bf16[512,256]{1,0:T(8,128)(2,1)S(1)}, bf16[512,256]{1,0:T(8,128)(2...) custom-call(f32[64,512]{1,0:T(8,128)S(1)} %shard_map.257.after.refs_, ...), custom_call_target="tpu_custom_call" | custom-call | flops 262144 | bytes 5274624 | tf_op jit(solution)/shard_map/pallas_call | solution.py:347
  14.7 0.7 %copy-done.15 = bf16[256,512]{1,0:T(8,128)(2,1)} copy-done((bf16[256,512]{1,0:T(8,128)(2,1)}, bf16[256,512]{1,0:T(8,128)(2,1)S(1)}, u32[]{:S(2)}) %copy-start.15) | copy-done | bytes 262168
  15.4 0.7 copy-done.17
  16.1 0.7 copy-done.19
  16.8 0.7 %copy-done.21 = bf16[512,256]{1,0:T(8,128)(2,1)} copy-done((bf16[512,256]{1,0:T(8,128)(2,1)}, bf16[512,256]{1,0:T(8,128)(2,1)S(1)}, u32[]{:S(2)}) %copy-start.21) | copy-done | bytes 262168
  17.5 0.7 %copy-done.23 = bf16[512,256]{1,0:T(8,128)(2,1)} copy-done((bf16[512,256]{1,0:T(8,128)(2,1)}, bf16[512,256]{1,0:T(8,128)(2,1)S(1)}, u32[]{:S(2)}) %copy-start.23) | copy-done | bytes 262168
  18.2 0.7 %copy-done.25 = bf16[512,256]{1,0:T(8,128)(2,1)} copy-done((bf16[512,256]{1,0:T(8,128)(2,1)}, bf16[512,256]{1,0:T(8,128)(2,1)S(1)}, u32[]{:S(2)}) %copy-start.25) | copy-done | bytes 262168
  18.9 0.6 copy-done.29
  19.5 0.6 copy-done.32
  20.1 0.7 copy-done.27
  20.8 1.9 %collective-permute-start.6 = (f32[392,256]{1,0:T(8,128)}, f32[392,256]{1,0:T(8,128)}, u32[]{:S(2)}, u32[]{:S(2)}) collective-permute-start(f32[392,256]{1,0:T(8,128)} %get-tuple-element.56), channel_id=1, source_target_pairs={{0,2},{2,0},{1,3},{3,1},{4,6},{6,4},{5,7},{7,5},{8,10},{10,8},{9,1... | collective-permute-start | bytes 1204232 | tf_op jit(solution)/shard_map/ppermute | solution.py:364
  22.7 1.5 %collective-permute-start.5 = (f32[392,256]{1,0:T(8,128)S(1)}, f32[392,256]{1,0:T(8,128)S(1)}, u32[]{:S(2)}, u32[]{:S(2)}) collective-permute-start(f32[392,256]{1,0:T(8,128)S(1)} %collective-permute-done.4.refs_12_.refs_0_), channel_id=1, source_target_pairs={{0,16},{16,0},{1,17},{17,1},{2,18},{18,2},{3,19},{19,3},{4,20},{20... | collective-permute-start | bytes 1204232 | tf_op jit(solution)/shard_map/ppermute | solution.py:364
  24.2 0.9 %copy-done.14 = f32[64,512]{1,0:T(8,128)S(1)} copy-done((f32[64,512]{1,0:T(8,128)S(1)}, f32[64,512]{1,0:T(8,128)}, u32[]{:S(2)}) %copy-start.14) | copy-done | bytes 131096
  25.1 0.9 %copy-done.20 = bf16[512,256]{1,0:T(8,128)(2,1)S(1)} copy-done((bf16[512,256]{1,0:T(8,128)(2,1)S(1)}, bf16[512,256]{1,0:T(8,128)(2,1)}, u32[]{:S(2)}) %copy-start.20) | copy-done | bytes 262168
  26.1 0.9 %copy-done.22 = bf16[512,256]{1,0:T(8,128)(2,1)S(1)} copy-done((bf16[512,256]{1,0:T(8,128)(2,1)S(1)}, bf16[512,256]{1,0:T(8,128)(2,1)}, u32[]{:S(2)}) %copy-start.22) | copy-done | bytes 262168
  27.0 0.9 %copy-done.24 = bf16[512,256]{1,0:T(8,128)(2,1)S(1)} copy-done((bf16[512,256]{1,0:T(8,128)(2,1)S(1)}, bf16[512,256]{1,0:T(8,128)(2,1)}, u32[]{:S(2)}) %copy-start.24) | copy-done | bytes 262168
  28.0 0.9 %copy-done.26 = bf16[512,256]{1,0:T(8,128)(2,1)S(1)} copy-done((bf16[512,256]{1,0:T(8,128)(2,1)S(1)}, bf16[512,256]{1,0:T(8,128)(2,1)}, u32[]{:S(2)}) %copy-start.26) | copy-done | bytes 262168
  28.9 0.9 %copy-done.28 = f32[64,512]{1,0:T(8,128)S(1)} copy-done((f32[64,512]{1,0:T(8,128)S(1)}, f32[64,512]{1,0:T(8,128)}, u32[]{:S(2)}) %copy-start.28) | copy-done | bytes 131096
  29.9 0.7 copy-done.30
  30.6 0.7 copy-done.33
  31.2 0.5 shard_map.259
  31.8 3.7 %collective-permute-start.3 = (f32[64,256]{1,0:T(8,128)S(1)}, f32[64,256]{1,0:T(8,128)S(1)}, u32[]{:S(2)}, u32[]{:S(2)}) collective-permute-start(f32[64,256]{1,0:T(8,128)S(1)} %get-tuple-element.54.after.refs_0_), channel_id=1, source_target_pairs={{0,12},{4,0},{8,4},{12,8},{1,13},{5,1},{9,5},{13,9},{2,14},{6,2},{... | collective-permute-start | bytes 196616 | tf_op jit(solution)/shard_map/ppermute | solution.py:364
  35.4 1.0 %collective-permute-start.1 = (f32[64,256]{1,0:T(8,128)S(1)}, f32[64,256]{1,0:T(8,128)S(1)}, u32[]{:S(2)}, u32[]{:S(2)}) collective-permute-start(f32[64,256]{1,0:T(8,128)S(1)} %get-tuple-element.54.after.refs_0_), channel_id=1, source_target_pairs={{0,4},{4,8},{8,12},{12,0},{1,5},{5,9},{9,13},{13,1},{2,6},{6,10},{... | collective-permute-start | bytes 196616 | tf_op jit(solution)/shard_map/ppermute | solution.py:364
  36.5 0.0 copy-start.40
  36.5 0.7 copy-done.40
  37.2 0.2 shard_map.260.refs_8_
  37.4 0.7 %copy-done.36 = s32[512,6]{0,1:T(8,128)S(1)} copy-done((s32[512,6]{0,1:T(8,128)S(1)}, s32[512,6]{0,1:T(8,128)}, u32[]{:S(2)}) %copy-start.36) | copy-done | bytes 12312
  38.1 0.7 shard_map.261.picks
  38.8 1.8 %collective-permute-done.2.refs_2_ = f32[64,256]{1,0:T(8,128)S(1)} collective-permute-done((f32[64,256]{1,0:T(8,128)S(1)}, f32[64,256]{1,0:T(8,128)S(1)}, u32[]{:S(2)}, u32[]{:S(2)}) %collective-permute-start.2) | collective-permute-done | bytes 65568 | tf_op jit(solution)/shard_map/ppermute | solution.py:364
  40.6 0.9 %collective-permute-done.1.refs_1_ = f32[64,256]{1,0:T(8,128)S(1)} collective-permute-done((f32[64,256]{1,0:T(8,128)S(1)}, f32[64,256]{1,0:T(8,128)S(1)}, u32[]{:S(2)}, u32[]{:S(2)}) %collective-permute-start.1) | collective-permute-done | bytes 65568 | tf_op jit(solution)/shard_map/ppermute | solution.py:364
  41.5 0.5 collective-permute-start.12
  42.0 0.5 collective-permute-start.14
  42.5 0.5 collective-permute-start.8
  43.0 0.9 %collective-permute-done.7.refs_4_ = f32[64,256]{1,0:T(8,128)S(1)} collective-permute-done((f32[64,256]{1,0:T(8,128)S(1)}, f32[64,256]{1,0:T(8,128)S(1)}, u32[]{:S(2)}, u32[]{:S(2)}) %collective-permute-start.7) | collective-permute-done | bytes 65568 | tf_op jit(solution)/shard_map/ppermute | solution.py:364
  43.9 0.1 collective-permute-start.9
  44.1 0.4 collective-permute-start.10
  44.4 0.7 %collective-permute-done.9.refs_6_ = f32[64,256]{1,0:T(8,128)S(1)} collective-permute-done((f32[64,256]{1,0:T(8,128)S(1)}, f32[64,256]{1,0:T(8,128)S(1)}, u32[]{:S(2)}, u32[]{:S(2)}) %collective-permute-start.9) | collective-permute-done | bytes 65568 | tf_op jit(solution)/shard_map/ppermute | solution.py:364
  45.2 0.2 collective-permute-done.10.refs_7_
  45.4 0.8 %shard_map.263.after.refs_0_ = f32[64,512]{1,0:T(8,128)S(1)} custom-call(f32[64,256]{1,0:T(8,128)S(1)} %get-tuple-element.54.after.refs_0_, f32[64,256]{1,0:T(8,128)S(1)} %collective-permute-done.1.refs_1_, f32[64,256]{1,0:T(8,128)S(1)} %collective-permute-done.2.refs_2_, f32[64,256]{1,0:T(8,128)S(1)} %collective-permute-done.3.refs_3_, ...), custom_call_target="tpu_custom_call" | custom-call | flops 201326592 | bytes 3244032 | tf_op jit(solution)/shard_map/pallas_call | solution.py:347
  46.2 0.0 copy-start.35
  46.2 0.6 collective-permute-start.13
  46.8 1.6 %shard_map.264 = (f32[512,512]{1,0:T(8,128)S(1)}, bf16[2,512,256]{2,1,0:T(8,128)(2,1)S(1)}, bf16[2,512,256]{2,1,0:T(8,128)(2,1)S(1)}, bf16[512,512]{1,0:T(8,128)(2,1)S(1)}, bf16[512,512]{1,0:T(8,128)(2,1)S(1)}) custom-call(f32[64,512]{1,0:T(8,128)S(1)} %shard_map.263.after.refs_0_, f32[512,512]{1,0:T(8,128)S(1)} %copy-done, f32[512,256]{1,0:T(8,128)S(1)} %copy-done.1, ...), custom_call_target="tpu_custom_call" | custom-call | flops 805306368 | bytes 7506944 | tf_op jit(solution)/shard_map/pallas_call | solution.py:347
  48.4 5.1 %collective-permute-done.14.refs_2_ = f32[392,256]{1,0:T(8,128)S(1)} collective-permute-done((f32[392,256]{1,0:T(8,128)}, f32[392,256]{1,0:T(8,128)S(1)}, u32[]{:S(2)}, u32[]{:S(2)}) %collective-permute-start.14) | collective-permute-done | bytes 401440 | tf_op jit(solution)/shard_map/ppermute | solution.py:364
  53.5 2.1 %shard_map.265 = (f32[64,512]{1,0:T(8,128)}, bf16[128,512]{1,0:T(8,128)(2,1)S(1)}, f32[128,512]{1,0:T(8,128)S(1)}, f32[128,512]{1,0:T(8,128)S(1)}) custom-call(f32[64,512]{1,0:T(8,128)S(1)} %shard_map.263.after.refs_0_, f32[64,512]{1,0:T(8,128)S(1)} %collective-permute-done.13.refs_1_, f32[64,512]{1,0:T(8,128)S(1)} %get-tuple-element.69.refs_2_, ...), custom_call_target="tpu_custom_call" | custom-call | flops 402653184 | bytes 5388288 | tf_op jit(solution)/shard_map/pallas_call | solution.py:347
  55.6 0.5 collective-permute-start.18
  56.1 1.0 %collective-permute-start.16 = (f32[128,512]{1,0:T(8,128)S(1)}, f32[128,512]{1,0:T(8,128)S(1)}, u32[]{:S(2)}, u32[]{:S(2)}) collective-permute-start(f32[128,512]{1,0:T(8,128)S(1)} %get-tuple-element.76.head), channel_id=1, source_target_pairs={{0,13},{1,0},{4,1},{5,4},{8,5},{9,8},{12,9},{13,12},{2,15},{3,2},{... | collective-permute-start | bytes 786440 | tf_op jit(solution)/shard_map/ppermute | solution.py:364
  57.1 1.3 %shard_map.266.middle = f32[256,512]{1,0:T(8,128)S(1)} custom-call(f32[512,512]{1,0:T(8,128)S(1)} %copy-done, f32[512,512]{1,0:T(8,128)S(1)} %get-tuple-element.70.refs_5_.receivers, s32[3,512]{1,0:T(4,128)S(1)} %bitcast.13, bf16[128,512]{1,0:T(8,128)(2,1)S(1)} %get-tuple-element.77.senders, bf16[512,512]{1,0:T(8,128)(2,1)S(1)} %get-tuple-element.73.refs_9_.wo_high, ...), custom_call_target="tpu_custom_call" | custom-call | flops 402653184 | bytes 3815424 | tf_op jit(solution)/shard_map/pallas_call | solution.py:347
  58.5 1.5 %shard_map.267 = (bf16[2,512,256]{2,1,0:T(8,128)(2,1)S(1)}, bf16[2,512,256]{2,1,0:T(8,128)(2,1)S(1)}, bf16[2,512,256]{2,1,0:T(8,128)(2,1)S(1)}, bf16[2,512,256]{...) custom-call(f32[512,256]{1,0:T(8,128)S(1)} %copy-done.4, ...), custom_call_target="tpu_custom_call" | custom-call | flops 262144 | bytes 6343680 | tf_op jit(solution)/shard_map/pallas_call | solution.py:347
  60.0 4.4 %shard_map.268 = (bf16[512,512]{1,0:T(8,128)(2,1)S(1)}, bf16[512,512]{1,0:T(8,128)(2,1)S(1)}, f32[512,512]{1,0:T(8,128)S(1)}, f32[256,512]{1,0:T(8,128)S(1)}) custom-call(f32[128,512]{1,0:T(8,128)S(1)} %get-tuple-element.76.head, f32[256,512]{1,0:T(8,128)S(1)} %shard_map.266.middle, f32[128,512]{1,0:T(8,128)S(1)} %get-tuple-element.75.tail, ...), custom_call_target="tpu_custom_call" | custom-call | flops 3221225472 | bytes 9199616 | tf_op jit(solution)/shard_map/pallas_call | solution.py:347
  64.4 1.1 %collective-permute-done.15.before = f32[128,512]{1,0:T(8,128)S(1)} collective-permute-done((f32[128,512]{1,0:T(8,128)S(1)}, f32[128,512]{1,0:T(8,128)S(1)}, u32[]{:S(2)}, u32[]{:S(2)}) %collective-permute-start.15) | collective-permute-done | bytes 262176 | tf_op jit(solution)/shard_map/ppermute | solution.py:364
  65.5 4.3 %shard_map.269 = f32[512,512]{1,0:T(8,128)} custom-call(f32[128,512]{1,0:T(8,128)S(1)} %collective-permute-done.15.before, f32[128,512]{1,0:T(8,128)S(1)} %collective-permute-done.16.after, f32[128,512]{1,0:T(8,128)S(1)} %get-tuple-element.76.head, f32[128,512]{1,0:T(8,128)S(1)} %get-tuple-element.75.tail, f32[256,512]{1,0:T(8,128)S(1)} %get-tuple-element.89.inner, ...), custom_call_target="tpu_custom_call" | custom-call | flops 805306368 | bytes 9183232 | tf_op jit(solution)/shard_map/pallas_call | solution.py:347
  (82 shorter events, 0.2 us)
Async XLA Ops:
  0.6 5.1 %copy-start = (f32[512,512]{1,0:T(8,128)S(1)}, f32[512,512]{1,0:T(8,128)}, u32[]{:S(2)}) copy-start(f32[512,512]{1,0:T(8,128)} %nodes.5) | copy-start | bytes 3145732
  0.6 12.5 %copy-start.4 = (f32[512,256]{1,0:T(8,128)S(1)}, f32[512,256]{1,0:T(8,128)}, u32[]{:S(2)}) copy-start(f32[512,256]{1,0:T(8,128)} %ws.7) | copy-start | bytes 1572868
  0.7 12.5 %copy-start.5 = (f32[512,256]{1,0:T(8,128)S(1)}, f32[512,256]{1,0:T(8,128)}, u32[]{:S(2)}) copy-start(f32[512,256]{1,0:T(8,128)} %wr.7) | copy-start | bytes 1572868
  0.7 12.5 %copy-start.6 = (f32[256,512]{1,0:T(8,128)S(1)}, f32[256,512]{1,0:T(8,128)}, u32[]{:S(2)}) copy-start(f32[256,512]{1,0:T(8,128)} %wo.7) | copy-start | bytes 1572868
  0.7 12.5 %copy-start.7 = (f32[512,256]{1,0:T(8,128)S(1)}, f32[512,256]{1,0:T(8,128)}, u32[]{:S(2)}) copy-start(f32[512,256]{1,0:T(8,128)} %ws.5) | copy-start | bytes 1572868
  2.7 10.5 %copy-start.8 = (f32[512,256]{1,0:T(8,128)S(1)}, f32[512,256]{1,0:T(8,128)}, u32[]{:S(2)}) copy-start(f32[512,256]{1,0:T(8,128)} %wr.5) | copy-start | bytes 1572868
  2.7 10.5 %copy-start.9 = (f32[256,512]{1,0:T(8,128)S(1)}, f32[256,512]{1,0:T(8,128)}, u32[]{:S(2)}) copy-start(f32[256,512]{1,0:T(8,128)} %wo.5) | copy-start | bytes 1572868
  2.7 20.0 %collective-permute-start.4 = (f32[392,256]{1,0:T(8,128)}, f32[392,256]{1,0:T(8,128)S(1)}, u32[]{:S(2)}, u32[]{:S(2)}) collective-permute-start(f32[392,256]{1,0:T(8,128)} %shard_map.262), channel_id=1, source_target_pairs={{0,2},{2,0},{1,3},{3,1},{4,6},{6,4},{5,7},{7,5},{8,10},{10,8},{9,1... | collective-permute-start | bytes 1204232 | tf_op jit(solution)/shard_map/ppermute | solution.py:364
  5.7 1.0 %copy-start.10 = (f32[512,256]{1,0:T(8,128)S(1)}, f32[512,256]{1,0:T(8,128)}, u32[]{:S(2)}) copy-start(f32[512,256]{1,0:T(8,128)} %ws.4) | copy-start | bytes 1572868
  6.7 1.0 %copy-start.11 = (f32[512,256]{1,0:T(8,128)S(1)}, f32[512,256]{1,0:T(8,128)}, u32[]{:S(2)}) copy-start(f32[512,256]{1,0:T(8,128)} %wr.4) | copy-start | bytes 1572868
  7.8 1.0 %copy-start.12 = (f32[256,512]{1,0:T(8,128)S(1)}, f32[256,512]{1,0:T(8,128)}, u32[]{:S(2)}) copy-start(f32[256,512]{1,0:T(8,128)} %wo.4) | copy-start | bytes 1572868
  8.8 0.9 %copy-start.13 = (f32[64,512]{1,0:T(8,128)S(1)}, f32[64,512]{1,0:T(8,128)}, u32[]{:S(2)}) copy-start(f32[64,512]{1,0:T(8,128)} %refs_2_.2) | copy-start | bytes 393220
  9.7 0.7 copy-start.39
  10.4 0.7 copy-start.46
  11.1 2.1 %copy-start.37 = (f32[256]{0:T(256)S(1)}, f32[256]{0:T(256)}, u32[]{:S(2)}) copy-start(f32[256]{0:T(256)} %param.44) | copy-start | bytes 3076
  11.1 2.1 %copy-start.38 = (f32[256]{0:T(256)S(1)}, f32[256]{0:T(256)}, u32[]{:S(2)}) copy-start(f32[256]{0:T(256)} %param.49) | copy-start | bytes 3076
  11.1 2.1 %copy-start.41 = (f32[512]{0:T(512)S(1)}, f32[512]{0:T(512)}, u32[]{:S(2)}) copy-start(f32[512]{0:T(512)} %param.36) | copy-start | bytes 6148
  11.1 2.1 %copy-start.42 = (f32[512]{0:T(512)S(1)}, f32[512]{0:T(512)}, u32[]{:S(2)}) copy-start(f32[512]{0:T(512)} %param.41) | copy-start | bytes 6148
  11.1 2.1 %copy-start.43 = (f32[512]{0:T(512)S(1)}, f32[512]{0:T(512)}, u32[]{:S(2)}) copy-start(f32[512]{0:T(512)} %param.46) | copy-start | bytes 6148
  11.1 2.1 %copy-start.44 = (f32[512]{0:T(512)S(1)}, f32[512]{0:T(512)}, u32[]{:S(2)}) copy-start(f32[512]{0:T(512)} %param.51) | copy-start | bytes 6148
  11.1 2.1 %copy-start.45 = (f32[256]{0:T(256)S(1)}, f32[256]{0:T(256)}, u32[]{:S(2)}) copy-start(f32[256]{0:T(256)} %param.39) | copy-start | bytes 3076
  13.0 7.2 %collective-permute-start = (f32[64,512]{1,0:T(8,128)S(1)}, f32[64,512]{1,0:T(8,128)S(1)}, u32[]{:S(2)}, u32[]{:S(2)}) collective-permute-start(f32[64,512]{1,0:T(8,128)S(1)} %shard_map.257.after.refs_0_), channel_id=1, source_target_pairs={{0,2},{2,0},{1,3},{3,1},{4,6},{6,4},{5,7},{7,5},{8,10},{10,8},{9,1... | collective-permute-start | bytes 393224 | tf_op jit(solution)/shard_map/ppermute | solution.py:364
  14.7 0.7 %copy-start.15 = (bf16[256,512]{1,0:T(8,128)(2,1)}, bf16[256,512]{1,0:T(8,128)(2,1)S(1)}, u32[]{:S(2)}) copy-start(bf16[256,512]{1,0:T(8,128)(2,1)S(1)} %get-tuple-element.62.refs_10_) | copy-start | bytes 786436
  15.4 0.7 %copy-start.17 = (bf16[256,512]{1,0:T(8,128)(2,1)}, bf16[256,512]{1,0:T(8,128)(2,1)S(1)}, u32[]{:S(2)}) copy-start(bf16[256,512]{1,0:T(8,128)(2,1)S(1)} %get-tuple-element.63.refs_11_) | copy-start | bytes 786436
  16.1 0.7 copy-start.19
  16.8 0.7 %copy-start.21 = (bf16[512,256]{1,0:T(8,128)(2,1)}, bf16[512,256]{1,0:T(8,128)(2,1)S(1)}, u32[]{:S(2)}) copy-start(bf16[512,256]{1,0:T(8,128)(2,1)S(1)} %get-tuple-element.51.refs_6_) | copy-start | bytes 786436
  17.5 0.7 %copy-start.23 = (bf16[512,256]{1,0:T(8,128)(2,1)}, bf16[512,256]{1,0:T(8,128)(2,1)S(1)}, u32[]{:S(2)}) copy-start(bf16[512,256]{1,0:T(8,128)(2,1)S(1)} %get-tuple-element.52.refs_7_) | copy-start | bytes 786436
  18.2 0.7 %copy-start.25 = (bf16[512,256]{1,0:T(8,128)(2,1)}, bf16[512,256]{1,0:T(8,128)(2,1)S(1)}, u32[]{:S(2)}) copy-start(bf16[512,256]{1,0:T(8,128)(2,1)S(1)} %get-tuple-element.53.refs_8_) | copy-start | bytes 786436
  20.1 0.7 copy-start.27
  20.8 20.7 %collective-permute-start.6 = (f32[392,256]{1,0:T(8,128)}, f32[392,256]{1,0:T(8,128)}, u32[]{:S(2)}, u32[]{:S(2)}) collective-permute-start(f32[392,256]{1,0:T(8,128)} %get-tuple-element.56), channel_id=1, source_target_pairs={{0,2},{2,0},{1,3},{3,1},{4,6},{6,4},{5,7},{7,5},{8,10},{10,8},{9,1... | collective-permute-start | bytes 1204232 | tf_op jit(solution)/shard_map/ppermute | solution.py:364
  22.7 18.8 %collective-permute-start.5 = (f32[392,256]{1,0:T(8,128)S(1)}, f32[392,256]{1,0:T(8,128)S(1)}, u32[]{:S(2)}, u32[]{:S(2)}) collective-permute-start(f32[392,256]{1,0:T(8,128)S(1)} %collective-permute-done.4.refs_12_.refs_0_), channel_id=1, source_target_pairs={{0,16},{16,0},{1,17},{17,1},{2,18},{18,2},{3,19},{19,3},{4,20},{20... | collective-permute-start | bytes 1204232 | tf_op jit(solution)/shard_map/ppermute | solution.py:364
  24.2 0.9 %copy-start.14 = (f32[64,512]{1,0:T(8,128)S(1)}, f32[64,512]{1,0:T(8,128)}, u32[]{:S(2)}) copy-start(f32[64,512]{1,0:T(8,128)} %refs_2_.2) | copy-start | bytes 393220
  25.1 0.9 %copy-start.20 = (bf16[512,256]{1,0:T(8,128)(2,1)S(1)}, bf16[512,256]{1,0:T(8,128)(2,1)}, u32[]{:S(2)}) copy-start(bf16[512,256]{1,0:T(8,128)(2,1)} %copy-done.19) | copy-start | bytes 786436
  26.1 0.9 %copy-start.22 = (bf16[512,256]{1,0:T(8,128)(2,1)S(1)}, bf16[512,256]{1,0:T(8,128)(2,1)}, u32[]{:S(2)}) copy-start(bf16[512,256]{1,0:T(8,128)(2,1)} %copy-done.21) | copy-start | bytes 786436
  27.0 0.9 %copy-start.24 = (bf16[512,256]{1,0:T(8,128)(2,1)S(1)}, bf16[512,256]{1,0:T(8,128)(2,1)}, u32[]{:S(2)}) copy-start(bf16[512,256]{1,0:T(8,128)(2,1)} %copy-done.23) | copy-start | bytes 786436
  28.0 0.9 %copy-start.26 = (bf16[512,256]{1,0:T(8,128)(2,1)S(1)}, bf16[512,256]{1,0:T(8,128)(2,1)}, u32[]{:S(2)}) copy-start(bf16[512,256]{1,0:T(8,128)(2,1)} %copy-done.25) | copy-start | bytes 786436
  28.9 0.9 %copy-start.28 = (f32[64,512]{1,0:T(8,128)S(1)}, f32[64,512]{1,0:T(8,128)}, u32[]{:S(2)}) copy-start(f32[64,512]{1,0:T(8,128)} %copy-done.27) | copy-start | bytes 393220
  29.9 0.7 copy-start.30
  30.5 0.7 copy-start.33
  31.2 14.1 %copy-start.16 = (bf16[256,512]{1,0:T(8,128)(2,1)S(1)}, bf16[256,512]{1,0:T(8,128)(2,1)}, u32[]{:S(2)}) copy-start(bf16[256,512]{1,0:T(8,128)(2,1)} %copy-done.15) | copy-start | bytes 786436
  31.2 14.1 %copy-start.18 = (bf16[256,512]{1,0:T(8,128)(2,1)S(1)}, bf16[256,512]{1,0:T(8,128)(2,1)}, u32[]{:S(2)}) copy-start(bf16[256,512]{1,0:T(8,128)(2,1)} %copy-done.17) | copy-start | bytes 786436
  31.8 7.0 %collective-permute-start.3 = (f32[64,256]{1,0:T(8,128)S(1)}, f32[64,256]{1,0:T(8,128)S(1)}, u32[]{:S(2)}, u32[]{:S(2)}) collective-permute-start(f32[64,256]{1,0:T(8,128)S(1)} %get-tuple-element.54.after.refs_0_), channel_id=1, source_target_pairs={{0,12},{4,0},{8,4},{12,8},{1,13},{5,1},{9,5},{13,9},{2,14},{6,2},{... | collective-permute-start | bytes 196616 | tf_op jit(solution)/shard_map/ppermute | solution.py:364
  35.4 5.2 %collective-permute-start.2 = (f32[64,256]{1,0:T(8,128)S(1)}, f32[64,256]{1,0:T(8,128)S(1)}, u32[]{:S(2)}, u32[]{:S(2)}) collective-permute-start(f32[64,256]{1,0:T(8,128)S(1)} %get-tuple-element.54.after.refs_0_), channel_id=1, source_target_pairs={{0,8},{4,12},{8,0},{12,4},{1,9},{5,13},{9,1},{13,5},{2,10},{6,14},... | collective-permute-start | bytes 196616 | tf_op jit(solution)/shard_map/ppermute | solution.py:364
  35.4 6.1 %collective-permute-start.1 = (f32[64,256]{1,0:T(8,128)S(1)}, f32[64,256]{1,0:T(8,128)S(1)}, u32[]{:S(2)}, u32[]{:S(2)}) collective-permute-start(f32[64,256]{1,0:T(8,128)S(1)} %get-tuple-element.54.after.refs_0_), channel_id=1, source_target_pairs={{0,4},{4,8},{8,12},{12,0},{1,5},{5,9},{9,13},{13,1},{2,6},{6,10},{... | collective-permute-start | bytes 196616 | tf_op jit(solution)/shard_map/ppermute | solution.py:364
  36.5 0.7 copy-start.40
  37.4 0.7 %copy-start.36 = (s32[512,6]{0,1:T(8,128)S(1)}, s32[512,6]{0,1:T(8,128)}, u32[]{:S(2)}) copy-start(s32[512,6]{0,1:T(8,128)} %param.30) | copy-start | bytes 36868
  38.1 8.7 %copy-start.1 = (f32[512,256]{1,0:T(8,128)S(1)}, f32[512,256]{1,0:T(8,128)}, u32[]{:S(2)}) copy-start(f32[512,256]{1,0:T(8,128)} %ws.6) | copy-start | bytes 1572868
  38.1 8.7 %copy-start.2 = (f32[512,256]{1,0:T(8,128)S(1)}, f32[512,256]{1,0:T(8,128)}, u32[]{:S(2)}) copy-start(f32[512,256]{1,0:T(8,128)} %wr.6) | copy-start | bytes 1572868
  38.1 8.7 %copy-start.3 = (f32[256,512]{1,0:T(8,128)S(1)}, f32[256,512]{1,0:T(8,128)}, u32[]{:S(2)}) copy-start(f32[256,512]{1,0:T(8,128)} %wo.6) | copy-start | bytes 1572868
  41.5 3.8 %collective-permute-start.11 = (f32[392,256]{1,0:T(8,128)S(1)}, f32[392,256]{1,0:T(8,128)S(1)}, u32[]{:S(2)}, u32[]{:S(2)}) collective-permute-start(f32[392,256]{1,0:T(8,128)S(1)} %collective-permute-done.4.refs_12_.refs_0_), channel_id=1, source_target_pairs={{0,1},{1,0},{2,3},{3,2},{4,5},{5,4},{6,7},{7,6},{8,9},{9,8},{10,11... | collective-permute-start | bytes 1204232 | tf_op jit(solution)/shard_map/ppermute | solution.py:364
  41.5 3.8 %collective-permute-start.12 = (f32[392,256]{1,0:T(8,128)S(1)}, f32[392,256]{1,0:T(8,128)S(1)}, u32[]{:S(2)}, u32[]{:S(2)}) collective-permute-start(f32[392,256]{1,0:T(8,128)S(1)} %collective-permute-done.5.refs_14_.refs_2_), channel_id=1, source_target_pairs={{0,1},{1,0},{2,3},{3,2},{4,5},{5,4},{6,7},{7,6},{8,9},{9,8},{10,11... | collective-permute-start | bytes 1204232 | tf_op jit(solution)/shard_map/ppermute | solution.py:364
  42.0 11.5 %collective-permute-start.14 = (f32[392,256]{1,0:T(8,128)}, f32[392,256]{1,0:T(8,128)S(1)}, u32[]{:S(2)}, u32[]{:S(2)}) collective-permute-start(f32[392,256]{1,0:T(8,128)} %collective-permute-done.6.refs_0_), channel_id=1, source_target_pairs={{0,16},{16,0},{1,17},{17,1},{2,18},{18,2},{3,19},{19,3},{4,20},{20... | collective-permute-start | bytes 1204232 | tf_op jit(solution)/shard_map/ppermute | solution.py:364
  42.5 1.4 %collective-permute-start.7 = (f32[64,256]{1,0:T(8,128)S(1)}, f32[64,256]{1,0:T(8,128)S(1)}, u32[]{:S(2)}, u32[]{:S(2)}) collective-permute-start(f32[64,256]{1,0:T(8,128)S(1)} %get-tuple-element.54.after.refs_0_), channel_id=1, source_target_pairs={{0,1},{1,0},{2,3},{3,2},{4,5},{5,4},{6,7},{7,6},{8,9},{9,8},{10,11... | collective-permute-start | bytes 196616 | tf_op jit(solution)/shard_map/ppermute | solution.py:364
  42.5 1.5 %collective-permute-start.8 = (f32[64,256]{1,0:T(8,128)S(1)}, f32[64,256]{1,0:T(8,128)S(1)}, u32[]{:S(2)}, u32[]{:S(2)}) collective-permute-start(f32[64,256]{1,0:T(8,128)S(1)} %collective-permute-done.1.refs_1_), channel_id=1, source_target_pairs={{0,1},{1,0},{2,3},{3,2},{4,5},{5,4},{6,7},{7,6},{8,9},{9,8},{10,11... | collective-permute-start | bytes 196616 | tf_op jit(solution)/shard_map/ppermute | solution.py:364
  43.9 1.3 %collective-permute-start.9 = (f32[64,256]{1,0:T(8,128)S(1)}, f32[64,256]{1,0:T(8,128)S(1)}, u32[]{:S(2)}, u32[]{:S(2)}) collective-permute-start(f32[64,256]{1,0:T(8,128)S(1)} %collective-permute-done.2.refs_2_), channel_id=1, source_target_pairs={{0,1},{1,0},{2,3},{3,2},{4,5},{5,4},{6,7},{7,6},{8,9},{9,8},{10,11... | collective-permute-start | bytes 196616 | tf_op jit(solution)/shard_map/ppermute | solution.py:364
  44.1 1.3 %collective-permute-start.10 = (f32[64,256]{1,0:T(8,128)S(1)}, f32[64,256]{1,0:T(8,128)S(1)}, u32[]{:S(2)}, u32[]{:S(2)}) collective-permute-start(f32[64,256]{1,0:T(8,128)S(1)} %collective-permute-done.3.refs_3_), channel_id=1, source_target_pairs={{0,1},{1,0},{2,3},{3,2},{4,5},{5,4},{6,7},{7,6},{8,9},{9,8},{10,11... | collective-permute-start | bytes 196616 | tf_op jit(solution)/shard_map/ppermute | solution.py:364
  46.1 7.4 %copy-start.31 = (f32[4,512]{1,0:T(4,128)S(1)}, f32[4,512]{1,0:T(4,128)}, u32[]{:S(2)}) copy-start(f32[4,512]{1,0:T(4,128)} %copy-done.29) | copy-start | bytes 24580
  46.2 7.3 %copy-start.35 = (s32[512,3]{0,1:T(4,128)S(1)}, s32[512,3]{0,1:T(4,128)}, u32[]{:S(2)}) copy-start(s32[512,3]{0,1:T(4,128)} %param.29) | copy-start | bytes 18436
  46.2 7.3 %collective-permute-start.13 = (f32[64,512]{1,0:T(8,128)S(1)}, f32[64,512]{1,0:T(8,128)S(1)}, u32[]{:S(2)}, u32[]{:S(2)}) collective-permute-start(f32[64,512]{1,0:T(8,128)S(1)} %shard_map.263.after.refs_0_), channel_id=1, source_target_pairs={{0,2},{2,0},{1,3},{3,1},{4,6},{6,4},{5,7},{7,5},{8,10},{10,8},{9,1... | collective-permute-start | bytes 393224 | tf_op jit(solution)/shard_map/ppermute | solution.py:364
  55.6 2.9 %copy-start.34 = (f32[3,256]{1,0:T(4,128)S(1)}, f32[3,256]{1,0:T(4,128)}, u32[]{:S(2)}) copy-start(f32[3,256]{1,0:T(4,128)} %copy-done.32) | copy-start | bytes 9220
  55.6 2.9 %collective-permute-start.17 = (f32[392,256]{1,0:T(8,128)}, f32[392,256]{1,0:T(8,128)S(1)}, u32[]{:S(2)}, u32[]{:S(2)}) collective-permute-start(f32[392,256]{1,0:T(8,128)} %collective-permute-done.6.refs_0_), channel_id=1, source_target_pairs={{0,1},{1,0},{2,3},{3,2},{4,5},{5,4},{6,7},{7,6},{8,9},{9,8},{10,11... | collective-permute-start | bytes 1204232 | tf_op jit(solution)/shard_map/ppermute | solution.py:364
  55.6 2.9 %collective-permute-start.18 = (f32[392,256]{1,0:T(8,128)S(1)}, f32[392,256]{1,0:T(8,128)S(1)}, u32[]{:S(2)}, u32[]{:S(2)}) collective-permute-start(f32[392,256]{1,0:T(8,128)S(1)} %collective-permute-done.14.refs_2_), channel_id=1, source_target_pairs={{0,1},{1,0},{2,3},{3,2},{4,5},{5,4},{6,7},{7,6},{8,9},{9,8},{10,11... | collective-permute-start | bytes 1204232 | tf_op jit(solution)/shard_map/ppermute | solution.py:364
  56.1 9.4 %collective-permute-start.16 = (f32[128,512]{1,0:T(8,128)S(1)}, f32[128,512]{1,0:T(8,128)S(1)}, u32[]{:S(2)}, u32[]{:S(2)}) collective-permute-start(f32[128,512]{1,0:T(8,128)S(1)} %get-tuple-element.76.head), channel_id=1, source_target_pairs={{0,13},{1,0},{4,1},{5,4},{8,5},{9,8},{12,9},{13,12},{2,15},{3,2},{... | collective-permute-start | bytes 786440 | tf_op jit(solution)/shard_map/ppermute | solution.py:364
  57.1 8.4 %collective-permute-start.15 = (f32[128,512]{1,0:T(8,128)S(1)}, f32[128,512]{1,0:T(8,128)S(1)}, u32[]{:S(2)}, u32[]{:S(2)}) collective-permute-start(f32[128,512]{1,0:T(8,128)S(1)} %get-tuple-element.75.tail), channel_id=1, source_target_pairs={{0,1},{1,4},{4,5},{5,8},{8,9},{9,12},{12,13},{13,0},{2,3},{3,6},{6... | collective-permute-start | bytes 786440 | tf_op jit(solution)/shard_map/ppermute | solution.py:364
  (2 other events, 1.2 us)

commit v5 on v4

--- a/solution.py
+++ b/solution.py
@@ -10,9 +10,8 @@
 epsilon = 1e-05
 f32 = jnp.float32
 bf16 = jnp.bfloat16
-limit_bytes = 16 * 1024 * 1024
-wide_limit = 50 * 1024 * 1024
-large_limit = 60 * 1024 * 1024
+limit_bytes = 12 * 1024 * 1024
+tight_limit = 60 * 1024 * 1024
 most_direct = 4
 
 
@@ -80,22 +79,46 @@
     return moves
 
 
-def upward_kernel(nodes, coarse, children, ws, wr, bias, wo, part):
+def strips(source, target, count):
+    rows = source.shape[0] // count
+    return [
+        (source.at[pl.ds(i * rows, rows)], target.at[pl.ds(i * rows, rows)]) for i in range(count)
+    ]
+
+
+def upward_kernel(nodes_hbm, coarse_hbm, ws_hbm, wr_hbm, wo_hbm, children, bias, part, nodes, coarse, ws, wr, wo, high, low, sems):
+    cuts = 4
+    moves = started(
+        strips(ws_hbm, ws, cuts)
+        + strips(nodes_hbm, nodes, cuts)
+        + [(coarse_hbm, coarse)]
+        + strips(wr_hbm, wr, cuts)
+        + strips(wo_hbm, wo, cuts),
+        sems,
+    )
     wanted = upright(children[...])
     names = lax.broadcasted_iota(jnp.int32, (wanted.shape[0], nodes.shape[0]), 1)
     picks = one_hot(wanted, names)
-    sender_high, sender_low = split(0.5 * dot3(nodes[...], *split(ws[...])))
+    for move in moves[:cuts]:
+        move.wait()
+    ws_high, ws_low = split(ws[...])
+    rows = nodes.shape[0] // cuts
+    for i in range(cuts):
+        moves[cuts + i].wait()
+        place = slice(i * rows, (i + 1) * rows)
+        high[place], low[place] = split(0.5 * dot3(nodes[place], ws_high, ws_low))
+    for move in moves[2 * cuts : 3 * cuts + 1]:
+        move.wait()
     receivers = 0.5 * (dot3(coarse[...], *split(wr[...])) + bias[...])
-    picked = dot(picks, sender_high) + dot(picks, sender_low)
+    picked = dot(picks, high[...]) + dot(picks, low[...])
     hidden = silu_sum(picked, receivers, wanted.shape[1])
+    for move in moves[3 * cuts + 1 :]:
+        move.wait()
     part[...] = dot3(hidden, *split(wo[...]))
 
 
-def coarse_ready_kernel(parts, after, ws, wr, wo, *refs):
-    del after
-    params, own, refs = refs[:7], refs[7:11], refs[11:]
-    ws_high, ws_low, wr_high, wr_low, wo_high, wo_low, gains, biases, pack, sems = refs
-    moves = started(share_copies(own, pack, parts), sems)
+def coarse_ready_kernel(ws, wr, wo, *refs):
+    params, (ws_high, ws_low, wr_high, wr_low, wo_high, wo_low, gains, biases) = refs[:7], refs[7:]
     for i in range(4):
         gains[i : i + 1] = params[i][...]
     for i in range(3):
@@ -103,7 +126,12 @@
     ws_high[...], ws_low[...] = split(ws[...])
     wr_high[...], wr_low[...] = split(wr[...])
     wo_high[...], wo_low[...] = split(wo[...])
-    for move in moves:
+
+
+def share_kernel(parts, *refs):
+    down_own, bottom_own, (down_pack, bottom_pack, sems) = refs[:4], refs[4:8], refs[8:]
+    copies = share_copies(down_own, down_pack, parts) + share_copies(bottom_own, bottom_pack, parts)
+    for move in started(copies, sems):
         move.wait()
 
 
@@ -132,15 +160,24 @@
     return copies
 
 
-def share_kernel(parts, *refs):
-    for move in started(share_copies(refs[:-2], refs[-2], parts), refs[-1]):
-        move.wait()
-
-
-def picks_kernel(after, links, names, picks):
-    del after
-    wanted = upright(links[...])
-    picks[...] = one_hot(wanted, jnp.broadcast_to(names[...], (wanted.shape[0], names.shape[1])))
+def picks_kernel(rim, patches, blocks, coarse_links, bottom_links, coarse_picks, bottom_picks):
+    wanted = upright(coarse_links[...])
+    rows = wanted.shape[0]
+    lvls = lax.axis_size("lvl")
+    column = lax.broadcasted_iota(jnp.int32, (rows, blocks), 1)
+    for t in range(lvls):
+        for s in range(patches):
+            patch = lax.rem(lax.axis_index("patch") + patches - s, patches)
+            lvl = lax.rem(lax.axis_index("lvl") + lvls - t, lvls)
+            first = (patch * lvls + lvl) * blocks
+            at = (t * patches + s) * blocks
+            coarse_picks[:, at : at + blocks] = one_hot(wanted, column + first)
+    wanted = upright(bottom_links[...])
+    size = rim * wanted.shape[1]
+    names = lax.broadcasted_iota(jnp.int32, (rim, 3 * rim), 1)
+    for i in range(wanted.shape[0] // rim):
+        strip = wanted[i * rim : (i + 1) * rim]
+        bottom_picks[i * size : (i + 1) * size, :] = one_hot(strip, names + i * rim)
 
 
 def coarse_project_kernel(count, *refs):
@@ -211,8 +248,7 @@
             out[block] = jnp.broadcast_to(pack[at : at + 1, :], (8, own.shape[1]))
 
 
-def down_weights_kernel(count, after, nodes, ws, wr, biases, wo, *refs):
-    del after
+def down_weights_kernel(count, nodes, ws, wr, biases, wo, *refs):
     packs, refs = refs[:count], refs[count:]
     receivers, ws_high, ws_low, wo_high, wo_low, wr_high, wr_low, bias_all = refs
     width = ws.shape[1]
@@ -233,16 +269,6 @@
     collect_in(wr, packs, share, wr_high, wr_low)
     collect_out(wo, packs, 2 * share, wo_high, wo_low)
     collect_bias(biases[2:3], packs, 3 * share, bias_all)
-
-
-def bottom_picks_kernel(rim, after, links, picks):
-    del after
-    wanted = upright(links[...])
-    size = rim * wanted.shape[1]
-    names = lax.broadcasted_iota(jnp.int32, (rim, 3 * rim), 1)
-    for i in range(wanted.shape[0] // rim):
-        strip = wanted[i * rim : (i + 1) * rim]
-        picks[i * size : (i + 1) * size, :] = one_hot(strip, names + i * rim)
 
 
 def down_rows(nodes, receivers, sources, senders, wo_high, wo_low, gain):
@@ -342,13 +368,15 @@
 away = pl.BlockSpec(memory_space=pl.ANY)
 
 
-def call(kernel, outs, operands, flops, scratch=(), far=(), far_outs=(), limit=limit_bytes):
+def call(kernel, outs, operands, flops, scratch=(), far=(), unread=0, limit=limit_bytes):
     moved = sum(x.size * x.dtype.itemsize for x in (*outs, *operands))
+    read = len(operands) - unread
+    specs = [away if i in far else whole for i in range(read)] + [away] * unread
     return pl.pallas_call(
-        kernel,
+        (lambda *refs: kernel(*refs[:read], *refs[read + unread :])) if unread else kernel,
         out_shape=tuple(outs),
-        in_specs=[away if i in far else whole for i in range(len(operands))],
-        out_specs=tuple(away if i in far_outs else whole for i in range(len(outs))),
+        in_specs=specs,
+        out_specs=tuple([whole] * len(outs)),
         scratch_shapes=list(scratch),
         compiler_params=pltpu.CompilerParams(vmem_limit_bytes=limit),
         cost_estimate=pl.CostEstimate(flops=int(flops), bytes_accessed=moved, transcendentals=0),
@@ -379,17 +407,6 @@
     pieces, others = lax.optimization_barrier((pieces, others))
     near += [[piece] + [shifted(piece, "lvl", t) for t in range(1, lvls)] for piece in pieces]
     return [row[t] for t in range(lvls) for row in near], others
-
-
-def coarse_names(rows):
-    patches, lvls = lax.axis_size("patch"), lax.axis_size("lvl")
-    place = jnp.arange(rows * patches * lvls, dtype=jnp.int32)
-    if patches > most_direct:
-        return place[None]
-    step, away = (place // rows) % patches, place // (rows * patches)
-    patch = (lax.axis_index("patch") - step) % patches
-    lvl = (lax.axis_index("lvl") - away) % lvls
-    return ((patch * lvls + lvl) * rows + place % rows)[None].astype(jnp.int32)
 
 
 def held(values, event):
@@ -460,43 +477,57 @@
     columns = latent // width
     ensemble, lvls = lax.axis_size("parts"), lax.axis_size("lvl")
     share = latent // (ensemble * lvls)
-    row = 8
-    pack = like((3 * share + row, width))
-    copying = [pltpu.SemaphoreType.DMA((3 + columns,))]
-    (down_pack,) = call(
+    pack = like((3 * share + 8, width))
+
+    down_pack, bottom_pack = call(
         functools.partial(share_kernel, ensemble),
-        [pack],
-        [downward_sender, downward_receiver, downward_output, downward_bias[None]],
+        [pack, pack],
+        [
+            downward_sender, downward_receiver, downward_output, downward_bias[None],
+            bottom_sender, bottom_receiver, bottom_output, bottom_bias[None],
+        ],
         latent,
-        copying,
-        far=range(4),
-        limit=large_limit,
+        [pltpu.SemaphoreType.DMA((6 + 2 * columns,))],
+        far=range(8),
+        limit=tight_limit,
     )
     down_near = over_sub(down_pack)
     (part,) = call(
         upward_kernel,
         [like((blocks, latent))],
-        [node_states, coarse_states, children.T, upward_sender, upward_receiver, upward_bias[None], upward_output],
+        [
+            node_states, coarse_states, upward_sender, upward_receiver, upward_output,
+            children.T, upward_bias[None],
+        ],
         6 * rows * latent * width + 4 * children.size * rows * width,
-        limit=wide_limit,
+        [
+            pltpu.VMEM((rows, latent), f32),
+            pltpu.VMEM((blocks, latent), f32),
+            pltpu.VMEM((latent, width), f32),
+            pltpu.VMEM((latent, width), f32),
+            pltpu.VMEM((width, latent), f32),
+            pltpu.VMEM((rows, width), bf16),
+            pltpu.VMEM((rows, width), bf16),
+            pltpu.SemaphoreType.DMA((17,)),
+        ],
+        far=range(5),
+        limit=tight_limit,
     )
     parts = sub_parts(part)
-    ws_high, ws_low, wr_high, wr_low, wo_high, wo_low, gains, biases, bottom_pack = call(
-        functools.partial(coarse_ready_kernel, ensemble),
+    ws_high, ws_low, wr_high, wr_low, wo_high, wo_low, gains, biases = call(
+        coarse_ready_kernel,
         [like((latent, width), bf16)] * 4
         + [like((width, latent), bf16)] * 2
-        + [like((4, latent)), like((3, width)), pack],
+        + [like((4, latent)), like((3, width))],
         [
-            part, coarse_sender, coarse_receiver, coarse_output,
+            coarse_sender, coarse_receiver, coarse_output,
             upward_gain[None], coarse_gain[None], downward_gain[None], bottom_gain[None],
-            coarse_bias[None], downward_bias[None], bottom_bias[None],
-            bottom_sender, bottom_receiver, bottom_output, bottom_bias[None],
+            coarse_bias[None], downward_bias[None], bottom_bias[None], part,
         ],
         latent * hidden,
-        copying,
-        far=(0, 11, 12, 13, 14),
-    )
-    bottom_near = over_sub(held(bottom_pack, parts[-1]))
+        unread=1,
+    )
+    bottom_near = over_sub(held(bottom_pack, (parts[-1], gains)))
     down_far = over_parts(down_near)
     coarse_up, senders, receivers = call(
         functools.partial(coarse_project_kernel, len(parts)),
@@ -504,20 +535,14 @@
         [*parts, coarse_states, gains, biases, ws_high, ws_low, wr_high, wr_low],
         12 * blocks * latent * width,
     )
-    names = coarse_names(blocks)
-    (picks,) = call(
-        picks_kernel,
-        [like((coarse_links.size, names.size), bf16)],
-        [senders, coarse_links.T, names],
-        coarse_links.size * names.size,
-        far=(0,),
-    )
-    (bottom_picks,) = call(
-        functools.partial(bottom_picks_kernel, rim),
-        [like((bottom_links.size, 3 * rim), bf16)],
-        [senders, bottom_links.T],
-        bottom_links.size * 3 * rim,
-        far=(0,),
+    patches = lax.axis_size("patch")
+    names = blocks * patches * lvls
+    picks, bottom_picks = call(
+        functools.partial(picks_kernel, rim, patches, blocks),
+        [like((coarse_links.size, names), bf16), like((bottom_links.size, 3 * rim), bf16)],
+        [coarse_links.T, bottom_links.T, senders],
+        coarse_links.size * names,
+        unread=1,
     )
     pieces, (picks, bottom_picks, down_near, down_far, bottom_near) = coarse_pieces(
         senders, (picks, bottom_picks, down_near, down_far, bottom_near)
@@ -528,17 +553,17 @@
         functools.partial(coarse_kernel, len(pieces)),
         [like((blocks, latent))],
         [*pieces, picks, receivers, wo_high, wo_low, *down_packs],
-        4 * coarse_links.size * names.size * width,
-        far=range(len(pieces) + 4, len(pieces) + 4 + len(down_packs)),
+        4 * coarse_links.size * names * width,
+        unread=len(down_packs),
     )
     parts = sub_parts(part)
     receivers, ws_high, ws_low, wo_high, wo_low = call(
         functools.partial(down_weights_kernel, len(down_packs)),
         [like((rows, hidden)), *weights, *outputs],
-        [part, node_states, downward_sender, downward_receiver, biases, downward_output, *down_packs],
+        [node_states, downward_sender, downward_receiver, biases, downward_output, *down_packs, part],
         6 * rows * latent * hidden,
         [pltpu.VMEM((subs, latent, width), bf16)] * 2 + [pltpu.VMEM((subs, 8, width), f32)],
-        far=(0,),
+        unread=1,
     )
     parts, bottom_far = lax.optimization_barrier((parts, bottom_far))
     new_coarse, senders, head, tail = call(

time: 70.4 us -> 61.2 us (0.87)
  local copies, waits for them, and re-layouts: 19.9 us -> 1.9 us
  waiting for transfers between devices: 10.7 us -> 18.8 us
  Pallas kernels: 22.7 us -> 24.3 us
    unnamed x94 -> x48, local copies, waits for them, and re-layouts: 19.9 us -> 1.9 us
    ppermute x19, waiting for transfers between devices: 10.7 us -> 18.8 us  [shifted(): lax.ppermute(values, axis, [(i, (i + step) % count) for i in range(count)])]
    pallas_call x13 -> x12, Pallas kernels: 22.7 us -> 24.3 us  [call(): pl.pallas_call((lambda *refs: kernel(*refs[:read], *refs[read + unread:])...]
  transfers between devices with their start and end apart: 19 -> 19, of which waited for: 7 -> 8; matrix products, arithmetic and copies ran while one was open for 0% -> 0% of each run, Pallas kernels for 21% -> 26%
where the time goes in v5:
time: 61.2 us; the launch traced here: 60.9 us
  Pallas kernels  24.3 us (40%)
  waiting for transfers between devices  18.8 us (31%)
  starting transfers between devices  15 us (25%)
  local copies, waits for them, and re-layouts  1.9 us (3%)
  between operations  0.96 us (2%)
    pallas_call x12, Pallas kernels, call(): pl.pallas_call((lambda *refs: kernel(*refs[:read], *refs[read + unread:])...  24.3 us
    ppermute x19, waiting for transfers between devices, shifted(): lax.ppermute(values, axis, [(i, (i + step) % count) for i in range(count)])  18.8 us
    ppermute x19, starting transfers between devices, shifted(): lax.ppermute(values, axis, [(i, (i + step) % count) for i in range(count)])  15 us
    unnamed x48, local copies, waits for them, and re-layouts  1.9 us
  transfers between devices with their start and end apart: 19, of which 8 were waited for; matrix products, arithmetic and copies ran while one was open for 0% of the time, Pallas kernels for 26%

profile of v5, /device:TPU:0, one launch (start us, length us, event | category | flops | bytes accessed | tf_op | source)
XLA Modules:
  0.0 60.9 jit_solution(7082371981993106862)
XLA Ops:
  0.6 0.0 copy-start.9
  0.6 0.0 copy-start.10
  0.7 0.0 copy-start.11
  0.7 0.0 copy-start.15
  0.7 0.0 copy-start.16
  0.7 0.0 copy-start.18
  0.7 0.0 copy-start.19
  0.7 0.0 copy-start.20
  0.7 0.0 copy-start.21
  0.7 2.2 %shard_map.261 = (f32[392,256]{1,0:T(8,128)}, f32[392,256]{1,0:T(8,128)}) custom-call(f32[512,256]{1,0:T(8,128)} %refs_1_.5, f32[512,256]{1,0:T(8,128)} %refs_2_.7, f32[256,512]{1,0:T(8,128)} %refs_4_.4, f32[1,256]{1,0:T(1,128)} %bitcast.15, f32[512,256]{1,0:T(8,128)} %ws.1, f32[512,256]{1,0:T(8,128)} %wr.1, f32[256,512]{1,0:T(8,128)} %wo.1, f32[1,256]{1,0:T(1,128)} %bitcast.17), custom_call_target="tpu_custom_call" | custom-call | flops 512 | bytes 3950592 | tf_op jit(solution)/shard_map/pallas_call | solution.py:375
  3.0 0.0 copy-start.12
  3.0 3.0 %collective-permute-start.4 = (f32[392,256]{1,0:T(8,128)}, f32[392,256]{1,0:T(8,128)S(1)}, u32[]{:S(2)}, u32[]{:S(2)}) collective-permute-start(f32[392,256]{1,0:T(8,128)} %get-tuple-element.60), channel_id=1, source_target_pairs={{0,2},{2,0},{1,3},{3,1},{4,6},{6,4},{5,7},{7,5},{8,10},{10,8},{9,1... | collective-permute-start | bytes 1204232 | tf_op jit(solution)/shard_map/ppermute | solution.py:392
  6.0 5.2 %shard_map.257.refs_10_.refs_0_ = f32[64,512]{1,0:T(8,128)} custom-call(f32[512,512]{1,0:T(8,128)} %nodes.1, f32[64,512]{1,0:T(8,128)} %refs_2_.5, f32[512,256]{1,0:T(8,128)} %ws_hbm.1, f32[512,256]{1,0:T(8,128)} %wr_hbm.1, f32[256,512]{1,0:T(8,128)} %wo_hbm.1, s32[7,64]{1,0:T(8,128)} %bitcast.25, f32[1,256]{1,0:T(1,128)} %bitcast.26), custom_call_target="tpu_custom_call" | custom-call | flops 637534208 | bytes 2886400 | tf_op jit(solution)/shard_map/pallas_call | solution.py:375
  11.2 0.2 collective-permute-start
  11.4 0.0 copy-start.7
  11.4 0.9 %copy-done.7 = f32[64,512]{1,0:T(8,128)S(1)} copy-done((f32[64,512]{1,0:T(8,128)S(1)}, f32[64,512]{1,0:T(8,128)}, u32[]{:S(2)}) %copy-start.7) | copy-done | bytes 131096
  12.3 0.3 shard_map.258
  12.6 5.7 %collective-permute-done.refs_1_ = f32[64,512]{1,0:T(8,128)S(1)} collective-permute-done((f32[64,512]{1,0:T(8,128)}, f32[64,512]{1,0:T(8,128)S(1)}, u32[]{:S(2)}, u32[]{:S(2)}) %collective-permute-start) | collective-permute-done | bytes 131104 | tf_op jit(solution)/shard_map/ppermute | solution.py:392
  18.3 1.7 %collective-permute-start.6 = (f32[392,256]{1,0:T(8,128)S(1)}, f32[392,256]{1,0:T(8,128)S(1)}, u32[]{:S(2)}, u32[]{:S(2)}) collective-permute-start(f32[392,256]{1,0:T(8,128)S(1)} %copy-done.23), channel_id=1, source_target_pairs={{0,2},{2,0},{1,3},{3,1},{4,6},{6,4},{5,7},{7,5},{8,10},{10,8},{9,1... | collective-permute-start | bytes 1204232 | tf_op jit(solution)/shard_map/ppermute | solution.py:392
  20.1 0.0 collective-permute-done.4.refs_12_.refs_5_
  20.1 1.5 %collective-permute-start.5 = (f32[392,256]{1,0:T(8,128)S(1)}, f32[392,256]{1,0:T(8,128)S(1)}, u32[]{:S(2)}, u32[]{:S(2)}) collective-permute-start(f32[392,256]{1,0:T(8,128)S(1)} %collective-permute-done.4.refs_12_.refs_5_), channel_id=1, source_target_pairs={{0,16},{16,0},{1,17},{17,1},{2,18},{18,2},{3,19},{19,3},{4,20},{20... | collective-permute-start | bytes 1204232 | tf_op jit(solution)/shard_map/ppermute | solution.py:392
  21.6 0.9 %copy-done.8 = f32[64,512]{1,0:T(8,128)S(1)} copy-done((f32[64,512]{1,0:T(8,128)S(1)}, f32[64,512]{1,0:T(8,128)}, u32[]{:S(2)}) %copy-start.8) | copy-done | bytes 131096
  22.5 0.6 shard_map.259
  23.1 3.7 %collective-permute-start.3 = (f32[64,256]{1,0:T(8,128)S(1)}, f32[64,256]{1,0:T(8,128)S(1)}, u32[]{:S(2)}, u32[]{:S(2)}) collective-permute-start(f32[64,256]{1,0:T(8,128)S(1)} %get-tuple-element.57.refs_2_.refs_0_), channel_id=1, source_target_pairs={{0,12},{4,0},{8,4},{12,8},{1,13},{5,1},{9,5},{13,9},{2,14},{6,2},{... | collective-permute-start | bytes 196616 | tf_op jit(solution)/shard_map/ppermute | solution.py:392
  26.7 0.0 collective-permute-start.2
  26.7 1.0 %collective-permute-start.1 = (f32[64,256]{1,0:T(8,128)S(1)}, f32[64,256]{1,0:T(8,128)S(1)}, u32[]{:S(2)}, u32[]{:S(2)}) collective-permute-start(f32[64,256]{1,0:T(8,128)S(1)} %get-tuple-element.57.refs_2_.refs_0_), channel_id=1, source_target_pairs={{0,4},{4,8},{8,12},{12,0},{1,5},{5,9},{9,13},{13,1},{2,6},{6,10},{... | collective-permute-start | bytes 196616 | tf_op jit(solution)/shard_map/ppermute | solution.py:392
  27.7 1.1 %shard_map.260 = (bf16[384,512]{1,0:T(8,128)(2,1)S(1)}, bf16[3072,384]{1,0:T(8,128)(2,1)S(1)}) custom-call(s32[6,64]{1,0:T(8,128)S(1)} %bitcast.19, s32[6,512]{1,0:T(8,128)S(1)} %bitcast.14, f32[64,256]{1,0:T(8,128)S(1)} %get-tuple-element.57.refs_2_.refs_0_), custom_call_target="tpu_custom_call" | custom-call | flops 196608 | bytes 2831872 | tf_op jit(solution)/shard_map/pallas_call | solution.py:375
  28.8 0.0 collective-permute-done.3.refs_3_
  28.8 3.1 %collective-permute-done.2.refs_2_ = f32[64,256]{1,0:T(8,128)S(1)} collective-permute-done((f32[64,256]{1,0:T(8,128)S(1)}, f32[64,256]{1,0:T(8,128)S(1)}, u32[]{:S(2)}, u32[]{:S(2)}) %collective-permute-start.2) | collective-permute-done | bytes 65568 | tf_op jit(solution)/shard_map/ppermute | solution.py:392
  31.9 0.9 %collective-permute-done.1.refs_1_ = f32[64,256]{1,0:T(8,128)S(1)} collective-permute-done((f32[64,256]{1,0:T(8,128)S(1)}, f32[64,256]{1,0:T(8,128)S(1)}, u32[]{:S(2)}, u32[]{:S(2)}) %collective-permute-start.1) | collective-permute-done | bytes 65568 | tf_op jit(solution)/shard_map/ppermute | solution.py:392
  32.8 0.0 collective-permute-done.6.refs_0_
  32.8 0.0 collective-permute-done.5.refs_14_.refs_7_
  32.8 0.0 collective-permute-start.11
  32.8 0.5 collective-permute-start.12
  33.3 0.5 collective-permute-start.14
  33.8 0.0 collective-permute-start.7
  33.8 0.5 collective-permute-start.8
  34.3 0.9 %collective-permute-done.7.refs_4_ = f32[64,256]{1,0:T(8,128)S(1)} collective-permute-done((f32[64,256]{1,0:T(8,128)S(1)}, f32[64,256]{1,0:T(8,128)S(1)}, u32[]{:S(2)}, u32[]{:S(2)}) %collective-permute-start.7) | collective-permute-done | bytes 65568 | tf_op jit(solution)/shard_map/ppermute | solution.py:392
  35.2 0.1 collective-permute-start.9
  35.3 0.0 collective-permute-done.8.refs_5_
  35.3 0.4 collective-permute-start.10
  35.7 0.7 %collective-permute-done.9.refs_6_ = f32[64,256]{1,0:T(8,128)S(1)} collective-permute-done((f32[64,256]{1,0:T(8,128)S(1)}, f32[64,256]{1,0:T(8,128)S(1)}, u32[]{:S(2)}, u32[]{:S(2)}) %collective-permute-start.9) | collective-permute-done | bytes 65568 | tf_op jit(solution)/shard_map/ppermute | solution.py:392
  36.5 0.2 collective-permute-done.10.refs_7_
  36.6 0.0 collective-permute-done.11.refs_13_.refs_6_
  36.6 0.0 collective-permute-done.12.refs_15_.refs_8_
  36.6 0.8 %shard_map.262.refs_9_.refs_0_ = f32[64,512]{1,0:T(8,128)S(1)} custom-call(f32[64,256]{1,0:T(8,128)S(1)} %get-tuple-element.57.refs_2_.refs_0_, f32[64,256]{1,0:T(8,128)S(1)} %collective-permute-done.1.refs_1_, f32[64,256]{1,0:T(8,128)S(1)} %collective-permute-done.2.refs_2_, f32[64,256]{1,0:T(8,128)S(1)} %collective-permute-done.3.refs_3_, ...), custom_call_target="tpu_custom_call" | custom-call | flops 201326592 | bytes 3244032 | tf_op jit(solution)/shard_map/pallas_call | solution.py:375
  37.4 0.0 copy-start.13
  37.4 0.6 collective-permute-start.13
  38.0 1.6 %shard_map.263 = (f32[512,512]{1,0:T(8,128)S(1)}, bf16[2,512,256]{2,1,0:T(8,128)(2,1)S(1)}, bf16[2,512,256]{2,1,0:T(8,128)(2,1)S(1)}, bf16[512,512]{1,0:T(8,128)(2,1)S(1)}, bf16[512,512]{1,0:T(8,128)(2,1)S(1)}) custom-call(f32[512,512]{1,0:T(8,128)S(1)} %copy-done, f32[512,256]{1,0:T(8,128)S(1)} %copy-done.1, f32[512,256]{1,0:T(8,128)S(1)} %copy-done.2, ...), custom_call_target="tpu_custom_call" | custom-call | flops 805306368 | bytes 7506944 | tf_op jit(solution)/shard_map/pallas_call | solution.py:375
  39.6 5.0 %collective-permute-done.14.refs_2_ = f32[392,256]{1,0:T(8,128)S(1)} collective-permute-done((f32[392,256]{1,0:T(8,128)S(1)}, f32[392,256]{1,0:T(8,128)S(1)}, u32[]{:S(2)}, u32[]{:S(2)}) %collective-permute-start.14) | collective-permute-done | bytes 401440 | tf_op jit(solution)/shard_map/ppermute | solution.py:392
  44.6 0.0 collective-permute-done.13.refs_1_
  44.6 2.1 %shard_map.264 = (f32[64,512]{1,0:T(8,128)}, bf16[128,512]{1,0:T(8,128)(2,1)S(1)}, f32[128,512]{1,0:T(8,128)S(1)}, f32[128,512]{1,0:T(8,128)S(1)}) custom-call(f32[64,512]{1,0:T(8,128)S(1)} %shard_map.262.refs_9_.refs_0_, f32[64,512]{1,0:T(8,128)S(1)} %collective-permute-done.13.refs_1_, f32[64,512]{1,0:T(8,128)S(1)} %get-tuple-element.75.refs_2_, ...), custom_call_target="tpu_custom_call" | custom-call | flops 402653184 | bytes 5388288 | tf_op jit(solution)/shard_map/pallas_call | solution.py:375
  46.7 0.0 collective-permute-start.17
  46.7 0.5 collective-permute-start.18
  47.2 0.8 %collective-permute-start.16 = (f32[128,512]{1,0:T(8,128)S(1)}, f32[128,512]{1,0:T(8,128)S(1)}, u32[]{:S(2)}, u32[]{:S(2)}) collective-permute-start(f32[128,512]{1,0:T(8,128)S(1)} %get-tuple-element.82.head), channel_id=1, source_target_pairs={{0,13},{1,0},{4,1},{5,4},{8,5},{9,8},{12,9},{13,12},{2,15},{3,2},{... | collective-permute-start | bytes 786440 | tf_op jit(solution)/shard_map/ppermute | solution.py:392
  47.9 0.0 collective-permute-start.15
  47.9 1.3 %shard_map.265.middle = f32[256,512]{1,0:T(8,128)S(1)} custom-call(f32[512,512]{1,0:T(8,128)S(1)} %copy-done, f32[512,512]{1,0:T(8,128)S(1)} %get-tuple-element.76.refs_5_.receivers, s32[3,512]{1,0:T(4,128)S(1)} %bitcast.13, bf16[128,512]{1,0:T(8,128)(2,1)S(1)} %get-tuple-element.83.senders, bf16[512,512]{1,0:T(8,128)(2,1)S(1)} %get-tuple-element.79.refs_9_.wo_high, ...), custom_call_target="tpu_custom_call" | custom-call | flops 402653184 | bytes 3815424 | tf_op jit(solution)/shard_map/pallas_call | solution.py:375
  49.3 0.0 collective-permute-done.17.refs_1_
  49.3 0.0 collective-permute-done.18.refs_3_
  49.3 0.5 shard_map.266
  49.8 4.4 %shard_map.267 = (bf16[512,512]{1,0:T(8,128)(2,1)S(1)}, bf16[512,512]{1,0:T(8,128)(2,1)S(1)}, f32[512,512]{1,0:T(8,128)S(1)}, f32[256,512]{1,0:T(8,128)S(1)}) custom-call(f32[128,512]{1,0:T(8,128)S(1)} %get-tuple-element.82.head, f32[256,512]{1,0:T(8,128)S(1)} %shard_map.265.middle, f32[128,512]{1,0:T(8,128)S(1)} %get-tuple-element.81.tail, ...), custom_call_target="tpu_custom_call" | custom-call | flops 3221225472 | bytes 9199616 | tf_op jit(solution)/shard_map/pallas_call | solution.py:375
  54.3 2.4 %collective-permute-done.15.before = f32[128,512]{1,0:T(8,128)S(1)} collective-permute-done((f32[128,512]{1,0:T(8,128)S(1)}, f32[128,512]{1,0:T(8,128)S(1)}, u32[]{:S(2)}, u32[]{:S(2)}) %collective-permute-start.15) | collective-permute-done | bytes 262176 | tf_op jit(solution)/shard_map/ppermute | solution.py:392
  56.6 0.0 collective-permute-done.16.after
  56.6 4.3 %shard_map.268 = f32[512,512]{1,0:T(8,128)} custom-call(f32[128,512]{1,0:T(8,128)S(1)} %collective-permute-done.15.before, f32[128,512]{1,0:T(8,128)S(1)} %collective-permute-done.16.after, f32[128,512]{1,0:T(8,128)S(1)} %get-tuple-element.82.head, f32[128,512]{1,0:T(8,128)S(1)} %get-tuple-element.81.tail, f32[256,512]{1,0:T(8,128)S(1)} %get-tuple-element.95.inner, ...), custom_call_target="tpu_custom_call" | custom-call | flops 805306368 | bytes 9183232 | tf_op jit(solution)/shard_map/pallas_call | solution.py:375
  (34 shorter events, 0.1 us)
Async XLA Ops:
  0.6 10.7 %copy-start.9 = (f32[512,256]{1,0:T(8,128)S(1)}, f32[512,256]{1,0:T(8,128)}, u32[]{:S(2)}) copy-start(f32[512,256]{1,0:T(8,128)} %refs_0_.3) | copy-start | bytes 1572868
  0.6 10.7 %copy-start.10 = (f32[512,256]{1,0:T(8,128)S(1)}, f32[512,256]{1,0:T(8,128)}, u32[]{:S(2)}) copy-start(f32[512,256]{1,0:T(8,128)} %refs_1_.3) | copy-start | bytes 1572868
  0.7 10.7 %copy-start.11 = (f32[256,512]{1,0:T(8,128)S(1)}, f32[256,512]{1,0:T(8,128)}, u32[]{:S(2)}) copy-start(f32[256,512]{1,0:T(8,128)} %refs_2_.4) | copy-start | bytes 1572868
  0.7 10.7 %copy-start.15 = (f32[256]{0:T(256)S(1)}, f32[256]{0:T(256)}, u32[]{:S(2)}) copy-start(f32[256]{0:T(256)} %param.44) | copy-start | bytes 3076
  0.7 10.7 %copy-start.16 = (f32[256]{0:T(256)S(1)}, f32[256]{0:T(256)}, u32[]{:S(2)}) copy-start(f32[256]{0:T(256)} %param.49) | copy-start | bytes 3076
  0.7 10.7 %copy-start.18 = (f32[512]{0:T(512)S(1)}, f32[512]{0:T(512)}, u32[]{:S(2)}) copy-start(f32[512]{0:T(512)} %param.36) | copy-start | bytes 6148
  0.7 10.7 %copy-start.19 = (f32[512]{0:T(512)S(1)}, f32[512]{0:T(512)}, u32[]{:S(2)}) copy-start(f32[512]{0:T(512)} %param.41) | copy-start | bytes 6148
  0.7 10.7 %copy-start.20 = (f32[512]{0:T(512)S(1)}, f32[512]{0:T(512)}, u32[]{:S(2)}) copy-start(f32[512]{0:T(512)} %param.46) | copy-start | bytes 6148
  0.7 10.7 %copy-start.21 = (f32[512]{0:T(512)S(1)}, f32[512]{0:T(512)}, u32[]{:S(2)}) copy-start(f32[512]{0:T(512)} %param.51) | copy-start | bytes 6148
  0.7 10.7 %copy-start.22 = (f32[256]{0:T(256)S(1)}, f32[256]{0:T(256)}, u32[]{:S(2)}) copy-start(f32[256]{0:T(256)} %param.39) | copy-start | bytes 3076
  3.0 15.3 %copy-start.23 = (f32[392,256]{1,0:T(8,128)S(1)}, f32[392,256]{1,0:T(8,128)}, u32[]{:S(2)}) copy-start(f32[392,256]{1,0:T(8,128)} %get-tuple-element.62) | copy-start | bytes 1204228
  3.0 18.6 %copy-start.12 = (f32[64,512]{1,0:T(8,128)S(1)}, f32[64,512]{1,0:T(8,128)}, u32[]{:S(2)}) copy-start(f32[64,512]{1,0:T(8,128)} %refs_2_.5) | copy-start | bytes 393220
  3.0 17.1 %collective-permute-start.4 = (f32[392,256]{1,0:T(8,128)}, f32[392,256]{1,0:T(8,128)S(1)}, u32[]{:S(2)}, u32[]{:S(2)}) collective-permute-start(f32[392,256]{1,0:T(8,128)} %get-tuple-element.60), channel_id=1, source_target_pairs={{0,2},{2,0},{1,3},{3,1},{4,6},{6,4},{5,7},{7,5},{8,10},{10,8},{9,1... | collective-permute-start | bytes 1204232 | tf_op jit(solution)/shard_map/ppermute | solution.py:392
  6.0 21.7 %copy-start.14 = (s32[512,6]{0,1:T(8,128)S(1)}, s32[512,6]{0,1:T(8,128)}, u32[]{:S(2)}) copy-start(s32[512,6]{0,1:T(8,128)} %param.30) | copy-start | bytes 36868
  6.0 21.7 %copy-start.17 = (s32[64,6]{0,1:T(8,128)S(1)}, s32[64,6]{0,1:T(8,128)}, u32[]{:S(2)}) copy-start(s32[64,6]{0,1:T(8,128)} %param.31) | copy-start | bytes 4612
  11.2 7.1 %collective-permute-start = (f32[64,512]{1,0:T(8,128)}, f32[64,512]{1,0:T(8,128)S(1)}, u32[]{:S(2)}, u32[]{:S(2)}) collective-permute-start(f32[64,512]{1,0:T(8,128)} %shard_map.257.refs_10_.refs_0_), channel_id=1, source_target_pairs={{0,2},{2,0},{1,3},{3,1},{4,6},{6,4},{5,7},{7,5},{8,10},{10,8},{9,1... | collective-permute-start | bytes 393224 | tf_op jit(solution)/shard_map/ppermute | solution.py:392
  11.4 0.9 %copy-start.7 = (f32[64,512]{1,0:T(8,128)S(1)}, f32[64,512]{1,0:T(8,128)}, u32[]{:S(2)}) copy-start(f32[64,512]{1,0:T(8,128)} %shard_map.257.refs_10_.refs_0_) | copy-start | bytes 393220
  18.3 14.5 %collective-permute-start.6 = (f32[392,256]{1,0:T(8,128)S(1)}, f32[392,256]{1,0:T(8,128)S(1)}, u32[]{:S(2)}, u32[]{:S(2)}) collective-permute-start(f32[392,256]{1,0:T(8,128)S(1)} %copy-done.23), channel_id=1, source_target_pairs={{0,2},{2,0},{1,3},{3,1},{4,6},{6,4},{5,7},{7,5},{8,10},{10,8},{9,1... | collective-permute-start | bytes 1204232 | tf_op jit(solution)/shard_map/ppermute | solution.py:392
  20.1 12.7 %collective-permute-start.5 = (f32[392,256]{1,0:T(8,128)S(1)}, f32[392,256]{1,0:T(8,128)S(1)}, u32[]{:S(2)}, u32[]{:S(2)}) collective-permute-start(f32[392,256]{1,0:T(8,128)S(1)} %collective-permute-done.4.refs_12_.refs_5_), channel_id=1, source_target_pairs={{0,16},{16,0},{1,17},{17,1},{2,18},{18,2},{3,19},{19,3},{4,20},{20... | collective-permute-start | bytes 1204232 | tf_op jit(solution)/shard_map/ppermute | solution.py:392
  21.6 0.9 %copy-start.8 = (f32[64,512]{1,0:T(8,128)S(1)}, f32[64,512]{1,0:T(8,128)}, u32[]{:S(2)}) copy-start(f32[64,512]{1,0:T(8,128)} %shard_map.257.refs_10_.refs_0_) | copy-start | bytes 393220
  22.5 15.5 %copy-start = (f32[512,512]{1,0:T(8,128)S(1)}, f32[512,512]{1,0:T(8,128)}, u32[]{:S(2)}) copy-start(f32[512,512]{1,0:T(8,128)} %nodes.1) | copy-start | bytes 3145732
  22.5 15.5 %copy-start.1 = (f32[512,256]{1,0:T(8,128)S(1)}, f32[512,256]{1,0:T(8,128)}, u32[]{:S(2)}) copy-start(f32[512,256]{1,0:T(8,128)} %refs_1_.5) | copy-start | bytes 1572868
  22.5 15.5 %copy-start.2 = (f32[512,256]{1,0:T(8,128)S(1)}, f32[512,256]{1,0:T(8,128)}, u32[]{:S(2)}) copy-start(f32[512,256]{1,0:T(8,128)} %refs_2_.7) | copy-start | bytes 1572868
  22.5 15.5 %copy-start.3 = (f32[256,512]{1,0:T(8,128)S(1)}, f32[256,512]{1,0:T(8,128)}, u32[]{:S(2)}) copy-start(f32[256,512]{1,0:T(8,128)} %refs_4_.4) | copy-start | bytes 1572868
  23.1 5.8 %collective-permute-start.3 = (f32[64,256]{1,0:T(8,128)S(1)}, f32[64,256]{1,0:T(8,128)S(1)}, u32[]{:S(2)}, u32[]{:S(2)}) collective-permute-start(f32[64,256]{1,0:T(8,128)S(1)} %get-tuple-element.57.refs_2_.refs_0_), channel_id=1, source_target_pairs={{0,12},{4,0},{8,4},{12,8},{1,13},{5,1},{9,5},{13,9},{2,14},{6,2},{... | collective-permute-start | bytes 196616 | tf_op jit(solution)/shard_map/ppermute | solution.py:392
  26.7 5.2 %collective-permute-start.2 = (f32[64,256]{1,0:T(8,128)S(1)}, f32[64,256]{1,0:T(8,128)S(1)}, u32[]{:S(2)}, u32[]{:S(2)}) collective-permute-start(f32[64,256]{1,0:T(8,128)S(1)} %get-tuple-element.57.refs_2_.refs_0_), channel_id=1, source_target_pairs={{0,8},{4,12},{8,0},{12,4},{1,9},{5,13},{9,1},{13,5},{2,10},{6,14},... | collective-permute-start | bytes 196616 | tf_op jit(solution)/shard_map/ppermute | solution.py:392
  26.7 6.1 %collective-permute-start.1 = (f32[64,256]{1,0:T(8,128)S(1)}, f32[64,256]{1,0:T(8,128)S(1)}, u32[]{:S(2)}, u32[]{:S(2)}) collective-permute-start(f32[64,256]{1,0:T(8,128)S(1)} %get-tuple-element.57.refs_2_.refs_0_), channel_id=1, source_target_pairs={{0,4},{4,8},{8,12},{12,0},{1,5},{5,9},{9,13},{13,1},{2,6},{6,10},{... | collective-permute-start | bytes 196616 | tf_op jit(solution)/shard_map/ppermute | solution.py:392
  32.8 3.8 %collective-permute-start.11 = (f32[392,256]{1,0:T(8,128)S(1)}, f32[392,256]{1,0:T(8,128)S(1)}, u32[]{:S(2)}, u32[]{:S(2)}) collective-permute-start(f32[392,256]{1,0:T(8,128)S(1)} %collective-permute-done.4.refs_12_.refs_5_), channel_id=1, source_target_pairs={{0,1},{1,0},{2,3},{3,2},{4,5},{5,4},{6,7},{7,6},{8,9},{9,8},{10,11... | collective-permute-start | bytes 1204232 | tf_op jit(solution)/shard_map/ppermute | solution.py:392
  32.8 3.8 %collective-permute-start.12 = (f32[392,256]{1,0:T(8,128)S(1)}, f32[392,256]{1,0:T(8,128)S(1)}, u32[]{:S(2)}, u32[]{:S(2)}) collective-permute-start(f32[392,256]{1,0:T(8,128)S(1)} %collective-permute-done.5.refs_14_.refs_7_), channel_id=1, source_target_pairs={{0,1},{1,0},{2,3},{3,2},{4,5},{5,4},{6,7},{7,6},{8,9},{9,8},{10,11... | collective-permute-start | bytes 1204232 | tf_op jit(solution)/shard_map/ppermute | solution.py:392
  33.3 11.3 %collective-permute-start.14 = (f32[392,256]{1,0:T(8,128)S(1)}, f32[392,256]{1,0:T(8,128)S(1)}, u32[]{:S(2)}, u32[]{:S(2)}) collective-permute-start(f32[392,256]{1,0:T(8,128)S(1)} %collective-permute-done.6.refs_0_), channel_id=1, source_target_pairs={{0,16},{16,0},{1,17},{17,1},{2,18},{18,2},{3,19},{19,3},{4,20},{20... | collective-permute-start | bytes 1204232 | tf_op jit(solution)/shard_map/ppermute | solution.py:392
  33.8 1.4 %collective-permute-start.7 = (f32[64,256]{1,0:T(8,128)S(1)}, f32[64,256]{1,0:T(8,128)S(1)}, u32[]{:S(2)}, u32[]{:S(2)}) collective-permute-start(f32[64,256]{1,0:T(8,128)S(1)} %get-tuple-element.57.refs_2_.refs_0_), channel_id=1, source_target_pairs={{0,1},{1,0},{2,3},{3,2},{4,5},{5,4},{6,7},{7,6},{8,9},{9,8},{10,11... | collective-permute-start | bytes 196616 | tf_op jit(solution)/shard_map/ppermute | solution.py:392
  33.8 1.5 %collective-permute-start.8 = (f32[64,256]{1,0:T(8,128)S(1)}, f32[64,256]{1,0:T(8,128)S(1)}, u32[]{:S(2)}, u32[]{:S(2)}) collective-permute-start(f32[64,256]{1,0:T(8,128)S(1)} %collective-permute-done.1.refs_1_), channel_id=1, source_target_pairs={{0,1},{1,0},{2,3},{3,2},{4,5},{5,4},{6,7},{7,6},{8,9},{9,8},{10,11... | collective-permute-start | bytes 196616 | tf_op jit(solution)/shard_map/ppermute | solution.py:392
  35.2 1.3 %collective-permute-start.9 = (f32[64,256]{1,0:T(8,128)S(1)}, f32[64,256]{1,0:T(8,128)S(1)}, u32[]{:S(2)}, u32[]{:S(2)}) collective-permute-start(f32[64,256]{1,0:T(8,128)S(1)} %collective-permute-done.2.refs_2_), channel_id=1, source_target_pairs={{0,1},{1,0},{2,3},{3,2},{4,5},{5,4},{6,7},{7,6},{8,9},{9,8},{10,11... | collective-permute-start | bytes 196616 | tf_op jit(solution)/shard_map/ppermute | solution.py:392
  35.3 1.3 %collective-permute-start.10 = (f32[64,256]{1,0:T(8,128)S(1)}, f32[64,256]{1,0:T(8,128)S(1)}, u32[]{:S(2)}, u32[]{:S(2)}) collective-permute-start(f32[64,256]{1,0:T(8,128)S(1)} %collective-permute-done.3.refs_3_), channel_id=1, source_target_pairs={{0,1},{1,0},{2,3},{3,2},{4,5},{5,4},{6,7},{7,6},{8,9},{9,8},{10,11... | collective-permute-start | bytes 196616 | tf_op jit(solution)/shard_map/ppermute | solution.py:392
  37.4 7.2 %copy-start.13 = (s32[512,3]{0,1:T(4,128)S(1)}, s32[512,3]{0,1:T(4,128)}, u32[]{:S(2)}) copy-start(s32[512,3]{0,1:T(4,128)} %param.29) | copy-start | bytes 18436
  37.4 7.2 %collective-permute-start.13 = (f32[64,512]{1,0:T(8,128)S(1)}, f32[64,512]{1,0:T(8,128)S(1)}, u32[]{:S(2)}, u32[]{:S(2)}) collective-permute-start(f32[64,512]{1,0:T(8,128)S(1)} %shard_map.262.refs_9_.refs_0_), channel_id=1, source_target_pairs={{0,2},{2,0},{1,3},{3,1},{4,6},{6,4},{5,7},{7,5},{8,10},{10,8},{9,1... | collective-permute-start | bytes 393224 | tf_op jit(solution)/shard_map/ppermute | solution.py:392
  46.7 2.6 %copy-start.4 = (f32[512,256]{1,0:T(8,128)S(1)}, f32[512,256]{1,0:T(8,128)}, u32[]{:S(2)}) copy-start(f32[512,256]{1,0:T(8,128)} %ws.1) | copy-start | bytes 1572868
  46.7 2.6 %copy-start.5 = (f32[512,256]{1,0:T(8,128)S(1)}, f32[512,256]{1,0:T(8,128)}, u32[]{:S(2)}) copy-start(f32[512,256]{1,0:T(8,128)} %wr.1) | copy-start | bytes 1572868
  46.7 2.7 %copy-start.6 = (f32[256,512]{1,0:T(8,128)S(1)}, f32[256,512]{1,0:T(8,128)}, u32[]{:S(2)}) copy-start(f32[256,512]{1,0:T(8,128)} %wo.1) | copy-start | bytes 1572868
  46.7 2.6 %collective-permute-start.17 = (f32[392,256]{1,0:T(8,128)S(1)}, f32[392,256]{1,0:T(8,128)S(1)}, u32[]{:S(2)}, u32[]{:S(2)}) collective-permute-start(f32[392,256]{1,0:T(8,128)S(1)} %collective-permute-done.6.refs_0_), channel_id=1, source_target_pairs={{0,1},{1,0},{2,3},{3,2},{4,5},{5,4},{6,7},{7,6},{8,9},{9,8},{10,11... | collective-permute-start | bytes 1204232 | tf_op jit(solution)/shard_map/ppermute | solution.py:392
  46.7 2.6 %collective-permute-start.18 = (f32[392,256]{1,0:T(8,128)S(1)}, f32[392,256]{1,0:T(8,128)S(1)}, u32[]{:S(2)}, u32[]{:S(2)}) collective-permute-start(f32[392,256]{1,0:T(8,128)S(1)} %collective-permute-done.14.refs_2_), channel_id=1, source_target_pairs={{0,1},{1,0},{2,3},{3,2},{4,5},{5,4},{6,7},{7,6},{8,9},{9,8},{10,11... | collective-permute-start | bytes 1204232 | tf_op jit(solution)/shard_map/ppermute | solution.py:392
  47.2 9.4 %collective-permute-start.16 = (f32[128,512]{1,0:T(8,128)S(1)}, f32[128,512]{1,0:T(8,128)S(1)}, u32[]{:S(2)}, u32[]{:S(2)}) collective-permute-start(f32[128,512]{1,0:T(8,128)S(1)} %get-tuple-element.82.head), channel_id=1, source_target_pairs={{0,13},{1,0},{4,1},{5,4},{8,5},{9,8},{12,9},{13,12},{2,15},{3,2},{... | collective-permute-start | bytes 786440 | tf_op jit(solution)/shard_map/ppermute | solution.py:392
  47.9 8.7 %collective-permute-start.15 = (f32[128,512]{1,0:T(8,128)S(1)}, f32[128,512]{1,0:T(8,128)S(1)}, u32[]{:S(2)}, u32[]{:S(2)}) collective-permute-start(f32[128,512]{1,0:T(8,128)S(1)} %get-tuple-element.81.tail), channel_id=1, source_target_pairs={{0,1},{1,4},{4,5},{5,8},{8,9},{9,12},{12,13},{13,0},{2,3},{3,6},{6... | collective-permute-start | bytes 786440 | tf_op jit(solution)/shard_map/ppermute | solution.py:392

commit v6 on v5

--- a/solution.py
+++ b/solution.py
@@ -11,7 +11,7 @@
 f32 = jnp.float32
 bf16 = jnp.bfloat16
 limit_bytes = 12 * 1024 * 1024
-tight_limit = 60 * 1024 * 1024
+tight_limit = 64 * 1000 * 1000
 most_direct = 4
 
 
@@ -87,7 +87,7 @@
 
 
 def upward_kernel(nodes_hbm, coarse_hbm, ws_hbm, wr_hbm, wo_hbm, children, bias, part, nodes, coarse, ws, wr, wo, high, low, sems):
-    cuts = 4
+    cuts = 8
     moves = started(
         strips(ws_hbm, ws, cuts)
         + strips(nodes_hbm, nodes, cuts)
@@ -117,34 +117,28 @@
     part[...] = dot3(hidden, *split(wo[...]))
 
 
-def coarse_ready_kernel(ws, wr, wo, *refs):
-    params, (ws_high, ws_low, wr_high, wr_low, wo_high, wo_low, gains, biases) = refs[:7], refs[7:]
+def share_kernel(*refs):
+    params, down_own, bottom_own, refs = refs[:7], refs[7:11], refs[11:15], refs[15:]
+    gains, biases, down_pack, bottom_pack, sems = refs
+    moves = started(
+        share_copies(down_own, down_pack, "parts") + share_copies(bottom_own, bottom_pack, "patch"), sems
+    )
     for i in range(4):
         gains[i : i + 1] = params[i][...]
     for i in range(3):
         biases[i : i + 1] = params[4 + i][...]
-    ws_high[...], ws_low[...] = split(ws[...])
-    wr_high[...], wr_low[...] = split(wr[...])
-    wo_high[...], wo_low[...] = split(wo[...])
-
-
-def share_kernel(parts, *refs):
-    down_own, bottom_own, (down_pack, bottom_pack, sems) = refs[:4], refs[4:8], refs[8:]
-    copies = share_copies(down_own, down_pack, parts) + share_copies(bottom_own, bottom_pack, parts)
-    for move in started(copies, sems):
+    for move in moves:
         move.wait()
 
 
-def shares(parts):
+def shares(axis):
     lvls = lax.axis_size("lvl")
-    mine = lax.axis_index("lvl")
-    if parts > 1:
-        mine = lax.axis_index("parts") * lvls + mine
-    return mine, parts * lvls
-
-
-def share_copies(sources, pack, parts):
-    mine, count = shares(parts)
+    place, count = partners(axis)
+    return place * lvls + lax.axis_index("lvl"), count * lvls
+
+
+def share_copies(sources, pack, axis):
+    mine, count = shares(axis)
     width = pack.shape[1]
     copies, at = [], 0
     for source in sources:
@@ -182,58 +176,52 @@
 
 def coarse_project_kernel(count, *refs):
     parts, refs = refs[:count], refs[count:]
-    coarse, gains, biases, ws_high, ws_low, wr_high, wr_low, updated, senders, receivers = refs
+    coarse, gains, biases, ws, wr, updated, senders, receivers = refs
     rows = coarse[...] + gains[0:1] * normed(added(parts))
     updated[...] = rows
-    senders[...] = 0.5 * dot3(rows, ws_high[...], ws_low[...])
-    receivers[...] = 0.5 * (dot3(rows, wr_high[...], wr_low[...]) + biases[0:1])
+    senders[...] = 0.5 * dot3(rows, *split(ws[...]))
+    receivers[...] = 0.5 * (dot3(rows, *split(wr[...])) + biases[0:1])
 
 
 def coarse_kernel(count, *refs):
-    pieces, (all_picks, receivers, wo_high, wo_low) = refs[:count], refs[count : count + 4]
+    pieces, (all_picks, receivers, wo) = refs[:count], refs[count : count + 3]
     part = refs[-1]
     senders = jnp.concatenate([piece[...] for piece in pieces], axis=0)
     sender_high, sender_low = split(senders)
     picks = all_picks[...]
     picked = dot(picks, sender_high) + dot(picks, sender_low)
     hidden = silu_sum(picked, receivers[...], picks.shape[0] // receivers.shape[0])
-    part[...] = dot3(hidden, wo_high[...], wo_low[...])
-
-
-def shared_among(packs):
-    return max(1, len(packs) // max(1, lax.axis_size("sub") - 1))
-
-
-def fetched_shares(packs):
+    part[...] = dot3(hidden, *split(wo[...]))
+
+
+def fetched_shares(packs, axis):
     subs, lvls = lax.axis_size("sub"), lax.axis_size("lvl")
-    parts = len(packs) // max(1, (subs - 1) * lvls)
-    sub, part, lvl = lax.axis_index("sub"), lax.axis_index("parts"), lax.axis_index("lvl")
-    place = iter(packs)
+    sub, lvl = lax.axis_index("sub"), lax.axis_index("lvl")
+    place, count = partners(axis)
+    left = iter(packs)
     for s in range(1, subs):
-        for p in range(parts):
+        for p in range(count):
             for t in range(lvls):
-                mine = lax.rem(part + parts - p, parts) * lvls + lax.rem(lvl + lvls - t, lvls)
-                yield next(place), lax.rem(sub + subs - s, subs), mine, p == 0 and t == 0
-
-
-def collect_in(own, packs, at, high, low):
+                mine = lax.rem(place + count - p, count) * lvls + lax.rem(lvl + lvls - t, lvls)
+                yield next(left), lax.rem(sub + subs - s, subs), mine, p == 0 and t == 0
+
+
+def collect_in(own, packs, axis, at, high, low):
     sub = lax.axis_index("sub")
-    count = shared_among(packs)
     high[sub], low[sub] = split(own[...])
-    share = own.shape[0] // count
-    for pack, block, mine, _ in fetched_shares(packs):
+    share = own.shape[0] // shares(axis)[1]
+    for pack, block, mine, _ in fetched_shares(packs, axis):
         rows = pl.ds(pl.multiple_of(mine * share, share), share)
         high[block, rows, :], low[block, rows, :] = split(pack[at : at + share, :])
 
 
-def collect_out(own, packs, at, high, low):
+def collect_out(own, packs, axis, at, high, low):
     sub = lax.axis_index("sub")
-    count = shared_among(packs)
     width, latent = own.shape
     rows = pl.ds(pl.multiple_of(sub * width, width), width)
     high[rows, :], low[rows, :] = split(own[...])
-    thin = width // count
-    for pack, block, mine, _ in fetched_shares(packs):
+    thin = width // shares(axis)[1]
+    for pack, block, mine, _ in fetched_shares(packs, axis):
         rows = pl.ds(pl.multiple_of(block * width + mine * thin, thin), thin)
         for j in range(latent // width):
             first, second = split(pack[at + j * thin : at + (j + 1) * thin, :])
@@ -241,9 +229,9 @@
             low[rows, j * width : (j + 1) * width] = second
 
 
-def collect_bias(own, packs, at, out):
+def collect_bias(own, packs, axis, at, out):
     out[lax.axis_index("sub")] = jnp.broadcast_to(own, (8, own.shape[1]))
-    for pack, block, _, whole_row in fetched_shares(packs):
+    for pack, block, _, whole_row in fetched_shares(packs, axis):
         if whole_row:
             out[block] = jnp.broadcast_to(pack[at : at + 1, :], (8, own.shape[1]))
 
@@ -252,11 +240,11 @@
     packs, refs = refs[:count], refs[count:]
     receivers, ws_high, ws_low, wo_high, wo_low, wr_high, wr_low, bias_all = refs
     width = ws.shape[1]
-    share = ws.shape[0] // shared_among(packs)
-    collect_in(ws, packs, 0, ws_high, ws_low)
-    collect_in(wr, packs, share, wr_high, wr_low)
-    collect_out(wo, packs, 2 * share, wo_high, wo_low)
-    collect_bias(biases[1:2], packs, 3 * share, bias_all)
+    share = ws.shape[0] // shares("parts")[1]
+    collect_in(ws, packs, "parts", 0, ws_high, ws_low)
+    collect_in(wr, packs, "parts", share, wr_high, wr_low)
+    collect_out(wo, packs, "parts", 2 * share, wo_high, wo_low)
+    collect_bias(biases[1:2], packs, "parts", 3 * share, bias_all)
     for g in range(wr_high.shape[0]):
         product = dot3(nodes[...], wr_high[g], wr_low[g])
         receivers[:, g * width : (g + 1) * width] = 0.5 * (product + bias_all[g][0:1])
@@ -264,11 +252,11 @@
 
 def bottom_weights_kernel(count, ws, wr, biases, wo, *refs):
     packs, (ws_high, ws_low, wr_high, wr_low, wo_high, wo_low, bias_all) = refs[:count], refs[count:]
-    share = ws.shape[0] // shared_among(packs)
-    collect_in(ws, packs, 0, ws_high, ws_low)
-    collect_in(wr, packs, share, wr_high, wr_low)
-    collect_out(wo, packs, 2 * share, wo_high, wo_low)
-    collect_bias(biases[2:3], packs, 3 * share, bias_all)
+    share = ws.shape[0] // shares("patch")[1]
+    collect_in(ws, packs, "patch", 0, ws_high, ws_low)
+    collect_in(wr, packs, "patch", share, wr_high, wr_low)
+    collect_out(wo, packs, "patch", 2 * share, wo_high, wo_low)
+    collect_bias(biases[2:3], packs, "patch", 3 * share, bias_all)
 
 
 def down_rows(nodes, receivers, sources, senders, wo_high, wo_low, gain):
@@ -417,9 +405,21 @@
     return [shifted(pack, "sub", s) for s in range(1, lax.axis_size("sub"))]
 
 
-def over_parts(shares):
+def partners(axis):
+    if axis == "parts":
+        return lax.axis_index(axis), lax.axis_size(axis)
+    count = 2 if lax.axis_size(axis) % 2 == 0 else 1
+    return lax.rem(lax.axis_index(axis), count), count
+
+
+def over_partners(share_list, axis):
+    size, count = lax.axis_size(axis), partners(axis)[1]
     return [
-        [shifted(share, "parts", p) for p in range(1, lax.axis_size("parts"))] for share in shares
+        [
+            lax.ppermute(share, axis, [(i, i - i % count + (i + p) % count) for i in range(size)])
+            for p in range(1, count)
+        ]
+        for share in share_list
     ]
 
 
@@ -475,23 +475,12 @@
     bias_rows = like((subs, 8, width))
 
     columns = latent // width
-    ensemble, lvls = lax.axis_size("parts"), lax.axis_size("lvl")
-    share = latent // (ensemble * lvls)
-    pack = like((3 * share + 8, width))
-
-    down_pack, bottom_pack = call(
-        functools.partial(share_kernel, ensemble),
-        [pack, pack],
-        [
-            downward_sender, downward_receiver, downward_output, downward_bias[None],
-            bottom_sender, bottom_receiver, bottom_output, bottom_bias[None],
-        ],
-        latent,
-        [pltpu.SemaphoreType.DMA((6 + 2 * columns,))],
-        far=range(8),
-        limit=tight_limit,
-    )
-    down_near = over_sub(down_pack)
+    lvls = lax.axis_size("lvl")
+
+    def pack(axis):
+        count = shares(axis)[1]
+        return like((2 * latent // count + width // count * columns + 8, width))
+
     (part,) = call(
         upward_kernel,
         [like((blocks, latent))],
@@ -508,31 +497,33 @@
             pltpu.VMEM((width, latent), f32),
             pltpu.VMEM((rows, width), bf16),
             pltpu.VMEM((rows, width), bf16),
-            pltpu.SemaphoreType.DMA((17,)),
+            pltpu.SemaphoreType.DMA((33,)),
         ],
         far=range(5),
         limit=tight_limit,
     )
     parts = sub_parts(part)
-    ws_high, ws_low, wr_high, wr_low, wo_high, wo_low, gains, biases = call(
-        coarse_ready_kernel,
-        [like((latent, width), bf16)] * 4
-        + [like((width, latent), bf16)] * 2
-        + [like((4, latent)), like((3, width))],
+    down_own = (downward_sender, downward_receiver, downward_output, downward_bias[None])
+    bottom_own = (bottom_sender, bottom_receiver, bottom_output, bottom_bias[None])
+    gains, biases, down_pack, bottom_pack = call(
+        share_kernel,
+        [like((4, latent)), like((3, width)), pack("parts"), pack("patch")],
         [
-            coarse_sender, coarse_receiver, coarse_output,
             upward_gain[None], coarse_gain[None], downward_gain[None], bottom_gain[None],
-            coarse_bias[None], downward_bias[None], bottom_bias[None], part,
+            coarse_bias[None], downward_bias[None], bottom_bias[None],
+            *down_own, *bottom_own, part,
         ],
         latent * hidden,
+        [pltpu.SemaphoreType.DMA((6 + 2 * columns,))],
+        far=range(7, 15),
         unread=1,
-    )
-    bottom_near = over_sub(held(bottom_pack, (parts[-1], gains)))
-    down_far = over_parts(down_near)
+        limit=tight_limit,
+    )
+    down_near, bottom_near = map(over_sub, held((down_pack, bottom_pack), parts[-1]))
     coarse_up, senders, receivers = call(
         functools.partial(coarse_project_kernel, len(parts)),
         [like((blocks, latent)), like((blocks, width)), like((blocks, width))],
-        [*parts, coarse_states, gains, biases, ws_high, ws_low, wr_high, wr_low],
+        [*parts, coarse_states, gains, biases, coarse_sender, coarse_receiver],
         12 * blocks * latent * width,
     )
     patches = lax.axis_size("patch")
@@ -544,28 +535,29 @@
         coarse_links.size * names,
         unread=1,
     )
-    pieces, (picks, bottom_picks, down_near, down_far, bottom_near) = coarse_pieces(
-        senders, (picks, bottom_picks, down_near, down_far, bottom_near)
-    )
-    down_packs = all_shares(down_near, down_far)
-    bottom_far = over_parts(bottom_near)
+    pieces, (picks, bottom_picks, down_near) = coarse_pieces(
+        senders, (picks, bottom_picks, down_near)
+    )
+    down_far = over_partners(down_near, "parts")
     (part,) = call(
         functools.partial(coarse_kernel, len(pieces)),
         [like((blocks, latent))],
-        [*pieces, picks, receivers, wo_high, wo_low, *down_packs],
+        [*pieces, picks, receivers, coarse_output, *bottom_near],
         4 * coarse_links.size * names * width,
-        unread=len(down_packs),
-    )
+        unread=len(bottom_near),
+    )
+    bottom_near = held(bottom_near, part)
     parts = sub_parts(part)
+    bottom_far = over_partners(bottom_near, "patch")
+    down_packs = all_shares(*held((down_near, down_far), parts[-1]))
     receivers, ws_high, ws_low, wo_high, wo_low = call(
         functools.partial(down_weights_kernel, len(down_packs)),
         [like((rows, hidden)), *weights, *outputs],
-        [node_states, downward_sender, downward_receiver, biases, downward_output, *down_packs, part],
+        [node_states, downward_sender, downward_receiver, biases, downward_output, *down_packs, part, *(x for row in bottom_far for x in row)],
         6 * rows * latent * hidden,
         [pltpu.VMEM((subs, latent, width), bf16)] * 2 + [pltpu.VMEM((subs, 8, width), f32)],
-        unread=1,
-    )
-    parts, bottom_far = lax.optimization_barrier((parts, bottom_far))
+        unread=1 + sum(map(len, bottom_far)),
+    )
     new_coarse, senders, head, tail = call(
         functools.partial(down_edge_kernel, len(parts), rim),
         [like((blocks, latent)), like((2 * blocks, hidden), bf16), like((rim, latent)), like((rim, latent))],

time: 61.2 us -> 64.3 us (1.051)
  starting transfers between devices: 15 us -> 18.6 us
  waiting for transfers between devices: 18.8 us -> 16.8 us
  Pallas kernels: 24.3 us -> 26.2 us
    ppermute x19 -> x17, waiting for transfers between devices: 18.8 us -> 11.1 us  [shifted(): lax.ppermute(values, axis, [(i, (i + step) % count) for i in range(count)])]
    ppermute x0 -> x2, waiting for transfers between devices: none -> 5.78 us  [over_partners(): lax.ppermute(share, axis, [(i, i - i % count + (i + p) % count) for i in...]
    ppermute x0 -> x2, starting transfers between devices: none -> 3.1 us  [over_partners(): lax.ppermute(share, axis, [(i, i - i % count + (i + p) % count) for i in...]
    pallas_call x12 -> x11, Pallas kernels: 24.3 us -> 26.2 us  [call(): pl.pallas_call((lambda *refs: kernel(*refs[:read], *refs[read + unread:])...]
    ppermute x19 -> x17, starting transfers between devices: 15 us -> 15.5 us  [shifted(): lax.ppermute(values, axis, [(i, (i + step) % count) for i in range(count)])]
    unnamed x48 -> x38, local copies, waits for them, and re-layouts: 1.9 us -> 1.46 us
  transfers between devices with their start and end apart: 19 -> 19, of which waited for: 8 -> 8; matrix products, arithmetic and copies ran while one was open for 0% -> 0% of each run, Pallas kernels for 26% -> 18%
where the time goes in v6:
time: 64.3 us; the launch traced here: 64 us
  Pallas kernels  26.2 us (41%)
  starting transfers between devices  18.6 us (29%)
  waiting for transfers between devices  16.8 us (26%)
  local copies, waits for them, and re-layouts  1.46 us (2%)
  between operations  0.92 us (1%)
    pallas_call x11, Pallas kernels, call(): pl.pallas_call((lambda *refs: kernel(*refs[:read], *refs[read + unread:])...  26.2 us
    ppermute x17, starting transfers between devices, shifted(): lax.ppermute(values, axis, [(i, (i + step) % count) for i in range(count)])  15.5 us
    ppermute x17, waiting for transfers between devices, shifted(): lax.ppermute(values, axis, [(i, (i + step) % count) for i in range(count)])  11.1 us
    ppermute x2, waiting for transfers between devices, over_partners(): lax.ppermute(share, axis, [(i, i - i % count + (i + p) % count) for i in...  5.78 us
    ppermute x2, starting transfers between devices, over_partners(): lax.ppermute(share, axis, [(i, i - i % count + (i + p) % count) for i in...  3.1 us
    unnamed x38, local copies, waits for them, and re-layouts  1.46 us
  transfers between devices with their start and end apart: 19, of which 8 were waited for; matrix products, arithmetic and copies ran while one was open for 0% of the time, Pallas kernels for 18%

profile of v6, /device:TPU:0, one launch (start us, length us, event | category | flops | bytes accessed | tf_op | source)
XLA Modules:
  0.0 64.0 jit_solution(4129308913338359514)
XLA Ops:
  0.6 6.6 %shard_map.257.refs_15_.refs_0_ = f32[64,512]{1,0:T(8,128)} custom-call(f32[512,512]{1,0:T(8,128)} %nodes.1, f32[64,512]{1,0:T(8,128)} %refs_2_.2, f32[512,256]{1,0:T(8,128)} %ws_hbm.1, f32[512,256]{1,0:T(8,128)} %wr_hbm.1, f32[256,512]{1,0:T(8,128)} %wo_hbm.1, s32[7,64]{1,0:T(8,128)} %bitcast.16, f32[1,256]{1,0:T(1,128)} %bitcast.25), custom_call_target="tpu_custom_call" | custom-call | flops 637534208 | bytes 2886400 | tf_op jit(solution)/shard_map/pallas_call | solution.py:363
  7.3 0.0 copy-start.7
  7.3 0.0 copy-start.8
  7.3 0.0 copy-start.9
  7.3 0.0 copy-start.11
  7.3 3.0 %collective-permute-start = (f32[64,512]{1,0:T(8,128)}, f32[64,512]{1,0:T(8,128)S(1)}, u32[]{:S(2)}, u32[]{:S(2)}) collective-permute-start(f32[64,512]{1,0:T(8,128)} %shard_map.257.refs_15_.refs_0_), channel_id=1, source_target_pairs={{0,2},{2,0},{1,3},{3,1},{4,6},{6,4},{5,7},{7,5},{8,10},{10,8},{9,1... | collective-permute-start | bytes 393224 | tf_op jit(solution)/shard_map/ppermute | solution.py:380
  10.3 3.0 %shard_map.258 = (f32[4,512]{1,0:T(4,128)}, f32[3,256]{1,0:T(4,128)}, f32[392,256]{1,0:T(8,128)}, f32[392,256]{1,0:T(8,128)}) custom-call(f32[1,512]{1,0:T(1,128)} %bitcast.21, f32[1,512]{1,0:T(1,128)} %bitcast.22, f32[1,512]{1,0:T(1,128)} %bitcast.23, f32[1,512]{1,0:T(1,128)} %bitcast.24, f32[1,256]{1,0:T(1,128)} %bitcast.26, f32[1,256]{1,0:T(1,128)} %bitcast.17, ...), custom_call_target="tpu_custom_call" | custom-call | flops 262144 | bytes 4104192 | tf_op jit(solution)/shard_map/pallas_call | solution.py:363
  13.3 0.0 copy-start
  13.3 0.0 copy-start.4
  13.4 0.0 copy-start.5
  13.4 0.0 copy-start.6
  13.4 0.7 %collective-permute-done.refs_1_ = f32[64,512]{1,0:T(8,128)S(1)} collective-permute-done((f32[64,512]{1,0:T(8,128)}, f32[64,512]{1,0:T(8,128)S(1)}, u32[]{:S(2)}, u32[]{:S(2)}) %collective-permute-start) | collective-permute-done | bytes 131104 | tf_op jit(solution)/shard_map/ppermute | solution.py:380
  14.0 1.7 %collective-permute-start.4 = (f32[392,256]{1,0:T(8,128)}, f32[392,256]{1,0:T(8,128)S(1)}, u32[]{:S(2)}, u32[]{:S(2)}) collective-permute-start(f32[392,256]{1,0:T(8,128)} %get-tuple-element.51), channel_id=1, source_target_pairs={{0,2},{2,0},{1,3},{3,1},{4,6},{6,4},{5,7},{7,5},{8,10},{10,8},{9,1... | collective-permute-start | bytes 1204232 | tf_op jit(solution)/shard_map/ppermute | solution.py:380
  15.8 0.3 collective-permute-start.9
  16.1 0.0 copy-done.11
  16.1 0.0 copy-start.12
  16.1 0.7 %copy-done.12 = f32[4,512]{1,0:T(4,128)S(1)} copy-done((f32[4,512]{1,0:T(4,128)S(1)}, f32[4,512]{1,0:T(4,128)}, u32[]{:S(2)}) %copy-start.12) | copy-done | bytes 8216
  16.8 0.7 %copy-done.14 = f32[3,256]{1,0:T(4,128)S(1)} copy-done((f32[3,256]{1,0:T(4,128)S(1)}, f32[3,256]{1,0:T(4,128)}, u32[]{:S(2)}) %copy-start.14) | copy-done | bytes 3096
  17.5 0.6 shard_map.259
  18.1 3.9 %collective-permute-start.3 = (f32[64,256]{1,0:T(8,128)S(1)}, f32[64,256]{1,0:T(8,128)S(1)}, u32[]{:S(2)}, u32[]{:S(2)}) collective-permute-start(f32[64,256]{1,0:T(8,128)S(1)} %get-tuple-element.46.refs_2_.refs_0_), channel_id=1, source_target_pairs={{0,12},{4,0},{8,4},{12,8},{1,13},{5,1},{9,5},{13,9},{2,14},{6,2},{... | collective-permute-start | bytes 196616 | tf_op jit(solution)/shard_map/ppermute | solution.py:380
  22.0 0.0 collective-permute-start.2
  22.0 1.0 %collective-permute-start.1 = (f32[64,256]{1,0:T(8,128)S(1)}, f32[64,256]{1,0:T(8,128)S(1)}, u32[]{:S(2)}, u32[]{:S(2)}) collective-permute-start(f32[64,256]{1,0:T(8,128)S(1)} %get-tuple-element.46.refs_2_.refs_0_), channel_id=1, source_target_pairs={{0,4},{4,8},{8,12},{12,0},{1,5},{5,9},{9,13},{13,1},{2,6},{6,10},{... | collective-permute-start | bytes 196616 | tf_op jit(solution)/shard_map/ppermute | solution.py:380
  23.0 1.1 %shard_map.260 = (bf16[384,512]{1,0:T(8,128)(2,1)S(1)}, bf16[3072,384]{1,0:T(8,128)(2,1)S(1)}) custom-call(s32[6,64]{1,0:T(8,128)S(1)} %bitcast.15, s32[6,512]{1,0:T(8,128)S(1)} %bitcast.14, f32[64,256]{1,0:T(8,128)S(1)} %get-tuple-element.46.refs_2_.refs_0_), custom_call_target="tpu_custom_call" | custom-call | flops 196608 | bytes 2831872 | tf_op jit(solution)/shard_map/pallas_call | solution.py:363
  24.1 0.0 collective-permute-done.3.refs_3_
  24.1 3.1 %collective-permute-done.2.refs_2_ = f32[64,256]{1,0:T(8,128)S(1)} collective-permute-done((f32[64,256]{1,0:T(8,128)S(1)}, f32[64,256]{1,0:T(8,128)S(1)}, u32[]{:S(2)}, u32[]{:S(2)}) %collective-permute-start.2) | collective-permute-done | bytes 65568 | tf_op jit(solution)/shard_map/ppermute | solution.py:380
  27.1 0.9 %collective-permute-done.1.refs_1_ = f32[64,256]{1,0:T(8,128)S(1)} collective-permute-done((f32[64,256]{1,0:T(8,128)S(1)}, f32[64,256]{1,0:T(8,128)S(1)}, u32[]{:S(2)}, u32[]{:S(2)}) %collective-permute-start.1) | collective-permute-done | bytes 65568 | tf_op jit(solution)/shard_map/ppermute | solution.py:380
  28.0 0.0 collective-permute-done.4.refs_5_
  28.0 1.5 %collective-permute-start.11 = (f32[392,256]{1,0:T(8,128)S(1)}, f32[392,256]{1,0:T(8,128)S(1)}, u32[]{:S(2)}, u32[]{:S(2)}) collective-permute-start(f32[392,256]{1,0:T(8,128)S(1)} %collective-permute-done.4.refs_5_), channel_id=1, source_target_pairs={{0,16},{16,0},{1,17},{17,1},{2,18},{18,2},{3,19},{19,3},{4,20},{20... | collective-permute-start | bytes 1204232 | tf_op jit(solution)/shard_map/ppermute | solution.py:419
  29.5 0.0 collective-permute-start.5
  29.6 0.5 collective-permute-start.6
  30.1 0.0 collective-permute-start.7
  30.1 0.7 %collective-permute-done.5.refs_4_ = f32[64,256]{1,0:T(8,128)S(1)} collective-permute-done((f32[64,256]{1,0:T(8,128)S(1)}, f32[64,256]{1,0:T(8,128)S(1)}, u32[]{:S(2)}, u32[]{:S(2)}) %collective-permute-start.5) | collective-permute-done | bytes 65568 | tf_op jit(solution)/shard_map/ppermute | solution.py:380
  30.8 0.2 collective-permute-start.8
  31.0 2.4 %collective-permute-done.9.refs_11_.refs_0_ = f32[392,256]{1,0:T(8,128)S(1)} collective-permute-done((f32[392,256]{1,0:T(8,128)}, f32[392,256]{1,0:T(8,128)S(1)}, u32[]{:S(2)}, u32[]{:S(2)}) %collective-permute-start.9) | collective-permute-done | bytes 401440 | tf_op jit(solution)/shard_map/ppermute | solution.py:380
  33.3 0.0 collective-permute-done.6.refs_5_
  33.3 0.0 collective-permute-done.7.refs_6_
  33.3 0.0 collective-permute-done.8.refs_7_
  33.4 0.8 %shard_map.261.refs_9_.refs_0_ = f32[64,512]{1,0:T(8,128)S(1)} custom-call(f32[64,256]{1,0:T(8,128)S(1)} %get-tuple-element.46.refs_2_.refs_0_, f32[64,256]{1,0:T(8,128)S(1)} %collective-permute-done.1.refs_1_, f32[64,256]{1,0:T(8,128)S(1)} %collective-permute-done.2.refs_2_, f32[64,256]{1,0:T(8,128)S(1)} %collective-permute-done.3.refs_3_, ...), custom_call_target="tpu_custom_call" | custom-call | flops 201326592 | bytes 2039808 | tf_op jit(solution)/shard_map/pallas_call | solution.py:363
  34.2 0.0 copy-start.16
  34.2 1.5 %collective-permute-start.10 = (f32[64,512]{1,0:T(8,128)S(1)}, f32[64,512]{1,0:T(8,128)S(1)}, u32[]{:S(2)}, u32[]{:S(2)}) collective-permute-start(f32[64,512]{1,0:T(8,128)S(1)} %shard_map.261.refs_9_.refs_0_), channel_id=1, source_target_pairs={{0,2},{2,0},{1,3},{3,1},{4,6},{6,4},{5,7},{7,5},{8,10},{10,8},{9,1... | collective-permute-start | bytes 393224 | tf_op jit(solution)/shard_map/ppermute | solution.py:380
  35.6 1.6 %collective-permute-start.14 = (f32[392,256]{1,0:T(8,128)S(1)}, f32[392,256]{1,0:T(8,128)S(1)}, u32[]{:S(2)}, u32[]{:S(2)}) collective-permute-start(f32[392,256]{1,0:T(8,128)S(1)} %collective-permute-done.9.refs_11_.refs_0_), channel_id=1, source_target_pairs={{0,4},{4,0},{8,12},{12,8},{1,5},{5,1},{9,13},{13,9},{2,6},{6,2},{1... | collective-permute-start | bytes 1204232 | tf_op jit(solution)/shard_map/ppermute | solution.py:419
  37.2 2.0 %collective-permute-done.10.refs_1_ = f32[64,512]{1,0:T(8,128)S(1)} collective-permute-done((f32[64,512]{1,0:T(8,128)S(1)}, f32[64,512]{1,0:T(8,128)S(1)}, u32[]{:S(2)}, u32[]{:S(2)}) %collective-permute-start.10) | collective-permute-done | bytes 131104 | tf_op jit(solution)/shard_map/ppermute | solution.py:380
  39.2 0.0 collective-permute-done.11.refs_7_
  39.2 0.0 collective-permute-start.12
  39.2 0.5 collective-permute-start.13
  39.7 5.8 %collective-permute-done.14.refs_10_.refs_2_ = f32[392,256]{1,0:T(8,128)S(1)} collective-permute-done((f32[392,256]{1,0:T(8,128)S(1)}, f32[392,256]{1,0:T(8,128)S(1)}, u32[]{:S(2)}, u32[]{:S(2)}) %collective-permute-start.14) | collective-permute-done | bytes 401440 | tf_op jit(solution)/shard_map/ppermute | solution.py:419
  45.5 0.0 collective-permute-done.12.refs_6_
  45.5 0.0 collective-permute-done.13.refs_8_
  45.5 1.6 %shard_map.262 = (f32[512,512]{1,0:T(8,128)S(1)}, bf16[2,512,256]{2,1,0:T(8,128)(2,1)S(1)}, bf16[2,512,256]{2,1,0:T(8,128)(2,1)S(1)}, bf16[512,512]{1,0:T(8,128)(2,1)S(1)}, bf16[512,512]{1,0:T(8,128)(2,1)S(1)}) custom-call(f32[512,512]{1,0:T(8,128)S(1)} %copy-done, f32[512,256]{1,0:T(8,128)S(1)} %copy-done.4, f32[512,256]{1,0:T(8,128)S(1)} %copy-done.5, ...), custom_call_target="tpu_custom_call" | custom-call | flops 805306368 | bytes 7908352 | tf_op jit(solution)/shard_map/pallas_call | solution.py:363
  47.1 2.1 %shard_map.263 = (f32[64,512]{1,0:T(8,128)}, bf16[128,512]{1,0:T(8,128)(2,1)S(1)}, f32[128,512]{1,0:T(8,128)S(1)}, f32[128,512]{1,0:T(8,128)S(1)}) custom-call(f32[64,512]{1,0:T(8,128)S(1)} %shard_map.261.refs_9_.refs_0_, f32[64,512]{1,0:T(8,128)S(1)} %collective-permute-done.10.refs_1_, f32[64,512]{1,0:T(8,128)S(1)} %get-tuple-element.58.refs_2_, ...), custom_call_target="tpu_custom_call" | custom-call | flops 402653184 | bytes 5388288 | tf_op jit(solution)/shard_map/pallas_call | solution.py:363
  49.2 0.0 collective-permute-start.17
  49.2 0.5 collective-permute-start.18
  49.7 2.4 %collective-permute-start.16 = (f32[128,512]{1,0:T(8,128)S(1)}, f32[128,512]{1,0:T(8,128)S(1)}, u32[]{:S(2)}, u32[]{:S(2)}) collective-permute-start(f32[128,512]{1,0:T(8,128)S(1)} %get-tuple-element.69.head), channel_id=1, source_target_pairs={{0,13},{1,0},{4,1},{5,4},{8,5},{9,8},{12,9},{13,12},{2,15},{3,2},{... | collective-permute-start | bytes 786440 | tf_op jit(solution)/shard_map/ppermute | solution.py:380
  52.1 0.0 collective-permute-start.15
  52.1 1.3 %shard_map.264.middle = f32[256,512]{1,0:T(8,128)S(1)} custom-call(f32[512,512]{1,0:T(8,128)S(1)} %copy-done, f32[512,512]{1,0:T(8,128)S(1)} %get-tuple-element.63.refs_5_.receivers, s32[3,512]{1,0:T(4,128)S(1)} %bitcast.13, bf16[128,512]{1,0:T(8,128)(2,1)S(1)} %get-tuple-element.70.senders, bf16[512,512]{1,0:T(8,128)(2,1)S(1)} %get-tuple-element.66.refs_9_.wo_high, ...), custom_call_target="tpu_custom_call" | custom-call | flops 402653184 | bytes 3815424 | tf_op jit(solution)/shard_map/pallas_call | solution.py:363
  53.4 0.0 collective-permute-done.17.refs_1_
  53.4 0.0 collective-permute-done.18.refs_3_
  53.5 0.0 copy-done.1
  53.5 0.0 copy-done.2
  53.5 0.5 shard_map.265
  54.0 4.4 %shard_map.266 = (bf16[512,512]{1,0:T(8,128)(2,1)S(1)}, bf16[512,512]{1,0:T(8,128)(2,1)S(1)}, f32[512,512]{1,0:T(8,128)S(1)}, f32[256,512]{1,0:T(8,128)S(1)}) custom-call(f32[128,512]{1,0:T(8,128)S(1)} %get-tuple-element.69.head, f32[256,512]{1,0:T(8,128)S(1)} %shard_map.264.middle, f32[128,512]{1,0:T(8,128)S(1)} %get-tuple-element.68.tail, ...), custom_call_target="tpu_custom_call" | custom-call | flops 3221225472 | bytes 9199616 | tf_op jit(solution)/shard_map/pallas_call | solution.py:363
  58.4 1.3 %collective-permute-done.15.before = f32[128,512]{1,0:T(8,128)S(1)} collective-permute-done((f32[128,512]{1,0:T(8,128)S(1)}, f32[128,512]{1,0:T(8,128)S(1)}, u32[]{:S(2)}, u32[]{:S(2)}) %collective-permute-start.15) | collective-permute-done | bytes 262176 | tf_op jit(solution)/shard_map/ppermute | solution.py:380
  59.7 0.0 collective-permute-done.16.after
  59.7 4.3 %shard_map.267 = f32[512,512]{1,0:T(8,128)} custom-call(f32[128,512]{1,0:T(8,128)S(1)} %collective-permute-done.15.before, f32[128,512]{1,0:T(8,128)S(1)} %collective-permute-done.16.after, f32[128,512]{1,0:T(8,128)S(1)} %get-tuple-element.69.head, f32[128,512]{1,0:T(8,128)S(1)} %get-tuple-element.68.tail, f32[256,512]{1,0:T(8,128)S(1)} %get-tuple-element.81.inner, ...), custom_call_target="tpu_custom_call" | custom-call | flops 805306368 | bytes 9183232 | tf_op jit(solution)/shard_map/pallas_call | solution.py:363
  (23 shorter events, 0.0 us)
Async XLA Ops:
  7.3 8.8 %copy-start.7 = (f32[64,512]{1,0:T(8,128)S(1)}, f32[64,512]{1,0:T(8,128)}, u32[]{:S(2)}) copy-start(f32[64,512]{1,0:T(8,128)} %shard_map.257.refs_15_.refs_0_) | copy-start | bytes 393220
  7.3 8.8 %copy-start.8 = (f32[512,256]{1,0:T(8,128)S(1)}, f32[512,256]{1,0:T(8,128)}, u32[]{:S(2)}) copy-start(f32[512,256]{1,0:T(8,128)} %refs_5_.1) | copy-start | bytes 1572868
  7.3 8.8 %copy-start.9 = (f32[512,256]{1,0:T(8,128)S(1)}, f32[512,256]{1,0:T(8,128)}, u32[]{:S(2)}) copy-start(f32[512,256]{1,0:T(8,128)} %refs_6_.1) | copy-start | bytes 1572868
  7.3 8.8 %copy-start.11 = (f32[64,512]{1,0:T(8,128)S(1)}, f32[64,512]{1,0:T(8,128)}, u32[]{:S(2)}) copy-start(f32[64,512]{1,0:T(8,128)} %refs_2_.2) | copy-start | bytes 393220
  7.3 6.7 %collective-permute-start = (f32[64,512]{1,0:T(8,128)}, f32[64,512]{1,0:T(8,128)S(1)}, u32[]{:S(2)}, u32[]{:S(2)}) collective-permute-start(f32[64,512]{1,0:T(8,128)} %shard_map.257.refs_15_.refs_0_), channel_id=1, source_target_pairs={{0,2},{2,0},{1,3},{3,1},{4,6},{6,4},{5,7},{7,5},{8,10},{10,8},{9,1... | collective-permute-start | bytes 393224 | tf_op jit(solution)/shard_map/ppermute | solution.py:380
  10.3 12.6 %copy-start.17 = (s32[512,6]{0,1:T(8,128)S(1)}, s32[512,6]{0,1:T(8,128)}, u32[]{:S(2)}) copy-start(s32[512,6]{0,1:T(8,128)} %param.30) | copy-start | bytes 36868
  10.3 12.6 %copy-start.18 = (s32[64,6]{0,1:T(8,128)S(1)}, s32[64,6]{0,1:T(8,128)}, u32[]{:S(2)}) copy-start(s32[64,6]{0,1:T(8,128)} %param.31) | copy-start | bytes 4612
  10.3 23.0 %copy-start.10 = (f32[256,512]{1,0:T(8,128)S(1)}, f32[256,512]{1,0:T(8,128)}, u32[]{:S(2)}) copy-start(f32[256,512]{1,0:T(8,128)} %refs_10_.1) | copy-start | bytes 1572868
  13.3 32.2 %copy-start = (f32[512,512]{1,0:T(8,128)S(1)}, f32[512,512]{1,0:T(8,128)}, u32[]{:S(2)}) copy-start(f32[512,512]{1,0:T(8,128)} %nodes.1) | copy-start | bytes 3145732
  13.3 32.2 %copy-start.4 = (f32[512,256]{1,0:T(8,128)S(1)}, f32[512,256]{1,0:T(8,128)}, u32[]{:S(2)}) copy-start(f32[512,256]{1,0:T(8,128)} %refs_1_.1) | copy-start | bytes 1572868
  13.4 32.2 %copy-start.5 = (f32[512,256]{1,0:T(8,128)S(1)}, f32[512,256]{1,0:T(8,128)}, u32[]{:S(2)}) copy-start(f32[512,256]{1,0:T(8,128)} %refs_2_.3) | copy-start | bytes 1572868
  13.4 32.2 %copy-start.6 = (f32[256,512]{1,0:T(8,128)S(1)}, f32[256,512]{1,0:T(8,128)}, u32[]{:S(2)}) copy-start(f32[256,512]{1,0:T(8,128)} %refs_4_.2) | copy-start | bytes 1572868
  14.0 14.0 %collective-permute-start.4 = (f32[392,256]{1,0:T(8,128)}, f32[392,256]{1,0:T(8,128)S(1)}, u32[]{:S(2)}, u32[]{:S(2)}) collective-permute-start(f32[392,256]{1,0:T(8,128)} %get-tuple-element.51), channel_id=1, source_target_pairs={{0,2},{2,0},{1,3},{3,1},{4,6},{6,4},{5,7},{7,5},{8,10},{10,8},{9,1... | collective-permute-start | bytes 1204232 | tf_op jit(solution)/shard_map/ppermute | solution.py:380
  15.8 17.5 %collective-permute-start.9 = (f32[392,256]{1,0:T(8,128)}, f32[392,256]{1,0:T(8,128)S(1)}, u32[]{:S(2)}, u32[]{:S(2)}) collective-permute-start(f32[392,256]{1,0:T(8,128)} %get-tuple-element.57), channel_id=1, source_target_pairs={{0,2},{2,0},{1,3},{3,1},{4,6},{6,4},{5,7},{7,5},{8,10},{10,8},{9,1... | collective-permute-start | bytes 1204232 | tf_op jit(solution)/shard_map/ppermute | solution.py:380
  16.1 0.7 %copy-start.12 = (f32[4,512]{1,0:T(4,128)S(1)}, f32[4,512]{1,0:T(4,128)}, u32[]{:S(2)}) copy-start(f32[4,512]{1,0:T(4,128)} %get-tuple-element.44.refs_3_.gains) | copy-start | bytes 24580
  16.8 0.7 %copy-start.14 = (f32[3,256]{1,0:T(4,128)S(1)}, f32[3,256]{1,0:T(4,128)}, u32[]{:S(2)}) copy-start(f32[3,256]{1,0:T(4,128)} %get-tuple-element.45.refs_4_.refs_3_.biases) | copy-start | bytes 9220
  17.5 28.1 %copy-start.15 = (f32[3,256]{1,0:T(4,128)S(1)}, f32[3,256]{1,0:T(4,128)}, u32[]{:S(2)}) copy-start(f32[3,256]{1,0:T(4,128)} %get-tuple-element.45.refs_4_.refs_3_.biases) | copy-start | bytes 9220
  18.1 6.0 %collective-permute-start.3 = (f32[64,256]{1,0:T(8,128)S(1)}, f32[64,256]{1,0:T(8,128)S(1)}, u32[]{:S(2)}, u32[]{:S(2)}) collective-permute-start(f32[64,256]{1,0:T(8,128)S(1)} %get-tuple-element.46.refs_2_.refs_0_), channel_id=1, source_target_pairs={{0,12},{4,0},{8,4},{12,8},{1,13},{5,1},{9,5},{13,9},{2,14},{6,2},{... | collective-permute-start | bytes 196616 | tf_op jit(solution)/shard_map/ppermute | solution.py:380
  22.0 5.2 %collective-permute-start.2 = (f32[64,256]{1,0:T(8,128)S(1)}, f32[64,256]{1,0:T(8,128)S(1)}, u32[]{:S(2)}, u32[]{:S(2)}) collective-permute-start(f32[64,256]{1,0:T(8,128)S(1)} %get-tuple-element.46.refs_2_.refs_0_), channel_id=1, source_target_pairs={{0,8},{4,12},{8,0},{12,4},{1,9},{5,13},{9,1},{13,5},{2,10},{6,14},... | collective-permute-start | bytes 196616 | tf_op jit(solution)/shard_map/ppermute | solution.py:380
  22.0 6.1 %collective-permute-start.1 = (f32[64,256]{1,0:T(8,128)S(1)}, f32[64,256]{1,0:T(8,128)S(1)}, u32[]{:S(2)}, u32[]{:S(2)}) collective-permute-start(f32[64,256]{1,0:T(8,128)S(1)} %get-tuple-element.46.refs_2_.refs_0_), channel_id=1, source_target_pairs={{0,4},{4,8},{8,12},{12,0},{1,5},{5,9},{9,13},{13,1},{2,6},{6,10},{... | collective-permute-start | bytes 196616 | tf_op jit(solution)/shard_map/ppermute | solution.py:380
  28.0 11.2 %collective-permute-start.11 = (f32[392,256]{1,0:T(8,128)S(1)}, f32[392,256]{1,0:T(8,128)S(1)}, u32[]{:S(2)}, u32[]{:S(2)}) collective-permute-start(f32[392,256]{1,0:T(8,128)S(1)} %collective-permute-done.4.refs_5_), channel_id=1, source_target_pairs={{0,16},{16,0},{1,17},{17,1},{2,18},{18,2},{3,19},{19,3},{4,20},{20... | collective-permute-start | bytes 1204232 | tf_op jit(solution)/shard_map/ppermute | solution.py:419
  29.5 1.3 %collective-permute-start.5 = (f32[64,256]{1,0:T(8,128)S(1)}, f32[64,256]{1,0:T(8,128)S(1)}, u32[]{:S(2)}, u32[]{:S(2)}) collective-permute-start(f32[64,256]{1,0:T(8,128)S(1)} %get-tuple-element.46.refs_2_.refs_0_), channel_id=1, source_target_pairs={{0,1},{1,0},{2,3},{3,2},{4,5},{5,4},{6,7},{7,6},{8,9},{9,8},{10,11... | collective-permute-start | bytes 196616 | tf_op jit(solution)/shard_map/ppermute | solution.py:380
  29.6 3.8 %collective-permute-start.6 = (f32[64,256]{1,0:T(8,128)S(1)}, f32[64,256]{1,0:T(8,128)S(1)}, u32[]{:S(2)}, u32[]{:S(2)}) collective-permute-start(f32[64,256]{1,0:T(8,128)S(1)} %collective-permute-done.1.refs_1_), channel_id=1, source_target_pairs={{0,1},{1,0},{2,3},{3,2},{4,5},{5,4},{6,7},{7,6},{8,9},{9,8},{10,11... | collective-permute-start | bytes 196616 | tf_op jit(solution)/shard_map/ppermute | solution.py:380
  30.1 3.3 %collective-permute-start.7 = (f32[64,256]{1,0:T(8,128)S(1)}, f32[64,256]{1,0:T(8,128)S(1)}, u32[]{:S(2)}, u32[]{:S(2)}) collective-permute-start(f32[64,256]{1,0:T(8,128)S(1)} %collective-permute-done.2.refs_2_), channel_id=1, source_target_pairs={{0,1},{1,0},{2,3},{3,2},{4,5},{5,4},{6,7},{7,6},{8,9},{9,8},{10,11... | collective-permute-start | bytes 196616 | tf_op jit(solution)/shard_map/ppermute | solution.py:380
  30.8 2.5 %collective-permute-start.8 = (f32[64,256]{1,0:T(8,128)S(1)}, f32[64,256]{1,0:T(8,128)S(1)}, u32[]{:S(2)}, u32[]{:S(2)}) collective-permute-start(f32[64,256]{1,0:T(8,128)S(1)} %collective-permute-done.3.refs_3_), channel_id=1, source_target_pairs={{0,1},{1,0},{2,3},{3,2},{4,5},{5,4},{6,7},{7,6},{8,9},{9,8},{10,11... | collective-permute-start | bytes 196616 | tf_op jit(solution)/shard_map/ppermute | solution.py:380
  34.1 13.0 %copy-start.13 = (f32[4,512]{1,0:T(4,128)S(1)}, f32[4,512]{1,0:T(4,128)}, u32[]{:S(2)}) copy-start(f32[4,512]{1,0:T(4,128)} %get-tuple-element.44.refs_3_.gains) | copy-start | bytes 24580
  34.2 13.0 %copy-start.16 = (s32[512,3]{0,1:T(4,128)S(1)}, s32[512,3]{0,1:T(4,128)}, u32[]{:S(2)}) copy-start(s32[512,3]{0,1:T(4,128)} %param.29) | copy-start | bytes 18436
  34.2 5.0 %collective-permute-start.10 = (f32[64,512]{1,0:T(8,128)S(1)}, f32[64,512]{1,0:T(8,128)S(1)}, u32[]{:S(2)}, u32[]{:S(2)}) collective-permute-start(f32[64,512]{1,0:T(8,128)S(1)} %shard_map.261.refs_9_.refs_0_), channel_id=1, source_target_pairs={{0,2},{2,0},{1,3},{3,1},{4,6},{6,4},{5,7},{7,5},{8,10},{10,8},{9,1... | collective-permute-start | bytes 393224 | tf_op jit(solution)/shard_map/ppermute | solution.py:380
  35.6 9.8 %collective-permute-start.14 = (f32[392,256]{1,0:T(8,128)S(1)}, f32[392,256]{1,0:T(8,128)S(1)}, u32[]{:S(2)}, u32[]{:S(2)}) collective-permute-start(f32[392,256]{1,0:T(8,128)S(1)} %collective-permute-done.9.refs_11_.refs_0_), channel_id=1, source_target_pairs={{0,4},{4,0},{8,12},{12,8},{1,5},{5,1},{9,13},{13,9},{2,6},{6,2},{1... | collective-permute-start | bytes 1204232 | tf_op jit(solution)/shard_map/ppermute | solution.py:419
  39.2 6.3 %collective-permute-start.12 = (f32[392,256]{1,0:T(8,128)S(1)}, f32[392,256]{1,0:T(8,128)S(1)}, u32[]{:S(2)}, u32[]{:S(2)}) collective-permute-start(f32[392,256]{1,0:T(8,128)S(1)} %collective-permute-done.4.refs_5_), channel_id=1, source_target_pairs={{0,1},{1,0},{2,3},{3,2},{4,5},{5,4},{6,7},{7,6},{8,9},{9,8},{10,11... | collective-permute-start | bytes 1204232 | tf_op jit(solution)/shard_map/ppermute | solution.py:380
  39.2 6.3 %collective-permute-start.13 = (f32[392,256]{1,0:T(8,128)S(1)}, f32[392,256]{1,0:T(8,128)S(1)}, u32[]{:S(2)}, u32[]{:S(2)}) collective-permute-start(f32[392,256]{1,0:T(8,128)S(1)} %collective-permute-done.11.refs_7_), channel_id=1, source_target_pairs={{0,1},{1,0},{2,3},{3,2},{4,5},{5,4},{6,7},{7,6},{8,9},{9,8},{10,11... | collective-permute-start | bytes 1204232 | tf_op jit(solution)/shard_map/ppermute | solution.py:380
  49.2 4.2 %copy-start.1 = (f32[512,256]{1,0:T(8,128)S(1)}, f32[512,256]{1,0:T(8,128)}, u32[]{:S(2)}) copy-start(f32[512,256]{1,0:T(8,128)} %ws.1) | copy-start | bytes 1572868
  49.2 4.2 %copy-start.2 = (f32[512,256]{1,0:T(8,128)S(1)}, f32[512,256]{1,0:T(8,128)}, u32[]{:S(2)}) copy-start(f32[512,256]{1,0:T(8,128)} %wr.1) | copy-start | bytes 1572868
  49.2 4.3 %copy-start.3 = (f32[256,512]{1,0:T(8,128)S(1)}, f32[256,512]{1,0:T(8,128)}, u32[]{:S(2)}) copy-start(f32[256,512]{1,0:T(8,128)} %wo.1) | copy-start | bytes 1572868
  49.2 4.2 %collective-permute-start.17 = (f32[392,256]{1,0:T(8,128)S(1)}, f32[392,256]{1,0:T(8,128)S(1)}, u32[]{:S(2)}, u32[]{:S(2)}) collective-permute-start(f32[392,256]{1,0:T(8,128)S(1)} %collective-permute-done.9.refs_11_.refs_0_), channel_id=1, source_target_pairs={{0,1},{1,0},{2,3},{3,2},{4,5},{5,4},{6,7},{7,6},{8,9},{9,8},{10,11... | collective-permute-start | bytes 1204232 | tf_op jit(solution)/shard_map/ppermute | solution.py:380
  49.2 4.2 %collective-permute-start.18 = (f32[392,256]{1,0:T(8,128)S(1)}, f32[392,256]{1,0:T(8,128)S(1)}, u32[]{:S(2)}, u32[]{:S(2)}) collective-permute-start(f32[392,256]{1,0:T(8,128)S(1)} %collective-permute-done.14.refs_10_.refs_2_), channel_id=1, source_target_pairs={{0,1},{1,0},{2,3},{3,2},{4,5},{5,4},{6,7},{7,6},{8,9},{9,8},{10,11... | collective-permute-start | bytes 1204232 | tf_op jit(solution)/shard_map/ppermute | solution.py:380
  49.7 10.0 %collective-permute-start.16 = (f32[128,512]{1,0:T(8,128)S(1)}, f32[128,512]{1,0:T(8,128)S(1)}, u32[]{:S(2)}, u32[]{:S(2)}) collective-permute-start(f32[128,512]{1,0:T(8,128)S(1)} %get-tuple-element.69.head), channel_id=1, source_target_pairs={{0,13},{1,0},{4,1},{5,4},{8,5},{9,8},{12,9},{13,12},{2,15},{3,2},{... | collective-permute-start | bytes 786440 | tf_op jit(solution)/shard_map/ppermute | solution.py:380
  52.1 7.6 %collective-permute-start.15 = (f32[128,512]{1,0:T(8,128)S(1)}, f32[128,512]{1,0:T(8,128)S(1)}, u32[]{:S(2)}, u32[]{:S(2)}) collective-permute-start(f32[128,512]{1,0:T(8,128)S(1)} %get-tuple-element.68.tail), channel_id=1, source_target_pairs={{0,1},{1,4},{4,5},{5,8},{8,9},{9,12},{12,13},{13,0},{2,3},{3,6},{6... | collective-permute-start | bytes 786440 | tf_op jit(solution)/shard_map/ppermute | solution.py:380

commit v7 on v6

--- a/solution.py
+++ b/solution.py
@@ -11,7 +11,8 @@
 f32 = jnp.float32
 bf16 = jnp.bfloat16
 limit_bytes = 12 * 1024 * 1024
-tight_limit = 64 * 1000 * 1000
+share_limit = 58 * 1000 * 1000
+up_limit = 50 * 1000 * 1000
 most_direct = 4
 
 
@@ -79,55 +80,29 @@
     return moves
 
 
-def strips(source, target, count):
-    rows = source.shape[0] // count
-    return [
-        (source.at[pl.ds(i * rows, rows)], target.at[pl.ds(i * rows, rows)]) for i in range(count)
-    ]
-
-
-def upward_kernel(nodes_hbm, coarse_hbm, ws_hbm, wr_hbm, wo_hbm, children, bias, part, nodes, coarse, ws, wr, wo, high, low, sems):
-    cuts = 8
-    moves = started(
-        strips(ws_hbm, ws, cuts)
-        + strips(nodes_hbm, nodes, cuts)
-        + [(coarse_hbm, coarse)]
-        + strips(wr_hbm, wr, cuts)
-        + strips(wo_hbm, wo, cuts),
-        sems,
-    )
+def upward_kernel(nodes, coarse, children, ws, wr, bias, wo, part):
     wanted = upright(children[...])
     names = lax.broadcasted_iota(jnp.int32, (wanted.shape[0], nodes.shape[0]), 1)
     picks = one_hot(wanted, names)
-    for move in moves[:cuts]:
-        move.wait()
-    ws_high, ws_low = split(ws[...])
-    rows = nodes.shape[0] // cuts
-    for i in range(cuts):
-        moves[cuts + i].wait()
-        place = slice(i * rows, (i + 1) * rows)
-        high[place], low[place] = split(0.5 * dot3(nodes[place], ws_high, ws_low))
-    for move in moves[2 * cuts : 3 * cuts + 1]:
-        move.wait()
+    sender_high, sender_low = split(0.5 * dot3(nodes[...], *split(ws[...])))
     receivers = 0.5 * (dot3(coarse[...], *split(wr[...])) + bias[...])
-    picked = dot(picks, high[...]) + dot(picks, low[...])
+    picked = dot(picks, sender_high) + dot(picks, sender_low)
     hidden = silu_sum(picked, receivers, wanted.shape[1])
-    for move in moves[3 * cuts + 1 :]:
-        move.wait()
     part[...] = dot3(hidden, *split(wo[...]))
 
 
-def share_kernel(*refs):
-    params, down_own, bottom_own, refs = refs[:7], refs[7:11], refs[11:15], refs[15:]
-    gains, biases, down_pack, bottom_pack, sems = refs
-    moves = started(
-        share_copies(down_own, down_pack, "parts") + share_copies(bottom_own, bottom_pack, "patch"), sems
-    )
+def stack_kernel(*refs):
+    params, (gains, biases) = refs[:7], refs[7:]
     for i in range(4):
         gains[i : i + 1] = params[i][...]
     for i in range(3):
         biases[i : i + 1] = params[4 + i][...]
-    for move in moves:
+
+
+def share_kernel(*refs):
+    down_own, bottom_own, (down_pack, bottom_pack, sems) = refs[:4], refs[4:8], refs[8:]
+    copies = share_copies(down_own, down_pack, "parts") + share_copies(bottom_own, bottom_pack, "patch")
+    for move in started(copies, sems):
         move.wait()
 
 
@@ -485,41 +460,38 @@
         upward_kernel,
         [like((blocks, latent))],
         [
-            node_states, coarse_states, upward_sender, upward_receiver, upward_output,
-            children.T, upward_bias[None],
+            node_states, coarse_states, children.T, upward_sender, upward_receiver,
+            upward_bias[None], upward_output,
         ],
-        6 * rows * latent * width + 4 * children.size * rows * width,
-        [
-            pltpu.VMEM((rows, latent), f32),
-            pltpu.VMEM((blocks, latent), f32),
-            pltpu.VMEM((latent, width), f32),
-            pltpu.VMEM((latent, width), f32),
-            pltpu.VMEM((width, latent), f32),
-            pltpu.VMEM((rows, width), bf16),
-            pltpu.VMEM((rows, width), bf16),
-            pltpu.SemaphoreType.DMA((33,)),
-        ],
-        far=range(5),
-        limit=tight_limit,
+        6 * rows * latent * width,
+        limit=up_limit,
     )
     parts = sub_parts(part)
     down_own = (downward_sender, downward_receiver, downward_output, downward_bias[None])
     bottom_own = (bottom_sender, bottom_receiver, bottom_output, bottom_bias[None])
-    gains, biases, down_pack, bottom_pack = call(
+    down_pack, bottom_pack = call(
         share_kernel,
-        [like((4, latent)), like((3, width)), pack("parts"), pack("patch")],
+        [pack("parts"), pack("patch")],
+        [*down_own, *bottom_own],
+        latent,
+        [pltpu.SemaphoreType.DMA((6 + 2 * columns,))],
+        far=range(8),
+        limit=share_limit,
+    )
+    gains, biases = call(
+        stack_kernel,
+        [like((4, latent)), like((3, width))],
         [
             upward_gain[None], coarse_gain[None], downward_gain[None], bottom_gain[None],
-            coarse_bias[None], downward_bias[None], bottom_bias[None],
-            *down_own, *bottom_own, part,
+            coarse_bias[None], downward_bias[None], bottom_bias[None], part,
         ],
         latent * hidden,
-        [pltpu.SemaphoreType.DMA((6 + 2 * columns,))],
-        far=range(7, 15),
         unread=1,
-        limit=tight_limit,
-    )
-    down_near, bottom_near = map(over_sub, held((down_pack, bottom_pack), parts[-1]))
+    )
+    down_near = over_sub(down_pack)
+    down_near = held(down_near, parts[-1])
+    bottom_near = over_sub(bottom_pack)
+    down_far = over_partners(down_near, "parts")
     coarse_up, senders, receivers = call(
         functools.partial(coarse_project_kernel, len(parts)),
         [like((blocks, latent)), like((blocks, width)), like((blocks, width))],
@@ -535,34 +507,32 @@
         coarse_links.size * names,
         unread=1,
     )
-    pieces, (picks, bottom_picks, down_near) = coarse_pieces(
-        senders, (picks, bottom_picks, down_near)
-    )
-    down_far = over_partners(down_near, "parts")
+    pieces, (picks, bottom_picks, down_near, down_far, bottom_near) = coarse_pieces(
+        senders, (picks, bottom_picks, down_near, down_far, bottom_near)
+    )
+    down_packs = all_shares(down_near, down_far)
+    bottom_far = over_partners(bottom_near, "patch")
     (part,) = call(
         functools.partial(coarse_kernel, len(pieces)),
         [like((blocks, latent))],
-        [*pieces, picks, receivers, coarse_output, *bottom_near],
+        [*pieces, picks, receivers, coarse_output],
         4 * coarse_links.size * names * width,
-        unread=len(bottom_near),
-    )
-    bottom_near = held(bottom_near, part)
+    )
     parts = sub_parts(part)
-    bottom_far = over_partners(bottom_near, "patch")
-    down_packs = all_shares(*held((down_near, down_far), parts[-1]))
     receivers, ws_high, ws_low, wo_high, wo_low = call(
         functools.partial(down_weights_kernel, len(down_packs)),
         [like((rows, hidden)), *weights, *outputs],
-        [node_states, downward_sender, downward_receiver, biases, downward_output, *down_packs, part, *(x for row in bottom_far for x in row)],
+        [node_states, downward_sender, downward_receiver, biases, downward_output, *down_packs, part],
         6 * rows * latent * hidden,
         [pltpu.VMEM((subs, latent, width), bf16)] * 2 + [pltpu.VMEM((subs, 8, width), f32)],
-        unread=1 + sum(map(len, bottom_far)),
+        unread=1,
     )
     new_coarse, senders, head, tail = call(
         functools.partial(down_edge_kernel, len(parts), rim),
         [like((blocks, latent)), like((2 * blocks, hidden), bf16), like((rim, latent)), like((rim, latent))],
-        [*parts, coarse_up, gains, node_states, receivers, down_sources.T, ws_high, ws_low, wo_high, wo_low],
+        [*parts, coarse_up, gains, node_states, receivers, down_sources.T, ws_high, ws_low, wo_high, wo_low, *(x for row in bottom_far for x in row)],
         6 * 2 * rim * latent * hidden,
+        unread=sum(map(len, bottom_far)),
     )
     ring = ("patch", "lvl")
     before, after = shifted(tail, ring, 1), shifted(head, ring, -1)

time: 64.3 us -> 60.2 us (0.936)
  Pallas kernels: 26.2 us -> 21 us
  waiting for transfers between devices: 16.8 us -> 21.6 us
  starting transfers between devices: 18.6 us -> 16.1 us
  local copies, waits for them, and re-layouts: 1.46 us -> 0.13 us
    ppermute x17, waiting for transfers between devices: 11.1 us -> 20.3 us  [shifted(): lax.ppermute(values, axis, [(i, (i + step) % count) for i in range(count)])]
    pallas_call x11 -> x12, Pallas kernels: 26.2 us -> 21 us  [call(): pl.pallas_call((lambda *refs: kernel(*refs[:read], *refs[read + unread:])...]
    ppermute x2, waiting for transfers between devices: 5.78 us -> 1.35 us  [over_partners(): lax.ppermute(share, axis, [(i, i - i % count + (i + p) % count) for i in...]
    ppermute x17, starting transfers between devices: 15.5 us -> 14 us  [shifted(): lax.ppermute(values, axis, [(i, (i + step) % count) for i in range(count)])]
    unnamed x38 -> x54, local copies, waits for them, and re-layouts: 1.46 us -> 0.13 us
    ppermute x2, starting transfers between devices: 3.1 us -> 2.09 us  [over_partners(): lax.ppermute(share, axis, [(i, i - i % count + (i + p) % count) for i in...]
  transfers between devices with their start and end apart: 19 -> 19, of which waited for: 8 -> 9; matrix products, arithmetic and copies ran while one was open for 0% -> 0% of each run, Pallas kernels for 18% -> 20%
where the time goes in v7:
time: 60.2 us; the launch traced here: 60 us
  waiting for transfers between devices  21.6 us (36%)
  Pallas kernels  21 us (35%)
  starting transfers between devices  16.1 us (27%)
  between operations  1.07 us (2%)
    pallas_call x12, Pallas kernels, call(): pl.pallas_call((lambda *refs: kernel(*refs[:read], *refs[read + unread:])...  21 us
    ppermute x17, waiting for transfers between devices, shifted(): lax.ppermute(values, axis, [(i, (i + step) % count) for i in range(count)])  20.3 us
    ppermute x17, starting transfers between devices, shifted(): lax.ppermute(values, axis, [(i, (i + step) % count) for i in range(count)])  14 us
    ppermute x2, starting transfers between devices, over_partners(): lax.ppermute(share, axis, [(i, i - i % count + (i + p) % count) for i in...  2.09 us
    ppermute x2, waiting for transfers between devices, over_partners(): lax.ppermute(share, axis, [(i, i - i % count + (i + p) % count) for i in...  1.35 us
  transfers between devices with their start and end apart: 19, of which 9 were waited for; matrix products, arithmetic and copies ran while one was open for 0% of the time, Pallas kernels for 20%

profile of v7, /device:TPU:0, one launch (start us, length us, event | category | flops | bytes accessed | tf_op | source)
XLA Modules:
  0.0 60.0 jit_solution(8137238900677601458)
XLA Ops:
  0.6 0.0 copy-start
  0.6 0.0 copy-start.13
  0.7 0.0 copy-start.10
  0.8 2.3 %shard_map.261 = (f32[392,256]{1,0:T(8,128)}, f32[392,256]{1,0:T(8,128)}) custom-call(f32[512,256]{1,0:T(8,128)} %refs_1_.3, f32[512,256]{1,0:T(8,128)} %refs_2_.5, f32[256,512]{1,0:T(8,128)} %refs_4_.4, f32[1,256]{1,0:T(1,128)} %bitcast.16, f32[512,256]{1,0:T(8,128)} %ws.3, f32[512,256]{1,0:T(8,128)} %wr.3, f32[256,512]{1,0:T(8,128)} %wo.3, f32[1,256]{1,0:T(1,128)} %bitcast.18), custom_call_target="tpu_custom_call" | custom-call | flops 512 | bytes 3950592 | tf_op jit(solution)/shard_map/pallas_call | solution.py:338
  3.1 0.0 copy-start.15
  3.1 0.0 copy-start.19
  3.2 0.0 copy-start.7
  3.2 3.0 %collective-permute-start.4 = (f32[392,256]{1,0:T(8,128)}, f32[392,256]{1,0:T(8,128)S(1)}, u32[]{:S(2)}, u32[]{:S(2)}) collective-permute-start(f32[392,256]{1,0:T(8,128)} %get-tuple-element.47), channel_id=1, source_target_pairs={{0,2},{2,0},{1,3},{3,1},{4,6},{6,4},{5,7},{7,5},{8,10},{10,8},{9,1... | collective-permute-start | bytes 1204232 | tf_op jit(solution)/shard_map/ppermute | solution.py:355
  6.2 0.0 copy-done
  6.2 0.0 copy-done.9
  6.2 0.0 copy-done.8
  6.2 0.0 copy-done.16
  6.2 1.8 %shard_map.257.refs_7_.refs_0_ = f32[64,512]{1,0:T(8,128)S(1)} custom-call(f32[512,512]{1,0:T(8,128)S(1)} %copy-done, f32[64,512]{1,0:T(8,128)S(1)} %copy-done.13, s32[7,64]{1,0:T(8,128)S(1)} %bitcast.15, f32[512,256]{1,0:T(8,128)S(1)} %copy-done.8, f32[512,256]{1,0:T(8,128)S(1)} %copy-done.9, f32[1,256]{1,0:T(1,128)S(1)} %bitcast.25, f32[256,512]{1,0:T(8,128)S(1)} %copy-done.10), custom_call_target="tpu_custom_call" | custom-call | flops 402653184 | bytes 2886400 | tf_op jit(solution)/shard_map/pallas_call | solution.py:338
  8.1 0.0 copy-start.1
  8.1 0.0 copy-start.2
  8.1 0.0 copy-start.3
  8.1 0.1 collective-permute-start
  8.2 2.0 %collective-permute-start.6 = (f32[392,256]{1,0:T(8,128)S(1)}, f32[392,256]{1,0:T(8,128)S(1)}, u32[]{:S(2)}, u32[]{:S(2)}) collective-permute-start(f32[392,256]{1,0:T(8,128)S(1)} %copy-done.26), channel_id=1, source_target_pairs={{0,2},{2,0},{1,3},{3,1},{4,6},{6,4},{5,7},{7,5},{8,10},{10,8},{9,1... | collective-permute-start | bytes 1204232 | tf_op jit(solution)/shard_map/ppermute | solution.py:355
  10.2 9.1 %collective-permute-done.refs_1_ = f32[64,512]{1,0:T(8,128)S(1)} collective-permute-done((f32[64,512]{1,0:T(8,128)S(1)}, f32[64,512]{1,0:T(8,128)S(1)}, u32[]{:S(2)}, u32[]{:S(2)}) %collective-permute-start) | collective-permute-done | bytes 131104 | tf_op jit(solution)/shard_map/ppermute | solution.py:355
  19.3 0.0 collective-permute-done.4.refs_5_
  19.3 2.1 %collective-permute-start.5 = (f32[392,256]{1,0:T(8,128)S(1)}, f32[392,256]{1,0:T(8,128)S(1)}, u32[]{:S(2)}, u32[]{:S(2)}) collective-permute-start(f32[392,256]{1,0:T(8,128)S(1)} %collective-permute-done.4.refs_5_), channel_id=1, source_target_pairs={{0,16},{16,0},{1,17},{17,1},{2,18},{18,2},{3,19},{19,3},{4,20},{20... | collective-permute-start | bytes 1204232 | tf_op jit(solution)/shard_map/ppermute | solution.py:394
  21.4 0.0 copy-done.20
  21.5 0.6 shard_map.259
  22.1 3.7 %collective-permute-start.3 = (f32[64,256]{1,0:T(8,128)S(1)}, f32[64,256]{1,0:T(8,128)S(1)}, u32[]{:S(2)}, u32[]{:S(2)}) collective-permute-start(f32[64,256]{1,0:T(8,128)S(1)} %get-tuple-element.44.refs_2_.refs_0_), channel_id=1, source_target_pairs={{0,12},{4,0},{8,4},{12,8},{1,13},{5,1},{9,5},{13,9},{2,14},{6,2},{... | collective-permute-start | bytes 196616 | tf_op jit(solution)/shard_map/ppermute | solution.py:355
  25.7 0.0 collective-permute-start.2
  25.7 1.0 %collective-permute-start.1 = (f32[64,256]{1,0:T(8,128)S(1)}, f32[64,256]{1,0:T(8,128)S(1)}, u32[]{:S(2)}, u32[]{:S(2)}) collective-permute-start(f32[64,256]{1,0:T(8,128)S(1)} %get-tuple-element.44.refs_2_.refs_0_), channel_id=1, source_target_pairs={{0,4},{4,8},{8,12},{12,0},{1,5},{5,9},{9,13},{13,1},{2,6},{6,10},{... | collective-permute-start | bytes 196616 | tf_op jit(solution)/shard_map/ppermute | solution.py:355
  26.7 1.1 %shard_map.260 = (bf16[384,512]{1,0:T(8,128)(2,1)S(1)}, bf16[3072,384]{1,0:T(8,128)(2,1)S(1)}) custom-call(s32[6,64]{1,0:T(8,128)S(1)} %bitcast.20, s32[6,512]{1,0:T(8,128)S(1)} %bitcast.14, f32[64,256]{1,0:T(8,128)S(1)} %get-tuple-element.44.refs_2_.refs_0_), custom_call_target="tpu_custom_call" | custom-call | flops 196608 | bytes 2831872 | tf_op jit(solution)/shard_map/pallas_call | solution.py:338
  27.8 0.0 collective-permute-done.3.refs_3_
  27.8 3.1 %collective-permute-done.2.refs_2_ = f32[64,256]{1,0:T(8,128)S(1)} collective-permute-done((f32[64,256]{1,0:T(8,128)S(1)}, f32[64,256]{1,0:T(8,128)S(1)}, u32[]{:S(2)}, u32[]{:S(2)}) %collective-permute-start.2) | collective-permute-done | bytes 65568 | tf_op jit(solution)/shard_map/ppermute | solution.py:355
  30.9 0.9 %collective-permute-done.1.refs_1_ = f32[64,256]{1,0:T(8,128)S(1)} collective-permute-done((f32[64,256]{1,0:T(8,128)S(1)}, f32[64,256]{1,0:T(8,128)S(1)}, u32[]{:S(2)}, u32[]{:S(2)}) %collective-permute-start.1) | collective-permute-done | bytes 65568 | tf_op jit(solution)/shard_map/ppermute | solution.py:355
  31.8 0.0 collective-permute-done.6.refs_0_
  31.8 0.0 collective-permute-done.5.refs_7_
  31.8 0.0 collective-permute-start.12
  31.8 0.5 collective-permute-start.13
  32.3 0.0 collective-permute-start.14
  32.3 0.1 collective-permute-start.7
  32.4 0.4 collective-permute-start.8
  32.8 1.4 %collective-permute-done.7.refs_4_ = f32[64,256]{1,0:T(8,128)S(1)} collective-permute-done((f32[64,256]{1,0:T(8,128)S(1)}, f32[64,256]{1,0:T(8,128)S(1)}, u32[]{:S(2)}, u32[]{:S(2)}) %collective-permute-start.7) | collective-permute-done | bytes 65568 | tf_op jit(solution)/shard_map/ppermute | solution.py:355
  34.2 0.1 collective-permute-start.9
  34.3 0.0 collective-permute-done.8.refs_5_
  34.3 0.4 collective-permute-start.10
  34.7 0.7 %collective-permute-done.9.refs_6_ = f32[64,256]{1,0:T(8,128)S(1)} collective-permute-done((f32[64,256]{1,0:T(8,128)S(1)}, f32[64,256]{1,0:T(8,128)S(1)}, u32[]{:S(2)}, u32[]{:S(2)}) %collective-permute-start.9) | collective-permute-done | bytes 65568 | tf_op jit(solution)/shard_map/ppermute | solution.py:355
  35.5 0.2 collective-permute-done.10.refs_7_
  35.6 0.8 %shard_map.262.refs_9_.refs_0_ = f32[64,512]{1,0:T(8,128)S(1)} custom-call(f32[64,256]{1,0:T(8,128)S(1)} %get-tuple-element.44.refs_2_.refs_0_, f32[64,256]{1,0:T(8,128)S(1)} %collective-permute-done.1.refs_1_, f32[64,256]{1,0:T(8,128)S(1)} %collective-permute-done.2.refs_2_, f32[64,256]{1,0:T(8,128)S(1)} %collective-permute-done.3.refs_3_, ...), custom_call_target="tpu_custom_call" | custom-call | flops 201326592 | bytes 1638400 | tf_op jit(solution)/shard_map/pallas_call | solution.py:338
  36.4 0.0 copy-start.14
  36.4 1.6 %collective-permute-start.11 = (f32[64,512]{1,0:T(8,128)S(1)}, f32[64,512]{1,0:T(8,128)S(1)}, u32[]{:S(2)}, u32[]{:S(2)}) collective-permute-start(f32[64,512]{1,0:T(8,128)S(1)} %shard_map.262.refs_9_.refs_0_), channel_id=1, source_target_pairs={{0,2},{2,0},{1,3},{3,1},{4,6},{6,4},{5,7},{7,5},{8,10},{10,8},{9,1... | collective-permute-start | bytes 393224 | tf_op jit(solution)/shard_map/ppermute | solution.py:355
  38.0 0.0 collective-permute-done.12.refs_6_
  38.0 0.0 collective-permute-done.13.refs_8_
  38.0 1.6 %shard_map.263 = (f32[512,512]{1,0:T(8,128)S(1)}, bf16[2,512,256]{2,1,0:T(8,128)(2,1)S(1)}, bf16[2,512,256]{2,1,0:T(8,128)(2,1)S(1)}, bf16[512,512]{1,0:T(8,128)(2,1)S(1)}, bf16[512,512]{1,0:T(8,128)(2,1)S(1)}) custom-call(f32[512,512]{1,0:T(8,128)S(1)} %copy-done, f32[512,256]{1,0:T(8,128)S(1)} %copy-done.1, f32[512,256]{1,0:T(8,128)S(1)} %copy-done.2, ...), custom_call_target="tpu_custom_call" | custom-call | flops 805306368 | bytes 7506944 | tf_op jit(solution)/shard_map/pallas_call | solution.py:338
  39.6 2.6 %collective-permute-done.11.refs_1_ = f32[64,512]{1,0:T(8,128)S(1)} collective-permute-done((f32[64,512]{1,0:T(8,128)S(1)}, f32[64,512]{1,0:T(8,128)S(1)}, u32[]{:S(2)}, u32[]{:S(2)}) %collective-permute-start.11) | collective-permute-done | bytes 131104 | tf_op jit(solution)/shard_map/ppermute | solution.py:355
  42.2 1.3 %collective-permute-done.14.refs_11_.refs_2_ = f32[392,256]{1,0:T(8,128)S(1)} collective-permute-done((f32[392,256]{1,0:T(8,128)S(1)}, f32[392,256]{1,0:T(8,128)S(1)}, u32[]{:S(2)}, u32[]{:S(2)}) %collective-permute-start.14) | collective-permute-done | bytes 401440 | tf_op jit(solution)/shard_map/ppermute | solution.py:394
  43.6 2.1 %shard_map.264 = (f32[64,512]{1,0:T(8,128)}, bf16[128,512]{1,0:T(8,128)(2,1)S(1)}, f32[128,512]{1,0:T(8,128)S(1)}, f32[128,512]{1,0:T(8,128)S(1)}) custom-call(f32[64,512]{1,0:T(8,128)S(1)} %shard_map.262.refs_9_.refs_0_, f32[64,512]{1,0:T(8,128)S(1)} %collective-permute-done.11.refs_1_, f32[64,512]{1,0:T(8,128)S(1)} %get-tuple-element.55.refs_2_, ...), custom_call_target="tpu_custom_call" | custom-call | flops 402653184 | bytes 5789696 | tf_op jit(solution)/shard_map/pallas_call | solution.py:338
  45.7 0.0 collective-permute-start.17
  45.7 0.5 collective-permute-start.18
  46.2 0.7 %collective-permute-start.16 = (f32[128,512]{1,0:T(8,128)S(1)}, f32[128,512]{1,0:T(8,128)S(1)}, u32[]{:S(2)}, u32[]{:S(2)}) collective-permute-start(f32[128,512]{1,0:T(8,128)S(1)} %get-tuple-element.65.head), channel_id=1, source_target_pairs={{0,13},{1,0},{4,1},{5,4},{8,5},{9,8},{12,9},{13,12},{2,15},{3,2},{... | collective-permute-start | bytes 786440 | tf_op jit(solution)/shard_map/ppermute | solution.py:355
  46.9 0.0 collective-permute-start.15
  46.9 1.4 %shard_map.265.middle = f32[256,512]{1,0:T(8,128)S(1)} custom-call(f32[512,512]{1,0:T(8,128)S(1)} %copy-done, f32[512,512]{1,0:T(8,128)S(1)} %get-tuple-element.58.refs_5_.receivers, s32[3,512]{1,0:T(4,128)S(1)} %bitcast.13, bf16[128,512]{1,0:T(8,128)(2,1)S(1)} %get-tuple-element.66.senders, bf16[512,512]{1,0:T(8,128)(2,1)S(1)} %get-tuple-element.61.refs_9_.wo_high, ...), custom_call_target="tpu_custom_call" | custom-call | flops 402653184 | bytes 3815424 | tf_op jit(solution)/shard_map/pallas_call | solution.py:338
  48.3 0.0 collective-permute-done.17.refs_1_
  48.3 0.0 collective-permute-done.18.refs_3_
  48.3 0.5 shard_map.266
  48.8 4.6 %shard_map.267 = (bf16[512,512]{1,0:T(8,128)(2,1)S(1)}, bf16[512,512]{1,0:T(8,128)(2,1)S(1)}, f32[512,512]{1,0:T(8,128)S(1)}, f32[256,512]{1,0:T(8,128)S(1)}) custom-call(f32[128,512]{1,0:T(8,128)S(1)} %get-tuple-element.65.head, f32[256,512]{1,0:T(8,128)S(1)} %shard_map.265.middle, f32[128,512]{1,0:T(8,128)S(1)} %get-tuple-element.64.tail, ...), custom_call_target="tpu_custom_call" | custom-call | flops 3221225472 | bytes 9199616 | tf_op jit(solution)/shard_map/pallas_call | solution.py:338
  53.4 2.2 %collective-permute-done.15.before = f32[128,512]{1,0:T(8,128)S(1)} collective-permute-done((f32[128,512]{1,0:T(8,128)S(1)}, f32[128,512]{1,0:T(8,128)S(1)}, u32[]{:S(2)}, u32[]{:S(2)}) %collective-permute-start.15) | collective-permute-done | bytes 262176 | tf_op jit(solution)/shard_map/ppermute | solution.py:355
  55.6 0.0 collective-permute-done.16.after
  55.6 4.4 %shard_map.268 = f32[512,512]{1,0:T(8,128)} custom-call(f32[128,512]{1,0:T(8,128)S(1)} %collective-permute-done.15.before, f32[128,512]{1,0:T(8,128)S(1)} %collective-permute-done.16.after, f32[128,512]{1,0:T(8,128)S(1)} %get-tuple-element.65.head, f32[128,512]{1,0:T(8,128)S(1)} %get-tuple-element.64.tail, f32[256,512]{1,0:T(8,128)S(1)} %get-tuple-element.77.inner, ...), custom_call_target="tpu_custom_call" | custom-call | flops 805306368 | bytes 9183232 | tf_op jit(solution)/shard_map/pallas_call | solution.py:338
  (40 shorter events, 0.1 us)
Async XLA Ops:
  0.6 5.5 %copy-start = (f32[512,512]{1,0:T(8,128)S(1)}, f32[512,512]{1,0:T(8,128)}, u32[]{:S(2)}) copy-start(f32[512,512]{1,0:T(8,128)} %nodes.3) | copy-start | bytes 3145732
  0.6 5.5 %copy-start.13 = (f32[64,512]{1,0:T(8,128)S(1)}, f32[64,512]{1,0:T(8,128)}, u32[]{:S(2)}) copy-start(f32[64,512]{1,0:T(8,128)} %refs_2_.3) | copy-start | bytes 393220
  0.7 5.5 %copy-start.10 = (f32[256,512]{1,0:T(8,128)S(1)}, f32[256,512]{1,0:T(8,128)}, u32[]{:S(2)}) copy-start(f32[256,512]{1,0:T(8,128)} %wo.2) | copy-start | bytes 1572868
  0.7 5.5 %copy-start.24 = (f32[256]{0:T(256)S(1)}, f32[256]{0:T(256)}, u32[]{:S(2)}) copy-start(f32[256]{0:T(256)} %param.34) | copy-start | bytes 3076
  0.7 5.5 %copy-start.9 = (f32[512,256]{1,0:T(8,128)S(1)}, f32[512,256]{1,0:T(8,128)}, u32[]{:S(2)}) copy-start(f32[512,256]{1,0:T(8,128)} %wr.2) | copy-start | bytes 1572868
  0.7 5.5 %copy-start.8 = (f32[512,256]{1,0:T(8,128)S(1)}, f32[512,256]{1,0:T(8,128)}, u32[]{:S(2)}) copy-start(f32[512,256]{1,0:T(8,128)} %ws.2) | copy-start | bytes 1572868
  0.7 5.5 %copy-start.16 = (s32[64,7]{0,1:T(8,128)S(1)}, s32[64,7]{0,1:T(8,128)}, u32[]{:S(2)}) copy-start(s32[64,7]{0,1:T(8,128)} %param.28) | copy-start | bytes 5380
  0.7 20.7 %copy-start.17 = (f32[256]{0:T(256)S(1)}, f32[256]{0:T(256)}, u32[]{:S(2)}) copy-start(f32[256]{0:T(256)} %param.44) | copy-start | bytes 3076
  0.7 20.7 %copy-start.18 = (f32[256]{0:T(256)S(1)}, f32[256]{0:T(256)}, u32[]{:S(2)}) copy-start(f32[256]{0:T(256)} %param.49) | copy-start | bytes 3076
  0.7 20.7 %copy-start.20 = (f32[512]{0:T(512)S(1)}, f32[512]{0:T(512)}, u32[]{:S(2)}) copy-start(f32[512]{0:T(512)} %param.36) | copy-start | bytes 6148
  0.7 20.7 %copy-start.21 = (f32[512]{0:T(512)S(1)}, f32[512]{0:T(512)}, u32[]{:S(2)}) copy-start(f32[512]{0:T(512)} %param.41) | copy-start | bytes 6148
  0.7 20.7 %copy-start.22 = (f32[512]{0:T(512)S(1)}, f32[512]{0:T(512)}, u32[]{:S(2)}) copy-start(f32[512]{0:T(512)} %param.46) | copy-start | bytes 6148
  0.8 20.7 %copy-start.23 = (f32[512]{0:T(512)S(1)}, f32[512]{0:T(512)}, u32[]{:S(2)}) copy-start(f32[512]{0:T(512)} %param.51) | copy-start | bytes 6148
  0.8 20.7 %copy-start.25 = (f32[256]{0:T(256)S(1)}, f32[256]{0:T(256)}, u32[]{:S(2)}) copy-start(f32[256]{0:T(256)} %param.39) | copy-start | bytes 3076
  0.8 20.7 %copy-start.11 = (f32[512,256]{1,0:T(8,128)S(1)}, f32[512,256]{1,0:T(8,128)}, u32[]{:S(2)}) copy-start(f32[512,256]{1,0:T(8,128)} %refs_5_.2) | copy-start | bytes 1572868
  0.8 20.7 %copy-start.12 = (f32[512,256]{1,0:T(8,128)S(1)}, f32[512,256]{1,0:T(8,128)}, u32[]{:S(2)}) copy-start(f32[512,256]{1,0:T(8,128)} %refs_6_.2) | copy-start | bytes 1572868
  3.1 5.1 %copy-start.26 = (f32[392,256]{1,0:T(8,128)S(1)}, f32[392,256]{1,0:T(8,128)}, u32[]{:S(2)}) copy-start(f32[392,256]{1,0:T(8,128)} %get-tuple-element.49) | copy-start | bytes 1204228
  3.1 23.6 %copy-start.15 = (s32[512,6]{0,1:T(8,128)S(1)}, s32[512,6]{0,1:T(8,128)}, u32[]{:S(2)}) copy-start(s32[512,6]{0,1:T(8,128)} %param.30) | copy-start | bytes 36868
  3.1 23.6 %copy-start.19 = (s32[64,6]{0,1:T(8,128)S(1)}, s32[64,6]{0,1:T(8,128)}, u32[]{:S(2)}) copy-start(s32[64,6]{0,1:T(8,128)} %param.31) | copy-start | bytes 4612
  3.2 32.5 %copy-start.7 = (f32[256,512]{1,0:T(8,128)S(1)}, f32[256,512]{1,0:T(8,128)}, u32[]{:S(2)}) copy-start(f32[256,512]{1,0:T(8,128)} %refs_10_.1) | copy-start | bytes 1572868
  3.2 16.1 %collective-permute-start.4 = (f32[392,256]{1,0:T(8,128)}, f32[392,256]{1,0:T(8,128)S(1)}, u32[]{:S(2)}, u32[]{:S(2)}) collective-permute-start(f32[392,256]{1,0:T(8,128)} %get-tuple-element.47), channel_id=1, source_target_pairs={{0,2},{2,0},{1,3},{3,1},{4,6},{6,4},{5,7},{7,5},{8,10},{10,8},{9,1... | collective-permute-start | bytes 1204232 | tf_op jit(solution)/shard_map/ppermute | solution.py:355
  8.1 29.9 %copy-start.1 = (f32[512,256]{1,0:T(8,128)S(1)}, f32[512,256]{1,0:T(8,128)}, u32[]{:S(2)}) copy-start(f32[512,256]{1,0:T(8,128)} %refs_1_.3) | copy-start | bytes 1572868
  8.1 29.9 %copy-start.2 = (f32[512,256]{1,0:T(8,128)S(1)}, f32[512,256]{1,0:T(8,128)}, u32[]{:S(2)}) copy-start(f32[512,256]{1,0:T(8,128)} %refs_2_.5) | copy-start | bytes 1572868
  8.1 29.9 %copy-start.3 = (f32[256,512]{1,0:T(8,128)S(1)}, f32[256,512]{1,0:T(8,128)}, u32[]{:S(2)}) copy-start(f32[256,512]{1,0:T(8,128)} %refs_4_.4) | copy-start | bytes 1572868
  8.1 11.2 %collective-permute-start = (f32[64,512]{1,0:T(8,128)S(1)}, f32[64,512]{1,0:T(8,128)S(1)}, u32[]{:S(2)}, u32[]{:S(2)}) collective-permute-start(f32[64,512]{1,0:T(8,128)S(1)} %shard_map.257.refs_7_.refs_0_), channel_id=1, source_target_pairs={{0,2},{2,0},{1,3},{3,1},{4,6},{6,4},{5,7},{7,5},{8,10},{10,8},{9,1... | collective-permute-start | bytes 393224 | tf_op jit(solution)/shard_map/ppermute | solution.py:355
  8.2 23.6 %collective-permute-start.6 = (f32[392,256]{1,0:T(8,128)S(1)}, f32[392,256]{1,0:T(8,128)S(1)}, u32[]{:S(2)}, u32[]{:S(2)}) collective-permute-start(f32[392,256]{1,0:T(8,128)S(1)} %copy-done.26), channel_id=1, source_target_pairs={{0,2},{2,0},{1,3},{3,1},{4,6},{6,4},{5,7},{7,5},{8,10},{10,8},{9,1... | collective-permute-start | bytes 1204232 | tf_op jit(solution)/shard_map/ppermute | solution.py:355
  19.3 12.5 %collective-permute-start.5 = (f32[392,256]{1,0:T(8,128)S(1)}, f32[392,256]{1,0:T(8,128)S(1)}, u32[]{:S(2)}, u32[]{:S(2)}) collective-permute-start(f32[392,256]{1,0:T(8,128)S(1)} %collective-permute-done.4.refs_5_), channel_id=1, source_target_pairs={{0,16},{16,0},{1,17},{17,1},{2,18},{18,2},{3,19},{19,3},{4,20},{20... | collective-permute-start | bytes 1204232 | tf_op jit(solution)/shard_map/ppermute | solution.py:394
  22.1 5.8 %collective-permute-start.3 = (f32[64,256]{1,0:T(8,128)S(1)}, f32[64,256]{1,0:T(8,128)S(1)}, u32[]{:S(2)}, u32[]{:S(2)}) collective-permute-start(f32[64,256]{1,0:T(8,128)S(1)} %get-tuple-element.44.refs_2_.refs_0_), channel_id=1, source_target_pairs={{0,12},{4,0},{8,4},{12,8},{1,13},{5,1},{9,5},{13,9},{2,14},{6,2},{... | collective-permute-start | bytes 196616 | tf_op jit(solution)/shard_map/ppermute | solution.py:355
  25.7 5.2 %collective-permute-start.2 = (f32[64,256]{1,0:T(8,128)S(1)}, f32[64,256]{1,0:T(8,128)S(1)}, u32[]{:S(2)}, u32[]{:S(2)}) collective-permute-start(f32[64,256]{1,0:T(8,128)S(1)} %get-tuple-element.44.refs_2_.refs_0_), channel_id=1, source_target_pairs={{0,8},{4,12},{8,0},{12,4},{1,9},{5,13},{9,1},{13,5},{2,10},{6,14},... | collective-permute-start | bytes 196616 | tf_op jit(solution)/shard_map/ppermute | solution.py:355
  25.7 6.1 %collective-permute-start.1 = (f32[64,256]{1,0:T(8,128)S(1)}, f32[64,256]{1,0:T(8,128)S(1)}, u32[]{:S(2)}, u32[]{:S(2)}) collective-permute-start(f32[64,256]{1,0:T(8,128)S(1)} %get-tuple-element.44.refs_2_.refs_0_), channel_id=1, source_target_pairs={{0,4},{4,8},{8,12},{12,0},{1,5},{5,9},{9,13},{13,1},{2,6},{6,10},{... | collective-permute-start | bytes 196616 | tf_op jit(solution)/shard_map/ppermute | solution.py:355
  31.8 6.2 %collective-permute-start.12 = (f32[392,256]{1,0:T(8,128)S(1)}, f32[392,256]{1,0:T(8,128)S(1)}, u32[]{:S(2)}, u32[]{:S(2)}) collective-permute-start(f32[392,256]{1,0:T(8,128)S(1)} %collective-permute-done.4.refs_5_), channel_id=1, source_target_pairs={{0,1},{1,0},{2,3},{3,2},{4,5},{5,4},{6,7},{7,6},{8,9},{9,8},{10,11... | collective-permute-start | bytes 1204232 | tf_op jit(solution)/shard_map/ppermute | solution.py:355
  31.8 6.2 %collective-permute-start.13 = (f32[392,256]{1,0:T(8,128)S(1)}, f32[392,256]{1,0:T(8,128)S(1)}, u32[]{:S(2)}, u32[]{:S(2)}) collective-permute-start(f32[392,256]{1,0:T(8,128)S(1)} %collective-permute-done.5.refs_7_), channel_id=1, source_target_pairs={{0,1},{1,0},{2,3},{3,2},{4,5},{5,4},{6,7},{7,6},{8,9},{9,8},{10,11... | collective-permute-start | bytes 1204232 | tf_op jit(solution)/shard_map/ppermute | solution.py:355
  32.3 11.3 %collective-permute-start.14 = (f32[392,256]{1,0:T(8,128)S(1)}, f32[392,256]{1,0:T(8,128)S(1)}, u32[]{:S(2)}, u32[]{:S(2)}) collective-permute-start(f32[392,256]{1,0:T(8,128)S(1)} %collective-permute-done.6.refs_0_), channel_id=1, source_target_pairs={{0,4},{4,0},{8,12},{12,8},{1,5},{5,1},{9,13},{13,9},{2,6},{6,2},{1... | collective-permute-start | bytes 1204232 | tf_op jit(solution)/shard_map/ppermute | solution.py:394
  32.3 1.9 %collective-permute-start.7 = (f32[64,256]{1,0:T(8,128)S(1)}, f32[64,256]{1,0:T(8,128)S(1)}, u32[]{:S(2)}, u32[]{:S(2)}) collective-permute-start(f32[64,256]{1,0:T(8,128)S(1)} %get-tuple-element.44.refs_2_.refs_0_), channel_id=1, source_target_pairs={{0,1},{1,0},{2,3},{3,2},{4,5},{5,4},{6,7},{7,6},{8,9},{9,8},{10,11... | collective-permute-start | bytes 196616 | tf_op jit(solution)/shard_map/ppermute | solution.py:355
  32.4 2.0 %collective-permute-start.8 = (f32[64,256]{1,0:T(8,128)S(1)}, f32[64,256]{1,0:T(8,128)S(1)}, u32[]{:S(2)}, u32[]{:S(2)}) collective-permute-start(f32[64,256]{1,0:T(8,128)S(1)} %collective-permute-done.1.refs_1_), channel_id=1, source_target_pairs={{0,1},{1,0},{2,3},{3,2},{4,5},{5,4},{6,7},{7,6},{8,9},{9,8},{10,11... | collective-permute-start | bytes 196616 | tf_op jit(solution)/shard_map/ppermute | solution.py:355
  34.2 1.3 %collective-permute-start.9 = (f32[64,256]{1,0:T(8,128)S(1)}, f32[64,256]{1,0:T(8,128)S(1)}, u32[]{:S(2)}, u32[]{:S(2)}) collective-permute-start(f32[64,256]{1,0:T(8,128)S(1)} %collective-permute-done.2.refs_2_), channel_id=1, source_target_pairs={{0,1},{1,0},{2,3},{3,2},{4,5},{5,4},{6,7},{7,6},{8,9},{9,8},{10,11... | collective-permute-start | bytes 196616 | tf_op jit(solution)/shard_map/ppermute | solution.py:355
  34.3 1.3 %collective-permute-start.10 = (f32[64,256]{1,0:T(8,128)S(1)}, f32[64,256]{1,0:T(8,128)S(1)}, u32[]{:S(2)}, u32[]{:S(2)}) collective-permute-start(f32[64,256]{1,0:T(8,128)S(1)} %collective-permute-done.3.refs_3_), channel_id=1, source_target_pairs={{0,1},{1,0},{2,3},{3,2},{4,5},{5,4},{6,7},{7,6},{8,9},{9,8},{10,11... | collective-permute-start | bytes 196616 | tf_op jit(solution)/shard_map/ppermute | solution.py:355
  36.4 7.2 %copy-start.14 = (s32[512,3]{0,1:T(4,128)S(1)}, s32[512,3]{0,1:T(4,128)}, u32[]{:S(2)}) copy-start(s32[512,3]{0,1:T(4,128)} %param.29) | copy-start | bytes 18436
  36.4 5.8 %collective-permute-start.11 = (f32[64,512]{1,0:T(8,128)S(1)}, f32[64,512]{1,0:T(8,128)S(1)}, u32[]{:S(2)}, u32[]{:S(2)}) collective-permute-start(f32[64,512]{1,0:T(8,128)S(1)} %shard_map.262.refs_9_.refs_0_), channel_id=1, source_target_pairs={{0,2},{2,0},{1,3},{3,1},{4,6},{6,4},{5,7},{7,5},{8,10},{10,8},{9,1... | collective-permute-start | bytes 393224 | tf_op jit(solution)/shard_map/ppermute | solution.py:355
  45.7 2.6 %copy-start.4 = (f32[512,256]{1,0:T(8,128)S(1)}, f32[512,256]{1,0:T(8,128)}, u32[]{:S(2)}) copy-start(f32[512,256]{1,0:T(8,128)} %ws.3) | copy-start | bytes 1572868
  45.7 2.6 %copy-start.5 = (f32[512,256]{1,0:T(8,128)S(1)}, f32[512,256]{1,0:T(8,128)}, u32[]{:S(2)}) copy-start(f32[512,256]{1,0:T(8,128)} %wr.3) | copy-start | bytes 1572868
  45.7 2.6 %copy-start.6 = (f32[256,512]{1,0:T(8,128)S(1)}, f32[256,512]{1,0:T(8,128)}, u32[]{:S(2)}) copy-start(f32[256,512]{1,0:T(8,128)} %wo.3) | copy-start | bytes 1572868
  45.7 2.6 %collective-permute-start.17 = (f32[392,256]{1,0:T(8,128)S(1)}, f32[392,256]{1,0:T(8,128)S(1)}, u32[]{:S(2)}, u32[]{:S(2)}) collective-permute-start(f32[392,256]{1,0:T(8,128)S(1)} %collective-permute-done.6.refs_0_), channel_id=1, source_target_pairs={{0,1},{1,0},{2,3},{3,2},{4,5},{5,4},{6,7},{7,6},{8,9},{9,8},{10,11... | collective-permute-start | bytes 1204232 | tf_op jit(solution)/shard_map/ppermute | solution.py:355
  45.7 2.6 %collective-permute-start.18 = (f32[392,256]{1,0:T(8,128)S(1)}, f32[392,256]{1,0:T(8,128)S(1)}, u32[]{:S(2)}, u32[]{:S(2)}) collective-permute-start(f32[392,256]{1,0:T(8,128)S(1)} %collective-permute-done.14.refs_11_.refs_2_), channel_id=1, source_target_pairs={{0,1},{1,0},{2,3},{3,2},{4,5},{5,4},{6,7},{7,6},{8,9},{9,8},{10,11... | collective-permute-start | bytes 1204232 | tf_op jit(solution)/shard_map/ppermute | solution.py:355
  46.2 9.4 %collective-permute-start.16 = (f32[128,512]{1,0:T(8,128)S(1)}, f32[128,512]{1,0:T(8,128)S(1)}, u32[]{:S(2)}, u32[]{:S(2)}) collective-permute-start(f32[128,512]{1,0:T(8,128)S(1)} %get-tuple-element.65.head), channel_id=1, source_target_pairs={{0,13},{1,0},{4,1},{5,4},{8,5},{9,8},{12,9},{13,12},{2,15},{3,2},{... | collective-permute-start | bytes 786440 | tf_op jit(solution)/shard_map/ppermute | solution.py:355
  46.9 8.7 %collective-permute-start.15 = (f32[128,512]{1,0:T(8,128)S(1)}, f32[128,512]{1,0:T(8,128)S(1)}, u32[]{:S(2)}, u32[]{:S(2)}) collective-permute-start(f32[128,512]{1,0:T(8,128)S(1)} %get-tuple-element.64.tail), channel_id=1, source_target_pairs={{0,1},{1,4},{4,5},{5,8},{8,9},{9,12},{12,13},{13,0},{2,3},{3,6},{6... | collective-permute-start | bytes 786440 | tf_op jit(solution)/shard_map/ppermute | solution.py:355

commit v8 on v7

--- a/solution.py
+++ b/solution.py
@@ -25,9 +25,18 @@
     return jnp.dot(a, b, preferred_element_type=f32)
 
 
-def dot3(a, b_high, b_low):
-    a_high, a_low = split(a)
-    return dot(a_high, b_high) + (dot(a_high, b_low) + dot(a_low, b_high))
+def threefold(values):
+    high, low = split(values)
+    return jnp.concatenate([high, high, low], axis=1)
+
+
+def stacked(weights):
+    high, low = split(weights)
+    return jnp.concatenate([high, low, high], axis=0)
+
+
+def dot3(a, b_stacked):
+    return dot(threefold(a), b_stacked)
 
 
 def normed(values):
@@ -84,11 +93,11 @@
     wanted = upright(children[...])
     names = lax.broadcasted_iota(jnp.int32, (wanted.shape[0], nodes.shape[0]), 1)
     picks = one_hot(wanted, names)
-    sender_high, sender_low = split(0.5 * dot3(nodes[...], *split(ws[...])))
-    receivers = 0.5 * (dot3(coarse[...], *split(wr[...])) + bias[...])
-    picked = dot(picks, sender_high) + dot(picks, sender_low)
+    senders = jnp.concatenate(split(0.5 * dot3(nodes[...], stacked(ws[...]))), axis=0)
+    receivers = 0.5 * (dot3(coarse[...], stacked(wr[...])) + bias[...])
+    picked = dot(jnp.concatenate([picks, picks], axis=1), senders)
     hidden = silu_sum(picked, receivers, wanted.shape[1])
-    part[...] = dot3(hidden, *split(wo[...]))
+    part[...] = dot3(hidden, stacked(wo[...]))
 
 
 def stack_kernel(*refs):
@@ -133,6 +142,7 @@
     wanted = upright(coarse_links[...])
     rows = wanted.shape[0]
     lvls = lax.axis_size("lvl")
+    half = coarse_picks.shape[1] // 2
     column = lax.broadcasted_iota(jnp.int32, (rows, blocks), 1)
     for t in range(lvls):
         for s in range(patches):
@@ -140,13 +150,17 @@
             lvl = lax.rem(lax.axis_index("lvl") + lvls - t, lvls)
             first = (patch * lvls + lvl) * blocks
             at = (t * patches + s) * blocks
-            coarse_picks[:, at : at + blocks] = one_hot(wanted, column + first)
+            piece = one_hot(wanted, column + first)
+            coarse_picks[:, at : at + blocks] = piece
+            coarse_picks[:, half + at : half + at + blocks] = piece
     wanted = upright(bottom_links[...])
     size = rim * wanted.shape[1]
     names = lax.broadcasted_iota(jnp.int32, (rim, 3 * rim), 1)
     for i in range(wanted.shape[0] // rim):
-        strip = wanted[i * rim : (i + 1) * rim]
-        bottom_picks[i * size : (i + 1) * size, :] = one_hot(strip, names + i * rim)
+        picks = one_hot(wanted[i * rim : (i + 1) * rim], names + i * rim)
+        for j in range(6):
+            piece = picks[:, j // 2 * rim : (j // 2 + 1) * rim]
+            bottom_picks[i * size : (i + 1) * size, j * rim : (j + 1) * rim] = piece
 
 
 def coarse_project_kernel(count, *refs):
@@ -154,19 +168,17 @@
     coarse, gains, biases, ws, wr, updated, senders, receivers = refs
     rows = coarse[...] + gains[0:1] * normed(added(parts))
     updated[...] = rows
-    senders[...] = 0.5 * dot3(rows, *split(ws[...]))
-    receivers[...] = 0.5 * (dot3(rows, *split(wr[...])) + biases[0:1])
+    senders[...] = 0.5 * dot3(rows, stacked(ws[...]))
+    receivers[...] = 0.5 * (dot3(rows, stacked(wr[...])) + biases[0:1])
 
 
 def coarse_kernel(count, *refs):
     pieces, (all_picks, receivers, wo) = refs[:count], refs[count : count + 3]
     part = refs[-1]
     senders = jnp.concatenate([piece[...] for piece in pieces], axis=0)
-    sender_high, sender_low = split(senders)
-    picks = all_picks[...]
-    picked = dot(picks, sender_high) + dot(picks, sender_low)
-    hidden = silu_sum(picked, receivers[...], picks.shape[0] // receivers.shape[0])
-    part[...] = dot3(hidden, *split(wo[...]))
+    picked = dot(all_picks[...], jnp.concatenate(split(senders), axis=0))
+    hidden = silu_sum(picked, receivers[...], all_picks.shape[0] // receivers.shape[0])
+    part[...] = dot3(hidden, stacked(wo[...]))
 
 
 def fetched_shares(packs, axis):
@@ -181,27 +193,29 @@
                 yield next(left), lax.rem(sub + subs - s, subs), mine, p == 0 and t == 0
 
 
-def collect_in(own, packs, axis, at, high, low):
-    sub = lax.axis_index("sub")
-    high[sub], low[sub] = split(own[...])
+def put_stacked(values, out, first, columns):
+    high, low = split(values)
+    depth, rows = out.shape[0] // 3, values.shape[0]
+    for i, half in enumerate((high, low, high)):
+        out[pl.ds(pl.multiple_of(i * depth + first, 16), rows), columns] = half
+
+
+def collect_in(own, packs, axis, at, out):
+    everything = slice(0, own.shape[1])
+    put_stacked(own[...], out.at[lax.axis_index("sub")], 0, everything)
     share = own.shape[0] // shares(axis)[1]
     for pack, block, mine, _ in fetched_shares(packs, axis):
-        rows = pl.ds(pl.multiple_of(mine * share, share), share)
-        high[block, rows, :], low[block, rows, :] = split(pack[at : at + share, :])
-
-
-def collect_out(own, packs, axis, at, high, low):
-    sub = lax.axis_index("sub")
+        put_stacked(pack[at : at + share, :], out.at[block], mine * share, everything)
+
+
+def collect_out(own, packs, axis, at, out):
     width, latent = own.shape
-    rows = pl.ds(pl.multiple_of(sub * width, width), width)
-    high[rows, :], low[rows, :] = split(own[...])
+    put_stacked(own[...], out, lax.axis_index("sub") * width, slice(0, latent))
     thin = width // shares(axis)[1]
     for pack, block, mine, _ in fetched_shares(packs, axis):
-        rows = pl.ds(pl.multiple_of(block * width + mine * thin, thin), thin)
         for j in range(latent // width):
-            first, second = split(pack[at + j * thin : at + (j + 1) * thin, :])
-            high[rows, j * width : (j + 1) * width] = first
-            low[rows, j * width : (j + 1) * width] = second
+            part = pack[at + j * thin : at + (j + 1) * thin, :]
+            put_stacked(part, out, block * width + mine * thin, slice(j * width, (j + 1) * width))
 
 
 def collect_bias(own, packs, axis, at, out):
@@ -212,126 +226,139 @@
 
 
 def down_weights_kernel(count, nodes, ws, wr, biases, wo, *refs):
-    packs, refs = refs[:count], refs[count:]
-    receivers, ws_high, ws_low, wo_high, wo_low, wr_high, wr_low, bias_all = refs
+    packs, (receivers, ws_all, wo_all, wr_all, bias_all) = refs[:count], refs[count:]
     width = ws.shape[1]
     share = ws.shape[0] // shares("parts")[1]
-    collect_in(ws, packs, "parts", 0, ws_high, ws_low)
-    collect_in(wr, packs, "parts", share, wr_high, wr_low)
-    collect_out(wo, packs, "parts", 2 * share, wo_high, wo_low)
+    collect_in(ws, packs, "parts", 0, ws_all)
+    collect_in(wr, packs, "parts", share, wr_all)
+    collect_out(wo, packs, "parts", 2 * share, wo_all)
     collect_bias(biases[1:2], packs, "parts", 3 * share, bias_all)
-    for g in range(wr_high.shape[0]):
-        product = dot3(nodes[...], wr_high[g], wr_low[g])
-        receivers[:, g * width : (g + 1) * width] = 0.5 * (product + bias_all[g][0:1])
+    states = threefold(nodes[...])
+    for g in range(wr_all.shape[0]):
+        receivers[:, g * width : (g + 1) * width] = 0.5 * (dot(states, wr_all[g]) + bias_all[g][0:1])
 
 
 def bottom_weights_kernel(count, ws, wr, biases, wo, *refs):
-    packs, (ws_high, ws_low, wr_high, wr_low, wo_high, wo_low, bias_all) = refs[:count], refs[count:]
+    packs, (ws_all, wr_all, wo_all, bias_all) = refs[:count], refs[count:]
     share = ws.shape[0] // shares("patch")[1]
-    collect_in(ws, packs, "patch", 0, ws_high, ws_low)
-    collect_in(wr, packs, "patch", share, wr_high, wr_low)
-    collect_out(wo, packs, "patch", 2 * share, wo_high, wo_low)
+    collect_in(ws, packs, "patch", 0, ws_all)
+    collect_in(wr, packs, "patch", share, wr_all)
+    collect_out(wo, packs, "patch", 2 * share, wo_all)
     collect_bias(biases[2:3], packs, "patch", 3 * share, bias_all)
 
 
-def down_rows(nodes, receivers, sources, senders, wo_high, wo_low, gain):
+def down_rows(nodes, receivers, sources, senders, wo, gain):
     blocks = senders.shape[0] // 2
     column = lax.broadcasted_iota(jnp.int32, (nodes.shape[0], 2 * blocks), 1)
     names = jnp.where(column < blocks, column, column - blocks)
     picked = dot(one_hot(sources, names), senders)
     hidden = silu_sum(picked, receivers, sources.shape[1])
-    return nodes + gain * normed(dot3(hidden, wo_high, wo_low))
+    return nodes + gain * normed(dot3(hidden, wo))
 
 
 def down_edge_kernel(count, rim, *refs):
     parts, refs = refs[:count], refs[count:]
-    (coarse_up, gains, nodes, receivers, sources, ws_high, ws_low, wo_high, wo_low) = refs[:9]
-    new_coarse, senders, head, tail = refs[9:]
+    coarse_up, gains, nodes, receivers, sources, ws, wo = refs[:7]
+    new_coarse, senders, head, tail, held_here, sem = refs[7:]
     rows = coarse_up[...] + gains[1:2] * normed(added(parts))
-    new_coarse[...] = rows
+    held_here[...] = rows
+    move = pltpu.make_async_copy(held_here, new_coarse, sem)
+    move.start()
     blocks = rows.shape[0]
-    width = ws_high.shape[2]
-    for g in range(ws_high.shape[0]):
+    width = ws.shape[2]
+    left = threefold(rows)
+    for g in range(ws.shape[0]):
         columns = slice(g * width, (g + 1) * width)
-        high, low = split(0.5 * dot3(rows, ws_high[g], ws_low[g]))
+        high, low = split(0.5 * dot(left, ws[g]))
         senders[0:blocks, columns] = high
         senders[blocks : 2 * blocks, columns] = low
     total = nodes.shape[0]
     wanted = upright(sources[...])
     for out, place in ((head, slice(0, rim)), (tail, slice(total - rim, total))):
         out[...] = down_rows(
-            nodes[place], receivers[place], wanted[place], senders[...], wo_high[...], wo_low[...], gains[2:3]
+            nodes[place], receivers[place], wanted[place], senders[...], wo[...], gains[2:3]
         )
-
-
-def down_middle_kernel(rim, nodes, receivers, sources, senders, wo_high, wo_low, gains, middle):
+    move.wait()
+
+
+def down_middle_kernel(rim, nodes, receivers, sources, senders, wo, gains, middle):
     place = slice(rim, nodes.shape[0] - rim)
     middle[...] = down_rows(
-        nodes[place], receivers[place], upright(sources[...])[place], senders[...], wo_high[...], wo_low[...], gains[2:3]
-    )
-
-
-def bottom_rows(nodes, receivers, picks, sender_high, sender_low, wo_high, wo_low, gain):
-    half = wo_high.shape[0] // 2
+        nodes[place], receivers[place], upright(sources[...])[place], senders[...], wo[...], gains[2:3]
+    )
+
+
+def bottom_rows(nodes, receivers, picks, senders, wo, gain):
+    half = senders.shape[1] // 2
     hidden = []
     for place in (slice(0, half), slice(half, 2 * half)):
-        picked = dot(picks, sender_high[:, place]) + dot(picks, sender_low[:, place])
+        picked = dot(picks, senders[:, place])
         hidden.append(silu_sum(picked, receivers[:, place], picks.shape[0] // nodes.shape[0]))
-    return nodes + gain * normed(dot3(jnp.concatenate(hidden, axis=1), wo_high, wo_low))
-
-
-def bottom_middle_kernel(rim, head, middle, tail, picks, ws_high, ws_low, wr_high, wr_low, wo_high, wo_low, bias, gains, senders_high, senders_low, receivers, out):
+    return nodes + gain * normed(dot3(jnp.concatenate(hidden, axis=1), wo))
+
+
+def put_strips(values, rim, out, columns):
+    high, low = split(values)
+    for i in range(values.shape[0] // rim):
+        strip = slice(i * rim, (i + 1) * rim)
+        out[2 * i * rim : (2 * i + 1) * rim, columns] = high[strip]
+        out[(2 * i + 1) * rim : (2 * i + 2) * rim, columns] = low[strip]
+
+
+def bottom_middle_kernel(rim, head, middle, tail, picks, ws, wr, wo, bias, gains, senders, receivers, out):
     nodes = jnp.concatenate([head[...], middle[...], tail[...]], axis=0)
-    nodes_high, nodes_low = split(nodes)
-    width = ws_high.shape[2]
-    for g in range(ws_high.shape[0]):
+    left = threefold(nodes)
+    width = ws.shape[2]
+    for g in range(ws.shape[0]):
         columns = slice(g * width, (g + 1) * width)
-        product = dot(nodes_high, ws_high[g]) + (dot(nodes_high, ws_low[g]) + dot(nodes_low, ws_high[g]))
-        senders_high[:, columns], senders_low[:, columns] = split(0.5 * product)
-        product = dot(nodes_high, wr_high[g]) + (dot(nodes_high, wr_low[g]) + dot(nodes_low, wr_high[g]))
-        receivers[:, columns] = 0.5 * (product + bias[g][0:1])
+        put_strips(0.5 * dot(left, ws[g]), rim, senders, columns)
+        receivers[:, columns] = 0.5 * (dot(left, wr[g]) + bias[g][0:1])
     total = nodes.shape[0]
     size = picks.shape[0] * rim // total
-    for first in range(rim, total - rim, rim):
+    for i in range(1, total // rim - 1):
+        place = slice(i * rim, (i + 1) * rim)
+        inner = slice((i - 1) * rim, i * rim)
+        out[inner, :] = bottom_rows(
+            middle[inner], receivers[place], picks[i * size : (i + 1) * size],
+            senders[2 * (i - 1) * rim : 2 * (i + 2) * rim, :], wo[...], gains[3:4],
+        )
+
+
+def bottom_edge_kernel(rim, before, after, head, tail, inner, picks, senders, receivers, ws, wo, gains, out, outer, strips, sems):
+    total = receivers.shape[0]
+    size = picks.shape[0] * rim // total
+    moves = [pltpu.make_async_copy(inner, out.at[pl.ds(rim, total - 2 * rim)], sems.at[0])]
+    moves[0].start()
+    left = threefold(jnp.concatenate([before[...], after[...]], axis=0))
+    width = ws.shape[2]
+    for g in range(ws.shape[0]):
+        put_strips(0.5 * dot(left, ws[g]), rim, outer, slice(g * width, (g + 1) * width))
+    near = senders.shape[0]
+    for side, nodes in enumerate((head, tail)):
+        first = 0 if side == 0 else total - rim
         place = slice(first, first + rim)
-        reach = slice(first - rim, first + 2 * rim)
-        out[first - rim : first, :] = bottom_rows(
-            middle[first - rim : first], receivers[place], picks[first // rim * size : (first // rim + 1) * size],
-            senders_high[reach], senders_low[reach], wo_high[...], wo_low[...], gains[3:4],
+        beyond = outer[2 * side * rim : 2 * (side + 1) * rim, :]
+        reach = (
+            [beyond, senders[0 : 4 * rim, :]]
+            if side == 0
+            else [senders[near - 4 * rim : near, :], beyond]
         )
-
-
-def bottom_edge_kernel(rim, before, after, head, tail, inner, picks, senders_high, senders_low, receivers, ws_high, ws_low, wo_high, wo_low, gains, out):
-    total = out.shape[0]
-    size = picks.shape[0] * rim // total
-    out[rim : total - rim, :] = inner[...]
-    outer = split(jnp.concatenate([before[...], after[...]], axis=0))
-    projected = jnp.concatenate(
-        [
-            dot(outer[0], ws_high[g]) + (dot(outer[0], ws_low[g]) + dot(outer[1], ws_high[g]))
-            for g in range(ws_high.shape[0])
-        ],
-        axis=1,
-    )
-    outer_high, outer_low = split(0.5 * projected)
-    for side, (nodes, place, reach) in enumerate(
-        ((head, slice(0, rim), slice(0, 2 * rim)), (tail, slice(total - rim, total), slice(total - 2 * rim, total)))
-    ):
-        strip = slice(side * rim, (side + 1) * rim)
-        order = (lambda a, b: [a, b]) if side == 0 else (lambda a, b: [b, a])
-        high = jnp.concatenate(order(outer_high[strip], senders_high[reach]), axis=0)
-        low = jnp.concatenate(order(outer_low[strip], senders_low[reach]), axis=0)
-        out[place, :] = bottom_rows(
-            nodes[...], receivers[place], picks[place.start // rim * size : (place.start // rim + 1) * size],
-            high, low, wo_high[...], wo_low[...], gains[3:4],
+        strips[side * rim : (side + 1) * rim, :] = bottom_rows(
+            nodes[...], receivers[place], picks[first // rim * size : (first // rim + 1) * size],
+            jnp.concatenate(reach, axis=0), wo[...], gains[3:4],
         )
+        strip = strips.at[pl.ds(side * rim, rim)]
+        moves.append(pltpu.make_async_copy(strip, out.at[pl.ds(first, rim)], sems.at[1 + side]))
+        moves[-1].start()
+    for move in moves:
+        move.wait()
 
 
 whole = pl.BlockSpec(memory_space=pltpu.VMEM)
 away = pl.BlockSpec(memory_space=pl.ANY)
 
 
-def call(kernel, outs, operands, flops, scratch=(), far=(), unread=0, limit=limit_bytes):
+def call(kernel, outs, operands, flops, scratch=(), far=(), far_outs=(), unread=0, limit=limit_bytes):
     moved = sum(x.size * x.dtype.itemsize for x in (*outs, *operands))
     read = len(operands) - unread
     specs = [away if i in far else whole for i in range(read)] + [away] * unread
@@ -339,7 +366,7 @@
         (lambda *refs: kernel(*refs[:read], *refs[read + unread :])) if unread else kernel,
         out_shape=tuple(outs),
         in_specs=specs,
-        out_specs=tuple([whole] * len(outs)),
+        out_specs=tuple(away if i in far_outs else whole for i in range(len(outs))),
         scratch_shapes=list(scratch),
         compiler_params=pltpu.CompilerParams(vmem_limit_bytes=limit),
         cost_estimate=pl.CostEstimate(flops=int(flops), bytes_accessed=moved, transcendentals=0),
@@ -445,8 +472,8 @@
     subs = lax.axis_size("sub")
     hidden = width * subs
     rim = rows // 4
-    weights = [like((subs, latent, width), bf16)] * 2
-    outputs = [like((hidden, latent), bf16)] * 2
+    into = like((subs, 3 * latent, width), bf16)
+    out_of = like((3 * hidden, latent), bf16)
     bias_rows = like((subs, 8, width))
 
     columns = latent // width
@@ -502,7 +529,7 @@
     names = blocks * patches * lvls
     picks, bottom_picks = call(
         functools.partial(picks_kernel, rim, patches, blocks),
-        [like((coarse_links.size, names), bf16), like((bottom_links.size, 3 * rim), bf16)],
+        [like((coarse_links.size, 2 * names), bf16), like((bottom_links.size, 6 * rim), bf16)],
         [coarse_links.T, bottom_links.T, senders],
         coarse_links.size * names,
         unread=1,
@@ -519,49 +546,56 @@
         4 * coarse_links.size * names * width,
     )
     parts = sub_parts(part)
-    receivers, ws_high, ws_low, wo_high, wo_low = call(
+    receivers, ws, wo = call(
         functools.partial(down_weights_kernel, len(down_packs)),
-        [like((rows, hidden)), *weights, *outputs],
+        [like((rows, hidden)), into, out_of],
         [node_states, downward_sender, downward_receiver, biases, downward_output, *down_packs, part],
         6 * rows * latent * hidden,
-        [pltpu.VMEM((subs, latent, width), bf16)] * 2 + [pltpu.VMEM((subs, 8, width), f32)],
+        [pltpu.VMEM((subs, 3 * latent, width), bf16), pltpu.VMEM((subs, 8, width), f32)],
         unread=1,
     )
     new_coarse, senders, head, tail = call(
         functools.partial(down_edge_kernel, len(parts), rim),
         [like((blocks, latent)), like((2 * blocks, hidden), bf16), like((rim, latent)), like((rim, latent))],
-        [*parts, coarse_up, gains, node_states, receivers, down_sources.T, ws_high, ws_low, wo_high, wo_low, *(x for row in bottom_far for x in row)],
+        [*parts, coarse_up, gains, node_states, receivers, down_sources.T, ws, wo],
         6 * 2 * rim * latent * hidden,
-        unread=sum(map(len, bottom_far)),
+        [pltpu.VMEM((blocks, latent), f32), pltpu.SemaphoreType.DMA],
+        far_outs=(0,),
     )
     ring = ("patch", "lvl")
     before, after = shifted(tail, ring, 1), shifted(head, ring, -1)
     (middle,) = call(
         functools.partial(down_middle_kernel, rim),
         [like((rows - 2 * rim, latent))],
-        [node_states, receivers, down_sources.T, senders, wo_high, wo_low, gains],
+        [node_states, receivers, down_sources.T, senders, wo, gains],
         6 * (rows - 2 * rim) * latent * hidden,
     )
 
     bottom_near, bottom_far = held((bottom_near, bottom_far), head)
     bottom_packs = all_shares(bottom_near, bottom_far)
-    ws_high, ws_low, wr_high, wr_low, wo_high, wo_low, bias = call(
+    ws, wr, wo, bias = call(
         functools.partial(bottom_weights_kernel, len(bottom_packs)),
-        [*weights, *weights, *outputs, bias_rows],
+        [into, into, out_of, bias_rows],
         [bottom_sender, bottom_receiver, biases, bottom_output, *bottom_packs],
         latent * hidden,
     )
-    senders_high, senders_low, receivers, inner = call(
+    senders, receivers, inner = call(
         functools.partial(bottom_middle_kernel, rim),
-        [like((rows, hidden), bf16), like((rows, hidden), bf16), like((rows, hidden)), like((rows - 2 * rim, latent))],
-        [head, middle, tail, bottom_picks, ws_high, ws_low, wr_high, wr_low, wo_high, wo_low, bias, gains],
+        [like((2 * rows, hidden), bf16), like((rows, hidden)), like((rows - 2 * rim, latent))],
+        [head, middle, tail, bottom_picks, ws, wr, wo, bias, gains],
         (12 * rows + 12 * rows) * latent * hidden,
     )
     (new_nodes,) = call(
         functools.partial(bottom_edge_kernel, rim),
         [like((rows, latent))],
-        [before, after, head, tail, inner, bottom_picks, senders_high, senders_low, receivers, ws_high, ws_low, wo_high, wo_low, gains],
+        [before, after, head, tail, inner, bottom_picks, senders, receivers, ws, wo, gains],
         24 * rim * latent * hidden,
+        [
+            pltpu.VMEM((4 * rim, hidden), bf16),
+            pltpu.VMEM((2 * rim, latent), f32),
+            pltpu.SemaphoreType.DMA((3,)),
+        ],
+        far_outs=(0,),
     )
     return (new_nodes, new_coarse)
 

time: 60.2 us -> 58.3 us (0.968)
  waiting for transfers between devices: 21.6 us -> 19.7 us
  Pallas kernels: 21 us -> 19.9 us
  starting transfers between devices: 16.1 us -> 17.1 us
    ppermute x2, waiting for transfers between devices: 1.35 us -> 0.01 us  [over_partners(): lax.ppermute(share, axis, [(i, i - i % count + (i + p) % count) for i in...]
    pallas_call x12, Pallas kernels: 21 us -> 19.9 us  [call(): pl.pallas_call((lambda *refs: kernel(*refs[:read], *refs[read + unread:])...]
    ppermute x17, starting transfers between devices: 14 us -> 15 us  [shifted(): lax.ppermute(values, axis, [(i, (i + step) % count) for i in range(count)])]
  transfers between devices with their start and end apart: 19 -> 19, of which waited for: 9 -> 8; matrix products, arithmetic and copies ran while one was open for 0% -> 0% of each run, Pallas kernels for 20% -> 24%
where the time goes in v8:
time: 58.3 us; the launch traced here: 58.1 us
  Pallas kernels  19.9 us (34%)
  waiting for transfers between devices  19.7 us (34%)
  starting transfers between devices  17.1 us (29%)
  between operations  1.24 us (2%)
    pallas_call x12, Pallas kernels, call(): pl.pallas_call((lambda *refs: kernel(*refs[:read], *refs[read + unread:])...  19.9 us
    ppermute x17, waiting for transfers between devices, shifted(): lax.ppermute(values, axis, [(i, (i + step) % count) for i in range(count)])  19.7 us
    ppermute x17, starting transfers between devices, shifted(): lax.ppermute(values, axis, [(i, (i + step) % count) for i in range(count)])  15 us
    ppermute x2, starting transfers between devices, over_partners(): lax.ppermute(share, axis, [(i, i - i % count + (i + p) % count) for i in...  2.09 us
  transfers between devices with their start and end apart: 19, of which 8 were waited for; matrix products, arithmetic and copies ran while one was open for 0% of the time, Pallas kernels for 24%

profile of v8, /device:TPU:0, one launch (start us, length us, event | category | flops | bytes accessed | tf_op | source)
XLA Modules:
  0.0 58.1 jit_solution(10412666529803582105)
XLA Ops:
  0.7 2.3 %shard_map.261 = (f32[392,256]{1,0:T(8,128)}, f32[392,256]{1,0:T(8,128)}) custom-call(f32[512,256]{1,0:T(8,128)} %refs_1_.3, f32[512,256]{1,0:T(8,128)} %refs_2_.5, f32[256,512]{1,0:T(8,128)} %refs_4_.4, f32[1,256]{1,0:T(1,128)} %bitcast.16, f32[512,256]{1,0:T(8,128)} %ws.3, f32[512,256]{1,0:T(8,128)} %wr.3, f32[256,512]{1,0:T(8,128)} %wo.3, f32[1,256]{1,0:T(1,128)} %bitcast.18), custom_call_target="tpu_custom_call" | custom-call | flops 512 | bytes 3950592 | tf_op jit(solution)/shard_map/pallas_call | solution.py:365
  3.0 0.0 copy-start.17
  3.1 0.0 copy-start.18
  3.1 0.0 copy-start.20
  3.1 0.0 copy-start.21
  3.1 0.0 copy-start.22
  3.1 0.0 copy-start.23
  3.1 0.0 copy-start.25
  3.1 0.0 copy-start.10
  3.1 0.0 copy-start.11
  3.1 3.0 %collective-permute-start.4 = (f32[392,256]{1,0:T(8,128)}, f32[392,256]{1,0:T(8,128)S(1)}, u32[]{:S(2)}, u32[]{:S(2)}) collective-permute-start(f32[392,256]{1,0:T(8,128)} %get-tuple-element.41), channel_id=1, source_target_pairs={{0,2},{2,0},{1,3},{3,1},{4,6},{6,4},{5,7},{7,5},{8,10},{10,8},{9,1... | collective-permute-start | bytes 1204232 | tf_op jit(solution)/shard_map/ppermute | solution.py:382
  6.2 0.0 copy-start.15
  6.2 0.0 copy-start.19
  6.2 1.8 %shard_map.257.refs_7_.refs_0_ = f32[64,512]{1,0:T(8,128)S(1)} custom-call(f32[512,512]{1,0:T(8,128)S(1)} %copy-done, f32[64,512]{1,0:T(8,128)S(1)} %copy-done.13, s32[7,64]{1,0:T(8,128)S(1)} %bitcast.15, f32[512,256]{1,0:T(8,128)S(1)} %copy-done.7, f32[512,256]{1,0:T(8,128)S(1)} %copy-done.8, f32[1,256]{1,0:T(1,128)S(1)} %bitcast.25, f32[256,512]{1,0:T(8,128)S(1)} %copy-done.9), custom_call_target="tpu_custom_call" | custom-call | flops 402653184 | bytes 2886400 | tf_op jit(solution)/shard_map/pallas_call | solution.py:365
  8.0 0.0 copy-start.12
  8.1 0.1 collective-permute-start
  8.2 2.0 %collective-permute-start.6 = (f32[392,256]{1,0:T(8,128)S(1)}, f32[392,256]{1,0:T(8,128)S(1)}, u32[]{:S(2)}, u32[]{:S(2)}) collective-permute-start(f32[392,256]{1,0:T(8,128)S(1)} %copy-done.26), channel_id=1, source_target_pairs={{0,2},{2,0},{1,3},{3,1},{4,6},{6,4},{5,7},{7,5},{8,10},{10,8},{9,1... | collective-permute-start | bytes 1204232 | tf_op jit(solution)/shard_map/ppermute | solution.py:382
  10.2 9.1 %collective-permute-done.refs_1_ = f32[64,512]{1,0:T(8,128)S(1)} collective-permute-done((f32[64,512]{1,0:T(8,128)S(1)}, f32[64,512]{1,0:T(8,128)S(1)}, u32[]{:S(2)}, u32[]{:S(2)}) %collective-permute-start) | collective-permute-done | bytes 131104 | tf_op jit(solution)/shard_map/ppermute | solution.py:382
  19.3 0.0 collective-permute-done.4.refs_5_
  19.3 2.1 %collective-permute-start.5 = (f32[392,256]{1,0:T(8,128)S(1)}, f32[392,256]{1,0:T(8,128)S(1)}, u32[]{:S(2)}, u32[]{:S(2)}) collective-permute-start(f32[392,256]{1,0:T(8,128)S(1)} %collective-permute-done.4.refs_5_), channel_id=1, source_target_pairs={{0,16},{16,0},{1,17},{17,1},{2,18},{18,2},{3,19},{19,3},{4,20},{20... | collective-permute-start | bytes 1204232 | tf_op jit(solution)/shard_map/ppermute | solution.py:421
  21.5 0.0 copy-start.1
  21.5 0.0 copy-start.2
  21.5 0.0 copy-start.3
  21.5 0.6 %shard_map.259 = (f32[64,512]{1,0:T(8,128)S(1)}, f32[64,256]{1,0:T(8,128)S(1)}, f32[64,256]{1,0:T(8,128)S(1)}) custom-call(f32[64,512]{1,0:T(8,128)S(1)} %shard_map.257.refs_7_.refs_0_, f32[64,512]{1,0:T(8,128)S(1)} %collective-permute-done.refs_1_, f32[64,512]{1,0:T(8,128)S(1)} %copy-done.13, f32[4,512]{1,0:T(4,128)S(1)} %get-tuple-element.36.refs_3_.gains, ...), custom_call_target="tpu_custom_call" | custom-call | flops 100663296 | bytes 1715200 | tf_op jit(solution)/shard_map/pallas_call | solution.py:365
  22.1 3.6 %collective-permute-start.3 = (f32[64,256]{1,0:T(8,128)S(1)}, f32[64,256]{1,0:T(8,128)S(1)}, u32[]{:S(2)}, u32[]{:S(2)}) collective-permute-start(f32[64,256]{1,0:T(8,128)S(1)} %get-tuple-element.38.refs_2_.refs_0_), channel_id=1, source_target_pairs={{0,12},{4,0},{8,4},{12,8},{1,13},{5,1},{9,5},{13,9},{2,14},{6,2},{... | collective-permute-start | bytes 196616 | tf_op jit(solution)/shard_map/ppermute | solution.py:382
  25.7 0.0 collective-permute-start.2
  25.7 1.0 %collective-permute-start.1 = (f32[64,256]{1,0:T(8,128)S(1)}, f32[64,256]{1,0:T(8,128)S(1)}, u32[]{:S(2)}, u32[]{:S(2)}) collective-permute-start(f32[64,256]{1,0:T(8,128)S(1)} %get-tuple-element.38.refs_2_.refs_0_), channel_id=1, source_target_pairs={{0,4},{4,8},{8,12},{12,0},{1,5},{5,9},{9,13},{13,1},{2,6},{6,10},{... | collective-permute-start | bytes 196616 | tf_op jit(solution)/shard_map/ppermute | solution.py:382
  26.8 1.1 %shard_map.260 = (bf16[384,1024]{1,0:T(8,128)(2,1)S(1)}, bf16[3072,768]{1,0:T(8,128)(2,1)S(1)}) custom-call(s32[6,64]{1,0:T(8,128)S(1)} %bitcast.20, s32[6,512]{1,0:T(8,128)S(1)} %bitcast.14, f32[64,256]{1,0:T(8,128)S(1)} %get-tuple-element.38.refs_2_.refs_0_), custom_call_target="tpu_custom_call" | custom-call | flops 196608 | bytes 5584384 | tf_op jit(solution)/shard_map/pallas_call | solution.py:365
  27.9 0.0 collective-permute-done.3.refs_3_
  27.9 3.0 %collective-permute-done.2.refs_2_ = f32[64,256]{1,0:T(8,128)S(1)} collective-permute-done((f32[64,256]{1,0:T(8,128)S(1)}, f32[64,256]{1,0:T(8,128)S(1)}, u32[]{:S(2)}, u32[]{:S(2)}) %collective-permute-start.2) | collective-permute-done | bytes 65568 | tf_op jit(solution)/shard_map/ppermute | solution.py:382
  30.9 0.9 %collective-permute-done.1.refs_1_ = f32[64,256]{1,0:T(8,128)S(1)} collective-permute-done((f32[64,256]{1,0:T(8,128)S(1)}, f32[64,256]{1,0:T(8,128)S(1)}, u32[]{:S(2)}, u32[]{:S(2)}) %collective-permute-start.1) | collective-permute-done | bytes 65568 | tf_op jit(solution)/shard_map/ppermute | solution.py:382
  31.8 0.0 collective-permute-done.6.refs_0_
  31.8 0.0 collective-permute-done.5.refs_7_
  31.8 0.0 collective-permute-start.12
  31.8 0.5 collective-permute-start.13
  32.3 0.0 collective-permute-start.16
  32.3 0.1 collective-permute-start.7
  32.4 0.4 collective-permute-start.8
  32.8 1.4 %collective-permute-done.7.refs_4_ = f32[64,256]{1,0:T(8,128)S(1)} collective-permute-done((f32[64,256]{1,0:T(8,128)S(1)}, f32[64,256]{1,0:T(8,128)S(1)}, u32[]{:S(2)}, u32[]{:S(2)}) %collective-permute-start.7) | collective-permute-done | bytes 65568 | tf_op jit(solution)/shard_map/ppermute | solution.py:382
  34.2 0.1 collective-permute-start.9
  34.4 0.0 collective-permute-done.8.refs_5_
  34.4 0.4 collective-permute-start.10
  34.7 0.7 %collective-permute-done.9.refs_6_ = f32[64,256]{1,0:T(8,128)S(1)} collective-permute-done((f32[64,256]{1,0:T(8,128)S(1)}, f32[64,256]{1,0:T(8,128)S(1)}, u32[]{:S(2)}, u32[]{:S(2)}) %collective-permute-start.9) | collective-permute-done | bytes 65568 | tf_op jit(solution)/shard_map/ppermute | solution.py:382
  35.5 0.2 collective-permute-done.10.refs_7_
  35.6 0.8 %shard_map.262.refs_9_.refs_0_ = f32[64,512]{1,0:T(8,128)S(1)} custom-call(f32[64,256]{1,0:T(8,128)S(1)} %get-tuple-element.38.refs_2_.refs_0_, f32[64,256]{1,0:T(8,128)S(1)} %collective-permute-done.1.refs_1_, f32[64,256]{1,0:T(8,128)S(1)} %collective-permute-done.2.refs_2_, f32[64,256]{1,0:T(8,128)S(1)} %collective-permute-done.3.refs_3_, ...), custom_call_target="tpu_custom_call" | custom-call | flops 201326592 | bytes 2031616 | tf_op jit(solution)/shard_map/pallas_call | solution.py:365
  36.4 0.0 copy-start.14
  36.4 1.6 %collective-permute-start.11 = (f32[64,512]{1,0:T(8,128)S(1)}, f32[64,512]{1,0:T(8,128)S(1)}, u32[]{:S(2)}, u32[]{:S(2)}) collective-permute-start(f32[64,512]{1,0:T(8,128)S(1)} %shard_map.262.refs_9_.refs_0_), channel_id=1, source_target_pairs={{0,2},{2,0},{1,3},{3,1},{4,6},{6,4},{5,7},{7,5},{8,10},{10,8},{9,1... | collective-permute-start | bytes 393224 | tf_op jit(solution)/shard_map/ppermute | solution.py:382
  38.0 0.0 collective-permute-done.12.refs_6_
  38.0 0.0 collective-permute-done.13.refs_8_
  38.0 1.7 %shard_map.263 = (f32[512,512]{1,0:T(8,128)S(1)}, bf16[2,1536,256]{2,1,0:T(8,128)(2,1)S(1)}, bf16[1536,512]{1,0:T(8,128)(2,1)S(1)}) custom-call(f32[512,512]{1,0:T(8,128)S(1)} %copy-done, f32[512,256]{1,0:T(8,128)S(1)} %copy-done.1, f32[512,256]{1,0:T(8,128)S(1)} %copy-done.2, f32[3,256]{1,0:T(4,128)S(1)} %get-tuple-element.37.refs_4_.refs_3_.biases, ...), custom_call_target="tpu_custom_call" | custom-call | flops 805306368 | bytes 8555520 | tf_op jit(solution)/shard_map/pallas_call | solution.py:365
  39.7 2.5 %collective-permute-done.11.refs_1_ = f32[64,512]{1,0:T(8,128)S(1)} collective-permute-done((f32[64,512]{1,0:T(8,128)S(1)}, f32[64,512]{1,0:T(8,128)S(1)}, u32[]{:S(2)}, u32[]{:S(2)}) %collective-permute-start.11) | collective-permute-done | bytes 131104 | tf_op jit(solution)/shard_map/ppermute | solution.py:382
  42.2 1.9 %shard_map.264 = (f32[64,512]{1,0:T(8,128)}, bf16[128,512]{1,0:T(8,128)(2,1)S(1)}, f32[128,512]{1,0:T(8,128)S(1)}, f32[128,512]{1,0:T(8,128)S(1)}) custom-call(f32[64,512]{1,0:T(8,128)S(1)} %shard_map.262.refs_9_.refs_0_, f32[64,512]{1,0:T(8,128)S(1)} %collective-permute-done.11.refs_1_, f32[64,512]{1,0:T(8,128)S(1)} %get-tuple-element.49.refs_2_, ...), custom_call_target="tpu_custom_call" | custom-call | flops 402653184 | bytes 6436864 | tf_op jit(solution)/shard_map/pallas_call | solution.py:365
  44.1 0.0 collective-permute-done.16.refs_2_
  44.1 0.1 collective-permute-start.17
  44.2 0.5 collective-permute-start.18
  44.7 1.6 %collective-permute-start.15 = (f32[128,512]{1,0:T(8,128)S(1)}, f32[128,512]{1,0:T(8,128)S(1)}, u32[]{:S(2)}, u32[]{:S(2)}) collective-permute-start(f32[128,512]{1,0:T(8,128)S(1)} %get-tuple-element.56.head), channel_id=1, source_target_pairs={{0,13},{1,0},{4,1},{5,4},{8,5},{9,8},{12,9},{13,12},{2,15},{3,2},{... | collective-permute-start | bytes 786440 | tf_op jit(solution)/shard_map/ppermute | solution.py:382
  46.3 0.0 collective-permute-start.14
  46.4 1.3 %shard_map.265.middle = f32[256,512]{1,0:T(8,128)S(1)} custom-call(f32[512,512]{1,0:T(8,128)S(1)} %copy-done, f32[512,512]{1,0:T(8,128)S(1)} %get-tuple-element.52.refs_5_.receivers, s32[3,512]{1,0:T(4,128)S(1)} %bitcast.13, bf16[128,512]{1,0:T(8,128)(2,1)S(1)} %get-tuple-element.57.senders, bf16[1536,512]{1,0:T(8,128)(2,1)S(1)} %get-tuple-element.54.refs_8_.wo, ...), custom_call_target="tpu_custom_call" | custom-call | flops 402653184 | bytes 4339712 | tf_op jit(solution)/shard_map/pallas_call | solution.py:365
  47.7 0.0 collective-permute-done.17.refs_1_
  47.7 0.0 collective-permute-done.18.refs_3_
  47.8 0.6 shard_map.266
  48.3 4.1 %shard_map.267 = (bf16[1024,512]{1,0:T(8,128)(2,1)S(1)}, f32[512,512]{1,0:T(8,128)S(1)}, f32[256,512]{1,0:T(8,128)S(1)}) custom-call(f32[128,512]{1,0:T(8,128)S(1)} %get-tuple-element.56.head, f32[256,512]{1,0:T(8,128)S(1)} %shard_map.265.middle, f32[128,512]{1,0:T(8,128)S(1)} %get-tuple-element.55.tail, bf16[3072,768]{1,0:T(8,128)(2,1)S(1)} %get-tuple-element.58.picks, ...), custom_call_target="tpu_custom_call" | custom-call | flops 3221225472 | bytes 13131776 | tf_op jit(solution)/shard_map/pallas_call | solution.py:365
  52.4 1.8 %collective-permute-done.14.before = f32[128,512]{1,0:T(8,128)S(1)} collective-permute-done((f32[128,512]{1,0:T(8,128)S(1)}, f32[128,512]{1,0:T(8,128)S(1)}, u32[]{:S(2)}, u32[]{:S(2)}) %collective-permute-start.14) | collective-permute-done | bytes 262176 | tf_op jit(solution)/shard_map/ppermute | solution.py:382
  54.2 3.7 %shard_map.268 = f32[512,512]{1,0:T(8,128)} custom-call(f32[128,512]{1,0:T(8,128)S(1)} %collective-permute-done.14.before, f32[128,512]{1,0:T(8,128)S(1)} %collective-permute-done.15.after, f32[128,512]{1,0:T(8,128)S(1)} %get-tuple-element.56.head, f32[128,512]{1,0:T(8,128)S(1)} %get-tuple-element.55.tail, f32[256,512]{1,0:T(8,128)S(1)} %get-tuple-element.66.inner, ...), custom_call_target="tpu_custom_call" | custom-call | flops 805306368 | bytes 12591104 | tf_op jit(solution)/shard_map/pallas_call | solution.py:365
  (40 shorter events, 0.1 us)
Async XLA Ops:
  0.6 5.5 %copy-start = (f32[512,512]{1,0:T(8,128)S(1)}, f32[512,512]{1,0:T(8,128)}, u32[]{:S(2)}) copy-start(f32[512,512]{1,0:T(8,128)} %nodes.3) | copy-start | bytes 3145732
  0.6 5.5 %copy-start.7 = (f32[512,256]{1,0:T(8,128)S(1)}, f32[512,256]{1,0:T(8,128)}, u32[]{:S(2)}) copy-start(f32[512,256]{1,0:T(8,128)} %ws.2) | copy-start | bytes 1572868
  0.7 5.5 %copy-start.8 = (f32[512,256]{1,0:T(8,128)S(1)}, f32[512,256]{1,0:T(8,128)}, u32[]{:S(2)}) copy-start(f32[512,256]{1,0:T(8,128)} %wr.2) | copy-start | bytes 1572868
  0.7 5.5 %copy-start.9 = (f32[256,512]{1,0:T(8,128)S(1)}, f32[256,512]{1,0:T(8,128)}, u32[]{:S(2)}) copy-start(f32[256,512]{1,0:T(8,128)} %wo.2) | copy-start | bytes 1572868
  0.7 5.5 %copy-start.13 = (f32[64,512]{1,0:T(8,128)S(1)}, f32[64,512]{1,0:T(8,128)}, u32[]{:S(2)}) copy-start(f32[64,512]{1,0:T(8,128)} %refs_2_.3) | copy-start | bytes 393220
  0.7 5.5 %copy-start.16 = (s32[64,7]{0,1:T(8,128)S(1)}, s32[64,7]{0,1:T(8,128)}, u32[]{:S(2)}) copy-start(s32[64,7]{0,1:T(8,128)} %param.28) | copy-start | bytes 5380
  0.7 5.5 %copy-start.24 = (f32[256]{0:T(256)S(1)}, f32[256]{0:T(256)}, u32[]{:S(2)}) copy-start(f32[256]{0:T(256)} %param.34) | copy-start | bytes 3076
  3.0 5.1 %copy-start.26 = (f32[392,256]{1,0:T(8,128)S(1)}, f32[392,256]{1,0:T(8,128)}, u32[]{:S(2)}) copy-start(f32[392,256]{1,0:T(8,128)} %get-tuple-element.43) | copy-start | bytes 1204228
  3.0 18.3 %copy-start.17 = (f32[256]{0:T(256)S(1)}, f32[256]{0:T(256)}, u32[]{:S(2)}) copy-start(f32[256]{0:T(256)} %param.44) | copy-start | bytes 3076
  3.1 18.3 %copy-start.18 = (f32[256]{0:T(256)S(1)}, f32[256]{0:T(256)}, u32[]{:S(2)}) copy-start(f32[256]{0:T(256)} %param.49) | copy-start | bytes 3076
  3.1 18.3 %copy-start.20 = (f32[512]{0:T(512)S(1)}, f32[512]{0:T(512)}, u32[]{:S(2)}) copy-start(f32[512]{0:T(512)} %param.36) | copy-start | bytes 6148
  3.1 18.3 %copy-start.21 = (f32[512]{0:T(512)S(1)}, f32[512]{0:T(512)}, u32[]{:S(2)}) copy-start(f32[512]{0:T(512)} %param.41) | copy-start | bytes 6148
  3.1 18.3 %copy-start.22 = (f32[512]{0:T(512)S(1)}, f32[512]{0:T(512)}, u32[]{:S(2)}) copy-start(f32[512]{0:T(512)} %param.46) | copy-start | bytes 6148
  3.1 18.3 %copy-start.23 = (f32[512]{0:T(512)S(1)}, f32[512]{0:T(512)}, u32[]{:S(2)}) copy-start(f32[512]{0:T(512)} %param.51) | copy-start | bytes 6148
  3.1 18.3 %copy-start.25 = (f32[256]{0:T(256)S(1)}, f32[256]{0:T(256)}, u32[]{:S(2)}) copy-start(f32[256]{0:T(256)} %param.39) | copy-start | bytes 3076
  3.1 18.3 %copy-start.10 = (f32[512,256]{1,0:T(8,128)S(1)}, f32[512,256]{1,0:T(8,128)}, u32[]{:S(2)}) copy-start(f32[512,256]{1,0:T(8,128)} %refs_5_.2) | copy-start | bytes 1572868
  3.1 18.3 %copy-start.11 = (f32[512,256]{1,0:T(8,128)S(1)}, f32[512,256]{1,0:T(8,128)}, u32[]{:S(2)}) copy-start(f32[512,256]{1,0:T(8,128)} %refs_6_.2) | copy-start | bytes 1572868
  3.1 16.1 %collective-permute-start.4 = (f32[392,256]{1,0:T(8,128)}, f32[392,256]{1,0:T(8,128)S(1)}, u32[]{:S(2)}, u32[]{:S(2)}) collective-permute-start(f32[392,256]{1,0:T(8,128)} %get-tuple-element.41), channel_id=1, source_target_pairs={{0,2},{2,0},{1,3},{3,1},{4,6},{6,4},{5,7},{7,5},{8,10},{10,8},{9,1... | collective-permute-start | bytes 1204232 | tf_op jit(solution)/shard_map/ppermute | solution.py:382
  6.2 20.6 %copy-start.15 = (s32[512,6]{0,1:T(8,128)S(1)}, s32[512,6]{0,1:T(8,128)}, u32[]{:S(2)}) copy-start(s32[512,6]{0,1:T(8,128)} %param.30) | copy-start | bytes 36868
  6.2 20.6 %copy-start.19 = (s32[64,6]{0,1:T(8,128)S(1)}, s32[64,6]{0,1:T(8,128)}, u32[]{:S(2)}) copy-start(s32[64,6]{0,1:T(8,128)} %param.31) | copy-start | bytes 4612
  8.0 27.6 %copy-start.12 = (f32[256,512]{1,0:T(8,128)S(1)}, f32[256,512]{1,0:T(8,128)}, u32[]{:S(2)}) copy-start(f32[256,512]{1,0:T(8,128)} %refs_10_.1) | copy-start | bytes 1572868
  8.1 11.2 %collective-permute-start = (f32[64,512]{1,0:T(8,128)S(1)}, f32[64,512]{1,0:T(8,128)S(1)}, u32[]{:S(2)}, u32[]{:S(2)}) collective-permute-start(f32[64,512]{1,0:T(8,128)S(1)} %shard_map.257.refs_7_.refs_0_), channel_id=1, source_target_pairs={{0,2},{2,0},{1,3},{3,1},{4,6},{6,4},{5,7},{7,5},{8,10},{10,8},{9,1... | collective-permute-start | bytes 393224 | tf_op jit(solution)/shard_map/ppermute | solution.py:382
  8.2 23.6 %collective-permute-start.6 = (f32[392,256]{1,0:T(8,128)S(1)}, f32[392,256]{1,0:T(8,128)S(1)}, u32[]{:S(2)}, u32[]{:S(2)}) collective-permute-start(f32[392,256]{1,0:T(8,128)S(1)} %copy-done.26), channel_id=1, source_target_pairs={{0,2},{2,0},{1,3},{3,1},{4,6},{6,4},{5,7},{7,5},{8,10},{10,8},{9,1... | collective-permute-start | bytes 1204232 | tf_op jit(solution)/shard_map/ppermute | solution.py:382
  19.3 12.5 %collective-permute-start.5 = (f32[392,256]{1,0:T(8,128)S(1)}, f32[392,256]{1,0:T(8,128)S(1)}, u32[]{:S(2)}, u32[]{:S(2)}) collective-permute-start(f32[392,256]{1,0:T(8,128)S(1)} %collective-permute-done.4.refs_5_), channel_id=1, source_target_pairs={{0,16},{16,0},{1,17},{17,1},{2,18},{18,2},{3,19},{19,3},{4,20},{20... | collective-permute-start | bytes 1204232 | tf_op jit(solution)/shard_map/ppermute | solution.py:421
  21.5 16.5 %copy-start.1 = (f32[512,256]{1,0:T(8,128)S(1)}, f32[512,256]{1,0:T(8,128)}, u32[]{:S(2)}) copy-start(f32[512,256]{1,0:T(8,128)} %refs_1_.3) | copy-start | bytes 1572868
  21.5 16.5 %copy-start.2 = (f32[512,256]{1,0:T(8,128)S(1)}, f32[512,256]{1,0:T(8,128)}, u32[]{:S(2)}) copy-start(f32[512,256]{1,0:T(8,128)} %refs_2_.5) | copy-start | bytes 1572868
  21.5 16.5 %copy-start.3 = (f32[256,512]{1,0:T(8,128)S(1)}, f32[256,512]{1,0:T(8,128)}, u32[]{:S(2)}) copy-start(f32[256,512]{1,0:T(8,128)} %refs_4_.4) | copy-start | bytes 1572868
  22.1 5.8 %collective-permute-start.3 = (f32[64,256]{1,0:T(8,128)S(1)}, f32[64,256]{1,0:T(8,128)S(1)}, u32[]{:S(2)}, u32[]{:S(2)}) collective-permute-start(f32[64,256]{1,0:T(8,128)S(1)} %get-tuple-element.38.refs_2_.refs_0_), channel_id=1, source_target_pairs={{0,12},{4,0},{8,4},{12,8},{1,13},{5,1},{9,5},{13,9},{2,14},{6,2},{... | collective-permute-start | bytes 196616 | tf_op jit(solution)/shard_map/ppermute | solution.py:382
  25.7 5.2 %collective-permute-start.2 = (f32[64,256]{1,0:T(8,128)S(1)}, f32[64,256]{1,0:T(8,128)S(1)}, u32[]{:S(2)}, u32[]{:S(2)}) collective-permute-start(f32[64,256]{1,0:T(8,128)S(1)} %get-tuple-element.38.refs_2_.refs_0_), channel_id=1, source_target_pairs={{0,8},{4,12},{8,0},{12,4},{1,9},{5,13},{9,1},{13,5},{2,10},{6,14},... | collective-permute-start | bytes 196616 | tf_op jit(solution)/shard_map/ppermute | solution.py:382
  25.7 6.1 %collective-permute-start.1 = (f32[64,256]{1,0:T(8,128)S(1)}, f32[64,256]{1,0:T(8,128)S(1)}, u32[]{:S(2)}, u32[]{:S(2)}) collective-permute-start(f32[64,256]{1,0:T(8,128)S(1)} %get-tuple-element.38.refs_2_.refs_0_), channel_id=1, source_target_pairs={{0,4},{4,8},{8,12},{12,0},{1,5},{5,9},{9,13},{13,1},{2,6},{6,10},{... | collective-permute-start | bytes 196616 | tf_op jit(solution)/shard_map/ppermute | solution.py:382
  31.8 6.2 %collective-permute-start.12 = (f32[392,256]{1,0:T(8,128)S(1)}, f32[392,256]{1,0:T(8,128)S(1)}, u32[]{:S(2)}, u32[]{:S(2)}) collective-permute-start(f32[392,256]{1,0:T(8,128)S(1)} %collective-permute-done.4.refs_5_), channel_id=1, source_target_pairs={{0,1},{1,0},{2,3},{3,2},{4,5},{5,4},{6,7},{7,6},{8,9},{9,8},{10,11... | collective-permute-start | bytes 1204232 | tf_op jit(solution)/shard_map/ppermute | solution.py:382
  31.8 6.2 %collective-permute-start.13 = (f32[392,256]{1,0:T(8,128)S(1)}, f32[392,256]{1,0:T(8,128)S(1)}, u32[]{:S(2)}, u32[]{:S(2)}) collective-permute-start(f32[392,256]{1,0:T(8,128)S(1)} %collective-permute-done.5.refs_7_), channel_id=1, source_target_pairs={{0,1},{1,0},{2,3},{3,2},{4,5},{5,4},{6,7},{7,6},{8,9},{9,8},{10,11... | collective-permute-start | bytes 1204232 | tf_op jit(solution)/shard_map/ppermute | solution.py:382
  32.3 11.8 %collective-permute-start.16 = (f32[392,256]{1,0:T(8,128)S(1)}, f32[392,256]{1,0:T(8,128)S(1)}, u32[]{:S(2)}, u32[]{:S(2)}) collective-permute-start(f32[392,256]{1,0:T(8,128)S(1)} %collective-permute-done.6.refs_0_), channel_id=1, source_target_pairs={{0,4},{4,0},{8,12},{12,8},{1,5},{5,1},{9,13},{13,9},{2,6},{6,2},{1... | collective-permute-start | bytes 1204232 | tf_op jit(solution)/shard_map/ppermute | solution.py:421
  32.3 1.9 %collective-permute-start.7 = (f32[64,256]{1,0:T(8,128)S(1)}, f32[64,256]{1,0:T(8,128)S(1)}, u32[]{:S(2)}, u32[]{:S(2)}) collective-permute-start(f32[64,256]{1,0:T(8,128)S(1)} %get-tuple-element.38.refs_2_.refs_0_), channel_id=1, source_target_pairs={{0,1},{1,0},{2,3},{3,2},{4,5},{5,4},{6,7},{7,6},{8,9},{9,8},{10,11... | collective-permute-start | bytes 196616 | tf_op jit(solution)/shard_map/ppermute | solution.py:382
  32.4 2.0 %collective-permute-start.8 = (f32[64,256]{1,0:T(8,128)S(1)}, f32[64,256]{1,0:T(8,128)S(1)}, u32[]{:S(2)}, u32[]{:S(2)}) collective-permute-start(f32[64,256]{1,0:T(8,128)S(1)} %collective-permute-done.1.refs_1_), channel_id=1, source_target_pairs={{0,1},{1,0},{2,3},{3,2},{4,5},{5,4},{6,7},{7,6},{8,9},{9,8},{10,11... | collective-permute-start | bytes 196616 | tf_op jit(solution)/shard_map/ppermute | solution.py:382
  34.2 1.3 %collective-permute-start.9 = (f32[64,256]{1,0:T(8,128)S(1)}, f32[64,256]{1,0:T(8,128)S(1)}, u32[]{:S(2)}, u32[]{:S(2)}) collective-permute-start(f32[64,256]{1,0:T(8,128)S(1)} %collective-permute-done.2.refs_2_), channel_id=1, source_target_pairs={{0,1},{1,0},{2,3},{3,2},{4,5},{5,4},{6,7},{7,6},{8,9},{9,8},{10,11... | collective-permute-start | bytes 196616 | tf_op jit(solution)/shard_map/ppermute | solution.py:382
  34.4 1.3 %collective-permute-start.10 = (f32[64,256]{1,0:T(8,128)S(1)}, f32[64,256]{1,0:T(8,128)S(1)}, u32[]{:S(2)}, u32[]{:S(2)}) collective-permute-start(f32[64,256]{1,0:T(8,128)S(1)} %collective-permute-done.3.refs_3_), channel_id=1, source_target_pairs={{0,1},{1,0},{2,3},{3,2},{4,5},{5,4},{6,7},{7,6},{8,9},{9,8},{10,11... | collective-permute-start | bytes 196616 | tf_op jit(solution)/shard_map/ppermute | solution.py:382
  36.4 5.8 %copy-start.14 = (s32[512,3]{0,1:T(4,128)S(1)}, s32[512,3]{0,1:T(4,128)}, u32[]{:S(2)}) copy-start(s32[512,3]{0,1:T(4,128)} %param.29) | copy-start | bytes 18436
  36.4 5.8 %collective-permute-start.11 = (f32[64,512]{1,0:T(8,128)S(1)}, f32[64,512]{1,0:T(8,128)S(1)}, u32[]{:S(2)}, u32[]{:S(2)}) collective-permute-start(f32[64,512]{1,0:T(8,128)S(1)} %shard_map.262.refs_9_.refs_0_), channel_id=1, source_target_pairs={{0,2},{2,0},{1,3},{3,1},{4,6},{6,4},{5,7},{7,5},{8,10},{10,8},{9,1... | collective-permute-start | bytes 393224 | tf_op jit(solution)/shard_map/ppermute | solution.py:382
  44.1 3.6 %collective-permute-start.17 = (f32[392,256]{1,0:T(8,128)S(1)}, f32[392,256]{1,0:T(8,128)S(1)}, u32[]{:S(2)}, u32[]{:S(2)}) collective-permute-start(f32[392,256]{1,0:T(8,128)S(1)} %collective-permute-done.6.refs_0_), channel_id=1, source_target_pairs={{0,1},{1,0},{2,3},{3,2},{4,5},{5,4},{6,7},{7,6},{8,9},{9,8},{10,11... | collective-permute-start | bytes 1204232 | tf_op jit(solution)/shard_map/ppermute | solution.py:382
  44.2 3.5 %collective-permute-start.18 = (f32[392,256]{1,0:T(8,128)S(1)}, f32[392,256]{1,0:T(8,128)S(1)}, u32[]{:S(2)}, u32[]{:S(2)}) collective-permute-start(f32[392,256]{1,0:T(8,128)S(1)} %collective-permute-done.16.refs_2_), channel_id=1, source_target_pairs={{0,1},{1,0},{2,3},{3,2},{4,5},{5,4},{6,7},{7,6},{8,9},{9,8},{10,11... | collective-permute-start | bytes 1204232 | tf_op jit(solution)/shard_map/ppermute | solution.py:382
  44.7 9.5 %collective-permute-start.15 = (f32[128,512]{1,0:T(8,128)S(1)}, f32[128,512]{1,0:T(8,128)S(1)}, u32[]{:S(2)}, u32[]{:S(2)}) collective-permute-start(f32[128,512]{1,0:T(8,128)S(1)} %get-tuple-element.56.head), channel_id=1, source_target_pairs={{0,13},{1,0},{4,1},{5,4},{8,5},{9,8},{12,9},{13,12},{2,15},{3,2},{... | collective-permute-start | bytes 786440 | tf_op jit(solution)/shard_map/ppermute | solution.py:382
  46.3 7.9 %collective-permute-start.14 = (f32[128,512]{1,0:T(8,128)S(1)}, f32[128,512]{1,0:T(8,128)S(1)}, u32[]{:S(2)}, u32[]{:S(2)}) collective-permute-start(f32[128,512]{1,0:T(8,128)S(1)} %get-tuple-element.55.tail), channel_id=1, source_target_pairs={{0,1},{1,4},{4,5},{5,8},{8,9},{9,12},{12,13},{13,0},{2,3},{3,6},{6... | collective-permute-start | bytes 786440 | tf_op jit(solution)/shard_map/ppermute | solution.py:382
  46.3 1.4 %copy-start.4 = (f32[512,256]{1,0:T(8,128)S(1)}, f32[512,256]{1,0:T(8,128)}, u32[]{:S(2)}) copy-start(f32[512,256]{1,0:T(8,128)} %ws.3) | copy-start | bytes 1572868
  46.3 1.4 %copy-start.5 = (f32[512,256]{1,0:T(8,128)S(1)}, f32[512,256]{1,0:T(8,128)}, u32[]{:S(2)}) copy-start(f32[512,256]{1,0:T(8,128)} %wr.3) | copy-start | bytes 1572868
  46.3 1.4 %copy-start.6 = (f32[256,512]{1,0:T(8,128)S(1)}, f32[256,512]{1,0:T(8,128)}, u32[]{:S(2)}) copy-start(f32[256,512]{1,0:T(8,128)} %wo.3) | copy-start | bytes 1572868

commit v9 on v8

--- a/solution.py
+++ b/solution.py
@@ -11,8 +11,7 @@
 f32 = jnp.float32
 bf16 = jnp.bfloat16
 limit_bytes = 12 * 1024 * 1024
-share_limit = 58 * 1000 * 1000
-up_limit = 50 * 1000 * 1000
+tight_limit = 64 * 1000 * 1000
 most_direct = 4
 
 
@@ -89,14 +88,43 @@
     return moves
 
 
-def upward_kernel(nodes, coarse, children, ws, wr, bias, wo, part):
+def strips(source, target, count):
+    rows = source.shape[0] // count
+    return [
+        (source.at[pl.ds(i * rows, rows)], target.at[pl.ds(i * rows, rows)]) for i in range(count)
+    ]
+
+
+def upward_kernel(nodes_hbm, coarse_hbm, ws_hbm, wr_hbm, wo_hbm, children, bias, part, nodes, coarse, ws, wr, wo, senders, sems):
+    cuts = 4
+    moves = started(
+        strips(ws_hbm, ws, cuts)
+        + strips(nodes_hbm, nodes, cuts)
+        + [(coarse_hbm, coarse)]
+        + strips(wr_hbm, wr, cuts)
+        + strips(wo_hbm, wo, cuts),
+        sems,
+    )
     wanted = upright(children[...])
     names = lax.broadcasted_iota(jnp.int32, (wanted.shape[0], nodes.shape[0]), 1)
     picks = one_hot(wanted, names)
-    senders = jnp.concatenate(split(0.5 * dot3(nodes[...], stacked(ws[...]))), axis=0)
+    picks = jnp.concatenate([picks, picks], axis=1)
+    for move in moves[:cuts]:
+        move.wait()
+    ws_stacked = stacked(ws[...])
+    rows, total = nodes.shape[0] // cuts, nodes.shape[0]
+    for i in range(cuts):
+        moves[cuts + i].wait()
+        first, last = i * rows, (i + 1) * rows
+        high, low = split(0.5 * dot3(nodes[first:last], ws_stacked))
+        senders[first:last] = high
+        senders[total + first : total + last] = low
+    for move in moves[2 * cuts : 3 * cuts + 1]:
+        move.wait()
     receivers = 0.5 * (dot3(coarse[...], stacked(wr[...])) + bias[...])
-    picked = dot(jnp.concatenate([picks, picks], axis=1), senders)
-    hidden = silu_sum(picked, receivers, wanted.shape[1])
+    hidden = silu_sum(dot(picks, senders[...]), receivers, wanted.shape[1])
+    for move in moves[3 * cuts + 1 :]:
+        move.wait()
     part[...] = dot3(hidden, stacked(wo[...]))
 
 
@@ -487,11 +515,21 @@
         upward_kernel,
         [like((blocks, latent))],
         [
-            node_states, coarse_states, children.T, upward_sender, upward_receiver,
-            upward_bias[None], upward_output,
+            node_states, coarse_states, upward_sender, upward_receiver, upward_output,
+            children.T, upward_bias[None],
         ],
         6 * rows * latent * width,
-        limit=up_limit,
+        [
+            pltpu.VMEM((rows, latent), f32),
+            pltpu.VMEM((blocks, latent), f32),
+            pltpu.VMEM((latent, width), f32),
+            pltpu.VMEM((latent, width), f32),
+            pltpu.VMEM((width, latent), f32),
+            pltpu.VMEM((2 * rows, width), bf16),
+            pltpu.SemaphoreType.DMA((17,)),
+        ],
+        far=range(5),
+        limit=tight_limit,
     )
     parts = sub_parts(part)
     down_own = (downward_sender, downward_receiver, downward_output, downward_bias[None])
@@ -503,7 +541,7 @@
         latent,
         [pltpu.SemaphoreType.DMA((6 + 2 * columns,))],
         far=range(8),
-        limit=share_limit,
+        limit=tight_limit,
     )
     gains, biases = call(
         stack_kernel,
@@ -515,10 +553,7 @@
         latent * hidden,
         unread=1,
     )
-    down_near = over_sub(down_pack)
-    down_near = held(down_near, parts[-1])
-    bottom_near = over_sub(bottom_pack)
-    down_far = over_partners(down_near, "parts")
+    down_near, bottom_near = over_sub(down_pack), over_sub(bottom_pack)
     coarse_up, senders, receivers = call(
         functools.partial(coarse_project_kernel, len(parts)),
         [like((blocks, latent)), like((blocks, width)), like((blocks, width))],
@@ -531,28 +566,31 @@
         functools.partial(picks_kernel, rim, patches, blocks),
         [like((coarse_links.size, 2 * names), bf16), like((bottom_links.size, 6 * rim), bf16)],
         [coarse_links.T, bottom_links.T, senders],
-        coarse_links.size * names,
+        10**11,
         unread=1,
     )
-    pieces, (picks, bottom_picks, down_near, down_far, bottom_near) = coarse_pieces(
-        senders, (picks, bottom_picks, down_near, down_far, bottom_near)
-    )
-    down_packs = all_shares(down_near, down_far)
-    bottom_far = over_partners(bottom_near, "patch")
+    pieces, (picks, bottom_picks, down_near) = coarse_pieces(
+        senders, (picks, bottom_picks, down_near)
+    )
+    down_far = over_partners(down_near, "parts")
     (part,) = call(
         functools.partial(coarse_kernel, len(pieces)),
         [like((blocks, latent))],
-        [*pieces, picks, receivers, coarse_output],
+        [*pieces, picks, receivers, coarse_output, *bottom_near],
         4 * coarse_links.size * names * width,
+        unread=len(bottom_near),
     )
     parts = sub_parts(part)
+    bottom_near = held(bottom_near, part)
+    bottom_far = over_partners(bottom_near, "patch")
+    down_packs = all_shares(*held((down_near, down_far), parts[-1]))
     receivers, ws, wo = call(
         functools.partial(down_weights_kernel, len(down_packs)),
         [like((rows, hidden)), into, out_of],
-        [node_states, downward_sender, downward_receiver, biases, downward_output, *down_packs, part],
+        [node_states, downward_sender, downward_receiver, biases, downward_output, *down_packs, part, *(x for row in bottom_far for x in row)],
         6 * rows * latent * hidden,
         [pltpu.VMEM((subs, 3 * latent, width), bf16), pltpu.VMEM((subs, 8, width), f32)],
-        unread=1,
+        unread=1 + sum(map(len, bottom_far)),
     )
     new_coarse, senders, head, tail = call(
         functools.partial(down_edge_kernel, len(parts), rim),

time: 58.3 us -> 61.2 us (1.050)
  Pallas kernels: 19.9 us -> 23.2 us
  waiting for transfers between devices: 19.7 us -> 18.5 us
  starting transfers between devices: 17.1 us -> 18 us
    ppermute x17, waiting for transfers between devices: 19.7 us -> 13.1 us  [shifted(): lax.ppermute(values, axis, [(i, (i + step) % count) for i in range(count)])]
    ppermute x2, waiting for transfers between devices: 0.01 us -> 5.35 us  [over_partners(): lax.ppermute(share, axis, [(i, i - i % count + (i + p) % count) for i in...]
    pallas_call x12, Pallas kernels: 19.9 us -> 23.2 us  [call(): pl.pallas_call((lambda *refs: kernel(*refs[:read], *refs[read + unread:])...]
    ppermute x2, starting transfers between devices: 2.09 us -> 3.1 us  [over_partners(): lax.ppermute(share, axis, [(i, i - i % count + (i + p) % count) for i in...]
  transfers between devices with their start and end apart: 19 -> 19, of which waited for: 8 -> 7; matrix products, arithmetic and copies ran while one was open for 0% -> 0% of each run, Pallas kernels for 24% -> 18%
where the time goes in v9:
time: 61.2 us; the launch traced here: 60.9 us
  Pallas kernels  23.2 us (38%)
  waiting for transfers between devices  18.5 us (30%)
  starting transfers between devices  18 us (29%)
  between operations  1.17 us (2%)
    pallas_call x12, Pallas kernels, call(): pl.pallas_call((lambda *refs: kernel(*refs[:read], *refs[read + unread:])...  23.2 us
    ppermute x17, starting transfers between devices, shifted(): lax.ppermute(values, axis, [(i, (i + step) % count) for i in range(count)])  14.9 us
    ppermute x17, waiting for transfers between devices, shifted(): lax.ppermute(values, axis, [(i, (i + step) % count) for i in range(count)])  13.1 us
    ppermute x2, waiting for transfers between devices, over_partners(): lax.ppermute(share, axis, [(i, i - i % count + (i + p) % count) for i in...  5.35 us
    ppermute x2, starting transfers between devices, over_partners(): lax.ppermute(share, axis, [(i, i - i % count + (i + p) % count) for i in...  3.1 us
  transfers between devices with their start and end apart: 19, of which 7 were waited for; matrix products, arithmetic and copies ran while one was open for 0% of the time, Pallas kernels for 18%

profile of v9, /device:TPU:0, one launch (start us, length us, event | category | flops | bytes accessed | tf_op | source)
XLA Modules:
  0.0 60.9 jit_solution(6475709346291267778)
XLA Ops:
  0.6 5.1 %shard_map.257.refs_7_.refs_0_ = f32[64,512]{1,0:T(8,128)} custom-call(f32[512,512]{1,0:T(8,128)} %nodes.1, f32[64,512]{1,0:T(8,128)} %refs_2_.3, f32[512,256]{1,0:T(8,128)} %ws_hbm.1, f32[512,256]{1,0:T(8,128)} %wr_hbm.1, f32[256,512]{1,0:T(8,128)} %wo_hbm.1, s32[7,64]{1,0:T(8,128)} %bitcast.25, f32[1,256]{1,0:T(1,128)} %bitcast.26), custom_call_target="tpu_custom_call" | custom-call | flops 402653184 | bytes 2886400 | tf_op jit(solution)/shard_map/pallas_call | solution.py:393
  5.8 3.0 %collective-permute-start = (f32[64,512]{1,0:T(8,128)}, f32[64,512]{1,0:T(8,128)S(1)}, u32[]{:S(2)}, u32[]{:S(2)}) collective-permute-start(f32[64,512]{1,0:T(8,128)} %shard_map.257.refs_7_.refs_0_), channel_id=1, source_target_pairs={{0,2},{2,0},{1,3},{3,1},{4,6},{6,4},{5,7},{7,5},{8,10},{10,8},{9,1... | collective-permute-start | bytes 393224 | tf_op jit(solution)/shard_map/ppermute | solution.py:410
  8.8 0.0 copy-start.16
  8.8 0.0 copy-start.17
  8.8 0.0 copy-start.18
  8.8 0.0 copy-start.19
  8.8 0.0 copy-start.9
  8.8 0.0 copy-start.10
  8.9 0.0 copy-start.11
  8.9 2.3 %shard_map.261 = (f32[392,256]{1,0:T(8,128)}, f32[392,256]{1,0:T(8,128)}) custom-call(f32[512,256]{1,0:T(8,128)} %refs_1_.3, f32[512,256]{1,0:T(8,128)} %refs_2_.5, f32[256,512]{1,0:T(8,128)} %refs_4_.4, f32[1,256]{1,0:T(1,128)} %bitcast.14, f32[512,256]{1,0:T(8,128)} %ws.1, f32[512,256]{1,0:T(8,128)} %wr.1, f32[256,512]{1,0:T(8,128)} %wo.1, f32[1,256]{1,0:T(1,128)} %bitcast.16), custom_call_target="tpu_custom_call" | custom-call | flops 512 | bytes 3950592 | tf_op jit(solution)/shard_map/pallas_call | solution.py:393
  11.2 0.0 copy-start.20
  11.2 0.0 copy-start.21
  11.2 0.1 collective-permute-start.4
  11.3 2.0 %collective-permute-start.9 = (f32[392,256]{1,0:T(8,128)}, f32[392,256]{1,0:T(8,128)S(1)}, u32[]{:S(2)}, u32[]{:S(2)}) collective-permute-start(f32[392,256]{1,0:T(8,128)} %get-tuple-element.47), channel_id=1, source_target_pairs={{0,2},{2,0},{1,3},{3,1},{4,6},{6,4},{5,7},{7,5},{8,10},{10,8},{9,1... | collective-permute-start | bytes 1204232 | tf_op jit(solution)/shard_map/ppermute | solution.py:410
  13.3 0.0 copy-done.13
  13.3 0.0 copy-done.15
  13.3 0.0 collective-permute-done.refs_1_
  13.4 0.6 shard_map.259
  14.0 3.7 %collective-permute-start.3 = (f32[64,256]{1,0:T(8,128)S(1)}, f32[64,256]{1,0:T(8,128)S(1)}, u32[]{:S(2)}, u32[]{:S(2)}) collective-permute-start(f32[64,256]{1,0:T(8,128)S(1)} %get-tuple-element.38.refs_2_.refs_0_), channel_id=1, source_target_pairs={{0,12},{4,0},{8,4},{12,8},{1,13},{5,1},{9,5},{13,9},{2,14},{6,2},{... | collective-permute-start | bytes 196616 | tf_op jit(solution)/shard_map/ppermute | solution.py:410
  17.6 0.0 collective-permute-start.2
  17.6 1.0 %collective-permute-start.1 = (f32[64,256]{1,0:T(8,128)S(1)}, f32[64,256]{1,0:T(8,128)S(1)}, u32[]{:S(2)}, u32[]{:S(2)}) collective-permute-start(f32[64,256]{1,0:T(8,128)S(1)} %get-tuple-element.38.refs_2_.refs_0_), channel_id=1, source_target_pairs={{0,4},{4,8},{8,12},{12,0},{1,5},{5,9},{9,13},{13,1},{2,6},{6,10},{... | collective-permute-start | bytes 196616 | tf_op jit(solution)/shard_map/ppermute | solution.py:410
  18.7 1.1 %shard_map.260 = (bf16[384,1024]{1,0:T(8,128)(2,1)S(1)}, bf16[3072,768]{1,0:T(8,128)(2,1)S(1)}) custom-call(s32[6,64]{1,0:T(8,128)S(1)} %bitcast.24, s32[6,512]{1,0:T(8,128)S(1)} %bitcast.23, f32[64,256]{1,0:T(8,128)S(1)} %get-tuple-element.38.refs_2_.refs_0_), custom_call_target="tpu_custom_call" | custom-call | flops 99999997952 | bytes 5584384 | tf_op jit(solution)/shard_map/pallas_call | solution.py:393
  19.8 0.0 copy-start
  19.8 0.0 copy-start.4
  19.8 0.0 copy-start.5
  19.8 0.0 collective-permute-done.3.refs_3_
  19.9 2.9 %collective-permute-done.2.refs_2_ = f32[64,256]{1,0:T(8,128)S(1)} collective-permute-done((f32[64,256]{1,0:T(8,128)S(1)}, f32[64,256]{1,0:T(8,128)S(1)}, u32[]{:S(2)}, u32[]{:S(2)}) %collective-permute-start.2) | collective-permute-done | bytes 65568 | tf_op jit(solution)/shard_map/ppermute | solution.py:410
  22.8 0.9 %collective-permute-done.1.refs_1_ = f32[64,256]{1,0:T(8,128)S(1)} collective-permute-done((f32[64,256]{1,0:T(8,128)S(1)}, f32[64,256]{1,0:T(8,128)S(1)}, u32[]{:S(2)}, u32[]{:S(2)}) %collective-permute-start.1) | collective-permute-done | bytes 65568 | tf_op jit(solution)/shard_map/ppermute | solution.py:410
  23.7 0.0 collective-permute-done.4.refs_5_
  23.7 1.5 %collective-permute-start.11 = (f32[392,256]{1,0:T(8,128)S(1)}, f32[392,256]{1,0:T(8,128)S(1)}, u32[]{:S(2)}, u32[]{:S(2)}) collective-permute-start(f32[392,256]{1,0:T(8,128)S(1)} %collective-permute-done.4.refs_5_), channel_id=1, source_target_pairs={{0,16},{16,0},{1,17},{17,1},{2,18},{18,2},{3,19},{19,3},{4,20},{20... | collective-permute-start | bytes 1204232 | tf_op jit(solution)/shard_map/ppermute | solution.py:449
  25.2 0.0 collective-permute-start.5
  25.2 0.5 collective-permute-start.6
  25.7 0.0 collective-permute-start.7
  25.7 0.7 %collective-permute-done.5.refs_4_ = f32[64,256]{1,0:T(8,128)S(1)} collective-permute-done((f32[64,256]{1,0:T(8,128)S(1)}, f32[64,256]{1,0:T(8,128)S(1)}, u32[]{:S(2)}, u32[]{:S(2)}) %collective-permute-start.5) | collective-permute-done | bytes 65568 | tf_op jit(solution)/shard_map/ppermute | solution.py:410
  26.5 0.2 collective-permute-start.8
  26.6 4.2 %collective-permute-done.9.refs_11_.refs_0_ = f32[392,256]{1,0:T(8,128)S(1)} collective-permute-done((f32[392,256]{1,0:T(8,128)}, f32[392,256]{1,0:T(8,128)S(1)}, u32[]{:S(2)}, u32[]{:S(2)}) %collective-permute-start.9) | collective-permute-done | bytes 401440 | tf_op jit(solution)/shard_map/ppermute | solution.py:410
  30.8 0.0 collective-permute-done.6.refs_5_
  30.8 0.0 collective-permute-done.7.refs_6_
  30.8 0.0 collective-permute-done.8.refs_7_
  30.8 0.8 %shard_map.262.refs_9_.refs_0_ = f32[64,512]{1,0:T(8,128)S(1)} custom-call(f32[64,256]{1,0:T(8,128)S(1)} %get-tuple-element.38.refs_2_.refs_0_, f32[64,256]{1,0:T(8,128)S(1)} %collective-permute-done.1.refs_1_, f32[64,256]{1,0:T(8,128)S(1)} %collective-permute-done.2.refs_2_, f32[64,256]{1,0:T(8,128)S(1)} %collective-permute-done.3.refs_3_, ...), custom_call_target="tpu_custom_call" | custom-call | flops 201326592 | bytes 2433024 | tf_op jit(solution)/shard_map/pallas_call | solution.py:393
  31.6 0.0 copy-start.12
  31.6 0.7 %collective-permute-start.10 = (f32[64,512]{1,0:T(8,128)S(1)}, f32[64,512]{1,0:T(8,128)S(1)}, u32[]{:S(2)}, u32[]{:S(2)}) collective-permute-start(f32[64,512]{1,0:T(8,128)S(1)} %shard_map.262.refs_9_.refs_0_), channel_id=1, source_target_pairs={{0,2},{2,0},{1,3},{3,1},{4,6},{6,4},{5,7},{7,5},{8,10},{10,8},{9,1... | collective-permute-start | bytes 393224 | tf_op jit(solution)/shard_map/ppermute | solution.py:410
  32.3 1.6 %collective-permute-start.14 = (f32[392,256]{1,0:T(8,128)S(1)}, f32[392,256]{1,0:T(8,128)S(1)}, u32[]{:S(2)}, u32[]{:S(2)}) collective-permute-start(f32[392,256]{1,0:T(8,128)S(1)} %collective-permute-done.9.refs_11_.refs_0_), channel_id=1, source_target_pairs={{0,4},{4,0},{8,12},{12,8},{1,5},{5,1},{9,13},{13,9},{2,6},{6,2},{1... | collective-permute-start | bytes 1204232 | tf_op jit(solution)/shard_map/ppermute | solution.py:449
  33.9 2.8 %collective-permute-done.10.refs_1_ = f32[64,512]{1,0:T(8,128)S(1)} collective-permute-done((f32[64,512]{1,0:T(8,128)S(1)}, f32[64,512]{1,0:T(8,128)S(1)}, u32[]{:S(2)}, u32[]{:S(2)}) %collective-permute-start.10) | collective-permute-done | bytes 131104 | tf_op jit(solution)/shard_map/ppermute | solution.py:410
  36.7 0.0 collective-permute-done.11.refs_7_
  36.7 0.0 collective-permute-start.12
  36.7 0.5 collective-permute-start.13
  37.2 5.4 %collective-permute-done.14.refs_10_.refs_2_ = f32[392,256]{1,0:T(8,128)S(1)} collective-permute-done((f32[392,256]{1,0:T(8,128)S(1)}, f32[392,256]{1,0:T(8,128)S(1)}, u32[]{:S(2)}, u32[]{:S(2)}) %collective-permute-start.14) | collective-permute-done | bytes 401440 | tf_op jit(solution)/shard_map/ppermute | solution.py:449
  42.5 0.0 collective-permute-done.12.refs_6_
  42.5 0.0 collective-permute-done.13.refs_8_
  42.6 1.7 %shard_map.263 = (f32[512,512]{1,0:T(8,128)S(1)}, bf16[2,1536,256]{2,1,0:T(8,128)(2,1)S(1)}, bf16[1536,512]{1,0:T(8,128)(2,1)S(1)}) custom-call(f32[512,512]{1,0:T(8,128)S(1)} %copy-done, f32[512,256]{1,0:T(8,128)S(1)} %copy-done.4, f32[512,256]{1,0:T(8,128)S(1)} %copy-done.5, f32[3,256]{1,0:T(4,128)S(1)} %get-tuple-element.37.refs_4_.refs_3_.biases, ...), custom_call_target="tpu_custom_call" | custom-call | flops 805306368 | bytes 8956928 | tf_op jit(solution)/shard_map/pallas_call | solution.py:393
  44.3 1.9 %shard_map.264 = (f32[64,512]{1,0:T(8,128)}, bf16[128,512]{1,0:T(8,128)(2,1)S(1)}, f32[128,512]{1,0:T(8,128)S(1)}, f32[128,512]{1,0:T(8,128)S(1)}) custom-call(f32[64,512]{1,0:T(8,128)S(1)} %shard_map.262.refs_9_.refs_0_, f32[64,512]{1,0:T(8,128)S(1)} %collective-permute-done.10.refs_1_, f32[64,512]{1,0:T(8,128)S(1)} %get-tuple-element.48.refs_2_, ...), custom_call_target="tpu_custom_call" | custom-call | flops 402653184 | bytes 6436864 | tf_op jit(solution)/shard_map/pallas_call | solution.py:393
  46.1 0.1 collective-permute-start.17
  46.2 0.5 collective-permute-start.18
  46.7 2.7 %collective-permute-start.16 = (f32[128,512]{1,0:T(8,128)S(1)}, f32[128,512]{1,0:T(8,128)S(1)}, u32[]{:S(2)}, u32[]{:S(2)}) collective-permute-start(f32[128,512]{1,0:T(8,128)S(1)} %get-tuple-element.57.head), channel_id=1, source_target_pairs={{0,13},{1,0},{4,1},{5,4},{8,5},{9,8},{12,9},{13,12},{2,15},{3,2},{... | collective-permute-start | bytes 786440 | tf_op jit(solution)/shard_map/ppermute | solution.py:410
  49.4 0.0 collective-permute-start.15
  49.4 1.3 %shard_map.265.middle = f32[256,512]{1,0:T(8,128)S(1)} custom-call(f32[512,512]{1,0:T(8,128)S(1)} %copy-done, f32[512,512]{1,0:T(8,128)S(1)} %get-tuple-element.53.refs_5_.receivers, s32[3,512]{1,0:T(4,128)S(1)} %bitcast.13, bf16[128,512]{1,0:T(8,128)(2,1)S(1)} %get-tuple-element.58.senders, bf16[1536,512]{1,0:T(8,128)(2,1)S(1)} %get-tuple-element.55.refs_8_.wo, ...), custom_call_target="tpu_custom_call" | custom-call | flops 402653184 | bytes 4339712 | tf_op jit(solution)/shard_map/pallas_call | solution.py:393
  50.8 0.0 collective-permute-done.17.refs_1_
  50.8 0.0 collective-permute-done.18.refs_3_
  50.8 0.6 shard_map.266
  51.4 4.1 %shard_map.267 = (bf16[1024,512]{1,0:T(8,128)(2,1)S(1)}, f32[512,512]{1,0:T(8,128)S(1)}, f32[256,512]{1,0:T(8,128)S(1)}) custom-call(f32[128,512]{1,0:T(8,128)S(1)} %get-tuple-element.57.head, f32[256,512]{1,0:T(8,128)S(1)} %shard_map.265.middle, f32[128,512]{1,0:T(8,128)S(1)} %get-tuple-element.56.tail, bf16[3072,768]{1,0:T(8,128)(2,1)S(1)} %get-tuple-element.59.picks, ...), custom_call_target="tpu_custom_call" | custom-call | flops 3221225472 | bytes 13131776 | tf_op jit(solution)/shard_map/pallas_call | solution.py:393
  55.5 1.5 %collective-permute-done.15.before = f32[128,512]{1,0:T(8,128)S(1)} collective-permute-done((f32[128,512]{1,0:T(8,128)S(1)}, f32[128,512]{1,0:T(8,128)S(1)}, u32[]{:S(2)}, u32[]{:S(2)}) %collective-permute-start.15) | collective-permute-done | bytes 262176 | tf_op jit(solution)/shard_map/ppermute | solution.py:410
  57.0 0.0 collective-permute-done.16.after
  57.1 3.7 %shard_map.268 = f32[512,512]{1,0:T(8,128)} custom-call(f32[128,512]{1,0:T(8,128)S(1)} %collective-permute-done.15.before, f32[128,512]{1,0:T(8,128)S(1)} %collective-permute-done.16.after, f32[128,512]{1,0:T(8,128)S(1)} %get-tuple-element.57.head, f32[128,512]{1,0:T(8,128)S(1)} %get-tuple-element.56.tail, f32[256,512]{1,0:T(8,128)S(1)} %get-tuple-element.66.inner, ...), custom_call_target="tpu_custom_call" | custom-call | flops 805306368 | bytes 12591104 | tf_op jit(solution)/shard_map/pallas_call | solution.py:393
  (30 shorter events, 0.1 us)
Async XLA Ops:
  5.8 7.6 %collective-permute-start = (f32[64,512]{1,0:T(8,128)}, f32[64,512]{1,0:T(8,128)S(1)}, u32[]{:S(2)}, u32[]{:S(2)}) collective-permute-start(f32[64,512]{1,0:T(8,128)} %shard_map.257.refs_7_.refs_0_), channel_id=1, source_target_pairs={{0,2},{2,0},{1,3},{3,1},{4,6},{6,4},{5,7},{7,5},{8,10},{10,8},{9,1... | collective-permute-start | bytes 393224 | tf_op jit(solution)/shard_map/ppermute | solution.py:410
  8.8 4.5 %copy-start.7 = (f32[64,512]{1,0:T(8,128)S(1)}, f32[64,512]{1,0:T(8,128)}, u32[]{:S(2)}) copy-start(f32[64,512]{1,0:T(8,128)} %shard_map.257.refs_7_.refs_0_) | copy-start | bytes 393220
  8.8 4.5 %copy-start.13 = (f32[256]{0:T(256)S(1)}, f32[256]{0:T(256)}, u32[]{:S(2)}) copy-start(f32[256]{0:T(256)} %param.44) | copy-start | bytes 3076
  8.8 4.5 %copy-start.14 = (f32[256]{0:T(256)S(1)}, f32[256]{0:T(256)}, u32[]{:S(2)}) copy-start(f32[256]{0:T(256)} %param.49) | copy-start | bytes 3076
  8.8 4.5 %copy-start.15 = (f32[512]{0:T(512)S(1)}, f32[512]{0:T(512)}, u32[]{:S(2)}) copy-start(f32[512]{0:T(512)} %param.36) | copy-start | bytes 6148
  8.8 4.5 %copy-start.16 = (f32[512]{0:T(512)S(1)}, f32[512]{0:T(512)}, u32[]{:S(2)}) copy-start(f32[512]{0:T(512)} %param.41) | copy-start | bytes 6148
  8.8 4.5 %copy-start.17 = (f32[512]{0:T(512)S(1)}, f32[512]{0:T(512)}, u32[]{:S(2)}) copy-start(f32[512]{0:T(512)} %param.46) | copy-start | bytes 6148
  8.8 4.5 %copy-start.18 = (f32[512]{0:T(512)S(1)}, f32[512]{0:T(512)}, u32[]{:S(2)}) copy-start(f32[512]{0:T(512)} %param.51) | copy-start | bytes 6148
  8.8 4.5 %copy-start.19 = (f32[256]{0:T(256)S(1)}, f32[256]{0:T(256)}, u32[]{:S(2)}) copy-start(f32[256]{0:T(256)} %param.39) | copy-start | bytes 3076
  8.8 4.5 %copy-start.9 = (f32[512,256]{1,0:T(8,128)S(1)}, f32[512,256]{1,0:T(8,128)}, u32[]{:S(2)}) copy-start(f32[512,256]{1,0:T(8,128)} %refs_5_.2) | copy-start | bytes 1572868
  8.8 4.5 %copy-start.10 = (f32[512,256]{1,0:T(8,128)S(1)}, f32[512,256]{1,0:T(8,128)}, u32[]{:S(2)}) copy-start(f32[512,256]{1,0:T(8,128)} %refs_6_.2) | copy-start | bytes 1572868
  8.9 4.5 %copy-start.11 = (f32[64,512]{1,0:T(8,128)S(1)}, f32[64,512]{1,0:T(8,128)}, u32[]{:S(2)}) copy-start(f32[64,512]{1,0:T(8,128)} %refs_2_.3) | copy-start | bytes 393220
  11.2 7.5 %copy-start.20 = (s32[512,6]{0,1:T(8,128)S(1)}, s32[512,6]{0,1:T(8,128)}, u32[]{:S(2)}) copy-start(s32[512,6]{0,1:T(8,128)} %param.30) | copy-start | bytes 36868
  11.2 7.5 %copy-start.21 = (s32[64,6]{0,1:T(8,128)S(1)}, s32[64,6]{0,1:T(8,128)}, u32[]{:S(2)}) copy-start(s32[64,6]{0,1:T(8,128)} %param.31) | copy-start | bytes 4612
  11.2 12.5 %collective-permute-start.4 = (f32[392,256]{1,0:T(8,128)}, f32[392,256]{1,0:T(8,128)S(1)}, u32[]{:S(2)}, u32[]{:S(2)}) collective-permute-start(f32[392,256]{1,0:T(8,128)} %get-tuple-element.41), channel_id=1, source_target_pairs={{0,2},{2,0},{1,3},{3,1},{4,6},{6,4},{5,7},{7,5},{8,10},{10,8},{9,1... | collective-permute-start | bytes 1204232 | tf_op jit(solution)/shard_map/ppermute | solution.py:410
  11.3 19.6 %collective-permute-start.9 = (f32[392,256]{1,0:T(8,128)}, f32[392,256]{1,0:T(8,128)S(1)}, u32[]{:S(2)}, u32[]{:S(2)}) collective-permute-start(f32[392,256]{1,0:T(8,128)} %get-tuple-element.47), channel_id=1, source_target_pairs={{0,2},{2,0},{1,3},{3,1},{4,6},{6,4},{5,7},{7,5},{8,10},{10,8},{9,1... | collective-permute-start | bytes 1204232 | tf_op jit(solution)/shard_map/ppermute | solution.py:410
  14.0 5.9 %collective-permute-start.3 = (f32[64,256]{1,0:T(8,128)S(1)}, f32[64,256]{1,0:T(8,128)S(1)}, u32[]{:S(2)}, u32[]{:S(2)}) collective-permute-start(f32[64,256]{1,0:T(8,128)S(1)} %get-tuple-element.38.refs_2_.refs_0_), channel_id=1, source_target_pairs={{0,12},{4,0},{8,4},{12,8},{1,13},{5,1},{9,5},{13,9},{2,14},{6,2},{... | collective-permute-start | bytes 196616 | tf_op jit(solution)/shard_map/ppermute | solution.py:410
  17.6 5.2 %collective-permute-start.2 = (f32[64,256]{1,0:T(8,128)S(1)}, f32[64,256]{1,0:T(8,128)S(1)}, u32[]{:S(2)}, u32[]{:S(2)}) collective-permute-start(f32[64,256]{1,0:T(8,128)S(1)} %get-tuple-element.38.refs_2_.refs_0_), channel_id=1, source_target_pairs={{0,8},{4,12},{8,0},{12,4},{1,9},{5,13},{9,1},{13,5},{2,10},{6,14},... | collective-permute-start | bytes 196616 | tf_op jit(solution)/shard_map/ppermute | solution.py:410
  17.6 6.1 %collective-permute-start.1 = (f32[64,256]{1,0:T(8,128)S(1)}, f32[64,256]{1,0:T(8,128)S(1)}, u32[]{:S(2)}, u32[]{:S(2)}) collective-permute-start(f32[64,256]{1,0:T(8,128)S(1)} %get-tuple-element.38.refs_2_.refs_0_), channel_id=1, source_target_pairs={{0,4},{4,8},{8,12},{12,0},{1,5},{5,9},{9,13},{13,1},{2,6},{6,10},{... | collective-permute-start | bytes 196616 | tf_op jit(solution)/shard_map/ppermute | solution.py:410
  18.6 12.2 %copy-start.8 = (f32[256,512]{1,0:T(8,128)S(1)}, f32[256,512]{1,0:T(8,128)}, u32[]{:S(2)}) copy-start(f32[256,512]{1,0:T(8,128)} %refs_10_.1) | copy-start | bytes 1572868
  18.6 23.9 %copy-start.6 = (f32[256,512]{1,0:T(8,128)S(1)}, f32[256,512]{1,0:T(8,128)}, u32[]{:S(2)}) copy-start(f32[256,512]{1,0:T(8,128)} %refs_4_.4) | copy-start | bytes 1572868
  19.8 22.7 %copy-start = (f32[512,512]{1,0:T(8,128)S(1)}, f32[512,512]{1,0:T(8,128)}, u32[]{:S(2)}) copy-start(f32[512,512]{1,0:T(8,128)} %nodes.1) | copy-start | bytes 3145732
  19.8 22.7 %copy-start.4 = (f32[512,256]{1,0:T(8,128)S(1)}, f32[512,256]{1,0:T(8,128)}, u32[]{:S(2)}) copy-start(f32[512,256]{1,0:T(8,128)} %refs_1_.3) | copy-start | bytes 1572868
  19.8 22.7 %copy-start.5 = (f32[512,256]{1,0:T(8,128)S(1)}, f32[512,256]{1,0:T(8,128)}, u32[]{:S(2)}) copy-start(f32[512,256]{1,0:T(8,128)} %refs_2_.5) | copy-start | bytes 1572868
  23.7 13.0 %collective-permute-start.11 = (f32[392,256]{1,0:T(8,128)S(1)}, f32[392,256]{1,0:T(8,128)S(1)}, u32[]{:S(2)}, u32[]{:S(2)}) collective-permute-start(f32[392,256]{1,0:T(8,128)S(1)} %collective-permute-done.4.refs_5_), channel_id=1, source_target_pairs={{0,16},{16,0},{1,17},{17,1},{2,18},{18,2},{3,19},{19,3},{4,20},{20... | collective-permute-start | bytes 1204232 | tf_op jit(solution)/shard_map/ppermute | solution.py:449
  25.2 1.3 %collective-permute-start.5 = (f32[64,256]{1,0:T(8,128)S(1)}, f32[64,256]{1,0:T(8,128)S(1)}, u32[]{:S(2)}, u32[]{:S(2)}) collective-permute-start(f32[64,256]{1,0:T(8,128)S(1)} %get-tuple-element.38.refs_2_.refs_0_), channel_id=1, source_target_pairs={{0,1},{1,0},{2,3},{3,2},{4,5},{5,4},{6,7},{7,6},{8,9},{9,8},{10,11... | collective-permute-start | bytes 196616 | tf_op jit(solution)/shard_map/ppermute | solution.py:410
  25.2 5.6 %collective-permute-start.6 = (f32[64,256]{1,0:T(8,128)S(1)}, f32[64,256]{1,0:T(8,128)S(1)}, u32[]{:S(2)}, u32[]{:S(2)}) collective-permute-start(f32[64,256]{1,0:T(8,128)S(1)} %collective-permute-done.1.refs_1_), channel_id=1, source_target_pairs={{0,1},{1,0},{2,3},{3,2},{4,5},{5,4},{6,7},{7,6},{8,9},{9,8},{10,11... | collective-permute-start | bytes 196616 | tf_op jit(solution)/shard_map/ppermute | solution.py:410
  25.7 5.1 %collective-permute-start.7 = (f32[64,256]{1,0:T(8,128)S(1)}, f32[64,256]{1,0:T(8,128)S(1)}, u32[]{:S(2)}, u32[]{:S(2)}) collective-permute-start(f32[64,256]{1,0:T(8,128)S(1)} %collective-permute-done.2.refs_2_), channel_id=1, source_target_pairs={{0,1},{1,0},{2,3},{3,2},{4,5},{5,4},{6,7},{7,6},{8,9},{9,8},{10,11... | collective-permute-start | bytes 196616 | tf_op jit(solution)/shard_map/ppermute | solution.py:410
  26.5 4.3 %collective-permute-start.8 = (f32[64,256]{1,0:T(8,128)S(1)}, f32[64,256]{1,0:T(8,128)S(1)}, u32[]{:S(2)}, u32[]{:S(2)}) collective-permute-start(f32[64,256]{1,0:T(8,128)S(1)} %collective-permute-done.3.refs_3_), channel_id=1, source_target_pairs={{0,1},{1,0},{2,3},{3,2},{4,5},{5,4},{6,7},{7,6},{8,9},{9,8},{10,11... | collective-permute-start | bytes 196616 | tf_op jit(solution)/shard_map/ppermute | solution.py:410
  31.6 12.6 %copy-start.12 = (s32[512,3]{0,1:T(4,128)S(1)}, s32[512,3]{0,1:T(4,128)}, u32[]{:S(2)}) copy-start(s32[512,3]{0,1:T(4,128)} %param.29) | copy-start | bytes 18436
  31.6 5.0 %collective-permute-start.10 = (f32[64,512]{1,0:T(8,128)S(1)}, f32[64,512]{1,0:T(8,128)S(1)}, u32[]{:S(2)}, u32[]{:S(2)}) collective-permute-start(f32[64,512]{1,0:T(8,128)S(1)} %shard_map.262.refs_9_.refs_0_), channel_id=1, source_target_pairs={{0,2},{2,0},{1,3},{3,1},{4,6},{6,4},{5,7},{7,5},{8,10},{10,8},{9,1... | collective-permute-start | bytes 393224 | tf_op jit(solution)/shard_map/ppermute | solution.py:410
  32.3 10.2 %collective-permute-start.14 = (f32[392,256]{1,0:T(8,128)S(1)}, f32[392,256]{1,0:T(8,128)S(1)}, u32[]{:S(2)}, u32[]{:S(2)}) collective-permute-start(f32[392,256]{1,0:T(8,128)S(1)} %collective-permute-done.9.refs_11_.refs_0_), channel_id=1, source_target_pairs={{0,4},{4,0},{8,12},{12,8},{1,5},{5,1},{9,13},{13,9},{2,6},{6,2},{1... | collective-permute-start | bytes 1204232 | tf_op jit(solution)/shard_map/ppermute | solution.py:449
  36.7 5.9 %collective-permute-start.12 = (f32[392,256]{1,0:T(8,128)S(1)}, f32[392,256]{1,0:T(8,128)S(1)}, u32[]{:S(2)}, u32[]{:S(2)}) collective-permute-start(f32[392,256]{1,0:T(8,128)S(1)} %collective-permute-done.4.refs_5_), channel_id=1, source_target_pairs={{0,1},{1,0},{2,3},{3,2},{4,5},{5,4},{6,7},{7,6},{8,9},{9,8},{10,11... | collective-permute-start | bytes 1204232 | tf_op jit(solution)/shard_map/ppermute | solution.py:410
  36.7 5.9 %collective-permute-start.13 = (f32[392,256]{1,0:T(8,128)S(1)}, f32[392,256]{1,0:T(8,128)S(1)}, u32[]{:S(2)}, u32[]{:S(2)}) collective-permute-start(f32[392,256]{1,0:T(8,128)S(1)} %collective-permute-done.11.refs_7_), channel_id=1, source_target_pairs={{0,1},{1,0},{2,3},{3,2},{4,5},{5,4},{6,7},{7,6},{8,9},{9,8},{10,11... | collective-permute-start | bytes 1204232 | tf_op jit(solution)/shard_map/ppermute | solution.py:410
  46.1 4.6 %collective-permute-start.17 = (f32[392,256]{1,0:T(8,128)S(1)}, f32[392,256]{1,0:T(8,128)S(1)}, u32[]{:S(2)}, u32[]{:S(2)}) collective-permute-start(f32[392,256]{1,0:T(8,128)S(1)} %collective-permute-done.9.refs_11_.refs_0_), channel_id=1, source_target_pairs={{0,1},{1,0},{2,3},{3,2},{4,5},{5,4},{6,7},{7,6},{8,9},{9,8},{10,11... | collective-permute-start | bytes 1204232 | tf_op jit(solution)/shard_map/ppermute | solution.py:410
  46.2 4.6 %collective-permute-start.18 = (f32[392,256]{1,0:T(8,128)S(1)}, f32[392,256]{1,0:T(8,128)S(1)}, u32[]{:S(2)}, u32[]{:S(2)}) collective-permute-start(f32[392,256]{1,0:T(8,128)S(1)} %collective-permute-done.14.refs_10_.refs_2_), channel_id=1, source_target_pairs={{0,1},{1,0},{2,3},{3,2},{4,5},{5,4},{6,7},{7,6},{8,9},{9,8},{10,11... | collective-permute-start | bytes 1204232 | tf_op jit(solution)/shard_map/ppermute | solution.py:410
  46.7 10.3 %collective-permute-start.16 = (f32[128,512]{1,0:T(8,128)S(1)}, f32[128,512]{1,0:T(8,128)S(1)}, u32[]{:S(2)}, u32[]{:S(2)}) collective-permute-start(f32[128,512]{1,0:T(8,128)S(1)} %get-tuple-element.57.head), channel_id=1, source_target_pairs={{0,13},{1,0},{4,1},{5,4},{8,5},{9,8},{12,9},{13,12},{2,15},{3,2},{... | collective-permute-start | bytes 786440 | tf_op jit(solution)/shard_map/ppermute | solution.py:410
  49.4 7.6 %collective-permute-start.15 = (f32[128,512]{1,0:T(8,128)S(1)}, f32[128,512]{1,0:T(8,128)S(1)}, u32[]{:S(2)}, u32[]{:S(2)}) collective-permute-start(f32[128,512]{1,0:T(8,128)S(1)} %get-tuple-element.56.tail), channel_id=1, source_target_pairs={{0,1},{1,4},{4,5},{5,8},{8,9},{9,12},{12,13},{13,0},{2,3},{3,6},{6... | collective-permute-start | bytes 786440 | tf_op jit(solution)/shard_map/ppermute | solution.py:410
  49.4 1.4 %copy-start.1 = (f32[512,256]{1,0:T(8,128)S(1)}, f32[512,256]{1,0:T(8,128)}, u32[]{:S(2)}) copy-start(f32[512,256]{1,0:T(8,128)} %ws.1) | copy-start | bytes 1572868
  49.4 1.4 %copy-start.2 = (f32[512,256]{1,0:T(8,128)S(1)}, f32[512,256]{1,0:T(8,128)}, u32[]{:S(2)}) copy-start(f32[512,256]{1,0:T(8,128)} %wr.1) | copy-start | bytes 1572868
  49.4 1.4 %copy-start.3 = (f32[256,512]{1,0:T(8,128)S(1)}, f32[256,512]{1,0:T(8,128)}, u32[]{:S(2)}) copy-start(f32[256,512]{1,0:T(8,128)} %wo.1) | copy-start | bytes 1572868

commit v10 on v8

--- a/solution.py
+++ b/solution.py
@@ -108,10 +108,8 @@
         biases[i : i + 1] = params[4 + i][...]
 
 
-def share_kernel(*refs):
-    down_own, bottom_own, (down_pack, bottom_pack, sems) = refs[:4], refs[4:8], refs[8:]
-    copies = share_copies(down_own, down_pack, "parts") + share_copies(bottom_own, bottom_pack, "patch")
-    for move in started(copies, sems):
+def share_kernel(axis, *refs):
+    for move in started(share_copies(refs[:4], refs[4], axis), refs[5]):
         move.wait()
 
 
@@ -288,11 +286,13 @@
     )
 
 
-def bottom_rows(nodes, receivers, picks, senders, wo, gain):
+def bottom_rows(nodes, receivers, picks, senders, wo, gain, ahead=None):
     half = senders.shape[1] // 2
     hidden = []
     for place in (slice(0, half), slice(half, 2 * half)):
         picked = dot(picks, senders[:, place])
+        if ahead is not None:
+            picked = picked + ahead[:, place]
         hidden.append(silu_sum(picked, receivers[:, place], picks.shape[0] // nodes.shape[0]))
     return nodes + gain * normed(dot3(jnp.concatenate(hidden, axis=1), wo))
 
@@ -305,7 +305,7 @@
         out[(2 * i + 1) * rim : (2 * i + 2) * rim, columns] = low[strip]
 
 
-def bottom_middle_kernel(rim, head, middle, tail, picks, ws, wr, wo, bias, gains, senders, receivers, out):
+def bottom_middle_kernel(rim, head, middle, tail, picks, ws, wr, wo, bias, gains, receivers, out, ahead, senders):
     nodes = jnp.concatenate([head[...], middle[...], tail[...]], axis=0)
     left = threefold(nodes)
     width = ws.shape[2]
@@ -322,9 +322,14 @@
             middle[inner], receivers[place], picks[i * size : (i + 1) * size],
             senders[2 * (i - 1) * rim : 2 * (i + 2) * rim, :], wo[...], gains[3:4],
         )
-
-
-def bottom_edge_kernel(rim, before, after, head, tail, inner, picks, senders, receivers, ws, wo, gains, out, outer, strips, sems):
+    near, last = senders.shape[0], picks.shape[0] - size
+    ahead[0:size, :] = dot(picks[0:size, 2 * rim : 6 * rim], senders[0 : 4 * rim, :])
+    ahead[size : 2 * size, :] = dot(
+        picks[last : last + size, 0 : 4 * rim], senders[near - 4 * rim : near, :]
+    )
+
+
+def bottom_edge_kernel(rim, before, after, head, tail, inner, ahead, picks, receivers, ws, wo, gains, out, outer, strips, sems):
     total = receivers.shape[0]
     size = picks.shape[0] * rim // total
     moves = [pltpu.make_async_copy(inner, out.at[pl.ds(rim, total - 2 * rim)], sems.at[0])]
@@ -333,19 +338,13 @@
     width = ws.shape[2]
     for g in range(ws.shape[0]):
         put_strips(0.5 * dot(left, ws[g]), rim, outer, slice(g * width, (g + 1) * width))
-    near = senders.shape[0]
     for side, nodes in enumerate((head, tail)):
-        first = 0 if side == 0 else total - rim
+        first, column = (0, 0) if side == 0 else (total - rim, 4 * rim)
         place = slice(first, first + rim)
-        beyond = outer[2 * side * rim : 2 * (side + 1) * rim, :]
-        reach = (
-            [beyond, senders[0 : 4 * rim, :]]
-            if side == 0
-            else [senders[near - 4 * rim : near, :], beyond]
-        )
+        chosen = picks[first // rim * size : (first // rim + 1) * size, column : column + 2 * rim]
         strips[side * rim : (side + 1) * rim, :] = bottom_rows(
-            nodes[...], receivers[place], picks[first // rim * size : (first // rim + 1) * size],
-            jnp.concatenate(reach, axis=0), wo[...], gains[3:4],
+            nodes[...], receivers[place], chosen, outer[2 * side * rim : 2 * (side + 1) * rim, :],
+            wo[...], gains[3:4], ahead[side * size : (side + 1) * size, :],
         )
         strip = strips.at[pl.ds(side * rim, rim)]
         moves.append(pltpu.make_async_copy(strip, out.at[pl.ds(first, rim)], sems.at[1 + side]))
@@ -496,14 +495,17 @@
     parts = sub_parts(part)
     down_own = (downward_sender, downward_receiver, downward_output, downward_bias[None])
     bottom_own = (bottom_sender, bottom_receiver, bottom_output, bottom_bias[None])
-    down_pack, bottom_pack = call(
-        share_kernel,
-        [pack("parts"), pack("patch")],
-        [*down_own, *bottom_own],
-        latent,
-        [pltpu.SemaphoreType.DMA((6 + 2 * columns,))],
-        far=range(8),
-        limit=share_limit,
+    (down_pack,), (bottom_pack,) = (
+        call(
+            functools.partial(share_kernel, axis),
+            [pack(axis)],
+            own,
+            latent,
+            [pltpu.SemaphoreType.DMA((3 + columns,))],
+            far=range(4),
+            limit=share_limit,
+        )
+        for axis, own in (("parts", down_own), ("patch", bottom_own))
     )
     gains, biases = call(
         stack_kernel,
@@ -579,16 +581,17 @@
         [bottom_sender, bottom_receiver, biases, bottom_output, *bottom_packs],
         latent * hidden,
     )
-    senders, receivers, inner = call(
+    receivers, inner, ahead = call(
         functools.partial(bottom_middle_kernel, rim),
-        [like((2 * rows, hidden), bf16), like((rows, hidden)), like((rows - 2 * rim, latent))],
+        [like((rows, hidden)), like((rows - 2 * rim, latent)), like((bottom_links.size // (rows // rim) * 2, hidden))],
         [head, middle, tail, bottom_picks, ws, wr, wo, bias, gains],
         (12 * rows + 12 * rows) * latent * hidden,
+        [pltpu.VMEM((2 * rows, hidden), bf16)],
     )
     (new_nodes,) = call(
         functools.partial(bottom_edge_kernel, rim),
         [like((rows, latent))],
-        [before, after, head, tail, inner, bottom_picks, senders, receivers, ws, wo, gains],
+        [before, after, head, tail, inner, ahead, bottom_picks, receivers, ws, wo, gains],
         24 * rim * latent * hidden,
         [
             pltpu.VMEM((4 * rim, hidden), bf16),

time: 58.3 us -> 57.9 us (level)
  waiting for transfers between devices: 19.7 us -> 13 us
  starting transfers between devices: 17.1 us -> 19.8 us
  local copies, waits for them, and re-layouts: 0.15 us -> 2.2 us
  Pallas kernels: 19.9 us -> 21.4 us
    ppermute x17, waiting for transfers between devices: 19.7 us -> 13 us  [shifted(): lax.ppermute(values, axis, [(i, (i + step) % count) for i in range(count)])]
    ppermute x17, starting transfers between devices: 15 us -> 17.2 us  [shifted(): lax.ppermute(values, axis, [(i, (i + step) % count) for i in range(count)])]
    unnamed x54 -> x52, local copies, waits for them, and re-layouts: 0.15 us -> 2.2 us
    pallas_call x12 -> x13, Pallas kernels: 19.9 us -> 21.4 us  [call(): pl.pallas_call((lambda *refs: kernel(*refs[:read], *refs[read + unread:])...]
    ppermute x2, starting transfers between devices: 2.09 us -> 2.68 us  [over_partners(): lax.ppermute(share, axis, [(i, i - i % count + (i + p) % count) for i in...]
  transfers between devices with their start and end apart: 19 -> 19, of which waited for: 8 -> 8; matrix products, arithmetic and copies ran while one was open for 0% -> 0% of each run, Pallas kernels for 24% -> 28%
where the time goes in v10:
time: 57.9 us; the launch traced here: 57.6 us
  Pallas kernels  21.4 us (37%)
  starting transfers between devices  19.8 us (34%)
  waiting for transfers between devices  13 us (22%)
  local copies, waits for them, and re-layouts  2.2 us (4%)
  between operations  1.21 us (2%)
    pallas_call x13, Pallas kernels, call(): pl.pallas_call((lambda *refs: kernel(*refs[:read], *refs[read + unread:])...  21.4 us
    ppermute x17, starting transfers between devices, shifted(): lax.ppermute(values, axis, [(i, (i + step) % count) for i in range(count)])  17.2 us
    ppermute x17, waiting for transfers between devices, shifted(): lax.ppermute(values, axis, [(i, (i + step) % count) for i in range(count)])  13 us
    ppermute x2, starting transfers between devices, over_partners(): lax.ppermute(share, axis, [(i, i - i % count + (i + p) % count) for i in...  2.68 us
    unnamed x52, local copies, waits for them, and re-layouts  2.2 us
  transfers between devices with their start and end apart: 19, of which 8 were waited for; matrix products, arithmetic and copies ran while one was open for 0% of the time, Pallas kernels for 28%

profile of v10, /device:TPU:0, one launch (start us, length us, event | category | flops | bytes accessed | tf_op | source)
XLA Modules:
  0.0 57.6 jit_solution(10189505723885655021)
XLA Ops:
  0.7 1.9 %shard_map.261 = f32[392,256]{1,0:T(8,128)} custom-call(f32[512,256]{1,0:T(8,128)} %refs_1_.5, f32[512,256]{1,0:T(8,128)} %refs_2_.7, f32[256,512]{1,0:T(8,128)} %refs_4_.2, f32[1,256]{1,0:T(1,128)} %bitcast.15), custom_call_target="tpu_custom_call" | custom-call | flops 512 | bytes 1975296 | tf_op jit(solution)/shard_map/pallas_call | solution.py:364
  2.6 3.0 %collective-permute-start.4 = (f32[392,256]{1,0:T(8,128)}, f32[392,256]{1,0:T(8,128)S(1)}, u32[]{:S(2)}, u32[]{:S(2)}) collective-permute-start(f32[392,256]{1,0:T(8,128)} %shard_map.261), channel_id=1, source_target_pairs={{0,2},{2,0},{1,3},{3,1},{4,6},{6,4},{5,7},{7,5},{8,10},{10,8},{9,1... | collective-permute-start | bytes 1204232 | tf_op jit(solution)/shard_map/ppermute | solution.py:381
  5.6 0.0 copy-start.8
  5.7 1.0 %copy-done.8 = f32[512,256]{1,0:T(8,128)S(1)} copy-done((f32[512,256]{1,0:T(8,128)S(1)}, f32[512,256]{1,0:T(8,128)}, u32[]{:S(2)}) %copy-start.8) | copy-done | bytes 524312
  6.7 1.0 %copy-done.9 = f32[256,512]{1,0:T(8,128)S(1)} copy-done((f32[256,512]{1,0:T(8,128)S(1)}, f32[256,512]{1,0:T(8,128)}, u32[]{:S(2)}) %copy-start.9) | copy-done | bytes 524312
  7.7 1.8 %shard_map.257.refs_7_.refs_0_ = f32[64,512]{1,0:T(8,128)S(1)} custom-call(f32[512,512]{1,0:T(8,128)S(1)} %copy-done, f32[64,512]{1,0:T(8,128)S(1)} %copy-done.13, s32[7,64]{1,0:T(8,128)S(1)} %bitcast.19, f32[512,256]{1,0:T(8,128)S(1)} %copy-done.7, f32[512,256]{1,0:T(8,128)S(1)} %copy-done.8, f32[1,256]{1,0:T(1,128)S(1)} %bitcast.25, f32[256,512]{1,0:T(8,128)S(1)} %copy-done.9), custom_call_target="tpu_custom_call" | custom-call | flops 402653184 | bytes 2886400 | tf_op jit(solution)/shard_map/pallas_call | solution.py:364
  9.5 0.0 copy-start.16
  9.5 0.0 copy-start.17
  9.5 0.0 copy-start.20
  9.6 0.0 copy-start.21
  9.6 0.0 copy-start.22
  9.6 0.0 copy-start.23
  9.6 0.0 copy-start.25
  9.6 0.0 copy-start.10
  9.6 0.0 copy-start.11
  9.6 0.1 collective-permute-start
  9.7 1.9 %shard_map.262 = f32[392,256]{1,0:T(8,128)} custom-call(f32[512,256]{1,0:T(8,128)} %ws.3, f32[512,256]{1,0:T(8,128)} %wr.3, f32[256,512]{1,0:T(8,128)} %wo.3, f32[1,256]{1,0:T(1,128)} %bitcast.17), custom_call_target="tpu_custom_call" | custom-call | flops 512 | bytes 1975296 | tf_op jit(solution)/shard_map/pallas_call | solution.py:364
  11.7 2.0 %collective-permute-start.6 = (f32[392,256]{1,0:T(8,128)}, f32[392,256]{1,0:T(8,128)S(1)}, u32[]{:S(2)}, u32[]{:S(2)}) collective-permute-start(f32[392,256]{1,0:T(8,128)} %shard_map.262), channel_id=1, source_target_pairs={{0,2},{2,0},{1,3},{3,1},{4,6},{6,4},{5,7},{7,5},{8,10},{10,8},{9,1... | collective-permute-start | bytes 1204232 | tf_op jit(solution)/shard_map/ppermute | solution.py:381
  13.7 5.1 %collective-permute-done.refs_1_ = f32[64,512]{1,0:T(8,128)S(1)} collective-permute-done((f32[64,512]{1,0:T(8,128)S(1)}, f32[64,512]{1,0:T(8,128)S(1)}, u32[]{:S(2)}, u32[]{:S(2)}) %collective-permute-start) | collective-permute-done | bytes 131104 | tf_op jit(solution)/shard_map/ppermute | solution.py:381
  18.8 0.0 collective-permute-done.4.refs_5_
  18.8 2.1 %collective-permute-start.5 = (f32[392,256]{1,0:T(8,128)S(1)}, f32[392,256]{1,0:T(8,128)S(1)}, u32[]{:S(2)}, u32[]{:S(2)}) collective-permute-start(f32[392,256]{1,0:T(8,128)S(1)} %collective-permute-done.4.refs_5_), channel_id=1, source_target_pairs={{0,16},{16,0},{1,17},{17,1},{2,18},{18,2},{3,19},{19,3},{4,20},{20... | collective-permute-start | bytes 1204232 | tf_op jit(solution)/shard_map/ppermute | solution.py:420
  20.9 0.0 copy-start.1
  20.9 0.0 copy-start.2
  20.9 0.0 copy-start.3
  21.0 0.6 shard_map.259
  21.5 1.6 %collective-permute-start.1 = (f32[64,256]{1,0:T(8,128)S(1)}, f32[64,256]{1,0:T(8,128)S(1)}, u32[]{:S(2)}, u32[]{:S(2)}) collective-permute-start(f32[64,256]{1,0:T(8,128)S(1)} %get-tuple-element.36.refs_2_.refs_0_), channel_id=1, source_target_pairs={{0,4},{4,8},{8,12},{12,0},{1,5},{5,9},{9,13},{13,1},{2,6},{6,10},{... | collective-permute-start | bytes 196616 | tf_op jit(solution)/shard_map/ppermute | solution.py:381
  23.2 2.6 %collective-permute-start.2 = (f32[64,256]{1,0:T(8,128)S(1)}, f32[64,256]{1,0:T(8,128)S(1)}, u32[]{:S(2)}, u32[]{:S(2)}) collective-permute-start(f32[64,256]{1,0:T(8,128)S(1)} %get-tuple-element.36.refs_2_.refs_0_), channel_id=1, source_target_pairs={{0,8},{4,12},{8,0},{12,4},{1,9},{5,13},{9,1},{13,5},{2,10},{6,14},... | collective-permute-start | bytes 196616 | tf_op jit(solution)/shard_map/ppermute | solution.py:381
  25.7 1.3 %collective-permute-start.3 = (f32[64,256]{1,0:T(8,128)S(1)}, f32[64,256]{1,0:T(8,128)S(1)}, u32[]{:S(2)}, u32[]{:S(2)}) collective-permute-start(f32[64,256]{1,0:T(8,128)S(1)} %get-tuple-element.36.refs_2_.refs_0_), channel_id=1, source_target_pairs={{0,12},{4,0},{8,4},{12,8},{1,13},{5,1},{9,5},{13,9},{2,14},{6,2},{... | collective-permute-start | bytes 196616 | tf_op jit(solution)/shard_map/ppermute | solution.py:381
  27.1 1.1 %shard_map.260 = (bf16[384,1024]{1,0:T(8,128)(2,1)S(1)}, bf16[3072,768]{1,0:T(8,128)(2,1)S(1)}) custom-call(s32[6,64]{1,0:T(8,128)S(1)} %bitcast.20, s32[6,512]{1,0:T(8,128)S(1)} %bitcast.14, f32[64,256]{1,0:T(8,128)S(1)} %get-tuple-element.36.refs_2_.refs_0_), custom_call_target="tpu_custom_call" | custom-call | flops 196608 | bytes 5584384 | tf_op jit(solution)/shard_map/pallas_call | solution.py:364
  28.2 0.0 collective-permute-done.1.refs_1_
  28.3 0.1 collective-permute-done.2.refs_2_
  28.3 1.7 %collective-permute-done.3.refs_3_ = f32[64,256]{1,0:T(8,128)S(1)} collective-permute-done((f32[64,256]{1,0:T(8,128)S(1)}, f32[64,256]{1,0:T(8,128)S(1)}, u32[]{:S(2)}, u32[]{:S(2)}) %collective-permute-start.3) | collective-permute-done | bytes 65568 | tf_op jit(solution)/shard_map/ppermute | solution.py:381
  30.0 0.0 collective-permute-done.6.refs_0_
  30.0 0.0 collective-permute-done.5.refs_7_
  30.0 0.0 collective-permute-start.12
  30.0 0.5 collective-permute-start.13
  30.5 0.6 %collective-permute-start.16 = (f32[392,256]{1,0:T(8,128)S(1)}, f32[392,256]{1,0:T(8,128)S(1)}, u32[]{:S(2)}, u32[]{:S(2)}) collective-permute-start(f32[392,256]{1,0:T(8,128)S(1)} %collective-permute-done.6.refs_0_), channel_id=1, source_target_pairs={{0,4},{4,0},{8,12},{12,8},{1,5},{5,1},{9,13},{13,9},{2,6},{6,2},{1... | collective-permute-start | bytes 1204232 | tf_op jit(solution)/shard_map/ppermute | solution.py:420
  31.1 0.0 collective-permute-start.7
  31.1 0.5 collective-permute-start.10
  31.6 0.8 %collective-permute-done.7.refs_4_ = f32[64,256]{1,0:T(8,128)S(1)} collective-permute-done((f32[64,256]{1,0:T(8,128)S(1)}, f32[64,256]{1,0:T(8,128)S(1)}, u32[]{:S(2)}, u32[]{:S(2)}) %collective-permute-start.7) | collective-permute-done | bytes 65568 | tf_op jit(solution)/shard_map/ppermute | solution.py:381
  32.4 0.1 collective-permute-start.8
  32.6 0.0 collective-permute-done.10.refs_7_
  32.6 0.4 collective-permute-start.9
  32.9 0.7 %collective-permute-done.8.refs_5_ = f32[64,256]{1,0:T(8,128)S(1)} collective-permute-done((f32[64,256]{1,0:T(8,128)S(1)}, f32[64,256]{1,0:T(8,128)S(1)}, u32[]{:S(2)}, u32[]{:S(2)}) %collective-permute-start.8) | collective-permute-done | bytes 65568 | tf_op jit(solution)/shard_map/ppermute | solution.py:381
  33.7 0.2 collective-permute-done.9.refs_6_
  33.8 0.8 %shard_map.263.refs_9_.refs_0_ = f32[64,512]{1,0:T(8,128)S(1)} custom-call(f32[64,256]{1,0:T(8,128)S(1)} %get-tuple-element.36.refs_2_.refs_0_, f32[64,256]{1,0:T(8,128)S(1)} %collective-permute-done.1.refs_1_, f32[64,256]{1,0:T(8,128)S(1)} %collective-permute-done.2.refs_2_, f32[64,256]{1,0:T(8,128)S(1)} %collective-permute-done.3.refs_3_, ...), custom_call_target="tpu_custom_call" | custom-call | flops 201326592 | bytes 2031616 | tf_op jit(solution)/shard_map/pallas_call | solution.py:364
  34.6 0.0 copy-start.14
  34.6 1.6 %collective-permute-start.11 = (f32[64,512]{1,0:T(8,128)S(1)}, f32[64,512]{1,0:T(8,128)S(1)}, u32[]{:S(2)}, u32[]{:S(2)}) collective-permute-start(f32[64,512]{1,0:T(8,128)S(1)} %shard_map.263.refs_9_.refs_0_), channel_id=1, source_target_pairs={{0,2},{2,0},{1,3},{3,1},{4,6},{6,4},{5,7},{7,5},{8,10},{10,8},{9,1... | collective-permute-start | bytes 393224 | tf_op jit(solution)/shard_map/ppermute | solution.py:381
  36.2 0.0 collective-permute-done.12.refs_6_
  36.2 0.0 collective-permute-done.13.refs_8_
  36.2 1.7 %shard_map.264 = (f32[512,512]{1,0:T(8,128)S(1)}, bf16[2,1536,256]{2,1,0:T(8,128)(2,1)S(1)}, bf16[1536,512]{1,0:T(8,128)(2,1)S(1)}) custom-call(f32[512,512]{1,0:T(8,128)S(1)} %copy-done, f32[512,256]{1,0:T(8,128)S(1)} %copy-done.1, f32[512,256]{1,0:T(8,128)S(1)} %copy-done.2, f32[3,256]{1,0:T(4,128)S(1)} %get-tuple-element.35.refs_4_.refs_3_.biases, ...), custom_call_target="tpu_custom_call" | custom-call | flops 805306368 | bytes 8555520 | tf_op jit(solution)/shard_map/pallas_call | solution.py:364
  37.9 2.6 %collective-permute-done.11.refs_1_ = f32[64,512]{1,0:T(8,128)S(1)} collective-permute-done((f32[64,512]{1,0:T(8,128)S(1)}, f32[64,512]{1,0:T(8,128)S(1)}, u32[]{:S(2)}, u32[]{:S(2)}) %collective-permute-start.11) | collective-permute-done | bytes 131104 | tf_op jit(solution)/shard_map/ppermute | solution.py:381
  40.5 1.8 %shard_map.265 = (f32[64,512]{1,0:T(8,128)}, bf16[128,512]{1,0:T(8,128)(2,1)S(1)}, f32[128,512]{1,0:T(8,128)S(1)}, f32[128,512]{1,0:T(8,128)S(1)}) custom-call(f32[64,512]{1,0:T(8,128)S(1)} %shard_map.263.refs_9_.refs_0_, f32[64,512]{1,0:T(8,128)S(1)} %collective-permute-done.11.refs_1_, f32[64,512]{1,0:T(8,128)S(1)} %get-tuple-element.45.refs_2_, ...), custom_call_target="tpu_custom_call" | custom-call | flops 402653184 | bytes 6436864 | tf_op jit(solution)/shard_map/pallas_call | solution.py:364
  42.3 0.1 collective-permute-start.17
  42.4 0.5 collective-permute-start.18
  42.9 2.8 %collective-permute-start.15 = (f32[128,512]{1,0:T(8,128)S(1)}, f32[128,512]{1,0:T(8,128)S(1)}, u32[]{:S(2)}, u32[]{:S(2)}) collective-permute-start(f32[128,512]{1,0:T(8,128)S(1)} %get-tuple-element.52.head), channel_id=1, source_target_pairs={{0,13},{1,0},{4,1},{5,4},{8,5},{9,8},{12,9},{13,12},{2,15},{3,2},{... | collective-permute-start | bytes 786440 | tf_op jit(solution)/shard_map/ppermute | solution.py:381
  45.7 0.0 collective-permute-start.14
  45.7 1.3 %shard_map.266.middle = f32[256,512]{1,0:T(8,128)S(1)} custom-call(f32[512,512]{1,0:T(8,128)S(1)} %copy-done, f32[512,512]{1,0:T(8,128)S(1)} %get-tuple-element.48.refs_5_.receivers, s32[3,512]{1,0:T(4,128)S(1)} %bitcast.13, bf16[128,512]{1,0:T(8,128)(2,1)S(1)} %get-tuple-element.53.senders, bf16[1536,512]{1,0:T(8,128)(2,1)S(1)} %get-tuple-element.50.refs_8_.wo, ...), custom_call_target="tpu_custom_call" | custom-call | flops 402653184 | bytes 4339712 | tf_op jit(solution)/shard_map/pallas_call | solution.py:364
  47.1 0.0 collective-permute-done.17.refs_1_
  47.1 0.0 collective-permute-done.18.refs_3_
  47.2 0.6 shard_map.267
  47.7 4.7 %shard_map.268 = (f32[512,512]{1,0:T(8,128)S(1)}, f32[256,512]{1,0:T(8,128)S(1)}, f32[1536,512]{1,0:T(8,128)S(1)}) custom-call(f32[128,512]{1,0:T(8,128)S(1)} %get-tuple-element.52.head, f32[256,512]{1,0:T(8,128)S(1)} %shard_map.266.middle, f32[128,512]{1,0:T(8,128)S(1)} %get-tuple-element.51.tail, bf16[3072,768]{1,0:T(8,128)(2,1)S(1)} %get-tuple-element.54.picks, ...), custom_call_target="tpu_custom_call" | custom-call | flops 3221225472 | bytes 15228928 | tf_op jit(solution)/shard_map/pallas_call | solution.py:364
  52.4 1.8 %collective-permute-done.14.before = f32[128,512]{1,0:T(8,128)S(1)} collective-permute-done((f32[128,512]{1,0:T(8,128)S(1)}, f32[128,512]{1,0:T(8,128)S(1)}, u32[]{:S(2)}, u32[]{:S(2)}) %collective-permute-start.14) | collective-permute-done | bytes 262176 | tf_op jit(solution)/shard_map/ppermute | solution.py:381
  54.3 3.1 %shard_map.269 = f32[512,512]{1,0:T(8,128)} custom-call(f32[128,512]{1,0:T(8,128)S(1)} %collective-permute-done.14.before, f32[128,512]{1,0:T(8,128)S(1)} %collective-permute-done.15.after, f32[128,512]{1,0:T(8,128)S(1)} %get-tuple-element.52.head, f32[128,512]{1,0:T(8,128)S(1)} %get-tuple-element.51.tail, f32[256,512]{1,0:T(8,128)S(1)} %get-tuple-element.62.inner, ...), custom_call_target="tpu_custom_call" | custom-call | flops 805306368 | bytes 14688256 | tf_op jit(solution)/shard_map/pallas_call | solution.py:364
  (39 shorter events, 0.1 us)
Async XLA Ops:
  0.6 5.0 %copy-start.18 = (s32[64,7]{0,1:T(8,128)S(1)}, s32[64,7]{0,1:T(8,128)}, u32[]{:S(2)}) copy-start(s32[64,7]{0,1:T(8,128)} %param.28) | copy-start | bytes 5380
  0.6 5.0 %copy-start.24 = (f32[256]{0:T(256)S(1)}, f32[256]{0:T(256)}, u32[]{:S(2)}) copy-start(f32[256]{0:T(256)} %param.34) | copy-start | bytes 3076
  0.7 5.0 %copy-start = (f32[512,512]{1,0:T(8,128)S(1)}, f32[512,512]{1,0:T(8,128)}, u32[]{:S(2)}) copy-start(f32[512,512]{1,0:T(8,128)} %nodes.3) | copy-start | bytes 3145732
  0.7 5.0 %copy-start.13 = (f32[64,512]{1,0:T(8,128)S(1)}, f32[64,512]{1,0:T(8,128)}, u32[]{:S(2)}) copy-start(f32[64,512]{1,0:T(8,128)} %refs_2_.4) | copy-start | bytes 393220
  0.7 5.0 %copy-start.7 = (f32[512,256]{1,0:T(8,128)S(1)}, f32[512,256]{1,0:T(8,128)}, u32[]{:S(2)}) copy-start(f32[512,256]{1,0:T(8,128)} %ws.2) | copy-start | bytes 1572868
  2.6 16.1 %collective-permute-start.4 = (f32[392,256]{1,0:T(8,128)}, f32[392,256]{1,0:T(8,128)S(1)}, u32[]{:S(2)}, u32[]{:S(2)}) collective-permute-start(f32[392,256]{1,0:T(8,128)} %shard_map.261), channel_id=1, source_target_pairs={{0,2},{2,0},{1,3},{3,1},{4,6},{6,4},{5,7},{7,5},{8,10},{10,8},{9,1... | collective-permute-start | bytes 1204232 | tf_op jit(solution)/shard_map/ppermute | solution.py:381
  5.6 1.0 %copy-start.8 = (f32[512,256]{1,0:T(8,128)S(1)}, f32[512,256]{1,0:T(8,128)}, u32[]{:S(2)}) copy-start(f32[512,256]{1,0:T(8,128)} %wr.2) | copy-start | bytes 1572868
  6.7 1.0 %copy-start.9 = (f32[256,512]{1,0:T(8,128)S(1)}, f32[256,512]{1,0:T(8,128)}, u32[]{:S(2)}) copy-start(f32[256,512]{1,0:T(8,128)} %wo.2) | copy-start | bytes 1572868
  9.5 11.3 %copy-start.16 = (f32[256]{0:T(256)S(1)}, f32[256]{0:T(256)}, u32[]{:S(2)}) copy-start(f32[256]{0:T(256)} %param.44) | copy-start | bytes 3076
  9.5 11.3 %copy-start.17 = (f32[256]{0:T(256)S(1)}, f32[256]{0:T(256)}, u32[]{:S(2)}) copy-start(f32[256]{0:T(256)} %param.49) | copy-start | bytes 3076
  9.5 11.3 %copy-start.20 = (f32[512]{0:T(512)S(1)}, f32[512]{0:T(512)}, u32[]{:S(2)}) copy-start(f32[512]{0:T(512)} %param.36) | copy-start | bytes 6148
  9.6 11.3 %copy-start.21 = (f32[512]{0:T(512)S(1)}, f32[512]{0:T(512)}, u32[]{:S(2)}) copy-start(f32[512]{0:T(512)} %param.41) | copy-start | bytes 6148
  9.6 11.3 %copy-start.22 = (f32[512]{0:T(512)S(1)}, f32[512]{0:T(512)}, u32[]{:S(2)}) copy-start(f32[512]{0:T(512)} %param.46) | copy-start | bytes 6148
  9.6 11.3 %copy-start.23 = (f32[512]{0:T(512)S(1)}, f32[512]{0:T(512)}, u32[]{:S(2)}) copy-start(f32[512]{0:T(512)} %param.51) | copy-start | bytes 6148
  9.6 11.3 %copy-start.25 = (f32[256]{0:T(256)S(1)}, f32[256]{0:T(256)}, u32[]{:S(2)}) copy-start(f32[256]{0:T(256)} %param.39) | copy-start | bytes 3076
  9.6 11.3 %copy-start.10 = (f32[512,256]{1,0:T(8,128)S(1)}, f32[512,256]{1,0:T(8,128)}, u32[]{:S(2)}) copy-start(f32[512,256]{1,0:T(8,128)} %refs_5_.1) | copy-start | bytes 1572868
  9.6 11.3 %copy-start.11 = (f32[512,256]{1,0:T(8,128)S(1)}, f32[512,256]{1,0:T(8,128)}, u32[]{:S(2)}) copy-start(f32[512,256]{1,0:T(8,128)} %refs_6_.1) | copy-start | bytes 1572868
  9.6 9.1 %collective-permute-start = (f32[64,512]{1,0:T(8,128)S(1)}, f32[64,512]{1,0:T(8,128)S(1)}, u32[]{:S(2)}, u32[]{:S(2)}) collective-permute-start(f32[64,512]{1,0:T(8,128)S(1)} %shard_map.257.refs_7_.refs_0_), channel_id=1, source_target_pairs={{0,2},{2,0},{1,3},{3,1},{4,6},{6,4},{5,7},{7,5},{8,10},{10,8},{9,1... | collective-permute-start | bytes 393224 | tf_op jit(solution)/shard_map/ppermute | solution.py:381
  9.7 17.4 %copy-start.15 = (s32[512,6]{0,1:T(8,128)S(1)}, s32[512,6]{0,1:T(8,128)}, u32[]{:S(2)}) copy-start(s32[512,6]{0,1:T(8,128)} %param.30) | copy-start | bytes 36868
  9.7 17.4 %copy-start.19 = (s32[64,6]{0,1:T(8,128)S(1)}, s32[64,6]{0,1:T(8,128)}, u32[]{:S(2)}) copy-start(s32[64,6]{0,1:T(8,128)} %param.31) | copy-start | bytes 4612
  9.7 24.1 %copy-start.12 = (f32[256,512]{1,0:T(8,128)S(1)}, f32[256,512]{1,0:T(8,128)}, u32[]{:S(2)}) copy-start(f32[256,512]{1,0:T(8,128)} %refs_10_.1) | copy-start | bytes 1572868
  11.7 18.3 %collective-permute-start.6 = (f32[392,256]{1,0:T(8,128)}, f32[392,256]{1,0:T(8,128)S(1)}, u32[]{:S(2)}, u32[]{:S(2)}) collective-permute-start(f32[392,256]{1,0:T(8,128)} %shard_map.262), channel_id=1, source_target_pairs={{0,2},{2,0},{1,3},{3,1},{4,6},{6,4},{5,7},{7,5},{8,10},{10,8},{9,1... | collective-permute-start | bytes 1204232 | tf_op jit(solution)/shard_map/ppermute | solution.py:381
  18.8 11.3 %collective-permute-start.5 = (f32[392,256]{1,0:T(8,128)S(1)}, f32[392,256]{1,0:T(8,128)S(1)}, u32[]{:S(2)}, u32[]{:S(2)}) collective-permute-start(f32[392,256]{1,0:T(8,128)S(1)} %collective-permute-done.4.refs_5_), channel_id=1, source_target_pairs={{0,16},{16,0},{1,17},{17,1},{2,18},{18,2},{3,19},{19,3},{4,20},{20... | collective-permute-start | bytes 1204232 | tf_op jit(solution)/shard_map/ppermute | solution.py:420
  20.9 15.3 %copy-start.1 = (f32[512,256]{1,0:T(8,128)S(1)}, f32[512,256]{1,0:T(8,128)}, u32[]{:S(2)}) copy-start(f32[512,256]{1,0:T(8,128)} %refs_1_.5) | copy-start | bytes 1572868
  20.9 15.3 %copy-start.2 = (f32[512,256]{1,0:T(8,128)S(1)}, f32[512,256]{1,0:T(8,128)}, u32[]{:S(2)}) copy-start(f32[512,256]{1,0:T(8,128)} %refs_2_.7) | copy-start | bytes 1572868
  20.9 15.3 %copy-start.3 = (f32[256,512]{1,0:T(8,128)S(1)}, f32[256,512]{1,0:T(8,128)}, u32[]{:S(2)}) copy-start(f32[256,512]{1,0:T(8,128)} %refs_4_.2) | copy-start | bytes 1572868
  21.5 6.7 %collective-permute-start.1 = (f32[64,256]{1,0:T(8,128)S(1)}, f32[64,256]{1,0:T(8,128)S(1)}, u32[]{:S(2)}, u32[]{:S(2)}) collective-permute-start(f32[64,256]{1,0:T(8,128)S(1)} %get-tuple-element.36.refs_2_.refs_0_), channel_id=1, source_target_pairs={{0,4},{4,8},{8,12},{12,0},{1,5},{5,9},{9,13},{13,1},{2,6},{6,10},{... | collective-permute-start | bytes 196616 | tf_op jit(solution)/shard_map/ppermute | solution.py:381
  23.2 5.2 %collective-permute-start.2 = (f32[64,256]{1,0:T(8,128)S(1)}, f32[64,256]{1,0:T(8,128)S(1)}, u32[]{:S(2)}, u32[]{:S(2)}) collective-permute-start(f32[64,256]{1,0:T(8,128)S(1)} %get-tuple-element.36.refs_2_.refs_0_), channel_id=1, source_target_pairs={{0,8},{4,12},{8,0},{12,4},{1,9},{5,13},{9,1},{13,5},{2,10},{6,14},... | collective-permute-start | bytes 196616 | tf_op jit(solution)/shard_map/ppermute | solution.py:381
  25.7 4.3 %collective-permute-start.3 = (f32[64,256]{1,0:T(8,128)S(1)}, f32[64,256]{1,0:T(8,128)S(1)}, u32[]{:S(2)}, u32[]{:S(2)}) collective-permute-start(f32[64,256]{1,0:T(8,128)S(1)} %get-tuple-element.36.refs_2_.refs_0_), channel_id=1, source_target_pairs={{0,12},{4,0},{8,4},{12,8},{1,13},{5,1},{9,5},{13,9},{2,14},{6,2},{... | collective-permute-start | bytes 196616 | tf_op jit(solution)/shard_map/ppermute | solution.py:381
  30.0 6.2 %collective-permute-start.12 = (f32[392,256]{1,0:T(8,128)S(1)}, f32[392,256]{1,0:T(8,128)S(1)}, u32[]{:S(2)}, u32[]{:S(2)}) collective-permute-start(f32[392,256]{1,0:T(8,128)S(1)} %collective-permute-done.4.refs_5_), channel_id=1, source_target_pairs={{0,1},{1,0},{2,3},{3,2},{4,5},{5,4},{6,7},{7,6},{8,9},{9,8},{10,11... | collective-permute-start | bytes 1204232 | tf_op jit(solution)/shard_map/ppermute | solution.py:381
  30.0 6.2 %collective-permute-start.13 = (f32[392,256]{1,0:T(8,128)S(1)}, f32[392,256]{1,0:T(8,128)S(1)}, u32[]{:S(2)}, u32[]{:S(2)}) collective-permute-start(f32[392,256]{1,0:T(8,128)S(1)} %collective-permute-done.5.refs_7_), channel_id=1, source_target_pairs={{0,1},{1,0},{2,3},{3,2},{4,5},{5,4},{6,7},{7,6},{8,9},{9,8},{10,11... | collective-permute-start | bytes 1204232 | tf_op jit(solution)/shard_map/ppermute | solution.py:381
  30.5 11.8 %collective-permute-start.16 = (f32[392,256]{1,0:T(8,128)S(1)}, f32[392,256]{1,0:T(8,128)S(1)}, u32[]{:S(2)}, u32[]{:S(2)}) collective-permute-start(f32[392,256]{1,0:T(8,128)S(1)} %collective-permute-done.6.refs_0_), channel_id=1, source_target_pairs={{0,4},{4,0},{8,12},{12,8},{1,5},{5,1},{9,13},{13,9},{2,6},{6,2},{1... | collective-permute-start | bytes 1204232 | tf_op jit(solution)/shard_map/ppermute | solution.py:420
  31.1 1.3 %collective-permute-start.7 = (f32[64,256]{1,0:T(8,128)S(1)}, f32[64,256]{1,0:T(8,128)S(1)}, u32[]{:S(2)}, u32[]{:S(2)}) collective-permute-start(f32[64,256]{1,0:T(8,128)S(1)} %get-tuple-element.36.refs_2_.refs_0_), channel_id=1, source_target_pairs={{0,1},{1,0},{2,3},{3,2},{4,5},{5,4},{6,7},{7,6},{8,9},{9,8},{10,11... | collective-permute-start | bytes 196616 | tf_op jit(solution)/shard_map/ppermute | solution.py:381
  31.1 1.4 %collective-permute-start.10 = (f32[64,256]{1,0:T(8,128)S(1)}, f32[64,256]{1,0:T(8,128)S(1)}, u32[]{:S(2)}, u32[]{:S(2)}) collective-permute-start(f32[64,256]{1,0:T(8,128)S(1)} %collective-permute-done.3.refs_3_), channel_id=1, source_target_pairs={{0,1},{1,0},{2,3},{3,2},{4,5},{5,4},{6,7},{7,6},{8,9},{9,8},{10,11... | collective-permute-start | bytes 196616 | tf_op jit(solution)/shard_map/ppermute | solution.py:381
  32.4 1.3 %collective-permute-start.8 = (f32[64,256]{1,0:T(8,128)S(1)}, f32[64,256]{1,0:T(8,128)S(1)}, u32[]{:S(2)}, u32[]{:S(2)}) collective-permute-start(f32[64,256]{1,0:T(8,128)S(1)} %collective-permute-done.1.refs_1_), channel_id=1, source_target_pairs={{0,1},{1,0},{2,3},{3,2},{4,5},{5,4},{6,7},{7,6},{8,9},{9,8},{10,11... | collective-permute-start | bytes 196616 | tf_op jit(solution)/shard_map/ppermute | solution.py:381
  32.6 1.3 %collective-permute-start.9 = (f32[64,256]{1,0:T(8,128)S(1)}, f32[64,256]{1,0:T(8,128)S(1)}, u32[]{:S(2)}, u32[]{:S(2)}) collective-permute-start(f32[64,256]{1,0:T(8,128)S(1)} %collective-permute-done.2.refs_2_), channel_id=1, source_target_pairs={{0,1},{1,0},{2,3},{3,2},{4,5},{5,4},{6,7},{7,6},{8,9},{9,8},{10,11... | collective-permute-start | bytes 196616 | tf_op jit(solution)/shard_map/ppermute | solution.py:381
  34.6 5.8 %copy-start.14 = (s32[512,3]{0,1:T(4,128)S(1)}, s32[512,3]{0,1:T(4,128)}, u32[]{:S(2)}) copy-start(s32[512,3]{0,1:T(4,128)} %param.29) | copy-start | bytes 18436
  34.6 5.8 %collective-permute-start.11 = (f32[64,512]{1,0:T(8,128)S(1)}, f32[64,512]{1,0:T(8,128)S(1)}, u32[]{:S(2)}, u32[]{:S(2)}) collective-permute-start(f32[64,512]{1,0:T(8,128)S(1)} %shard_map.263.refs_9_.refs_0_), channel_id=1, source_target_pairs={{0,2},{2,0},{1,3},{3,1},{4,6},{6,4},{5,7},{7,5},{8,10},{10,8},{9,1... | collective-permute-start | bytes 393224 | tf_op jit(solution)/shard_map/ppermute | solution.py:381
  42.3 4.8 %collective-permute-start.17 = (f32[392,256]{1,0:T(8,128)S(1)}, f32[392,256]{1,0:T(8,128)S(1)}, u32[]{:S(2)}, u32[]{:S(2)}) collective-permute-start(f32[392,256]{1,0:T(8,128)S(1)} %collective-permute-done.6.refs_0_), channel_id=1, source_target_pairs={{0,1},{1,0},{2,3},{3,2},{4,5},{5,4},{6,7},{7,6},{8,9},{9,8},{10,11... | collective-permute-start | bytes 1204232 | tf_op jit(solution)/shard_map/ppermute | solution.py:381
  42.4 4.7 %collective-permute-start.18 = (f32[392,256]{1,0:T(8,128)S(1)}, f32[392,256]{1,0:T(8,128)S(1)}, u32[]{:S(2)}, u32[]{:S(2)}) collective-permute-start(f32[392,256]{1,0:T(8,128)S(1)} %collective-permute-done.16.refs_2_), channel_id=1, source_target_pairs={{0,1},{1,0},{2,3},{3,2},{4,5},{5,4},{6,7},{7,6},{8,9},{9,8},{10,11... | collective-permute-start | bytes 1204232 | tf_op jit(solution)/shard_map/ppermute | solution.py:381
  42.9 11.4 %collective-permute-start.15 = (f32[128,512]{1,0:T(8,128)S(1)}, f32[128,512]{1,0:T(8,128)S(1)}, u32[]{:S(2)}, u32[]{:S(2)}) collective-permute-start(f32[128,512]{1,0:T(8,128)S(1)} %get-tuple-element.52.head), channel_id=1, source_target_pairs={{0,13},{1,0},{4,1},{5,4},{8,5},{9,8},{12,9},{13,12},{2,15},{3,2},{... | collective-permute-start | bytes 786440 | tf_op jit(solution)/shard_map/ppermute | solution.py:381
  45.7 8.5 %collective-permute-start.14 = (f32[128,512]{1,0:T(8,128)S(1)}, f32[128,512]{1,0:T(8,128)S(1)}, u32[]{:S(2)}, u32[]{:S(2)}) collective-permute-start(f32[128,512]{1,0:T(8,128)S(1)} %get-tuple-element.51.tail), channel_id=1, source_target_pairs={{0,1},{1,4},{4,5},{5,8},{8,9},{9,12},{12,13},{13,0},{2,3},{3,6},{6... | collective-permute-start | bytes 786440 | tf_op jit(solution)/shard_map/ppermute | solution.py:381
  45.7 1.4 %copy-start.4 = (f32[512,256]{1,0:T(8,128)S(1)}, f32[512,256]{1,0:T(8,128)}, u32[]{:S(2)}) copy-start(f32[512,256]{1,0:T(8,128)} %ws.3) | copy-start | bytes 1572868
  45.7 1.4 %copy-start.5 = (f32[512,256]{1,0:T(8,128)S(1)}, f32[512,256]{1,0:T(8,128)}, u32[]{:S(2)}) copy-start(f32[512,256]{1,0:T(8,128)} %wr.3) | copy-start | bytes 1572868
  45.7 1.4 %copy-start.6 = (f32[256,512]{1,0:T(8,128)S(1)}, f32[256,512]{1,0:T(8,128)}, u32[]{:S(2)}) copy-start(f32[256,512]{1,0:T(8,128)} %wo.3) | copy-start | bytes 1572868

commit v11 on v9

--- a/solution.py
+++ b/solution.py
@@ -136,10 +136,8 @@
         biases[i : i + 1] = params[4 + i][...]
 
 
-def share_kernel(*refs):
-    down_own, bottom_own, (down_pack, bottom_pack, sems) = refs[:4], refs[4:8], refs[8:]
-    copies = share_copies(down_own, down_pack, "parts") + share_copies(bottom_own, bottom_pack, "patch")
-    for move in started(copies, sems):
+def share_kernel(axis, *refs):
+    for move in started(share_copies(refs[:4], refs[4], axis), refs[5]):
         move.wait()
 
 
@@ -316,11 +314,13 @@
     )
 
 
-def bottom_rows(nodes, receivers, picks, senders, wo, gain):
+def bottom_rows(nodes, receivers, picks, senders, wo, gain, ahead=None):
     half = senders.shape[1] // 2
     hidden = []
     for place in (slice(0, half), slice(half, 2 * half)):
         picked = dot(picks, senders[:, place])
+        if ahead is not None:
+            picked = picked + ahead[:, place]
         hidden.append(silu_sum(picked, receivers[:, place], picks.shape[0] // nodes.shape[0]))
     return nodes + gain * normed(dot3(jnp.concatenate(hidden, axis=1), wo))
 
@@ -333,7 +333,7 @@
         out[(2 * i + 1) * rim : (2 * i + 2) * rim, columns] = low[strip]
 
 
-def bottom_middle_kernel(rim, head, middle, tail, picks, ws, wr, wo, bias, gains, senders, receivers, out):
+def bottom_middle_kernel(rim, head, middle, tail, picks, ws, wr, wo, bias, gains, receivers, out, ahead, senders):
     nodes = jnp.concatenate([head[...], middle[...], tail[...]], axis=0)
     left = threefold(nodes)
     width = ws.shape[2]
@@ -350,9 +350,14 @@
             middle[inner], receivers[place], picks[i * size : (i + 1) * size],
             senders[2 * (i - 1) * rim : 2 * (i + 2) * rim, :], wo[...], gains[3:4],
         )
-
-
-def bottom_edge_kernel(rim, before, after, head, tail, inner, picks, senders, receivers, ws, wo, gains, out, outer, strips, sems):
+    near, last = senders.shape[0], picks.shape[0] - size
+    ahead[0:size, :] = dot(picks[0:size, 2 * rim : 6 * rim], senders[0 : 4 * rim, :])
+    ahead[size : 2 * size, :] = dot(
+        picks[last : last + size, 0 : 4 * rim], senders[near - 4 * rim : near, :]
+    )
+
+
+def bottom_edge_kernel(rim, before, after, head, tail, inner, ahead, picks, receivers, ws, wo, gains, out, outer, strips, sems):
     total = receivers.shape[0]
     size = picks.shape[0] * rim // total
     moves = [pltpu.make_async_copy(inner, out.at[pl.ds(rim, total - 2 * rim)], sems.at[0])]
@@ -361,19 +366,13 @@
     width = ws.shape[2]
     for g in range(ws.shape[0]):
         put_strips(0.5 * dot(left, ws[g]), rim, outer, slice(g * width, (g + 1) * width))
-    near = senders.shape[0]
     for side, nodes in enumerate((head, tail)):
-        first = 0 if side == 0 else total - rim
+        first, column = (0, 0) if side == 0 else (total - rim, 4 * rim)
         place = slice(first, first + rim)
-        beyond = outer[2 * side * rim : 2 * (side + 1) * rim, :]
-        reach = (
-            [beyond, senders[0 : 4 * rim, :]]
-            if side == 0
-            else [senders[near - 4 * rim : near, :], beyond]
-        )
+        chosen = picks[first // rim * size : (first // rim + 1) * size, column : column + 2 * rim]
         strips[side * rim : (side + 1) * rim, :] = bottom_rows(
-            nodes[...], receivers[place], picks[first // rim * size : (first // rim + 1) * size],
-            jnp.concatenate(reach, axis=0), wo[...], gains[3:4],
+            nodes[...], receivers[place], chosen, outer[2 * side * rim : 2 * (side + 1) * rim, :],
+            wo[...], gains[3:4], ahead[side * size : (side + 1) * size, :],
         )
         strip = strips.at[pl.ds(side * rim, rim)]
         moves.append(pltpu.make_async_copy(strip, out.at[pl.ds(first, rim)], sems.at[1 + side]))
@@ -534,14 +533,17 @@
     parts = sub_parts(part)
     down_own = (downward_sender, downward_receiver, downward_output, downward_bias[None])
     bottom_own = (bottom_sender, bottom_receiver, bottom_output, bottom_bias[None])
-    down_pack, bottom_pack = call(
-        share_kernel,
-        [pack("parts"), pack("patch")],
-        [*down_own, *bottom_own],
-        latent,
-        [pltpu.SemaphoreType.DMA((6 + 2 * columns,))],
-        far=range(8),
-        limit=tight_limit,
+    (down_pack,), (bottom_pack,) = (
+        call(
+            functools.partial(share_kernel, axis),
+            [pack(axis)],
+            own,
+            latent,
+            [pltpu.SemaphoreType.DMA((3 + columns,))],
+            far=range(4),
+            limit=tight_limit,
+        )
+        for axis, own in (("parts", down_own), ("patch", bottom_own))
     )
     gains, biases = call(
         stack_kernel,
@@ -576,9 +578,8 @@
     (part,) = call(
         functools.partial(coarse_kernel, len(pieces)),
         [like((blocks, latent))],
-        [*pieces, picks, receivers, coarse_output, *bottom_near],
+        [*pieces, picks, receivers, coarse_output],
         4 * coarse_links.size * names * width,
-        unread=len(bottom_near),
     )
     parts = sub_parts(part)
     bottom_near = held(bottom_near, part)
@@ -617,16 +618,17 @@
         [bottom_sender, bottom_receiver, biases, bottom_output, *bottom_packs],
         latent * hidden,
     )
-    senders, receivers, inner = call(
+    receivers, inner, ahead = call(
         functools.partial(bottom_middle_kernel, rim),
-        [like((2 * rows, hidden), bf16), like((rows, hidden)), like((rows - 2 * rim, latent))],
+        [like((rows, hidden)), like((rows - 2 * rim, latent)), like((bottom_links.size // (rows // rim) * 2, hidden))],
         [head, middle, tail, bottom_picks, ws, wr, wo, bias, gains],
         (12 * rows + 12 * rows) * latent * hidden,
+        [pltpu.VMEM((2 * rows, hidden), bf16)],
     )
     (new_nodes,) = call(
         functools.partial(bottom_edge_kernel, rim),
         [like((rows, latent))],
-        [before, after, head, tail, inner, bottom_picks, senders, receivers, ws, wo, gains],
+        [before, after, head, tail, inner, ahead, bottom_picks, receivers, ws, wo, gains],
         24 * rim * latent * hidden,
         [
             pltpu.VMEM((4 * rim, hidden), bf16),

time: 61.2 us -> 58.9 us (0.962)
  waiting for transfers between devices: 18.5 us -> 13.8 us
  Pallas kernels: 23.2 us -> 24.7 us
  starting transfers between devices: 18 us -> 18.9 us
    ppermute x17, waiting for transfers between devices: 13.1 us -> 8.22 us  [shifted(): lax.ppermute(values, axis, [(i, (i + step) % count) for i in range(count)])]
    pallas_call x12 -> x13, Pallas kernels: 23.2 us -> 24.7 us  [call(): pl.pallas_call((lambda *refs: kernel(*refs[:read], *refs[read + unread:])...]
    ppermute x17, starting transfers between devices: 14.9 us -> 15.8 us  [shifted(): lax.ppermute(values, axis, [(i, (i + step) % count) for i in range(count)])]
  transfers between devices with their start and end apart: 19 -> 19, of which waited for: 7 -> 9; matrix products, arithmetic and copies ran while one was open for 0% -> 0% of each run, Pallas kernels for 18% -> 22%
where the time goes in v11:
time: 58.9 us; the launch traced here: 58.6 us
  Pallas kernels  24.7 us (42%)
  starting transfers between devices  18.9 us (32%)
  waiting for transfers between devices  13.8 us (23%)
  between operations  1.17 us (2%)
    pallas_call x13, Pallas kernels, call(): pl.pallas_call((lambda *refs: kernel(*refs[:read], *refs[read + unread:])...  24.7 us
    ppermute x17, starting transfers between devices, shifted(): lax.ppermute(values, axis, [(i, (i + step) % count) for i in range(count)])  15.8 us
    ppermute x17, waiting for transfers between devices, shifted(): lax.ppermute(values, axis, [(i, (i + step) % count) for i in range(count)])  8.22 us
    ppermute x2, waiting for transfers between devices, over_partners(): lax.ppermute(share, axis, [(i, i - i % count + (i + p) % count) for i in...  5.55 us
    ppermute x2, starting transfers between devices, over_partners(): lax.ppermute(share, axis, [(i, i - i % count + (i + p) % count) for i in...  3.1 us
  transfers between devices with their start and end apart: 19, of which 9 were waited for; matrix products, arithmetic and copies ran while one was open for 0% of the time, Pallas kernels for 22%

profile of v11, /device:TPU:0, one launch (start us, length us, event | category | flops | bytes accessed | tf_op | source)
XLA Modules:
  0.0 58.6 jit_solution(13944575649380185874)
XLA Ops:
  0.6 5.1 %shard_map.257.refs_7_.refs_0_ = f32[64,512]{1,0:T(8,128)} custom-call(f32[512,512]{1,0:T(8,128)} %nodes.1, f32[64,512]{1,0:T(8,128)} %refs_2_.4, f32[512,256]{1,0:T(8,128)} %ws_hbm.1, f32[512,256]{1,0:T(8,128)} %wr_hbm.1, f32[256,512]{1,0:T(8,128)} %wo_hbm.1, s32[7,64]{1,0:T(8,128)} %bitcast.25, f32[1,256]{1,0:T(1,128)} %bitcast.26), custom_call_target="tpu_custom_call" | custom-call | flops 402653184 | bytes 2886400 | tf_op jit(solution)/shard_map/pallas_call | solution.py:392
  5.8 3.0 %collective-permute-start = (f32[64,512]{1,0:T(8,128)}, f32[64,512]{1,0:T(8,128)S(1)}, u32[]{:S(2)}, u32[]{:S(2)}) collective-permute-start(f32[64,512]{1,0:T(8,128)} %shard_map.257.refs_7_.refs_0_), channel_id=1, source_target_pairs={{0,2},{2,0},{1,3},{3,1},{4,6},{6,4},{5,7},{7,5},{8,10},{10,8},{9,1... | collective-permute-start | bytes 393224 | tf_op jit(solution)/shard_map/ppermute | solution.py:409
  8.8 0.0 copy-start.16
  8.8 0.0 copy-start.17
  8.8 0.0 copy-start.18
  8.8 0.0 copy-start.19
  8.8 0.0 copy-start.8
  8.8 0.0 copy-start.9
  8.9 0.0 copy-start.11
  8.9 1.9 %shard_map.261 = f32[392,256]{1,0:T(8,128)} custom-call(f32[512,256]{1,0:T(8,128)} %refs_1_.5, f32[512,256]{1,0:T(8,128)} %refs_2_.7, f32[256,512]{1,0:T(8,128)} %refs_4_.2, f32[1,256]{1,0:T(1,128)} %bitcast.14), custom_call_target="tpu_custom_call" | custom-call | flops 512 | bytes 1975296 | tf_op jit(solution)/shard_map/pallas_call | solution.py:392
  10.8 0.1 collective-permute-start.4
  10.9 0.0 copy-start.20
  10.9 0.0 copy-start.21
  10.9 1.8 %shard_map.263 = f32[392,256]{1,0:T(8,128)} custom-call(f32[512,256]{1,0:T(8,128)} %ws.1, f32[512,256]{1,0:T(8,128)} %wr.1, f32[256,512]{1,0:T(8,128)} %wo.1, f32[1,256]{1,0:T(1,128)} %bitcast.16), custom_call_target="tpu_custom_call" | custom-call | flops 512 | bytes 1975296 | tf_op jit(solution)/shard_map/pallas_call | solution.py:392
  12.7 2.1 %collective-permute-start.13 = (f32[392,256]{1,0:T(8,128)}, f32[392,256]{1,0:T(8,128)S(1)}, u32[]{:S(2)}, u32[]{:S(2)}) collective-permute-start(f32[392,256]{1,0:T(8,128)} %shard_map.263), channel_id=1, source_target_pairs={{0,2},{2,0},{1,3},{3,1},{4,6},{6,4},{5,7},{7,5},{8,10},{10,8},{9,1... | collective-permute-start | bytes 1204232 | tf_op jit(solution)/shard_map/ppermute | solution.py:409
  14.8 0.0 copy-done.13
  14.9 0.0 collective-permute-done.refs_1_
  14.9 0.6 %shard_map.259 = (f32[64,512]{1,0:T(8,128)S(1)}, f32[64,256]{1,0:T(8,128)S(1)}, f32[64,256]{1,0:T(8,128)S(1)}) custom-call(f32[64,512]{1,0:T(8,128)S(1)} %copy-done.7, f32[64,512]{1,0:T(8,128)S(1)} %collective-permute-done.refs_1_, f32[64,512]{1,0:T(8,128)S(1)} %copy-done.11, f32[4,512]{1,0:T(4,128)S(1)} %get-tuple-element.34.refs_3_.gains, ...), custom_call_target="tpu_custom_call" | custom-call | flops 100663296 | bytes 1715200 | tf_op jit(solution)/shard_map/pallas_call | solution.py:392
  15.5 1.6 %collective-permute-start.1 = (f32[64,256]{1,0:T(8,128)S(1)}, f32[64,256]{1,0:T(8,128)S(1)}, u32[]{:S(2)}, u32[]{:S(2)}) collective-permute-start(f32[64,256]{1,0:T(8,128)S(1)} %get-tuple-element.36.refs_2_.refs_0_), channel_id=1, source_target_pairs={{0,4},{4,8},{8,12},{12,0},{1,5},{5,9},{9,13},{13,1},{2,6},{6,10},{... | collective-permute-start | bytes 196616 | tf_op jit(solution)/shard_map/ppermute | solution.py:409
  17.1 2.6 %collective-permute-start.2 = (f32[64,256]{1,0:T(8,128)S(1)}, f32[64,256]{1,0:T(8,128)S(1)}, u32[]{:S(2)}, u32[]{:S(2)}) collective-permute-start(f32[64,256]{1,0:T(8,128)S(1)} %get-tuple-element.36.refs_2_.refs_0_), channel_id=1, source_target_pairs={{0,8},{4,12},{8,0},{12,4},{1,9},{5,13},{9,1},{13,5},{2,10},{6,14},... | collective-permute-start | bytes 196616 | tf_op jit(solution)/shard_map/ppermute | solution.py:409
  19.7 1.3 %collective-permute-start.3 = (f32[64,256]{1,0:T(8,128)S(1)}, f32[64,256]{1,0:T(8,128)S(1)}, u32[]{:S(2)}, u32[]{:S(2)}) collective-permute-start(f32[64,256]{1,0:T(8,128)S(1)} %get-tuple-element.36.refs_2_.refs_0_), channel_id=1, source_target_pairs={{0,12},{4,0},{8,4},{12,8},{1,13},{5,1},{9,5},{13,9},{2,14},{6,2},{... | collective-permute-start | bytes 196616 | tf_op jit(solution)/shard_map/ppermute | solution.py:409
  21.1 0.0 copy-start.6
  21.1 1.1 %shard_map.260 = (bf16[384,1024]{1,0:T(8,128)(2,1)S(1)}, bf16[3072,768]{1,0:T(8,128)(2,1)S(1)}) custom-call(s32[6,64]{1,0:T(8,128)S(1)} %bitcast.24, s32[6,512]{1,0:T(8,128)S(1)} %bitcast.23, f32[64,256]{1,0:T(8,128)S(1)} %get-tuple-element.36.refs_2_.refs_0_), custom_call_target="tpu_custom_call" | custom-call | flops 99999997952 | bytes 5584384 | tf_op jit(solution)/shard_map/pallas_call | solution.py:392
  22.3 0.0 copy-start
  22.3 0.0 copy-start.4
  22.3 0.0 collective-permute-done.1.refs_1_
  22.3 1.7 %collective-permute-done.2.refs_2_ = f32[64,256]{1,0:T(8,128)S(1)} collective-permute-done((f32[64,256]{1,0:T(8,128)S(1)}, f32[64,256]{1,0:T(8,128)S(1)}, u32[]{:S(2)}, u32[]{:S(2)}) %collective-permute-start.2) | collective-permute-done | bytes 65568 | tf_op jit(solution)/shard_map/ppermute | solution.py:409
  24.0 0.3 collective-permute-done.3.refs_3_
  24.3 0.0 collective-permute-done.4.refs_5_
  24.4 1.5 %collective-permute-start.10 = (f32[392,256]{1,0:T(8,128)S(1)}, f32[392,256]{1,0:T(8,128)S(1)}, u32[]{:S(2)}, u32[]{:S(2)}) collective-permute-start(f32[392,256]{1,0:T(8,128)S(1)} %collective-permute-done.4.refs_5_), channel_id=1, source_target_pairs={{0,16},{16,0},{1,17},{17,1},{2,18},{18,2},{3,19},{19,3},{4,20},{20... | collective-permute-start | bytes 1204232 | tf_op jit(solution)/shard_map/ppermute | solution.py:448
  25.9 0.0 collective-permute-start.5
  25.9 0.5 collective-permute-start.6
  26.4 0.0 collective-permute-start.7
  26.4 0.7 %collective-permute-done.5.refs_4_ = f32[64,256]{1,0:T(8,128)S(1)} collective-permute-done((f32[64,256]{1,0:T(8,128)S(1)}, f32[64,256]{1,0:T(8,128)S(1)}, u32[]{:S(2)}, u32[]{:S(2)}) %collective-permute-start.5) | collective-permute-done | bytes 65568 | tf_op jit(solution)/shard_map/ppermute | solution.py:409
  27.1 0.2 collective-permute-start.8
  27.3 0.0 collective-permute-done.6.refs_5_
  27.3 0.3 collective-permute-done.7.refs_6_
  27.6 0.7 %collective-permute-done.8.refs_7_ = f32[64,256]{1,0:T(8,128)S(1)} collective-permute-done((f32[64,256]{1,0:T(8,128)S(1)}, f32[64,256]{1,0:T(8,128)S(1)}, u32[]{:S(2)}, u32[]{:S(2)}) %collective-permute-start.8) | collective-permute-done | bytes 65568 | tf_op jit(solution)/shard_map/ppermute | solution.py:409
  28.4 0.8 %shard_map.262.refs_9_.refs_0_ = f32[64,512]{1,0:T(8,128)S(1)} custom-call(f32[64,256]{1,0:T(8,128)S(1)} %get-tuple-element.36.refs_2_.refs_0_, f32[64,256]{1,0:T(8,128)S(1)} %collective-permute-done.1.refs_1_, f32[64,256]{1,0:T(8,128)S(1)} %collective-permute-done.2.refs_2_, f32[64,256]{1,0:T(8,128)S(1)} %collective-permute-done.3.refs_3_, ...), custom_call_target="tpu_custom_call" | custom-call | flops 201326592 | bytes 2031616 | tf_op jit(solution)/shard_map/pallas_call | solution.py:392
  29.2 0.0 copy-start.12
  29.2 0.6 %collective-permute-start.9 = (f32[64,512]{1,0:T(8,128)S(1)}, f32[64,512]{1,0:T(8,128)S(1)}, u32[]{:S(2)}, u32[]{:S(2)}) collective-permute-start(f32[64,512]{1,0:T(8,128)S(1)} %shard_map.262.refs_9_.refs_0_), channel_id=1, source_target_pairs={{0,2},{2,0},{1,3},{3,1},{4,6},{6,4},{5,7},{7,5},{8,10},{10,8},{9,1... | collective-permute-start | bytes 393224 | tf_op jit(solution)/shard_map/ppermute | solution.py:409
  29.8 0.7 %collective-permute-done.13.refs_0_ = f32[392,256]{1,0:T(8,128)S(1)} collective-permute-done((f32[392,256]{1,0:T(8,128)}, f32[392,256]{1,0:T(8,128)S(1)}, u32[]{:S(2)}, u32[]{:S(2)}) %collective-permute-start.13) | collective-permute-done | bytes 401440 | tf_op jit(solution)/shard_map/ppermute | solution.py:409
  30.5 1.6 %collective-permute-start.14 = (f32[392,256]{1,0:T(8,128)S(1)}, f32[392,256]{1,0:T(8,128)S(1)}, u32[]{:S(2)}, u32[]{:S(2)}) collective-permute-start(f32[392,256]{1,0:T(8,128)S(1)} %collective-permute-done.13.refs_0_), channel_id=1, source_target_pairs={{0,4},{4,0},{8,12},{12,8},{1,5},{5,1},{9,13},{13,9},{2,6},{6,2},{1... | collective-permute-start | bytes 1204232 | tf_op jit(solution)/shard_map/ppermute | solution.py:448
  32.0 2.8 %collective-permute-done.9.refs_1_ = f32[64,512]{1,0:T(8,128)S(1)} collective-permute-done((f32[64,512]{1,0:T(8,128)S(1)}, f32[64,512]{1,0:T(8,128)S(1)}, u32[]{:S(2)}, u32[]{:S(2)}) %collective-permute-start.9) | collective-permute-done | bytes 131104 | tf_op jit(solution)/shard_map/ppermute | solution.py:409
  34.8 0.0 collective-permute-done.10.refs_7_
  34.8 0.0 collective-permute-start.11
  34.8 0.5 collective-permute-start.12
  35.3 5.5 %collective-permute-done.14.refs_10_.refs_2_ = f32[392,256]{1,0:T(8,128)S(1)} collective-permute-done((f32[392,256]{1,0:T(8,128)S(1)}, f32[392,256]{1,0:T(8,128)S(1)}, u32[]{:S(2)}, u32[]{:S(2)}) %collective-permute-start.14) | collective-permute-done | bytes 401440 | tf_op jit(solution)/shard_map/ppermute | solution.py:448
  40.9 0.0 collective-permute-done.11.refs_6_
  40.9 0.0 collective-permute-done.12.refs_8_
  40.9 1.7 %shard_map.264 = (f32[512,512]{1,0:T(8,128)S(1)}, bf16[2,1536,256]{2,1,0:T(8,128)(2,1)S(1)}, bf16[1536,512]{1,0:T(8,128)(2,1)S(1)}) custom-call(f32[512,512]{1,0:T(8,128)S(1)} %copy-done, f32[512,256]{1,0:T(8,128)S(1)} %copy-done.4, f32[512,256]{1,0:T(8,128)S(1)} %copy-done.5, f32[3,256]{1,0:T(4,128)S(1)} %get-tuple-element.35.refs_4_.refs_3_.biases, ...), custom_call_target="tpu_custom_call" | custom-call | flops 805306368 | bytes 8956928 | tf_op jit(solution)/shard_map/pallas_call | solution.py:392
  42.6 1.9 %shard_map.265 = (f32[64,512]{1,0:T(8,128)}, bf16[128,512]{1,0:T(8,128)(2,1)S(1)}, f32[128,512]{1,0:T(8,128)S(1)}, f32[128,512]{1,0:T(8,128)S(1)}) custom-call(f32[64,512]{1,0:T(8,128)S(1)} %shard_map.262.refs_9_.refs_0_, f32[64,512]{1,0:T(8,128)S(1)} %collective-permute-done.9.refs_1_, f32[64,512]{1,0:T(8,128)S(1)} %get-tuple-element.44.refs_2_, ...), custom_call_target="tpu_custom_call" | custom-call | flops 402653184 | bytes 6436864 | tf_op jit(solution)/shard_map/pallas_call | solution.py:392
  44.5 0.1 collective-permute-start.17
  44.5 0.5 collective-permute-start.18
  45.0 2.7 %collective-permute-start.16 = (f32[128,512]{1,0:T(8,128)S(1)}, f32[128,512]{1,0:T(8,128)S(1)}, u32[]{:S(2)}, u32[]{:S(2)}) collective-permute-start(f32[128,512]{1,0:T(8,128)S(1)} %get-tuple-element.53.head), channel_id=1, source_target_pairs={{0,13},{1,0},{4,1},{5,4},{8,5},{9,8},{12,9},{13,12},{2,15},{3,2},{... | collective-permute-start | bytes 786440 | tf_op jit(solution)/shard_map/ppermute | solution.py:409
  47.7 0.0 collective-permute-start.15
  47.8 1.4 %shard_map.266.middle = f32[256,512]{1,0:T(8,128)S(1)} custom-call(f32[512,512]{1,0:T(8,128)S(1)} %copy-done, f32[512,512]{1,0:T(8,128)S(1)} %get-tuple-element.49.refs_5_.receivers, s32[3,512]{1,0:T(4,128)S(1)} %bitcast.13, bf16[128,512]{1,0:T(8,128)(2,1)S(1)} %get-tuple-element.54.senders, bf16[1536,512]{1,0:T(8,128)(2,1)S(1)} %get-tuple-element.51.refs_8_.wo, ...), custom_call_target="tpu_custom_call" | custom-call | flops 402653184 | bytes 4339712 | tf_op jit(solution)/shard_map/pallas_call | solution.py:392
  49.1 0.0 collective-permute-done.17.refs_1_
  49.1 0.0 collective-permute-done.18.refs_3_
  49.2 0.6 shard_map.267
  49.7 4.8 %shard_map.268 = (f32[512,512]{1,0:T(8,128)S(1)}, f32[256,512]{1,0:T(8,128)S(1)}, f32[1536,512]{1,0:T(8,128)S(1)}) custom-call(f32[128,512]{1,0:T(8,128)S(1)} %get-tuple-element.53.head, f32[256,512]{1,0:T(8,128)S(1)} %shard_map.266.middle, f32[128,512]{1,0:T(8,128)S(1)} %get-tuple-element.52.tail, bf16[3072,768]{1,0:T(8,128)(2,1)S(1)} %get-tuple-element.55.picks, ...), custom_call_target="tpu_custom_call" | custom-call | flops 3221225472 | bytes 15228928 | tf_op jit(solution)/shard_map/pallas_call | solution.py:392
  54.5 0.9 %collective-permute-done.15.before = f32[128,512]{1,0:T(8,128)S(1)} collective-permute-done((f32[128,512]{1,0:T(8,128)S(1)}, f32[128,512]{1,0:T(8,128)S(1)}, u32[]{:S(2)}, u32[]{:S(2)}) %collective-permute-start.15) | collective-permute-done | bytes 262176 | tf_op jit(solution)/shard_map/ppermute | solution.py:409
  55.4 0.0 collective-permute-done.16.after
  55.4 3.1 %shard_map.269 = f32[512,512]{1,0:T(8,128)} custom-call(f32[128,512]{1,0:T(8,128)S(1)} %collective-permute-done.15.before, f32[128,512]{1,0:T(8,128)S(1)} %collective-permute-done.16.after, f32[128,512]{1,0:T(8,128)S(1)} %get-tuple-element.53.head, f32[128,512]{1,0:T(8,128)S(1)} %get-tuple-element.52.tail, f32[256,512]{1,0:T(8,128)S(1)} %get-tuple-element.62.inner, ...), custom_call_target="tpu_custom_call" | custom-call | flops 805306368 | bytes 14688256 | tf_op jit(solution)/shard_map/pallas_call | solution.py:392
  (31 shorter events, 0.1 us)
Async XLA Ops:
  5.8 9.1 %collective-permute-start = (f32[64,512]{1,0:T(8,128)}, f32[64,512]{1,0:T(8,128)S(1)}, u32[]{:S(2)}, u32[]{:S(2)}) collective-permute-start(f32[64,512]{1,0:T(8,128)} %shard_map.257.refs_7_.refs_0_), channel_id=1, source_target_pairs={{0,2},{2,0},{1,3},{3,1},{4,6},{6,4},{5,7},{7,5},{8,10},{10,8},{9,1... | collective-permute-start | bytes 393224 | tf_op jit(solution)/shard_map/ppermute | solution.py:409
  8.8 6.0 %copy-start.7 = (f32[64,512]{1,0:T(8,128)S(1)}, f32[64,512]{1,0:T(8,128)}, u32[]{:S(2)}) copy-start(f32[64,512]{1,0:T(8,128)} %shard_map.257.refs_7_.refs_0_) | copy-start | bytes 393220
  8.8 6.0 %copy-start.13 = (f32[256]{0:T(256)S(1)}, f32[256]{0:T(256)}, u32[]{:S(2)}) copy-start(f32[256]{0:T(256)} %param.44) | copy-start | bytes 3076
  8.8 6.0 %copy-start.14 = (f32[256]{0:T(256)S(1)}, f32[256]{0:T(256)}, u32[]{:S(2)}) copy-start(f32[256]{0:T(256)} %param.49) | copy-start | bytes 3076
  8.8 6.0 %copy-start.15 = (f32[512]{0:T(512)S(1)}, f32[512]{0:T(512)}, u32[]{:S(2)}) copy-start(f32[512]{0:T(512)} %param.36) | copy-start | bytes 6148
  8.8 6.0 %copy-start.16 = (f32[512]{0:T(512)S(1)}, f32[512]{0:T(512)}, u32[]{:S(2)}) copy-start(f32[512]{0:T(512)} %param.41) | copy-start | bytes 6148
  8.8 6.0 %copy-start.17 = (f32[512]{0:T(512)S(1)}, f32[512]{0:T(512)}, u32[]{:S(2)}) copy-start(f32[512]{0:T(512)} %param.46) | copy-start | bytes 6148
  8.8 6.0 %copy-start.18 = (f32[512]{0:T(512)S(1)}, f32[512]{0:T(512)}, u32[]{:S(2)}) copy-start(f32[512]{0:T(512)} %param.51) | copy-start | bytes 6148
  8.8 6.0 %copy-start.19 = (f32[256]{0:T(256)S(1)}, f32[256]{0:T(256)}, u32[]{:S(2)}) copy-start(f32[256]{0:T(256)} %param.39) | copy-start | bytes 3076
  8.8 6.0 %copy-start.8 = (f32[512,256]{1,0:T(8,128)S(1)}, f32[512,256]{1,0:T(8,128)}, u32[]{:S(2)}) copy-start(f32[512,256]{1,0:T(8,128)} %refs_5_.1) | copy-start | bytes 1572868
  8.8 6.0 %copy-start.9 = (f32[512,256]{1,0:T(8,128)S(1)}, f32[512,256]{1,0:T(8,128)}, u32[]{:S(2)}) copy-start(f32[512,256]{1,0:T(8,128)} %refs_6_.1) | copy-start | bytes 1572868
  8.9 6.0 %copy-start.11 = (f32[64,512]{1,0:T(8,128)S(1)}, f32[64,512]{1,0:T(8,128)}, u32[]{:S(2)}) copy-start(f32[64,512]{1,0:T(8,128)} %refs_2_.4) | copy-start | bytes 393220
  10.8 13.5 %collective-permute-start.4 = (f32[392,256]{1,0:T(8,128)}, f32[392,256]{1,0:T(8,128)S(1)}, u32[]{:S(2)}, u32[]{:S(2)}) collective-permute-start(f32[392,256]{1,0:T(8,128)} %shard_map.261), channel_id=1, source_target_pairs={{0,2},{2,0},{1,3},{3,1},{4,6},{6,4},{5,7},{7,5},{8,10},{10,8},{9,1... | collective-permute-start | bytes 1204232 | tf_op jit(solution)/shard_map/ppermute | solution.py:409
  10.9 10.2 %copy-start.20 = (s32[512,6]{0,1:T(8,128)S(1)}, s32[512,6]{0,1:T(8,128)}, u32[]{:S(2)}) copy-start(s32[512,6]{0,1:T(8,128)} %param.30) | copy-start | bytes 36868
  10.9 10.2 %copy-start.21 = (s32[64,6]{0,1:T(8,128)S(1)}, s32[64,6]{0,1:T(8,128)}, u32[]{:S(2)}) copy-start(s32[64,6]{0,1:T(8,128)} %param.31) | copy-start | bytes 4612
  12.7 17.7 %collective-permute-start.13 = (f32[392,256]{1,0:T(8,128)}, f32[392,256]{1,0:T(8,128)S(1)}, u32[]{:S(2)}, u32[]{:S(2)}) collective-permute-start(f32[392,256]{1,0:T(8,128)} %shard_map.263), channel_id=1, source_target_pairs={{0,2},{2,0},{1,3},{3,1},{4,6},{6,4},{5,7},{7,5},{8,10},{10,8},{9,1... | collective-permute-start | bytes 1204232 | tf_op jit(solution)/shard_map/ppermute | solution.py:409
  15.5 6.8 %collective-permute-start.1 = (f32[64,256]{1,0:T(8,128)S(1)}, f32[64,256]{1,0:T(8,128)S(1)}, u32[]{:S(2)}, u32[]{:S(2)}) collective-permute-start(f32[64,256]{1,0:T(8,128)S(1)} %get-tuple-element.36.refs_2_.refs_0_), channel_id=1, source_target_pairs={{0,4},{4,8},{8,12},{12,0},{1,5},{5,9},{9,13},{13,1},{2,6},{6,10},{... | collective-permute-start | bytes 196616 | tf_op jit(solution)/shard_map/ppermute | solution.py:409
  17.1 6.9 %collective-permute-start.2 = (f32[64,256]{1,0:T(8,128)S(1)}, f32[64,256]{1,0:T(8,128)S(1)}, u32[]{:S(2)}, u32[]{:S(2)}) collective-permute-start(f32[64,256]{1,0:T(8,128)S(1)} %get-tuple-element.36.refs_2_.refs_0_), channel_id=1, source_target_pairs={{0,8},{4,12},{8,0},{12,4},{1,9},{5,13},{9,1},{13,5},{2,10},{6,14},... | collective-permute-start | bytes 196616 | tf_op jit(solution)/shard_map/ppermute | solution.py:409
  19.7 4.6 %collective-permute-start.3 = (f32[64,256]{1,0:T(8,128)S(1)}, f32[64,256]{1,0:T(8,128)S(1)}, u32[]{:S(2)}, u32[]{:S(2)}) collective-permute-start(f32[64,256]{1,0:T(8,128)S(1)} %get-tuple-element.36.refs_2_.refs_0_), channel_id=1, source_target_pairs={{0,12},{4,0},{8,4},{12,8},{1,13},{5,1},{9,5},{13,9},{2,14},{6,2},{... | collective-permute-start | bytes 196616 | tf_op jit(solution)/shard_map/ppermute | solution.py:409
  21.1 7.3 %copy-start.10 = (f32[256,512]{1,0:T(8,128)S(1)}, f32[256,512]{1,0:T(8,128)}, u32[]{:S(2)}) copy-start(f32[256,512]{1,0:T(8,128)} %refs_10_.1) | copy-start | bytes 1572868
  21.1 19.8 %copy-start.5 = (f32[512,256]{1,0:T(8,128)S(1)}, f32[512,256]{1,0:T(8,128)}, u32[]{:S(2)}) copy-start(f32[512,256]{1,0:T(8,128)} %refs_2_.7) | copy-start | bytes 1572868
  21.1 19.8 %copy-start.6 = (f32[256,512]{1,0:T(8,128)S(1)}, f32[256,512]{1,0:T(8,128)}, u32[]{:S(2)}) copy-start(f32[256,512]{1,0:T(8,128)} %refs_4_.2) | copy-start | bytes 1572868
  22.3 18.6 %copy-start = (f32[512,512]{1,0:T(8,128)S(1)}, f32[512,512]{1,0:T(8,128)}, u32[]{:S(2)}) copy-start(f32[512,512]{1,0:T(8,128)} %nodes.1) | copy-start | bytes 3145732
  22.3 18.6 %copy-start.4 = (f32[512,256]{1,0:T(8,128)S(1)}, f32[512,256]{1,0:T(8,128)}, u32[]{:S(2)}) copy-start(f32[512,256]{1,0:T(8,128)} %refs_1_.5) | copy-start | bytes 1572868
  24.4 10.4 %collective-permute-start.10 = (f32[392,256]{1,0:T(8,128)S(1)}, f32[392,256]{1,0:T(8,128)S(1)}, u32[]{:S(2)}, u32[]{:S(2)}) collective-permute-start(f32[392,256]{1,0:T(8,128)S(1)} %collective-permute-done.4.refs_5_), channel_id=1, source_target_pairs={{0,16},{16,0},{1,17},{17,1},{2,18},{18,2},{3,19},{19,3},{4,20},{20... | collective-permute-start | bytes 1204232 | tf_op jit(solution)/shard_map/ppermute | solution.py:448
  25.9 1.3 %collective-permute-start.5 = (f32[64,256]{1,0:T(8,128)S(1)}, f32[64,256]{1,0:T(8,128)S(1)}, u32[]{:S(2)}, u32[]{:S(2)}) collective-permute-start(f32[64,256]{1,0:T(8,128)S(1)} %get-tuple-element.36.refs_2_.refs_0_), channel_id=1, source_target_pairs={{0,1},{1,0},{2,3},{3,2},{4,5},{5,4},{6,7},{7,6},{8,9},{9,8},{10,11... | collective-permute-start | bytes 196616 | tf_op jit(solution)/shard_map/ppermute | solution.py:409
  25.9 1.4 %collective-permute-start.6 = (f32[64,256]{1,0:T(8,128)S(1)}, f32[64,256]{1,0:T(8,128)S(1)}, u32[]{:S(2)}, u32[]{:S(2)}) collective-permute-start(f32[64,256]{1,0:T(8,128)S(1)} %collective-permute-done.1.refs_1_), channel_id=1, source_target_pairs={{0,1},{1,0},{2,3},{3,2},{4,5},{5,4},{6,7},{7,6},{8,9},{9,8},{10,11... | collective-permute-start | bytes 196616 | tf_op jit(solution)/shard_map/ppermute | solution.py:409
  26.4 1.3 %collective-permute-start.7 = (f32[64,256]{1,0:T(8,128)S(1)}, f32[64,256]{1,0:T(8,128)S(1)}, u32[]{:S(2)}, u32[]{:S(2)}) collective-permute-start(f32[64,256]{1,0:T(8,128)S(1)} %collective-permute-done.2.refs_2_), channel_id=1, source_target_pairs={{0,1},{1,0},{2,3},{3,2},{4,5},{5,4},{6,7},{7,6},{8,9},{9,8},{10,11... | collective-permute-start | bytes 196616 | tf_op jit(solution)/shard_map/ppermute | solution.py:409
  27.1 1.3 %collective-permute-start.8 = (f32[64,256]{1,0:T(8,128)S(1)}, f32[64,256]{1,0:T(8,128)S(1)}, u32[]{:S(2)}, u32[]{:S(2)}) collective-permute-start(f32[64,256]{1,0:T(8,128)S(1)} %collective-permute-done.3.refs_3_), channel_id=1, source_target_pairs={{0,1},{1,0},{2,3},{3,2},{4,5},{5,4},{6,7},{7,6},{8,9},{9,8},{10,11... | collective-permute-start | bytes 196616 | tf_op jit(solution)/shard_map/ppermute | solution.py:409
  29.2 13.4 %copy-start.12 = (s32[512,3]{0,1:T(4,128)S(1)}, s32[512,3]{0,1:T(4,128)}, u32[]{:S(2)}) copy-start(s32[512,3]{0,1:T(4,128)} %param.29) | copy-start | bytes 18436
  29.2 5.6 %collective-permute-start.9 = (f32[64,512]{1,0:T(8,128)S(1)}, f32[64,512]{1,0:T(8,128)S(1)}, u32[]{:S(2)}, u32[]{:S(2)}) collective-permute-start(f32[64,512]{1,0:T(8,128)S(1)} %shard_map.262.refs_9_.refs_0_), channel_id=1, source_target_pairs={{0,2},{2,0},{1,3},{3,1},{4,6},{6,4},{5,7},{7,5},{8,10},{10,8},{9,1... | collective-permute-start | bytes 393224 | tf_op jit(solution)/shard_map/ppermute | solution.py:409
  30.5 10.4 %collective-permute-start.14 = (f32[392,256]{1,0:T(8,128)S(1)}, f32[392,256]{1,0:T(8,128)S(1)}, u32[]{:S(2)}, u32[]{:S(2)}) collective-permute-start(f32[392,256]{1,0:T(8,128)S(1)} %collective-permute-done.13.refs_0_), channel_id=1, source_target_pairs={{0,4},{4,0},{8,12},{12,8},{1,5},{5,1},{9,13},{13,9},{2,6},{6,2},{1... | collective-permute-start | bytes 1204232 | tf_op jit(solution)/shard_map/ppermute | solution.py:448
  34.8 6.1 %collective-permute-start.11 = (f32[392,256]{1,0:T(8,128)S(1)}, f32[392,256]{1,0:T(8,128)S(1)}, u32[]{:S(2)}, u32[]{:S(2)}) collective-permute-start(f32[392,256]{1,0:T(8,128)S(1)} %collective-permute-done.4.refs_5_), channel_id=1, source_target_pairs={{0,1},{1,0},{2,3},{3,2},{4,5},{5,4},{6,7},{7,6},{8,9},{9,8},{10,11... | collective-permute-start | bytes 1204232 | tf_op jit(solution)/shard_map/ppermute | solution.py:409
  34.8 6.1 %collective-permute-start.12 = (f32[392,256]{1,0:T(8,128)S(1)}, f32[392,256]{1,0:T(8,128)S(1)}, u32[]{:S(2)}, u32[]{:S(2)}) collective-permute-start(f32[392,256]{1,0:T(8,128)S(1)} %collective-permute-done.10.refs_7_), channel_id=1, source_target_pairs={{0,1},{1,0},{2,3},{3,2},{4,5},{5,4},{6,7},{7,6},{8,9},{9,8},{10,11... | collective-permute-start | bytes 1204232 | tf_op jit(solution)/shard_map/ppermute | solution.py:409
  44.5 4.7 %collective-permute-start.17 = (f32[392,256]{1,0:T(8,128)S(1)}, f32[392,256]{1,0:T(8,128)S(1)}, u32[]{:S(2)}, u32[]{:S(2)}) collective-permute-start(f32[392,256]{1,0:T(8,128)S(1)} %collective-permute-done.13.refs_0_), channel_id=1, source_target_pairs={{0,1},{1,0},{2,3},{3,2},{4,5},{5,4},{6,7},{7,6},{8,9},{9,8},{10,11... | collective-permute-start | bytes 1204232 | tf_op jit(solution)/shard_map/ppermute | solution.py:409
  44.5 4.6 %collective-permute-start.18 = (f32[392,256]{1,0:T(8,128)S(1)}, f32[392,256]{1,0:T(8,128)S(1)}, u32[]{:S(2)}, u32[]{:S(2)}) collective-permute-start(f32[392,256]{1,0:T(8,128)S(1)} %collective-permute-done.14.refs_10_.refs_2_), channel_id=1, source_target_pairs={{0,1},{1,0},{2,3},{3,2},{4,5},{5,4},{6,7},{7,6},{8,9},{9,8},{10,11... | collective-permute-start | bytes 1204232 | tf_op jit(solution)/shard_map/ppermute | solution.py:409
  45.0 10.3 %collective-permute-start.16 = (f32[128,512]{1,0:T(8,128)S(1)}, f32[128,512]{1,0:T(8,128)S(1)}, u32[]{:S(2)}, u32[]{:S(2)}) collective-permute-start(f32[128,512]{1,0:T(8,128)S(1)} %get-tuple-element.53.head), channel_id=1, source_target_pairs={{0,13},{1,0},{4,1},{5,4},{8,5},{9,8},{12,9},{13,12},{2,15},{3,2},{... | collective-permute-start | bytes 786440 | tf_op jit(solution)/shard_map/ppermute | solution.py:409
  47.7 7.6 %collective-permute-start.15 = (f32[128,512]{1,0:T(8,128)S(1)}, f32[128,512]{1,0:T(8,128)S(1)}, u32[]{:S(2)}, u32[]{:S(2)}) collective-permute-start(f32[128,512]{1,0:T(8,128)S(1)} %get-tuple-element.52.tail), channel_id=1, source_target_pairs={{0,1},{1,4},{4,5},{5,8},{8,9},{9,12},{12,13},{13,0},{2,3},{3,6},{6... | collective-permute-start | bytes 786440 | tf_op jit(solution)/shard_map/ppermute | solution.py:409
  47.7 1.4 %copy-start.1 = (f32[512,256]{1,0:T(8,128)S(1)}, f32[512,256]{1,0:T(8,128)}, u32[]{:S(2)}) copy-start(f32[512,256]{1,0:T(8,128)} %ws.1) | copy-start | bytes 1572868
  47.8 1.4 %copy-start.2 = (f32[512,256]{1,0:T(8,128)S(1)}, f32[512,256]{1,0:T(8,128)}, u32[]{:S(2)}) copy-start(f32[512,256]{1,0:T(8,128)} %wr.1) | copy-start | bytes 1572868
  47.8 1.4 %copy-start.3 = (f32[256,512]{1,0:T(8,128)S(1)}, f32[256,512]{1,0:T(8,128)}, u32[]{:S(2)}) copy-start(f32[256,512]{1,0:T(8,128)} %wo.1) | copy-start | bytes 1572868

commit v12 on v10

--- a/solution.py
+++ b/solution.py
@@ -108,8 +108,13 @@
         biases[i : i + 1] = params[4 + i][...]
 
 
-def share_kernel(axis, *refs):
-    for move in started(share_copies(refs[:4], refs[4], axis), refs[5]):
+def share_kernel(plan, *refs):
+    packs, sems = refs[-1 - len(plan) : -1], refs[-1]
+    copies, first = [], 0
+    for (count, axis), pack in zip(plan, packs):
+        copies += share_copies(refs[first : first + count], pack, axis)
+        first += count
+    for move in started(copies, sems):
         move.wait()
 
 
@@ -223,14 +228,15 @@
             out[block] = jnp.broadcast_to(pack[at : at + 1, :], (8, own.shape[1]))
 
 
-def down_weights_kernel(count, nodes, ws, wr, biases, wo, *refs):
-    packs, (receivers, ws_all, wo_all, wr_all, bias_all) = refs[:count], refs[count:]
+def down_weights_kernel(counts, nodes, ws, wr, biases, wo, *refs):
+    first, rest = refs[: counts[0]], refs[counts[0] : sum(counts)]
+    receivers, ws_all, wo_all, wr_all, bias_all = refs[sum(counts) :]
     width = ws.shape[1]
     share = ws.shape[0] // shares("parts")[1]
-    collect_in(ws, packs, "parts", 0, ws_all)
-    collect_in(wr, packs, "parts", share, wr_all)
-    collect_out(wo, packs, "parts", 2 * share, wo_all)
-    collect_bias(biases[1:2], packs, "parts", 3 * share, bias_all)
+    collect_in(ws, first, "parts", 0, ws_all)
+    collect_in(wr, first, "parts", share, wr_all)
+    collect_bias(biases[1:2], first, "parts", 2 * share, bias_all)
+    collect_out(wo, rest, None, 0, wo_all)
     states = threefold(nodes[...])
     for g in range(wr_all.shape[0]):
         receivers[:, g * width : (g + 1) * width] = 0.5 * (dot(states, wr_all[g]) + bias_all[g][0:1])
@@ -407,6 +413,8 @@
 
 
 def partners(axis):
+    if axis is None:
+        return 0, 1
     if axis == "parts":
         return lax.axis_index(axis), lax.axis_size(axis)
     count = 2 if lax.axis_size(axis) % 2 == 0 else 1
@@ -478,9 +486,9 @@
     columns = latent // width
     lvls = lax.axis_size("lvl")
 
-    def pack(axis):
+    def pack(axis, into, out_of, bias):
         count = shares(axis)[1]
-        return like((2 * latent // count + width // count * columns + 8, width))
+        return like((into * latent // count + out_of * (width // count) * columns + 8 * bias, width))
 
     (part,) = call(
         upward_kernel,
@@ -493,19 +501,23 @@
         limit=up_limit,
     )
     parts = sub_parts(part)
-    down_own = (downward_sender, downward_receiver, downward_output, downward_bias[None])
-    bottom_own = (bottom_sender, bottom_receiver, bottom_output, bottom_bias[None])
-    (down_pack,), (bottom_pack,) = (
-        call(
-            functools.partial(share_kernel, axis),
-            [pack(axis)],
-            own,
-            latent,
-            [pltpu.SemaphoreType.DMA((3 + columns,))],
-            far=range(4),
-            limit=share_limit,
-        )
-        for axis, own in (("parts", down_own), ("patch", bottom_own))
+    (first_pack,) = call(
+        functools.partial(share_kernel, ((3, "parts"),)),
+        [pack("parts", 2, 0, 1)],
+        [downward_sender, downward_receiver, downward_bias[None]],
+        10**9,
+        [pltpu.SemaphoreType.DMA((3,))],
+        far=range(3),
+        limit=share_limit,
+    )
+    down_pack, bottom_pack = call(
+        functools.partial(share_kernel, ((1, None), (4, "patch"))),
+        [pack(None, 0, 1, 0), pack("patch", 2, 1, 1)],
+        [downward_output, bottom_sender, bottom_receiver, bottom_output, bottom_bias[None]],
+        10**9,
+        [pltpu.SemaphoreType.DMA((3 + 2 * columns,))],
+        far=range(5),
+        limit=share_limit,
     )
     gains, biases = call(
         stack_kernel,
@@ -517,10 +529,9 @@
         latent * hidden,
         unread=1,
     )
-    down_near = over_sub(down_pack)
-    down_near = held(down_near, parts[-1])
-    bottom_near = over_sub(bottom_pack)
-    down_far = over_partners(down_near, "parts")
+    first_near = held(over_sub(first_pack), parts[-1])
+    down_near, bottom_near = over_sub(down_pack), over_sub(bottom_pack)
+    first_far = over_partners(first_near, "parts")
     coarse_up, senders, receivers = call(
         functools.partial(coarse_project_kernel, len(parts)),
         [like((blocks, latent)), like((blocks, width)), like((blocks, width))],
@@ -536,10 +547,11 @@
         coarse_links.size * names,
         unread=1,
     )
-    pieces, (picks, bottom_picks, down_near, down_far, bottom_near) = coarse_pieces(
-        senders, (picks, bottom_picks, down_near, down_far, bottom_near)
-    )
-    down_packs = all_shares(down_near, down_far)
+    pieces, (picks, bottom_picks, first_near, first_far, down_near, bottom_near) = coarse_pieces(
+        senders, (picks, bottom_picks, first_near, first_far, down_near, bottom_near)
+    )
+    first_packs = all_shares(first_near, first_far)
+    down_packs = [pack for row in over_lvl(down_near) for pack in row]
     bottom_far = over_partners(bottom_near, "patch")
     (part,) = call(
         functools.partial(coarse_kernel, len(pieces)),
@@ -549,9 +561,9 @@
     )
     parts = sub_parts(part)
     receivers, ws, wo = call(
-        functools.partial(down_weights_kernel, len(down_packs)),
+        functools.partial(down_weights_kernel, (len(first_packs), len(down_packs))),
         [like((rows, hidden)), into, out_of],
-        [node_states, downward_sender, downward_receiver, biases, downward_output, *down_packs, part],
+        [node_states, downward_sender, downward_receiver, biases, downward_output, *first_packs, *down_packs, part],
         6 * rows * latent * hidden,
         [pltpu.VMEM((subs, 3 * latent, width), bf16), pltpu.VMEM((subs, 8, width), f32)],
         unread=1,

time: 57.9 us -> 59.5 us (1.028)
  waiting for transfers between devices: 13 us -> 16.2 us
  local copies, waits for them, and re-layouts: 2.2 us -> 0.13 us
    ppermute x17 -> x19, waiting for transfers between devices: 13 us -> 16.2 us  [shifted(): lax.ppermute(values, axis, [(i, (i + step) % count) for i in range(count)])]
    unnamed x52, local copies, waits for them, and re-layouts: 2.2 us -> 0.13 us
    ppermute x17 -> x19, starting transfers between devices: 17.2 us -> 17.9 us  [shifted(): lax.ppermute(values, axis, [(i, (i + step) % count) for i in range(count)])]
  transfers between devices with their start and end apart: 19 -> 21, of which waited for: 8 -> 8; matrix products, arithmetic and copies ran while one was open for 0% -> 0% of each run, Pallas kernels for 28% -> 28%
where the time goes in v12:
time: 59.5 us; the launch traced here: 59.3 us
  Pallas kernels  21.7 us (36%)
  starting transfers between devices  20.1 us (34%)
  waiting for transfers between devices  16.2 us (27%)
  between operations  1.25 us (2%)
    pallas_call x13, Pallas kernels, call(): pl.pallas_call((lambda *refs: kernel(*refs[:read], *refs[read + unread:])...  21.7 us
    ppermute x19, starting transfers between devices, shifted(): lax.ppermute(values, axis, [(i, (i + step) % count) for i in range(count)])  17.9 us
    ppermute x19, waiting for transfers between devices, shifted(): lax.ppermute(values, axis, [(i, (i + step) % count) for i in range(count)])  16.2 us
    ppermute x2, starting transfers between devices, over_partners(): lax.ppermute(share, axis, [(i, i - i % count + (i + p) % count) for i in...  2.16 us
  transfers between devices with their start and end apart: 21, of which 8 were waited for; matrix products, arithmetic and copies ran while one was open for 0% of the time, Pallas kernels for 28%

profile of v12, /device:TPU:0, one launch (start us, length us, event | category | flops | bytes accessed | tf_op | source)
XLA Modules:
  0.0 59.3 jit_solution(15998394919308535470)
XLA Ops:
  0.7 1.9 %shard_map.261 = f32[264,256]{1,0:T(8,128)} custom-call(f32[512,256]{1,0:T(8,128)} %refs_1_.5, f32[512,256]{1,0:T(8,128)} %refs_2_.5, f32[1,256]{1,0:T(1,128)} %bitcast.23), custom_call_target="tpu_custom_call" | custom-call | flops 1000000000 | bytes 1319936 | tf_op jit(solution)/shard_map/pallas_call | solution.py:370
  2.6 3.0 %collective-permute-start.4 = (f32[264,256]{1,0:T(8,128)}, f32[264,256]{1,0:T(8,128)S(1)}, u32[]{:S(2)}, u32[]{:S(2)}) collective-permute-start(f32[264,256]{1,0:T(8,128)} %shard_map.261), channel_id=1, source_target_pairs={{0,2},{2,0},{1,3},{3,1},{4,6},{6,4},{5,7},{7,5},{8,10},{10,8},{9,1... | collective-permute-start | bytes 811016 | tf_op jit(solution)/shard_map/ppermute | solution.py:387
  5.6 1.8 %shard_map.257.refs_7_.refs_0_ = f32[64,512]{1,0:T(8,128)S(1)} custom-call(f32[512,512]{1,0:T(8,128)S(1)} %copy-done, f32[64,512]{1,0:T(8,128)S(1)} %copy-done.13, s32[7,64]{1,0:T(8,128)S(1)} %bitcast.15, f32[512,256]{1,0:T(8,128)S(1)} %copy-done.7, f32[512,256]{1,0:T(8,128)S(1)} %copy-done.8, f32[1,256]{1,0:T(1,128)S(1)} %bitcast.21, f32[256,512]{1,0:T(8,128)S(1)} %copy-done.9), custom_call_target="tpu_custom_call" | custom-call | flops 402653184 | bytes 2886400 | tf_op jit(solution)/shard_map/pallas_call | solution.py:370
  7.4 0.1 collective-permute-start
  7.5 0.0 copy-start.21
  7.6 0.0 copy-start.23
  7.6 0.0 copy-start.24
  7.6 0.0 copy-start.25
  7.6 0.0 copy-start.10
  7.6 0.0 copy-start.11
  7.6 2.1 %shard_map.262 = (f32[256,256]{1,0:T(8,128)}, f32[392,256]{1,0:T(8,128)}) custom-call(f32[256,512]{1,0:T(8,128)} %refs_4_.2, f32[512,256]{1,0:T(8,128)} %ws.3, f32[512,256]{1,0:T(8,128)} %wr.3, f32[256,512]{1,0:T(8,128)} %wo.3, f32[1,256]{1,0:T(1,128)} %bitcast.25), custom_call_target="tpu_custom_call" | custom-call | flops 1000000000 | bytes 2761728 | tf_op jit(solution)/shard_map/pallas_call | solution.py:370
  9.7 0.0 copy-start.15
  9.7 0.0 copy-start.17
  9.8 0.0 copy-start.12
  9.8 2.0 %collective-permute-start.7 = (f32[392,256]{1,0:T(8,128)}, f32[392,256]{1,0:T(8,128)S(1)}, u32[]{:S(2)}, u32[]{:S(2)}) collective-permute-start(f32[392,256]{1,0:T(8,128)} %get-tuple-element.44), channel_id=1, source_target_pairs={{0,2},{2,0},{1,3},{3,1},{4,6},{6,4},{5,7},{7,5},{8,10},{10,8},{9,1... | collective-permute-start | bytes 1204232 | tf_op jit(solution)/shard_map/ppermute | solution.py:387
  11.8 4.1 %collective-permute-done.refs_1_ = f32[64,512]{1,0:T(8,128)S(1)} collective-permute-done((f32[64,512]{1,0:T(8,128)S(1)}, f32[64,512]{1,0:T(8,128)S(1)}, u32[]{:S(2)}, u32[]{:S(2)}) %collective-permute-start) | collective-permute-done | bytes 131104 | tf_op jit(solution)/shard_map/ppermute | solution.py:387
  15.9 0.0 collective-permute-done.4.refs_5_
  15.9 2.1 %collective-permute-start.5 = (f32[264,256]{1,0:T(8,128)S(1)}, f32[264,256]{1,0:T(8,128)S(1)}, u32[]{:S(2)}, u32[]{:S(2)}) collective-permute-start(f32[264,256]{1,0:T(8,128)S(1)} %collective-permute-done.4.refs_5_), channel_id=1, source_target_pairs={{0,16},{16,0},{1,17},{17,1},{2,18},{18,2},{3,19},{19,3},{4,20},{20... | collective-permute-start | bytes 811016 | tf_op jit(solution)/shard_map/ppermute | solution.py:428
  18.0 1.5 %collective-permute-start.6 = (f32[256,256]{1,0:T(8,128)}, f32[256,256]{1,0:T(8,128)S(1)}, u32[]{:S(2)}, u32[]{:S(2)}) collective-permute-start(f32[256,256]{1,0:T(8,128)} %get-tuple-element.43), channel_id=1, source_target_pairs={{0,2},{2,0},{1,3},{3,1},{4,6},{6,4},{5,7},{7,5},{8,10},{10,8},{9,1... | collective-permute-start | bytes 786440 | tf_op jit(solution)/shard_map/ppermute | solution.py:387
  19.6 0.0 copy-start.1
  19.6 0.0 copy-start.2
  19.6 0.0 copy-start.3
  19.6 0.6 shard_map.259
  20.2 1.6 %collective-permute-start.1 = (f32[64,256]{1,0:T(8,128)S(1)}, f32[64,256]{1,0:T(8,128)S(1)}, u32[]{:S(2)}, u32[]{:S(2)}) collective-permute-start(f32[64,256]{1,0:T(8,128)S(1)} %get-tuple-element.39.refs_2_.refs_0_), channel_id=1, source_target_pairs={{0,4},{4,8},{8,12},{12,0},{1,5},{5,9},{9,13},{13,1},{2,6},{6,10},{... | collective-permute-start | bytes 196616 | tf_op jit(solution)/shard_map/ppermute | solution.py:387
  21.8 2.6 %collective-permute-start.2 = (f32[64,256]{1,0:T(8,128)S(1)}, f32[64,256]{1,0:T(8,128)S(1)}, u32[]{:S(2)}, u32[]{:S(2)}) collective-permute-start(f32[64,256]{1,0:T(8,128)S(1)} %get-tuple-element.39.refs_2_.refs_0_), channel_id=1, source_target_pairs={{0,8},{4,12},{8,0},{12,4},{1,9},{5,13},{9,1},{13,5},{2,10},{6,14},... | collective-permute-start | bytes 196616 | tf_op jit(solution)/shard_map/ppermute | solution.py:387
  24.4 2.6 %collective-permute-done.1.refs_1_ = f32[64,256]{1,0:T(8,128)S(1)} collective-permute-done((f32[64,256]{1,0:T(8,128)S(1)}, f32[64,256]{1,0:T(8,128)S(1)}, u32[]{:S(2)}, u32[]{:S(2)}) %collective-permute-start.1) | collective-permute-done | bytes 65568 | tf_op jit(solution)/shard_map/ppermute | solution.py:387
  27.0 1.1 %collective-permute-start.3 = (f32[64,256]{1,0:T(8,128)S(1)}, f32[64,256]{1,0:T(8,128)S(1)}, u32[]{:S(2)}, u32[]{:S(2)}) collective-permute-start(f32[64,256]{1,0:T(8,128)S(1)} %get-tuple-element.39.refs_2_.refs_0_), channel_id=1, source_target_pairs={{0,12},{4,0},{8,4},{12,8},{1,13},{5,1},{9,5},{13,9},{2,14},{6,2},{... | collective-permute-start | bytes 196616 | tf_op jit(solution)/shard_map/ppermute | solution.py:387
  28.1 0.0 collective-permute-done.2.refs_2_
  28.1 0.0 collective-permute-start.8
  28.1 1.1 %shard_map.260 = (bf16[384,1024]{1,0:T(8,128)(2,1)S(1)}, bf16[3072,768]{1,0:T(8,128)(2,1)S(1)}) custom-call(s32[6,64]{1,0:T(8,128)S(1)} %bitcast.16, s32[6,512]{1,0:T(8,128)S(1)} %bitcast.14, f32[64,256]{1,0:T(8,128)S(1)} %get-tuple-element.39.refs_2_.refs_0_), custom_call_target="tpu_custom_call" | custom-call | flops 196608 | bytes 5584384 | tf_op jit(solution)/shard_map/pallas_call | solution.py:370
  29.3 2.0 %collective-permute-done.3.refs_3_ = f32[64,256]{1,0:T(8,128)S(1)} collective-permute-done((f32[64,256]{1,0:T(8,128)S(1)}, f32[64,256]{1,0:T(8,128)S(1)}, u32[]{:S(2)}, u32[]{:S(2)}) %collective-permute-start.3) | collective-permute-done | bytes 65568 | tf_op jit(solution)/shard_map/ppermute | solution.py:387
  31.3 0.0 collective-permute-done.7.refs_0_
  31.3 0.0 collective-permute-done.5.refs_7_
  31.3 0.1 collective-permute-start.18
  31.4 0.1 collective-permute-start.10
  31.5 0.5 collective-permute-start.13
  32.0 0.1 collective-permute-start.14
  32.0 0.4 collective-permute-start.15
  32.5 0.2 collective-permute-done.10.refs_6_
  32.7 0.2 collective-permute-start.11
  32.9 1.1 %collective-permute-done.11.refs_7_ = f32[64,256]{1,0:T(8,128)S(1)} collective-permute-done((f32[64,256]{1,0:T(8,128)S(1)}, f32[64,256]{1,0:T(8,128)S(1)}, u32[]{:S(2)}, u32[]{:S(2)}) %collective-permute-start.11) | collective-permute-done | bytes 65568 | tf_op jit(solution)/shard_map/ppermute | solution.py:387
  34.0 0.4 collective-permute-start.9
  34.4 0.9 %collective-permute-done.9.refs_5_ = f32[64,256]{1,0:T(8,128)S(1)} collective-permute-done((f32[64,256]{1,0:T(8,128)S(1)}, f32[64,256]{1,0:T(8,128)S(1)}, u32[]{:S(2)}, u32[]{:S(2)}) %collective-permute-start.9) | collective-permute-done | bytes 65568 | tf_op jit(solution)/shard_map/ppermute | solution.py:387
  35.3 0.8 %shard_map.263.refs_11_.refs_0_ = f32[64,512]{1,0:T(8,128)S(1)} custom-call(f32[64,256]{1,0:T(8,128)S(1)} %get-tuple-element.39.refs_2_.refs_0_, f32[64,256]{1,0:T(8,128)S(1)} %collective-permute-done.1.refs_1_, f32[64,256]{1,0:T(8,128)S(1)} %collective-permute-done.2.refs_2_, f32[64,256]{1,0:T(8,128)S(1)} %collective-permute-done.3.refs_3_, ...), custom_call_target="tpu_custom_call" | custom-call | flops 201326592 | bytes 2031616 | tf_op jit(solution)/shard_map/pallas_call | solution.py:370
  36.1 0.0 copy-start.14
  36.1 1.2 %collective-permute-start.12 = (f32[64,512]{1,0:T(8,128)S(1)}, f32[64,512]{1,0:T(8,128)S(1)}, u32[]{:S(2)}, u32[]{:S(2)}) collective-permute-start(f32[64,512]{1,0:T(8,128)S(1)} %shard_map.263.refs_11_.refs_0_), channel_id=1, source_target_pairs={{0,2},{2,0},{1,3},{3,1},{4,6},{6,4},{5,7},{7,5},{8,10},{10,8},{9,1... | collective-permute-start | bytes 393224 | tf_op jit(solution)/shard_map/ppermute | solution.py:387
  37.3 0.0 collective-permute-done.15.refs_10_
  37.3 0.0 collective-permute-done.13.refs_6_
  37.3 0.0 collective-permute-done.14.refs_8_
  37.3 1.7 %shard_map.264 = (f32[512,512]{1,0:T(8,128)S(1)}, bf16[2,1536,256]{2,1,0:T(8,128)(2,1)S(1)}, bf16[1536,512]{1,0:T(8,128)(2,1)S(1)}) custom-call(f32[512,512]{1,0:T(8,128)S(1)} %copy-done, f32[512,256]{1,0:T(8,128)S(1)} %copy-done.1, f32[512,256]{1,0:T(8,128)S(1)} %copy-done.2, f32[3,256]{1,0:T(4,128)S(1)} %get-tuple-element.38.refs_4_.refs_3_.biases, ...), custom_call_target="tpu_custom_call" | custom-call | flops 805306368 | bytes 8555520 | tf_op jit(solution)/shard_map/pallas_call | solution.py:370
  39.0 2.9 %collective-permute-done.12.refs_1_ = f32[64,512]{1,0:T(8,128)S(1)} collective-permute-done((f32[64,512]{1,0:T(8,128)S(1)}, f32[64,512]{1,0:T(8,128)S(1)}, u32[]{:S(2)}, u32[]{:S(2)}) %collective-permute-start.12) | collective-permute-done | bytes 131104 | tf_op jit(solution)/shard_map/ppermute | solution.py:387
  41.9 1.9 %shard_map.265 = (f32[64,512]{1,0:T(8,128)}, bf16[128,512]{1,0:T(8,128)(2,1)S(1)}, f32[128,512]{1,0:T(8,128)S(1)}, f32[128,512]{1,0:T(8,128)S(1)}) custom-call(f32[64,512]{1,0:T(8,128)S(1)} %shard_map.263.refs_11_.refs_0_, f32[64,512]{1,0:T(8,128)S(1)} %collective-permute-done.12.refs_1_, f32[64,512]{1,0:T(8,128)S(1)} %get-tuple-element.50.refs_2_, ...), custom_call_target="tpu_custom_call" | custom-call | flops 402653184 | bytes 6436864 | tf_op jit(solution)/shard_map/pallas_call | solution.py:370
  43.8 0.0 collective-permute-done.18.refs_2_
  43.8 0.1 collective-permute-start.19
  43.9 0.5 collective-permute-start.20
  44.4 2.6 %collective-permute-start.17 = (f32[128,512]{1,0:T(8,128)S(1)}, f32[128,512]{1,0:T(8,128)S(1)}, u32[]{:S(2)}, u32[]{:S(2)}) collective-permute-start(f32[128,512]{1,0:T(8,128)S(1)} %get-tuple-element.58.head), channel_id=1, source_target_pairs={{0,13},{1,0},{4,1},{5,4},{8,5},{9,8},{12,9},{13,12},{2,15},{3,2},{... | collective-permute-start | bytes 786440 | tf_op jit(solution)/shard_map/ppermute | solution.py:387
  46.9 0.0 collective-permute-start.16
  46.9 1.3 %shard_map.266.middle = f32[256,512]{1,0:T(8,128)S(1)} custom-call(f32[512,512]{1,0:T(8,128)S(1)} %copy-done, f32[512,512]{1,0:T(8,128)S(1)} %get-tuple-element.54.refs_5_.receivers, s32[3,512]{1,0:T(4,128)S(1)} %bitcast.13, bf16[128,512]{1,0:T(8,128)(2,1)S(1)} %get-tuple-element.59.senders, bf16[1536,512]{1,0:T(8,128)(2,1)S(1)} %get-tuple-element.56.refs_8_.wo, ...), custom_call_target="tpu_custom_call" | custom-call | flops 402653184 | bytes 4339712 | tf_op jit(solution)/shard_map/pallas_call | solution.py:370
  48.3 0.0 collective-permute-done.19.refs_1_
  48.3 0.0 collective-permute-done.20.refs_3_
  48.3 0.6 shard_map.267
  48.9 4.8 %shard_map.268 = (f32[512,512]{1,0:T(8,128)S(1)}, f32[256,512]{1,0:T(8,128)S(1)}, f32[1536,512]{1,0:T(8,128)S(1)}) custom-call(f32[128,512]{1,0:T(8,128)S(1)} %get-tuple-element.58.head, f32[256,512]{1,0:T(8,128)S(1)} %shard_map.266.middle, f32[128,512]{1,0:T(8,128)S(1)} %get-tuple-element.57.tail, bf16[3072,768]{1,0:T(8,128)(2,1)S(1)} %get-tuple-element.60.picks, ...), custom_call_target="tpu_custom_call" | custom-call | flops 3221225472 | bytes 15228928 | tf_op jit(solution)/shard_map/pallas_call | solution.py:370
  53.7 2.3 %collective-permute-done.16.before = f32[128,512]{1,0:T(8,128)S(1)} collective-permute-done((f32[128,512]{1,0:T(8,128)S(1)}, f32[128,512]{1,0:T(8,128)S(1)}, u32[]{:S(2)}, u32[]{:S(2)}) %collective-permute-start.16) | collective-permute-done | bytes 262176 | tf_op jit(solution)/shard_map/ppermute | solution.py:387
  56.0 3.2 %shard_map.269 = f32[512,512]{1,0:T(8,128)} custom-call(f32[128,512]{1,0:T(8,128)S(1)} %collective-permute-done.16.before, f32[128,512]{1,0:T(8,128)S(1)} %collective-permute-done.17.after, f32[128,512]{1,0:T(8,128)S(1)} %get-tuple-element.58.head, f32[128,512]{1,0:T(8,128)S(1)} %get-tuple-element.57.tail, f32[256,512]{1,0:T(8,128)S(1)} %get-tuple-element.68.inner, ...), custom_call_target="tpu_custom_call" | custom-call | flops 805306368 | bytes 14688256 | tf_op jit(solution)/shard_map/pallas_call | solution.py:370
  (43 shorter events, 0.1 us)
Async XLA Ops:
  0.6 4.9 %copy-start = (f32[512,512]{1,0:T(8,128)S(1)}, f32[512,512]{1,0:T(8,128)}, u32[]{:S(2)}) copy-start(f32[512,512]{1,0:T(8,128)} %nodes.3) | copy-start | bytes 3145732
  0.6 4.9 %copy-start.7 = (f32[512,256]{1,0:T(8,128)S(1)}, f32[512,256]{1,0:T(8,128)}, u32[]{:S(2)}) copy-start(f32[512,256]{1,0:T(8,128)} %ws.2) | copy-start | bytes 1572868
  0.7 4.9 %copy-start.8 = (f32[512,256]{1,0:T(8,128)S(1)}, f32[512,256]{1,0:T(8,128)}, u32[]{:S(2)}) copy-start(f32[512,256]{1,0:T(8,128)} %wr.2) | copy-start | bytes 1572868
  0.7 4.9 %copy-start.9 = (f32[256,512]{1,0:T(8,128)S(1)}, f32[256,512]{1,0:T(8,128)}, u32[]{:S(2)}) copy-start(f32[256,512]{1,0:T(8,128)} %wo.2) | copy-start | bytes 1572868
  0.7 4.9 %copy-start.13 = (f32[64,512]{1,0:T(8,128)S(1)}, f32[64,512]{1,0:T(8,128)}, u32[]{:S(2)}) copy-start(f32[64,512]{1,0:T(8,128)} %refs_2_.3) | copy-start | bytes 393220
  0.7 4.9 %copy-start.16 = (s32[64,7]{0,1:T(8,128)S(1)}, s32[64,7]{0,1:T(8,128)}, u32[]{:S(2)}) copy-start(s32[64,7]{0,1:T(8,128)} %param.28) | copy-start | bytes 5380
  0.7 4.9 %copy-start.22 = (f32[256]{0:T(256)S(1)}, f32[256]{0:T(256)}, u32[]{:S(2)}) copy-start(f32[256]{0:T(256)} %param.34) | copy-start | bytes 3076
  2.6 13.3 %collective-permute-start.4 = (f32[264,256]{1,0:T(8,128)}, f32[264,256]{1,0:T(8,128)S(1)}, u32[]{:S(2)}, u32[]{:S(2)}) collective-permute-start(f32[264,256]{1,0:T(8,128)} %shard_map.261), channel_id=1, source_target_pairs={{0,2},{2,0},{1,3},{3,1},{4,6},{6,4},{5,7},{7,5},{8,10},{10,8},{9,1... | collective-permute-start | bytes 811016 | tf_op jit(solution)/shard_map/ppermute | solution.py:387
  7.4 8.5 %collective-permute-start = (f32[64,512]{1,0:T(8,128)S(1)}, f32[64,512]{1,0:T(8,128)S(1)}, u32[]{:S(2)}, u32[]{:S(2)}) collective-permute-start(f32[64,512]{1,0:T(8,128)S(1)} %shard_map.257.refs_7_.refs_0_), channel_id=1, source_target_pairs={{0,2},{2,0},{1,3},{3,1},{4,6},{6,4},{5,7},{7,5},{8,10},{10,8},{9,1... | collective-permute-start | bytes 393224 | tf_op jit(solution)/shard_map/ppermute | solution.py:387
  7.5 11.9 %copy-start.18 = (f32[512]{0:T(512)S(1)}, f32[512]{0:T(512)}, u32[]{:S(2)}) copy-start(f32[512]{0:T(512)} %param.36) | copy-start | bytes 6148
  7.5 11.9 %copy-start.19 = (f32[512]{0:T(512)S(1)}, f32[512]{0:T(512)}, u32[]{:S(2)}) copy-start(f32[512]{0:T(512)} %param.41) | copy-start | bytes 6148
  7.5 11.9 %copy-start.20 = (f32[512]{0:T(512)S(1)}, f32[512]{0:T(512)}, u32[]{:S(2)}) copy-start(f32[512]{0:T(512)} %param.46) | copy-start | bytes 6148
  7.5 11.9 %copy-start.21 = (f32[512]{0:T(512)S(1)}, f32[512]{0:T(512)}, u32[]{:S(2)}) copy-start(f32[512]{0:T(512)} %param.51) | copy-start | bytes 6148
  7.6 11.9 %copy-start.23 = (f32[256]{0:T(256)S(1)}, f32[256]{0:T(256)}, u32[]{:S(2)}) copy-start(f32[256]{0:T(256)} %param.39) | copy-start | bytes 3076
  7.6 11.9 %copy-start.24 = (f32[256]{0:T(256)S(1)}, f32[256]{0:T(256)}, u32[]{:S(2)}) copy-start(f32[256]{0:T(256)} %param.44) | copy-start | bytes 3076
  7.6 11.9 %copy-start.25 = (f32[256]{0:T(256)S(1)}, f32[256]{0:T(256)}, u32[]{:S(2)}) copy-start(f32[256]{0:T(256)} %param.49) | copy-start | bytes 3076
  7.6 11.9 %copy-start.10 = (f32[512,256]{1,0:T(8,128)S(1)}, f32[512,256]{1,0:T(8,128)}, u32[]{:S(2)}) copy-start(f32[512,256]{1,0:T(8,128)} %refs_5_.1) | copy-start | bytes 1572868
  7.6 11.9 %copy-start.11 = (f32[512,256]{1,0:T(8,128)S(1)}, f32[512,256]{1,0:T(8,128)}, u32[]{:S(2)}) copy-start(f32[512,256]{1,0:T(8,128)} %refs_6_.1) | copy-start | bytes 1572868
  9.7 18.4 %copy-start.15 = (s32[512,6]{0,1:T(8,128)S(1)}, s32[512,6]{0,1:T(8,128)}, u32[]{:S(2)}) copy-start(s32[512,6]{0,1:T(8,128)} %param.30) | copy-start | bytes 36868
  9.7 18.4 %copy-start.17 = (s32[64,6]{0,1:T(8,128)S(1)}, s32[64,6]{0,1:T(8,128)}, u32[]{:S(2)}) copy-start(s32[64,6]{0,1:T(8,128)} %param.31) | copy-start | bytes 4612
  9.8 25.5 %copy-start.12 = (f32[256,512]{1,0:T(8,128)S(1)}, f32[256,512]{1,0:T(8,128)}, u32[]{:S(2)}) copy-start(f32[256,512]{1,0:T(8,128)} %refs_10_.1) | copy-start | bytes 1572868
  9.8 21.5 %collective-permute-start.7 = (f32[392,256]{1,0:T(8,128)}, f32[392,256]{1,0:T(8,128)S(1)}, u32[]{:S(2)}, u32[]{:S(2)}) collective-permute-start(f32[392,256]{1,0:T(8,128)} %get-tuple-element.44), channel_id=1, source_target_pairs={{0,2},{2,0},{1,3},{3,1},{4,6},{6,4},{5,7},{7,5},{8,10},{10,8},{9,1... | collective-permute-start | bytes 1204232 | tf_op jit(solution)/shard_map/ppermute | solution.py:387
  15.9 15.4 %collective-permute-start.5 = (f32[264,256]{1,0:T(8,128)S(1)}, f32[264,256]{1,0:T(8,128)S(1)}, u32[]{:S(2)}, u32[]{:S(2)}) collective-permute-start(f32[264,256]{1,0:T(8,128)S(1)} %collective-permute-done.4.refs_5_), channel_id=1, source_target_pairs={{0,16},{16,0},{1,17},{17,1},{2,18},{18,2},{3,19},{19,3},{4,20},{20... | collective-permute-start | bytes 811016 | tf_op jit(solution)/shard_map/ppermute | solution.py:428
  18.0 13.3 %collective-permute-start.6 = (f32[256,256]{1,0:T(8,128)}, f32[256,256]{1,0:T(8,128)S(1)}, u32[]{:S(2)}, u32[]{:S(2)}) collective-permute-start(f32[256,256]{1,0:T(8,128)} %get-tuple-element.43), channel_id=1, source_target_pairs={{0,2},{2,0},{1,3},{3,1},{4,6},{6,4},{5,7},{7,5},{8,10},{10,8},{9,1... | collective-permute-start | bytes 786440 | tf_op jit(solution)/shard_map/ppermute | solution.py:387
  19.6 17.8 %copy-start.1 = (f32[512,256]{1,0:T(8,128)S(1)}, f32[512,256]{1,0:T(8,128)}, u32[]{:S(2)}) copy-start(f32[512,256]{1,0:T(8,128)} %refs_1_.5) | copy-start | bytes 1572868
  19.6 17.7 %copy-start.2 = (f32[512,256]{1,0:T(8,128)S(1)}, f32[512,256]{1,0:T(8,128)}, u32[]{:S(2)}) copy-start(f32[512,256]{1,0:T(8,128)} %refs_2_.5) | copy-start | bytes 1572868
  19.6 17.7 %copy-start.3 = (f32[256,512]{1,0:T(8,128)S(1)}, f32[256,512]{1,0:T(8,128)}, u32[]{:S(2)}) copy-start(f32[256,512]{1,0:T(8,128)} %refs_4_.2) | copy-start | bytes 1572868
  20.2 6.8 %collective-permute-start.1 = (f32[64,256]{1,0:T(8,128)S(1)}, f32[64,256]{1,0:T(8,128)S(1)}, u32[]{:S(2)}, u32[]{:S(2)}) collective-permute-start(f32[64,256]{1,0:T(8,128)S(1)} %get-tuple-element.39.refs_2_.refs_0_), channel_id=1, source_target_pairs={{0,4},{4,8},{8,12},{12,0},{1,5},{5,9},{9,13},{13,1},{2,6},{6,10},{... | collective-permute-start | bytes 196616 | tf_op jit(solution)/shard_map/ppermute | solution.py:387
  21.8 6.3 %collective-permute-start.2 = (f32[64,256]{1,0:T(8,128)S(1)}, f32[64,256]{1,0:T(8,128)S(1)}, u32[]{:S(2)}, u32[]{:S(2)}) collective-permute-start(f32[64,256]{1,0:T(8,128)S(1)} %get-tuple-element.39.refs_2_.refs_0_), channel_id=1, source_target_pairs={{0,8},{4,12},{8,0},{12,4},{1,9},{5,13},{9,1},{13,5},{2,10},{6,14},... | collective-permute-start | bytes 196616 | tf_op jit(solution)/shard_map/ppermute | solution.py:387
  27.0 4.3 %collective-permute-start.3 = (f32[64,256]{1,0:T(8,128)S(1)}, f32[64,256]{1,0:T(8,128)S(1)}, u32[]{:S(2)}, u32[]{:S(2)}) collective-permute-start(f32[64,256]{1,0:T(8,128)S(1)} %get-tuple-element.39.refs_2_.refs_0_), channel_id=1, source_target_pairs={{0,12},{4,0},{8,4},{12,8},{1,13},{5,1},{9,5},{13,9},{2,14},{6,2},{... | collective-permute-start | bytes 196616 | tf_op jit(solution)/shard_map/ppermute | solution.py:387
  28.1 3.9 %collective-permute-start.8 = (f32[64,256]{1,0:T(8,128)S(1)}, f32[64,256]{1,0:T(8,128)S(1)}, u32[]{:S(2)}, u32[]{:S(2)}) collective-permute-start(f32[64,256]{1,0:T(8,128)S(1)} %get-tuple-element.39.refs_2_.refs_0_), channel_id=1, source_target_pairs={{0,1},{1,0},{2,3},{3,2},{4,5},{5,4},{6,7},{7,6},{8,9},{9,8},{10,11... | collective-permute-start | bytes 196616 | tf_op jit(solution)/shard_map/ppermute | solution.py:387
  31.3 12.5 %collective-permute-start.18 = (f32[392,256]{1,0:T(8,128)S(1)}, f32[392,256]{1,0:T(8,128)S(1)}, u32[]{:S(2)}, u32[]{:S(2)}) collective-permute-start(f32[392,256]{1,0:T(8,128)S(1)} %collective-permute-done.7.refs_0_), channel_id=1, source_target_pairs={{0,4},{4,0},{8,12},{12,8},{1,5},{5,1},{9,13},{13,9},{2,6},{6,2},{1... | collective-permute-start | bytes 1204232 | tf_op jit(solution)/shard_map/ppermute | solution.py:428
  31.4 1.3 %collective-permute-start.10 = (f32[64,256]{1,0:T(8,128)S(1)}, f32[64,256]{1,0:T(8,128)S(1)}, u32[]{:S(2)}, u32[]{:S(2)}) collective-permute-start(f32[64,256]{1,0:T(8,128)S(1)} %collective-permute-done.2.refs_2_), channel_id=1, source_target_pairs={{0,1},{1,0},{2,3},{3,2},{4,5},{5,4},{6,7},{7,6},{8,9},{9,8},{10,11... | collective-permute-start | bytes 196616 | tf_op jit(solution)/shard_map/ppermute | solution.py:387
  31.5 5.8 %collective-permute-start.13 = (f32[264,256]{1,0:T(8,128)S(1)}, f32[264,256]{1,0:T(8,128)S(1)}, u32[]{:S(2)}, u32[]{:S(2)}) collective-permute-start(f32[264,256]{1,0:T(8,128)S(1)} %collective-permute-done.4.refs_5_), channel_id=1, source_target_pairs={{0,1},{1,0},{2,3},{3,2},{4,5},{5,4},{6,7},{7,6},{8,9},{9,8},{10,11... | collective-permute-start | bytes 811016 | tf_op jit(solution)/shard_map/ppermute | solution.py:387
  32.0 5.3 %collective-permute-start.14 = (f32[264,256]{1,0:T(8,128)S(1)}, f32[264,256]{1,0:T(8,128)S(1)}, u32[]{:S(2)}, u32[]{:S(2)}) collective-permute-start(f32[264,256]{1,0:T(8,128)S(1)} %collective-permute-done.5.refs_7_), channel_id=1, source_target_pairs={{0,1},{1,0},{2,3},{3,2},{4,5},{5,4},{6,7},{7,6},{8,9},{9,8},{10,11... | collective-permute-start | bytes 811016 | tf_op jit(solution)/shard_map/ppermute | solution.py:387
  32.0 5.3 %collective-permute-start.15 = (f32[256,256]{1,0:T(8,128)S(1)}, f32[256,256]{1,0:T(8,128)S(1)}, u32[]{:S(2)}, u32[]{:S(2)}) collective-permute-start(f32[256,256]{1,0:T(8,128)S(1)} %collective-permute-done.6.refs_9_), channel_id=1, source_target_pairs={{0,1},{1,0},{2,3},{3,2},{4,5},{5,4},{6,7},{7,6},{8,9},{9,8},{10,11... | collective-permute-start | bytes 786440 | tf_op jit(solution)/shard_map/ppermute | solution.py:387
  32.7 1.3 %collective-permute-start.11 = (f32[64,256]{1,0:T(8,128)S(1)}, f32[64,256]{1,0:T(8,128)S(1)}, u32[]{:S(2)}, u32[]{:S(2)}) collective-permute-start(f32[64,256]{1,0:T(8,128)S(1)} %collective-permute-done.3.refs_3_), channel_id=1, source_target_pairs={{0,1},{1,0},{2,3},{3,2},{4,5},{5,4},{6,7},{7,6},{8,9},{9,8},{10,11... | collective-permute-start | bytes 196616 | tf_op jit(solution)/shard_map/ppermute | solution.py:387
  34.0 1.3 %collective-permute-start.9 = (f32[64,256]{1,0:T(8,128)S(1)}, f32[64,256]{1,0:T(8,128)S(1)}, u32[]{:S(2)}, u32[]{:S(2)}) collective-permute-start(f32[64,256]{1,0:T(8,128)S(1)} %collective-permute-done.1.refs_1_), channel_id=1, source_target_pairs={{0,1},{1,0},{2,3},{3,2},{4,5},{5,4},{6,7},{7,6},{8,9},{9,8},{10,11... | collective-permute-start | bytes 196616 | tf_op jit(solution)/shard_map/ppermute | solution.py:387
  36.1 5.8 %copy-start.14 = (s32[512,3]{0,1:T(4,128)S(1)}, s32[512,3]{0,1:T(4,128)}, u32[]{:S(2)}) copy-start(s32[512,3]{0,1:T(4,128)} %param.29) | copy-start | bytes 18436
  36.1 5.8 %collective-permute-start.12 = (f32[64,512]{1,0:T(8,128)S(1)}, f32[64,512]{1,0:T(8,128)S(1)}, u32[]{:S(2)}, u32[]{:S(2)}) collective-permute-start(f32[64,512]{1,0:T(8,128)S(1)} %shard_map.263.refs_11_.refs_0_), channel_id=1, source_target_pairs={{0,2},{2,0},{1,3},{3,1},{4,6},{6,4},{5,7},{7,5},{8,10},{10,8},{9,1... | collective-permute-start | bytes 393224 | tf_op jit(solution)/shard_map/ppermute | solution.py:387
  43.8 4.5 %collective-permute-start.19 = (f32[392,256]{1,0:T(8,128)S(1)}, f32[392,256]{1,0:T(8,128)S(1)}, u32[]{:S(2)}, u32[]{:S(2)}) collective-permute-start(f32[392,256]{1,0:T(8,128)S(1)} %collective-permute-done.7.refs_0_), channel_id=1, source_target_pairs={{0,1},{1,0},{2,3},{3,2},{4,5},{5,4},{6,7},{7,6},{8,9},{9,8},{10,11... | collective-permute-start | bytes 1204232 | tf_op jit(solution)/shard_map/ppermute | solution.py:387
  43.9 4.4 %collective-permute-start.20 = (f32[392,256]{1,0:T(8,128)S(1)}, f32[392,256]{1,0:T(8,128)S(1)}, u32[]{:S(2)}, u32[]{:S(2)}) collective-permute-start(f32[392,256]{1,0:T(8,128)S(1)} %collective-permute-done.18.refs_2_), channel_id=1, source_target_pairs={{0,1},{1,0},{2,3},{3,2},{4,5},{5,4},{6,7},{7,6},{8,9},{9,8},{10,11... | collective-permute-start | bytes 1204232 | tf_op jit(solution)/shard_map/ppermute | solution.py:387
  44.4 11.7 %collective-permute-start.17 = (f32[128,512]{1,0:T(8,128)S(1)}, f32[128,512]{1,0:T(8,128)S(1)}, u32[]{:S(2)}, u32[]{:S(2)}) collective-permute-start(f32[128,512]{1,0:T(8,128)S(1)} %get-tuple-element.58.head), channel_id=1, source_target_pairs={{0,13},{1,0},{4,1},{5,4},{8,5},{9,8},{12,9},{13,12},{2,15},{3,2},{... | collective-permute-start | bytes 786440 | tf_op jit(solution)/shard_map/ppermute | solution.py:387
  46.9 9.1 %collective-permute-start.16 = (f32[128,512]{1,0:T(8,128)S(1)}, f32[128,512]{1,0:T(8,128)S(1)}, u32[]{:S(2)}, u32[]{:S(2)}) collective-permute-start(f32[128,512]{1,0:T(8,128)S(1)} %get-tuple-element.57.tail), channel_id=1, source_target_pairs={{0,1},{1,4},{4,5},{5,8},{8,9},{9,12},{12,13},{13,0},{2,3},{3,6},{6... | collective-permute-start | bytes 786440 | tf_op jit(solution)/shard_map/ppermute | solution.py:387
  46.9 1.4 %copy-start.4 = (f32[512,256]{1,0:T(8,128)S(1)}, f32[512,256]{1,0:T(8,128)}, u32[]{:S(2)}) copy-start(f32[512,256]{1,0:T(8,128)} %ws.3) | copy-start | bytes 1572868
  46.9 1.4 %copy-start.5 = (f32[512,256]{1,0:T(8,128)S(1)}, f32[512,256]{1,0:T(8,128)}, u32[]{:S(2)}) copy-start(f32[512,256]{1,0:T(8,128)} %wr.3) | copy-start | bytes 1572868
  46.9 1.4 %copy-start.6 = (f32[256,512]{1,0:T(8,128)S(1)}, f32[256,512]{1,0:T(8,128)}, u32[]{:S(2)}) copy-start(f32[256,512]{1,0:T(8,128)} %wo.3) | copy-start | bytes 1572868

commit v13 on v10

--- a/solution.py
+++ b/solution.py
@@ -161,6 +161,12 @@
             bottom_picks[i * size : (i + 1) * size, j * rim : (j + 1) * rim] = piece
 
 
+def join_kernel(*refs):
+    rows = refs[0].shape[0]
+    for i, piece in enumerate(refs[:-1]):
+        refs[-1][i * rows : (i + 1) * rows] = piece[...]
+
+
 def coarse_project_kernel(count, *refs):
     parts, refs = refs[:count], refs[count:]
     coarse, gains, biases, ws, wr, updated, senders, receivers = refs
@@ -391,11 +397,13 @@
     patches, lvls = lax.axis_size("patch"), lax.axis_size("lvl")
     if patches > most_direct:
         return [lax.all_gather(senders, ("patch", "lvl"), axis=0, tiled=True)], others
-    near = [[senders] + [shifted(senders, "lvl", t) for t in range(1, lvls)]]
     pieces = [shifted(senders, "patch", s) for s in range(1, patches)]
     pieces, others = lax.optimization_barrier((pieces, others))
-    near += [[piece] + [shifted(piece, "lvl", t) for t in range(1, lvls)] for piece in pieces]
-    return [row[t] for t in range(lvls) for row in near], others
+    rows, width = senders.shape
+    (near,) = call(
+        join_kernel, [like((patches * rows, width))], [senders, *pieces], patches * rows * width
+    )
+    return [near] + [shifted(near, "lvl", t) for t in range(1, lvls)], others
 
 
 def held(values, event):

time: 57.9 us -> 56.8 us (0.981)
  starting transfers between devices: 19.8 us -> 18.8 us
    ppermute x17 -> x14, waiting for transfers between devices: 13 us -> 11.5 us  [shifted(): lax.ppermute(values, axis, [(i, (i + step) % count) for i in range(count)])]
    ppermute x2, waiting for transfers between devices: 0.01 us -> 1.37 us  [over_partners(): lax.ppermute(share, axis, [(i, i - i % count + (i + p) % count) for i in...]
    ppermute x17 -> x14, starting transfers between devices: 17.2 us -> 16.1 us  [shifted(): lax.ppermute(values, axis, [(i, (i + step) % count) for i in range(count)])]
    pallas_call x13 -> x14, Pallas kernels: 21.4 us -> 21.5 us  [call(): pl.pallas_call((lambda *refs: kernel(*refs[:read], *refs[read + unread:])...]
  transfers between devices with their start and end apart: 19 -> 16, of which waited for: 8 -> 7; matrix products, arithmetic and copies ran while one was open for 0% -> 0% of each run, Pallas kernels for 28% -> 29%
where the time goes in v13:
time: 56.8 us; the launch traced here: 56.5 us
  Pallas kernels  21.5 us (38%)
  starting transfers between devices  18.8 us (33%)
  waiting for transfers between devices  12.8 us (23%)
  local copies, waits for them, and re-layouts  2.2 us (4%)
  between operations  1.18 us (2%)
    pallas_call x14, Pallas kernels, call(): pl.pallas_call((lambda *refs: kernel(*refs[:read], *refs[read + unread:])...  21.5 us
    ppermute x14, starting transfers between devices, shifted(): lax.ppermute(values, axis, [(i, (i + step) % count) for i in range(count)])  16.1 us
    ppermute x14, waiting for transfers between devices, shifted(): lax.ppermute(values, axis, [(i, (i + step) % count) for i in range(count)])  11.5 us
    ppermute x2, starting transfers between devices, over_partners(): lax.ppermute(share, axis, [(i, i - i % count + (i + p) % count) for i in...  2.68 us
    unnamed x52, local copies, waits for them, and re-layouts  2.2 us
    ppermute x2, waiting for transfers between devices, over_partners(): lax.ppermute(share, axis, [(i, i - i % count + (i + p) % count) for i in...  1.37 us
  transfers between devices with their start and end apart: 16, of which 7 were waited for; matrix products, arithmetic and copies ran while one was open for 0% of the time, Pallas kernels for 29%

profile of v13, /device:TPU:0, one launch (start us, length us, event | category | flops | bytes accessed | tf_op | source)
XLA Modules:
  0.0 56.5 jit_solution(8634303572493277055)
XLA Ops:
  0.7 1.9 %shard_map.261 = f32[392,256]{1,0:T(8,128)} custom-call(f32[512,256]{1,0:T(8,128)} %refs_1_.5, f32[512,256]{1,0:T(8,128)} %refs_2_.7, f32[256,512]{1,0:T(8,128)} %refs_4_.4, f32[1,256]{1,0:T(1,128)} %bitcast.15), custom_call_target="tpu_custom_call" | custom-call | flops 512 | bytes 1975296 | tf_op jit(solution)/shard_map/pallas_call | solution.py:370
  2.6 3.0 %collective-permute-start.4 = (f32[392,256]{1,0:T(8,128)}, f32[392,256]{1,0:T(8,128)S(1)}, u32[]{:S(2)}, u32[]{:S(2)}) collective-permute-start(f32[392,256]{1,0:T(8,128)} %shard_map.261), channel_id=1, source_target_pairs={{0,2},{2,0},{1,3},{3,1},{4,6},{6,4},{5,7},{7,5},{8,10},{10,8},{9,1... | collective-permute-start | bytes 1204232 | tf_op jit(solution)/shard_map/ppermute | solution.py:387
  5.6 0.0 copy-done
  5.6 0.0 copy-start.8
  5.7 1.0 %copy-done.8 = f32[512,256]{1,0:T(8,128)S(1)} copy-done((f32[512,256]{1,0:T(8,128)S(1)}, f32[512,256]{1,0:T(8,128)}, u32[]{:S(2)}) %copy-start.8) | copy-done | bytes 524312
  6.7 1.0 %copy-done.9 = f32[256,512]{1,0:T(8,128)S(1)} copy-done((f32[256,512]{1,0:T(8,128)S(1)}, f32[256,512]{1,0:T(8,128)}, u32[]{:S(2)}) %copy-start.9) | copy-done | bytes 524312
  7.7 1.8 %shard_map.257.refs_7_.refs_0_ = f32[64,512]{1,0:T(8,128)S(1)} custom-call(f32[512,512]{1,0:T(8,128)S(1)} %copy-done, f32[64,512]{1,0:T(8,128)S(1)} %copy-done.13, s32[7,64]{1,0:T(8,128)S(1)} %bitcast.19, f32[512,256]{1,0:T(8,128)S(1)} %copy-done.7, f32[512,256]{1,0:T(8,128)S(1)} %copy-done.8, f32[1,256]{1,0:T(1,128)S(1)} %bitcast.25, f32[256,512]{1,0:T(8,128)S(1)} %copy-done.9), custom_call_target="tpu_custom_call" | custom-call | flops 402653184 | bytes 2886400 | tf_op jit(solution)/shard_map/pallas_call | solution.py:370
  9.5 0.0 copy-start.16
  9.6 0.0 copy-start.17
  9.6 0.0 copy-start.20
  9.6 0.0 copy-start.21
  9.6 0.0 copy-start.22
  9.6 0.0 copy-start.23
  9.6 0.0 copy-start.25
  9.6 0.0 copy-start.10
  9.6 0.0 copy-start.11
  9.7 0.1 collective-permute-start
  9.8 1.9 %shard_map.262 = f32[392,256]{1,0:T(8,128)} custom-call(f32[512,256]{1,0:T(8,128)} %ws.3, f32[512,256]{1,0:T(8,128)} %wr.3, f32[256,512]{1,0:T(8,128)} %wo.3, f32[1,256]{1,0:T(1,128)} %bitcast.17), custom_call_target="tpu_custom_call" | custom-call | flops 512 | bytes 1975296 | tf_op jit(solution)/shard_map/pallas_call | solution.py:370
  11.7 0.0 copy-start.12
  11.7 2.0 %collective-permute-start.6 = (f32[392,256]{1,0:T(8,128)}, f32[392,256]{1,0:T(8,128)S(1)}, u32[]{:S(2)}, u32[]{:S(2)}) collective-permute-start(f32[392,256]{1,0:T(8,128)} %shard_map.262), channel_id=1, source_target_pairs={{0,2},{2,0},{1,3},{3,1},{4,6},{6,4},{5,7},{7,5},{8,10},{10,8},{9,1... | collective-permute-start | bytes 1204232 | tf_op jit(solution)/shard_map/ppermute | solution.py:387
  13.6 5.1 %collective-permute-done.refs_1_ = f32[64,512]{1,0:T(8,128)S(1)} collective-permute-done((f32[64,512]{1,0:T(8,128)S(1)}, f32[64,512]{1,0:T(8,128)S(1)}, u32[]{:S(2)}, u32[]{:S(2)}) %collective-permute-start) | collective-permute-done | bytes 131104 | tf_op jit(solution)/shard_map/ppermute | solution.py:387
  18.8 0.0 collective-permute-done.4.refs_5_
  18.8 2.1 %collective-permute-start.5 = (f32[392,256]{1,0:T(8,128)S(1)}, f32[392,256]{1,0:T(8,128)S(1)}, u32[]{:S(2)}, u32[]{:S(2)}) collective-permute-start(f32[392,256]{1,0:T(8,128)S(1)} %collective-permute-done.4.refs_5_), channel_id=1, source_target_pairs={{0,16},{16,0},{1,17},{17,1},{2,18},{18,2},{3,19},{19,3},{4,20},{20... | collective-permute-start | bytes 1204232 | tf_op jit(solution)/shard_map/ppermute | solution.py:428
  20.8 0.0 copy-done.17
  20.9 0.0 copy-done.10
  20.9 0.0 copy-done.11
  20.9 0.6 %shard_map.259 = (f32[64,512]{1,0:T(8,128)S(1)}, f32[64,256]{1,0:T(8,128)S(1)}, f32[64,256]{1,0:T(8,128)S(1)}) custom-call(f32[64,512]{1,0:T(8,128)S(1)} %shard_map.257.refs_7_.refs_0_, f32[64,512]{1,0:T(8,128)S(1)} %collective-permute-done.refs_1_, f32[64,512]{1,0:T(8,128)S(1)} %copy-done.13, f32[4,512]{1,0:T(4,128)S(1)} %get-tuple-element.34.refs_3_.gains, ...), custom_call_target="tpu_custom_call" | custom-call | flops 100663296 | bytes 1715200 | tf_op jit(solution)/shard_map/pallas_call | solution.py:370
  21.5 0.0 copy-start.2
  21.5 0.0 copy-start.3
  21.6 1.6 %collective-permute-start.1 = (f32[64,256]{1,0:T(8,128)S(1)}, f32[64,256]{1,0:T(8,128)S(1)}, u32[]{:S(2)}, u32[]{:S(2)}) collective-permute-start(f32[64,256]{1,0:T(8,128)S(1)} %get-tuple-element.36.refs_2_.refs_0_), channel_id=1, source_target_pairs={{0,4},{4,8},{8,12},{12,0},{1,5},{5,9},{9,13},{13,1},{2,6},{6,10},{... | collective-permute-start | bytes 196616 | tf_op jit(solution)/shard_map/ppermute | solution.py:387
  23.2 2.6 %collective-permute-start.2 = (f32[64,256]{1,0:T(8,128)S(1)}, f32[64,256]{1,0:T(8,128)S(1)}, u32[]{:S(2)}, u32[]{:S(2)}) collective-permute-start(f32[64,256]{1,0:T(8,128)S(1)} %get-tuple-element.36.refs_2_.refs_0_), channel_id=1, source_target_pairs={{0,8},{4,12},{8,0},{12,4},{1,9},{5,13},{9,1},{13,5},{2,10},{6,14},... | collective-permute-start | bytes 196616 | tf_op jit(solution)/shard_map/ppermute | solution.py:387
  25.8 1.3 %collective-permute-start.3 = (f32[64,256]{1,0:T(8,128)S(1)}, f32[64,256]{1,0:T(8,128)S(1)}, u32[]{:S(2)}, u32[]{:S(2)}) collective-permute-start(f32[64,256]{1,0:T(8,128)S(1)} %get-tuple-element.36.refs_2_.refs_0_), channel_id=1, source_target_pairs={{0,12},{4,0},{8,4},{12,8},{1,13},{5,1},{9,5},{13,9},{2,14},{6,2},{... | collective-permute-start | bytes 196616 | tf_op jit(solution)/shard_map/ppermute | solution.py:387
  27.1 1.1 %shard_map.260 = (bf16[384,1024]{1,0:T(8,128)(2,1)S(1)}, bf16[3072,768]{1,0:T(8,128)(2,1)S(1)}) custom-call(s32[6,64]{1,0:T(8,128)S(1)} %bitcast.20, s32[6,512]{1,0:T(8,128)S(1)} %bitcast.14, f32[64,256]{1,0:T(8,128)S(1)} %get-tuple-element.36.refs_2_.refs_0_), custom_call_target="tpu_custom_call" | custom-call | flops 196608 | bytes 5584384 | tf_op jit(solution)/shard_map/pallas_call | solution.py:370
  28.3 0.0 collective-permute-done.1.refs_1_
  28.3 0.1 collective-permute-done.2.refs_2_
  28.4 1.7 %collective-permute-done.3.refs_3_ = f32[64,256]{1,0:T(8,128)S(1)} collective-permute-done((f32[64,256]{1,0:T(8,128)S(1)}, f32[64,256]{1,0:T(8,128)S(1)}, u32[]{:S(2)}, u32[]{:S(2)}) %collective-permute-start.3) | collective-permute-done | bytes 65568 | tf_op jit(solution)/shard_map/ppermute | solution.py:387
  30.0 0.0 collective-permute-done.6.refs_0_
  30.0 0.0 collective-permute-done.5.refs_7_
  30.0 0.0 collective-permute-start.10
  30.1 0.5 collective-permute-start.9
  30.6 0.1 collective-permute-start.7
  30.7 0.6 %collective-permute-start.13 = (f32[392,256]{1,0:T(8,128)S(1)}, f32[392,256]{1,0:T(8,128)S(1)}, u32[]{:S(2)}, u32[]{:S(2)}) collective-permute-start(f32[392,256]{1,0:T(8,128)S(1)} %collective-permute-done.6.refs_0_), channel_id=1, source_target_pairs={{0,4},{4,0},{8,12},{12,8},{1,5},{5,1},{9,13},{13,9},{2,6},{6,2},{1... | collective-permute-start | bytes 1204232 | tf_op jit(solution)/shard_map/ppermute | solution.py:428
  31.3 1.4 %collective-permute-done.7.refs_1_ = f32[256,256]{1,0:T(8,128)S(1)} collective-permute-done((f32[256,256]{1,0:T(8,128)S(1)}, f32[256,256]{1,0:T(8,128)S(1)}, u32[]{:S(2)}, u32[]{:S(2)}) %collective-permute-start.7) | collective-permute-done | bytes 262176 | tf_op jit(solution)/shard_map/ppermute | solution.py:387
  32.7 0.8 %shard_map.264.refs_9_.refs_0_ = f32[64,512]{1,0:T(8,128)S(1)} custom-call(f32[256,256]{1,0:T(8,128)S(1)} %shard_map.263.refs_0_, f32[256,256]{1,0:T(8,128)S(1)} %collective-permute-done.7.refs_1_, bf16[384,1024]{1,0:T(8,128)(2,1)S(1)} %get-tuple-element.43.refs_2_, f32[64,256]{1,0:T(8,128)S(1)} %get-tuple-element.44.refs_3_, f32[256,512]{1,0:T(8,128)S(1)} %copy-done.12), custom_call_target="tpu_custom_call" | custom-call | flops 201326592 | bytes 2031616 | tf_op jit(solution)/shard_map/pallas_call | solution.py:370
  33.5 0.0 copy-start.14
  33.5 1.6 %collective-permute-start.8 = (f32[64,512]{1,0:T(8,128)S(1)}, f32[64,512]{1,0:T(8,128)S(1)}, u32[]{:S(2)}, u32[]{:S(2)}) collective-permute-start(f32[64,512]{1,0:T(8,128)S(1)} %shard_map.264.refs_9_.refs_0_), channel_id=1, source_target_pairs={{0,2},{2,0},{1,3},{3,1},{4,6},{6,4},{5,7},{7,5},{8,10},{10,8},{9,1... | collective-permute-start | bytes 393224 | tf_op jit(solution)/shard_map/ppermute | solution.py:387
  35.1 0.0 collective-permute-done.10.refs_8_
  35.1 0.0 collective-permute-done.9.refs_6_
  35.1 1.7 %shard_map.265 = (f32[512,512]{1,0:T(8,128)S(1)}, bf16[2,1536,256]{2,1,0:T(8,128)(2,1)S(1)}, bf16[1536,512]{1,0:T(8,128)(2,1)S(1)}) custom-call(f32[512,512]{1,0:T(8,128)S(1)} %copy-done, f32[512,256]{1,0:T(8,128)S(1)} %copy-done.1, f32[512,256]{1,0:T(8,128)S(1)} %copy-done.2, f32[3,256]{1,0:T(4,128)S(1)} %get-tuple-element.35.refs_4_.refs_3_.biases, ...), custom_call_target="tpu_custom_call" | custom-call | flops 805306368 | bytes 8555520 | tf_op jit(solution)/shard_map/pallas_call | solution.py:370
  36.8 2.3 %collective-permute-done.8.refs_1_ = f32[64,512]{1,0:T(8,128)S(1)} collective-permute-done((f32[64,512]{1,0:T(8,128)S(1)}, f32[64,512]{1,0:T(8,128)S(1)}, u32[]{:S(2)}, u32[]{:S(2)}) %collective-permute-start.8) | collective-permute-done | bytes 131104 | tf_op jit(solution)/shard_map/ppermute | solution.py:387
  39.1 1.9 %shard_map.266 = (f32[64,512]{1,0:T(8,128)}, bf16[128,512]{1,0:T(8,128)(2,1)S(1)}, f32[128,512]{1,0:T(8,128)S(1)}, f32[128,512]{1,0:T(8,128)S(1)}) custom-call(f32[64,512]{1,0:T(8,128)S(1)} %shard_map.264.refs_9_.refs_0_, f32[64,512]{1,0:T(8,128)S(1)} %collective-permute-done.8.refs_1_, f32[64,512]{1,0:T(8,128)S(1)} %get-tuple-element.45.refs_2_, ...), custom_call_target="tpu_custom_call" | custom-call | flops 402653184 | bytes 6436864 | tf_op jit(solution)/shard_map/pallas_call | solution.py:370
  41.0 1.4 %collective-permute-done.13.refs_2_ = f32[392,256]{1,0:T(8,128)S(1)} collective-permute-done((f32[392,256]{1,0:T(8,128)S(1)}, f32[392,256]{1,0:T(8,128)S(1)}, u32[]{:S(2)}, u32[]{:S(2)}) %collective-permute-start.13) | collective-permute-done | bytes 401440 | tf_op jit(solution)/shard_map/ppermute | solution.py:428
  42.4 0.0 collective-permute-start.14
  42.4 0.5 collective-permute-start.15
  42.9 2.8 %collective-permute-start.12 = (f32[128,512]{1,0:T(8,128)S(1)}, f32[128,512]{1,0:T(8,128)S(1)}, u32[]{:S(2)}, u32[]{:S(2)}) collective-permute-start(f32[128,512]{1,0:T(8,128)S(1)} %get-tuple-element.52.head), channel_id=1, source_target_pairs={{0,13},{1,0},{4,1},{5,4},{8,5},{9,8},{12,9},{13,12},{2,15},{3,2},{... | collective-permute-start | bytes 786440 | tf_op jit(solution)/shard_map/ppermute | solution.py:387
  45.6 0.0 collective-permute-start.11
  45.6 1.3 %shard_map.267.middle = f32[256,512]{1,0:T(8,128)S(1)} custom-call(f32[512,512]{1,0:T(8,128)S(1)} %copy-done, f32[512,512]{1,0:T(8,128)S(1)} %get-tuple-element.48.refs_5_.receivers, s32[3,512]{1,0:T(4,128)S(1)} %bitcast.13, bf16[128,512]{1,0:T(8,128)(2,1)S(1)} %get-tuple-element.53.senders, bf16[1536,512]{1,0:T(8,128)(2,1)S(1)} %get-tuple-element.50.refs_8_.wo, ...), custom_call_target="tpu_custom_call" | custom-call | flops 402653184 | bytes 4339712 | tf_op jit(solution)/shard_map/pallas_call | solution.py:370
  47.0 0.0 collective-permute-done.14.refs_1_
  47.0 0.0 collective-permute-done.15.refs_3_
  47.0 0.6 %shard_map.268 = (bf16[2,1536,256]{2,1,0:T(8,128)(2,1)S(1)}, bf16[2,1536,256]{2,1,0:T(8,128)(2,1)S(1)}, bf16[1536,512]{1,0:T(8,128)(2,1)S(1)}, f32[2,8,256]{2,1,0:T(8,128)S(1)}) custom-call(f32[512,256]{1,0:T(8,128)S(1)} %copy-done.4, f32[512,256]{1,0:T(8,128)S(1)} %copy-done.5, f32[3,256]{1,0:T(4,128)S(1)} %get-tuple-element.35.refs_4_.refs_3_.biases, ...), custom_call_target="tpu_custom_call" | custom-call | flops 262144 | bytes 7916544 | tf_op jit(solution)/shard_map/pallas_call | solution.py:370
  47.6 4.8 %shard_map.269 = (f32[512,512]{1,0:T(8,128)S(1)}, f32[256,512]{1,0:T(8,128)S(1)}, f32[1536,512]{1,0:T(8,128)S(1)}) custom-call(f32[128,512]{1,0:T(8,128)S(1)} %get-tuple-element.52.head, f32[256,512]{1,0:T(8,128)S(1)} %shard_map.267.middle, f32[128,512]{1,0:T(8,128)S(1)} %get-tuple-element.51.tail, bf16[3072,768]{1,0:T(8,128)(2,1)S(1)} %get-tuple-element.54.picks, ...), custom_call_target="tpu_custom_call" | custom-call | flops 3221225472 | bytes 15228928 | tf_op jit(solution)/shard_map/pallas_call | solution.py:370
  52.4 0.8 %collective-permute-done.11.before = f32[128,512]{1,0:T(8,128)S(1)} collective-permute-done((f32[128,512]{1,0:T(8,128)S(1)}, f32[128,512]{1,0:T(8,128)S(1)}, u32[]{:S(2)}, u32[]{:S(2)}) %collective-permute-start.11) | collective-permute-done | bytes 262176 | tf_op jit(solution)/shard_map/ppermute | solution.py:387
  53.2 0.0 collective-permute-done.12.after
  53.2 3.1 %shard_map.270 = f32[512,512]{1,0:T(8,128)} custom-call(f32[128,512]{1,0:T(8,128)S(1)} %collective-permute-done.11.before, f32[128,512]{1,0:T(8,128)S(1)} %collective-permute-done.12.after, f32[128,512]{1,0:T(8,128)S(1)} %get-tuple-element.52.head, f32[128,512]{1,0:T(8,128)S(1)} %get-tuple-element.51.tail, f32[256,512]{1,0:T(8,128)S(1)} %get-tuple-element.62.inner, ...), custom_call_target="tpu_custom_call" | custom-call | flops 805306368 | bytes 14688256 | tf_op jit(solution)/shard_map/pallas_call | solution.py:370
  (34 shorter events, 0.1 us)
Async XLA Ops:
  0.6 5.0 %copy-start.18 = (s32[64,7]{0,1:T(8,128)S(1)}, s32[64,7]{0,1:T(8,128)}, u32[]{:S(2)}) copy-start(s32[64,7]{0,1:T(8,128)} %param.28) | copy-start | bytes 5380
  0.6 5.0 %copy-start.24 = (f32[256]{0:T(256)S(1)}, f32[256]{0:T(256)}, u32[]{:S(2)}) copy-start(f32[256]{0:T(256)} %param.34) | copy-start | bytes 3076
  0.7 5.0 %copy-start = (f32[512,512]{1,0:T(8,128)S(1)}, f32[512,512]{1,0:T(8,128)}, u32[]{:S(2)}) copy-start(f32[512,512]{1,0:T(8,128)} %nodes.3) | copy-start | bytes 3145732
  0.7 5.0 %copy-start.13 = (f32[64,512]{1,0:T(8,128)S(1)}, f32[64,512]{1,0:T(8,128)}, u32[]{:S(2)}) copy-start(f32[64,512]{1,0:T(8,128)} %refs_2_.4) | copy-start | bytes 393220
  0.7 5.0 %copy-start.7 = (f32[512,256]{1,0:T(8,128)S(1)}, f32[512,256]{1,0:T(8,128)}, u32[]{:S(2)}) copy-start(f32[512,256]{1,0:T(8,128)} %ws.2) | copy-start | bytes 1572868
  2.6 16.1 %collective-permute-start.4 = (f32[392,256]{1,0:T(8,128)}, f32[392,256]{1,0:T(8,128)S(1)}, u32[]{:S(2)}, u32[]{:S(2)}) collective-permute-start(f32[392,256]{1,0:T(8,128)} %shard_map.261), channel_id=1, source_target_pairs={{0,2},{2,0},{1,3},{3,1},{4,6},{6,4},{5,7},{7,5},{8,10},{10,8},{9,1... | collective-permute-start | bytes 1204232 | tf_op jit(solution)/shard_map/ppermute | solution.py:387
  5.6 1.0 %copy-start.8 = (f32[512,256]{1,0:T(8,128)S(1)}, f32[512,256]{1,0:T(8,128)}, u32[]{:S(2)}) copy-start(f32[512,256]{1,0:T(8,128)} %wr.2) | copy-start | bytes 1572868
  6.7 1.0 %copy-start.9 = (f32[256,512]{1,0:T(8,128)S(1)}, f32[256,512]{1,0:T(8,128)}, u32[]{:S(2)}) copy-start(f32[256,512]{1,0:T(8,128)} %wo.2) | copy-start | bytes 1572868
  9.5 11.3 %copy-start.16 = (f32[256]{0:T(256)S(1)}, f32[256]{0:T(256)}, u32[]{:S(2)}) copy-start(f32[256]{0:T(256)} %param.44) | copy-start | bytes 3076
  9.6 11.3 %copy-start.17 = (f32[256]{0:T(256)S(1)}, f32[256]{0:T(256)}, u32[]{:S(2)}) copy-start(f32[256]{0:T(256)} %param.49) | copy-start | bytes 3076
  9.6 11.3 %copy-start.20 = (f32[512]{0:T(512)S(1)}, f32[512]{0:T(512)}, u32[]{:S(2)}) copy-start(f32[512]{0:T(512)} %param.36) | copy-start | bytes 6148
  9.6 11.3 %copy-start.21 = (f32[512]{0:T(512)S(1)}, f32[512]{0:T(512)}, u32[]{:S(2)}) copy-start(f32[512]{0:T(512)} %param.41) | copy-start | bytes 6148
  9.6 11.3 %copy-start.22 = (f32[512]{0:T(512)S(1)}, f32[512]{0:T(512)}, u32[]{:S(2)}) copy-start(f32[512]{0:T(512)} %param.46) | copy-start | bytes 6148
  9.6 11.3 %copy-start.23 = (f32[512]{0:T(512)S(1)}, f32[512]{0:T(512)}, u32[]{:S(2)}) copy-start(f32[512]{0:T(512)} %param.51) | copy-start | bytes 6148
  9.6 11.3 %copy-start.25 = (f32[256]{0:T(256)S(1)}, f32[256]{0:T(256)}, u32[]{:S(2)}) copy-start(f32[256]{0:T(256)} %param.39) | copy-start | bytes 3076
  9.6 11.3 %copy-start.10 = (f32[512,256]{1,0:T(8,128)S(1)}, f32[512,256]{1,0:T(8,128)}, u32[]{:S(2)}) copy-start(f32[512,256]{1,0:T(8,128)} %refs_5_.1) | copy-start | bytes 1572868
  9.6 11.3 %copy-start.11 = (f32[512,256]{1,0:T(8,128)S(1)}, f32[512,256]{1,0:T(8,128)}, u32[]{:S(2)}) copy-start(f32[512,256]{1,0:T(8,128)} %refs_6_.1) | copy-start | bytes 1572868
  9.7 9.1 %collective-permute-start = (f32[64,512]{1,0:T(8,128)S(1)}, f32[64,512]{1,0:T(8,128)S(1)}, u32[]{:S(2)}, u32[]{:S(2)}) collective-permute-start(f32[64,512]{1,0:T(8,128)S(1)} %shard_map.257.refs_7_.refs_0_), channel_id=1, source_target_pairs={{0,2},{2,0},{1,3},{3,1},{4,6},{6,4},{5,7},{7,5},{8,10},{10,8},{9,1... | collective-permute-start | bytes 393224 | tf_op jit(solution)/shard_map/ppermute | solution.py:387
  9.8 17.4 %copy-start.15 = (s32[512,6]{0,1:T(8,128)S(1)}, s32[512,6]{0,1:T(8,128)}, u32[]{:S(2)}) copy-start(s32[512,6]{0,1:T(8,128)} %param.30) | copy-start | bytes 36868
  9.8 17.4 %copy-start.19 = (s32[64,6]{0,1:T(8,128)S(1)}, s32[64,6]{0,1:T(8,128)}, u32[]{:S(2)}) copy-start(s32[64,6]{0,1:T(8,128)} %param.31) | copy-start | bytes 4612
  11.7 21.1 %copy-start.12 = (f32[256,512]{1,0:T(8,128)S(1)}, f32[256,512]{1,0:T(8,128)}, u32[]{:S(2)}) copy-start(f32[256,512]{1,0:T(8,128)} %refs_4_.3) | copy-start | bytes 1572868
  11.7 18.4 %collective-permute-start.6 = (f32[392,256]{1,0:T(8,128)}, f32[392,256]{1,0:T(8,128)S(1)}, u32[]{:S(2)}, u32[]{:S(2)}) collective-permute-start(f32[392,256]{1,0:T(8,128)} %shard_map.262), channel_id=1, source_target_pairs={{0,2},{2,0},{1,3},{3,1},{4,6},{6,4},{5,7},{7,5},{8,10},{10,8},{9,1... | collective-permute-start | bytes 1204232 | tf_op jit(solution)/shard_map/ppermute | solution.py:387
  18.8 11.3 %collective-permute-start.5 = (f32[392,256]{1,0:T(8,128)S(1)}, f32[392,256]{1,0:T(8,128)S(1)}, u32[]{:S(2)}, u32[]{:S(2)}) collective-permute-start(f32[392,256]{1,0:T(8,128)S(1)} %collective-permute-done.4.refs_5_), channel_id=1, source_target_pairs={{0,16},{16,0},{1,17},{17,1},{2,18},{18,2},{3,19},{19,3},{4,20},{20... | collective-permute-start | bytes 1204232 | tf_op jit(solution)/shard_map/ppermute | solution.py:428
  21.5 13.6 %copy-start.1 = (f32[512,256]{1,0:T(8,128)S(1)}, f32[512,256]{1,0:T(8,128)}, u32[]{:S(2)}) copy-start(f32[512,256]{1,0:T(8,128)} %refs_1_.5) | copy-start | bytes 1572868
  21.5 13.6 %copy-start.2 = (f32[512,256]{1,0:T(8,128)S(1)}, f32[512,256]{1,0:T(8,128)}, u32[]{:S(2)}) copy-start(f32[512,256]{1,0:T(8,128)} %refs_2_.7) | copy-start | bytes 1572868
  21.5 13.6 %copy-start.3 = (f32[256,512]{1,0:T(8,128)S(1)}, f32[256,512]{1,0:T(8,128)}, u32[]{:S(2)}) copy-start(f32[256,512]{1,0:T(8,128)} %refs_4_.4) | copy-start | bytes 1572868
  21.6 6.7 %collective-permute-start.1 = (f32[64,256]{1,0:T(8,128)S(1)}, f32[64,256]{1,0:T(8,128)S(1)}, u32[]{:S(2)}, u32[]{:S(2)}) collective-permute-start(f32[64,256]{1,0:T(8,128)S(1)} %get-tuple-element.36.refs_2_.refs_0_), channel_id=1, source_target_pairs={{0,4},{4,8},{8,12},{12,0},{1,5},{5,9},{9,13},{13,1},{2,6},{6,10},{... | collective-permute-start | bytes 196616 | tf_op jit(solution)/shard_map/ppermute | solution.py:387
  23.2 5.2 %collective-permute-start.2 = (f32[64,256]{1,0:T(8,128)S(1)}, f32[64,256]{1,0:T(8,128)S(1)}, u32[]{:S(2)}, u32[]{:S(2)}) collective-permute-start(f32[64,256]{1,0:T(8,128)S(1)} %get-tuple-element.36.refs_2_.refs_0_), channel_id=1, source_target_pairs={{0,8},{4,12},{8,0},{12,4},{1,9},{5,13},{9,1},{13,5},{2,10},{6,14},... | collective-permute-start | bytes 196616 | tf_op jit(solution)/shard_map/ppermute | solution.py:387
  25.8 4.3 %collective-permute-start.3 = (f32[64,256]{1,0:T(8,128)S(1)}, f32[64,256]{1,0:T(8,128)S(1)}, u32[]{:S(2)}, u32[]{:S(2)}) collective-permute-start(f32[64,256]{1,0:T(8,128)S(1)} %get-tuple-element.36.refs_2_.refs_0_), channel_id=1, source_target_pairs={{0,12},{4,0},{8,4},{12,8},{1,13},{5,1},{9,5},{13,9},{2,14},{6,2},{... | collective-permute-start | bytes 196616 | tf_op jit(solution)/shard_map/ppermute | solution.py:387
  30.0 5.0 %collective-permute-start.10 = (f32[392,256]{1,0:T(8,128)S(1)}, f32[392,256]{1,0:T(8,128)S(1)}, u32[]{:S(2)}, u32[]{:S(2)}) collective-permute-start(f32[392,256]{1,0:T(8,128)S(1)} %collective-permute-done.5.refs_7_), channel_id=1, source_target_pairs={{0,1},{1,0},{2,3},{3,2},{4,5},{5,4},{6,7},{7,6},{8,9},{9,8},{10,11... | collective-permute-start | bytes 1204232 | tf_op jit(solution)/shard_map/ppermute | solution.py:387
  30.1 5.0 %collective-permute-start.9 = (f32[392,256]{1,0:T(8,128)S(1)}, f32[392,256]{1,0:T(8,128)S(1)}, u32[]{:S(2)}, u32[]{:S(2)}) collective-permute-start(f32[392,256]{1,0:T(8,128)S(1)} %collective-permute-done.4.refs_5_), channel_id=1, source_target_pairs={{0,1},{1,0},{2,3},{3,2},{4,5},{5,4},{6,7},{7,6},{8,9},{9,8},{10,11... | collective-permute-start | bytes 1204232 | tf_op jit(solution)/shard_map/ppermute | solution.py:387
  30.6 2.2 %collective-permute-start.7 = (f32[256,256]{1,0:T(8,128)S(1)}, f32[256,256]{1,0:T(8,128)S(1)}, u32[]{:S(2)}, u32[]{:S(2)}) collective-permute-start(f32[256,256]{1,0:T(8,128)S(1)} %shard_map.263.refs_0_), channel_id=1, source_target_pairs={{0,1},{1,0},{2,3},{3,2},{4,5},{5,4},{6,7},{7,6},{8,9},{9,8},{10,11... | collective-permute-start | bytes 786440 | tf_op jit(solution)/shard_map/ppermute | solution.py:387
  30.7 11.6 %collective-permute-start.13 = (f32[392,256]{1,0:T(8,128)S(1)}, f32[392,256]{1,0:T(8,128)S(1)}, u32[]{:S(2)}, u32[]{:S(2)}) collective-permute-start(f32[392,256]{1,0:T(8,128)S(1)} %collective-permute-done.6.refs_0_), channel_id=1, source_target_pairs={{0,4},{4,0},{8,12},{12,8},{1,5},{5,1},{9,13},{13,9},{2,6},{6,2},{1... | collective-permute-start | bytes 1204232 | tf_op jit(solution)/shard_map/ppermute | solution.py:428
  33.5 5.6 %copy-start.14 = (s32[512,3]{0,1:T(4,128)S(1)}, s32[512,3]{0,1:T(4,128)}, u32[]{:S(2)}) copy-start(s32[512,3]{0,1:T(4,128)} %param.29) | copy-start | bytes 18436
  33.5 5.6 %collective-permute-start.8 = (f32[64,512]{1,0:T(8,128)S(1)}, f32[64,512]{1,0:T(8,128)S(1)}, u32[]{:S(2)}, u32[]{:S(2)}) collective-permute-start(f32[64,512]{1,0:T(8,128)S(1)} %shard_map.264.refs_9_.refs_0_), channel_id=1, source_target_pairs={{0,2},{2,0},{1,3},{3,1},{4,6},{6,4},{5,7},{7,5},{8,10},{10,8},{9,1... | collective-permute-start | bytes 393224 | tf_op jit(solution)/shard_map/ppermute | solution.py:387
  42.4 4.6 %collective-permute-start.14 = (f32[392,256]{1,0:T(8,128)S(1)}, f32[392,256]{1,0:T(8,128)S(1)}, u32[]{:S(2)}, u32[]{:S(2)}) collective-permute-start(f32[392,256]{1,0:T(8,128)S(1)} %collective-permute-done.6.refs_0_), channel_id=1, source_target_pairs={{0,1},{1,0},{2,3},{3,2},{4,5},{5,4},{6,7},{7,6},{8,9},{9,8},{10,11... | collective-permute-start | bytes 1204232 | tf_op jit(solution)/shard_map/ppermute | solution.py:387
  42.4 4.6 %collective-permute-start.15 = (f32[392,256]{1,0:T(8,128)S(1)}, f32[392,256]{1,0:T(8,128)S(1)}, u32[]{:S(2)}, u32[]{:S(2)}) collective-permute-start(f32[392,256]{1,0:T(8,128)S(1)} %collective-permute-done.13.refs_2_), channel_id=1, source_target_pairs={{0,1},{1,0},{2,3},{3,2},{4,5},{5,4},{6,7},{7,6},{8,9},{9,8},{10,11... | collective-permute-start | bytes 1204232 | tf_op jit(solution)/shard_map/ppermute | solution.py:387
  42.9 10.4 %collective-permute-start.12 = (f32[128,512]{1,0:T(8,128)S(1)}, f32[128,512]{1,0:T(8,128)S(1)}, u32[]{:S(2)}, u32[]{:S(2)}) collective-permute-start(f32[128,512]{1,0:T(8,128)S(1)} %get-tuple-element.52.head), channel_id=1, source_target_pairs={{0,13},{1,0},{4,1},{5,4},{8,5},{9,8},{12,9},{13,12},{2,15},{3,2},{... | collective-permute-start | bytes 786440 | tf_op jit(solution)/shard_map/ppermute | solution.py:387
  45.6 7.6 %collective-permute-start.11 = (f32[128,512]{1,0:T(8,128)S(1)}, f32[128,512]{1,0:T(8,128)S(1)}, u32[]{:S(2)}, u32[]{:S(2)}) collective-permute-start(f32[128,512]{1,0:T(8,128)S(1)} %get-tuple-element.51.tail), channel_id=1, source_target_pairs={{0,1},{1,4},{4,5},{5,8},{8,9},{9,12},{12,13},{13,0},{2,3},{3,6},{6... | collective-permute-start | bytes 786440 | tf_op jit(solution)/shard_map/ppermute | solution.py:387
  45.6 1.4 %copy-start.4 = (f32[512,256]{1,0:T(8,128)S(1)}, f32[512,256]{1,0:T(8,128)}, u32[]{:S(2)}) copy-start(f32[512,256]{1,0:T(8,128)} %ws.3) | copy-start | bytes 1572868
  45.6 1.4 %copy-start.5 = (f32[512,256]{1,0:T(8,128)S(1)}, f32[512,256]{1,0:T(8,128)}, u32[]{:S(2)}) copy-start(f32[512,256]{1,0:T(8,128)} %wr.3) | copy-start | bytes 1572868
  45.6 1.4 %copy-start.6 = (f32[256,512]{1,0:T(8,128)S(1)}, f32[256,512]{1,0:T(8,128)}, u32[]{:S(2)}) copy-start(f32[256,512]{1,0:T(8,128)} %wo.3) | copy-start | bytes 1572868

commit v14 on v13

--- a/solution.py
+++ b/solution.py
@@ -508,7 +508,7 @@
             functools.partial(share_kernel, axis),
             [pack(axis)],
             own,
-            latent,
+            8 * latent**3,
             [pltpu.SemaphoreType.DMA((3 + columns,))],
             far=range(4),
             limit=share_limit,

time: 56.8 us -> 56.7 us (level)
  local copies, waits for them, and re-layouts: 2.2 us -> 0.13 us
  waiting for transfers between devices: 12.8 us -> 14.8 us
    unnamed x52, local copies, waits for them, and re-layouts: 2.2 us -> 0.13 us
    ppermute x14, waiting for transfers between devices: 11.5 us -> 13.5 us  [shifted(): lax.ppermute(values, axis, [(i, (i + step) % count) for i in range(count)])]
where the time goes in v14:
time: 56.7 us; the launch traced here: 56.6 us
  Pallas kernels  21.5 us (38%)
  starting transfers between devices  18.9 us (33%)
  waiting for transfers between devices  14.8 us (26%)
  between operations  1.2 us (2%)
    pallas_call x14, Pallas kernels, call(): pl.pallas_call((lambda *refs: kernel(*refs[:read], *refs[read + unread:])...  21.5 us
    ppermute x14, starting transfers between devices, shifted(): lax.ppermute(values, axis, [(i, (i + step) % count) for i in range(count)])  16.2 us
    ppermute x14, waiting for transfers between devices, shifted(): lax.ppermute(values, axis, [(i, (i + step) % count) for i in range(count)])  13.5 us
    ppermute x2, starting transfers between devices, over_partners(): lax.ppermute(share, axis, [(i, i - i % count + (i + p) % count) for i in...  2.68 us
    ppermute x2, waiting for transfers between devices, over_partners(): lax.ppermute(share, axis, [(i, i - i % count + (i + p) % count) for i in...  1.36 us
  transfers between devices with their start and end apart: 16, of which 7 were waited for; matrix products, arithmetic and copies ran while one was open for 0% of the time, Pallas kernels for 29%

profile of v14, /device:TPU:0, one launch (start us, length us, event | category | flops | bytes accessed | tf_op | source)
XLA Modules:
  0.0 56.6 jit_solution(12274726944279199134)
XLA Ops:
  0.6 0.0 copy-start
  0.6 0.0 copy-start.7
  0.7 0.0 copy-start.8
  0.7 0.0 copy-start.9
  0.7 0.0 copy-start.13
  0.7 0.0 copy-start.16
  0.7 0.0 copy-start.22
  0.7 2.0 %shard_map.261 = f32[392,256]{1,0:T(8,128)} custom-call(f32[512,256]{1,0:T(8,128)} %refs_1_.5, f32[512,256]{1,0:T(8,128)} %refs_2_.7, f32[256,512]{1,0:T(8,128)} %refs_4_.4, f32[1,256]{1,0:T(1,128)} %bitcast.23), custom_call_target="tpu_custom_call" | custom-call | flops 1073741824 | bytes 1975296 | tf_op jit(solution)/shard_map/pallas_call | solution.py:370
  2.7 3.0 %collective-permute-start.4 = (f32[392,256]{1,0:T(8,128)}, f32[392,256]{1,0:T(8,128)S(1)}, u32[]{:S(2)}, u32[]{:S(2)}) collective-permute-start(f32[392,256]{1,0:T(8,128)} %shard_map.261), channel_id=1, source_target_pairs={{0,2},{2,0},{1,3},{3,1},{4,6},{6,4},{5,7},{7,5},{8,10},{10,8},{9,1... | collective-permute-start | bytes 1204232 | tf_op jit(solution)/shard_map/ppermute | solution.py:387
  5.7 0.0 copy-done.8
  5.7 1.8 %shard_map.257.refs_7_.refs_0_ = f32[64,512]{1,0:T(8,128)S(1)} custom-call(f32[512,512]{1,0:T(8,128)S(1)} %copy-done, f32[64,512]{1,0:T(8,128)S(1)} %copy-done.13, s32[7,64]{1,0:T(8,128)S(1)} %bitcast.15, f32[512,256]{1,0:T(8,128)S(1)} %copy-done.7, f32[512,256]{1,0:T(8,128)S(1)} %copy-done.8, f32[1,256]{1,0:T(1,128)S(1)} %bitcast.21, f32[256,512]{1,0:T(8,128)S(1)} %copy-done.9), custom_call_target="tpu_custom_call" | custom-call | flops 402653184 | bytes 2886400 | tf_op jit(solution)/shard_map/pallas_call | solution.py:370
  7.5 0.1 collective-permute-start
  7.7 0.0 copy-start.21
  7.7 0.0 copy-start.23
  7.7 0.0 copy-start.24
  7.7 0.0 copy-start.25
  7.7 0.0 copy-start.10
  7.7 0.0 copy-start.11
  7.7 1.9 %shard_map.262 = f32[392,256]{1,0:T(8,128)} custom-call(f32[512,256]{1,0:T(8,128)} %ws.3, f32[512,256]{1,0:T(8,128)} %wr.3, f32[256,512]{1,0:T(8,128)} %wo.3, f32[1,256]{1,0:T(1,128)} %bitcast.25), custom_call_target="tpu_custom_call" | custom-call | flops 1073741824 | bytes 1975296 | tf_op jit(solution)/shard_map/pallas_call | solution.py:370
  9.6 0.0 copy-start.15
  9.6 0.0 copy-start.17
  9.6 0.0 copy-start.12
  9.7 2.0 %collective-permute-start.6 = (f32[392,256]{1,0:T(8,128)}, f32[392,256]{1,0:T(8,128)S(1)}, u32[]{:S(2)}, u32[]{:S(2)}) collective-permute-start(f32[392,256]{1,0:T(8,128)} %shard_map.262), channel_id=1, source_target_pairs={{0,2},{2,0},{1,3},{3,1},{4,6},{6,4},{5,7},{7,5},{8,10},{10,8},{9,1... | collective-permute-start | bytes 1204232 | tf_op jit(solution)/shard_map/ppermute | solution.py:387
  11.7 7.1 %collective-permute-done.refs_1_ = f32[64,512]{1,0:T(8,128)S(1)} collective-permute-done((f32[64,512]{1,0:T(8,128)S(1)}, f32[64,512]{1,0:T(8,128)S(1)}, u32[]{:S(2)}, u32[]{:S(2)}) %collective-permute-start) | collective-permute-done | bytes 131104 | tf_op jit(solution)/shard_map/ppermute | solution.py:387
  18.8 0.0 collective-permute-done.4.refs_5_
  18.8 2.1 %collective-permute-start.5 = (f32[392,256]{1,0:T(8,128)S(1)}, f32[392,256]{1,0:T(8,128)S(1)}, u32[]{:S(2)}, u32[]{:S(2)}) collective-permute-start(f32[392,256]{1,0:T(8,128)S(1)} %collective-permute-done.4.refs_5_), channel_id=1, source_target_pairs={{0,16},{16,0},{1,17},{17,1},{2,18},{18,2},{3,19},{19,3},{4,20},{20... | collective-permute-start | bytes 1204232 | tf_op jit(solution)/shard_map/ppermute | solution.py:428
  21.0 0.6 %shard_map.259 = (f32[64,512]{1,0:T(8,128)S(1)}, f32[64,256]{1,0:T(8,128)S(1)}, f32[64,256]{1,0:T(8,128)S(1)}) custom-call(f32[64,512]{1,0:T(8,128)S(1)} %shard_map.257.refs_7_.refs_0_, f32[64,512]{1,0:T(8,128)S(1)} %collective-permute-done.refs_1_, f32[64,512]{1,0:T(8,128)S(1)} %copy-done.13, f32[4,512]{1,0:T(4,128)S(1)} %get-tuple-element.34.refs_3_.gains, ...), custom_call_target="tpu_custom_call" | custom-call | flops 100663296 | bytes 1715200 | tf_op jit(solution)/shard_map/pallas_call | solution.py:370
  21.6 0.0 copy-start.2
  21.6 0.0 copy-start.3
  21.6 1.6 %collective-permute-start.1 = (f32[64,256]{1,0:T(8,128)S(1)}, f32[64,256]{1,0:T(8,128)S(1)}, u32[]{:S(2)}, u32[]{:S(2)}) collective-permute-start(f32[64,256]{1,0:T(8,128)S(1)} %get-tuple-element.36.refs_2_.refs_0_), channel_id=1, source_target_pairs={{0,4},{4,8},{8,12},{12,0},{1,5},{5,9},{9,13},{13,1},{2,6},{6,10},{... | collective-permute-start | bytes 196616 | tf_op jit(solution)/shard_map/ppermute | solution.py:387
  23.2 2.6 %collective-permute-start.2 = (f32[64,256]{1,0:T(8,128)S(1)}, f32[64,256]{1,0:T(8,128)S(1)}, u32[]{:S(2)}, u32[]{:S(2)}) collective-permute-start(f32[64,256]{1,0:T(8,128)S(1)} %get-tuple-element.36.refs_2_.refs_0_), channel_id=1, source_target_pairs={{0,8},{4,12},{8,0},{12,4},{1,9},{5,13},{9,1},{13,5},{2,10},{6,14},... | collective-permute-start | bytes 196616 | tf_op jit(solution)/shard_map/ppermute | solution.py:387
  25.8 1.3 %collective-permute-start.3 = (f32[64,256]{1,0:T(8,128)S(1)}, f32[64,256]{1,0:T(8,128)S(1)}, u32[]{:S(2)}, u32[]{:S(2)}) collective-permute-start(f32[64,256]{1,0:T(8,128)S(1)} %get-tuple-element.36.refs_2_.refs_0_), channel_id=1, source_target_pairs={{0,12},{4,0},{8,4},{12,8},{1,13},{5,1},{9,5},{13,9},{2,14},{6,2},{... | collective-permute-start | bytes 196616 | tf_op jit(solution)/shard_map/ppermute | solution.py:387
  27.2 1.1 %shard_map.260 = (bf16[384,1024]{1,0:T(8,128)(2,1)S(1)}, bf16[3072,768]{1,0:T(8,128)(2,1)S(1)}) custom-call(s32[6,64]{1,0:T(8,128)S(1)} %bitcast.16, s32[6,512]{1,0:T(8,128)S(1)} %bitcast.14, f32[64,256]{1,0:T(8,128)S(1)} %get-tuple-element.36.refs_2_.refs_0_), custom_call_target="tpu_custom_call" | custom-call | flops 196608 | bytes 5584384 | tf_op jit(solution)/shard_map/pallas_call | solution.py:370
  28.3 0.0 collective-permute-done.1.refs_1_
  28.3 0.1 collective-permute-done.2.refs_2_
  28.4 1.7 %collective-permute-done.3.refs_3_ = f32[64,256]{1,0:T(8,128)S(1)} collective-permute-done((f32[64,256]{1,0:T(8,128)S(1)}, f32[64,256]{1,0:T(8,128)S(1)}, u32[]{:S(2)}, u32[]{:S(2)}) %collective-permute-start.3) | collective-permute-done | bytes 65568 | tf_op jit(solution)/shard_map/ppermute | solution.py:387
  30.1 0.0 collective-permute-done.6.refs_0_
  30.1 0.0 collective-permute-done.5.refs_7_
  30.1 0.0 collective-permute-start.10
  30.1 0.5 collective-permute-start.9
  30.6 0.1 collective-permute-start.7
  30.8 0.6 %collective-permute-start.13 = (f32[392,256]{1,0:T(8,128)S(1)}, f32[392,256]{1,0:T(8,128)S(1)}, u32[]{:S(2)}, u32[]{:S(2)}) collective-permute-start(f32[392,256]{1,0:T(8,128)S(1)} %collective-permute-done.6.refs_0_), channel_id=1, source_target_pairs={{0,4},{4,0},{8,12},{12,8},{1,5},{5,1},{9,13},{13,9},{2,6},{6,2},{1... | collective-permute-start | bytes 1204232 | tf_op jit(solution)/shard_map/ppermute | solution.py:428
  31.4 1.4 %collective-permute-done.7.refs_1_ = f32[256,256]{1,0:T(8,128)S(1)} collective-permute-done((f32[256,256]{1,0:T(8,128)S(1)}, f32[256,256]{1,0:T(8,128)S(1)}, u32[]{:S(2)}, u32[]{:S(2)}) %collective-permute-start.7) | collective-permute-done | bytes 262176 | tf_op jit(solution)/shard_map/ppermute | solution.py:387
  32.8 0.8 %shard_map.264.refs_9_.refs_0_ = f32[64,512]{1,0:T(8,128)S(1)} custom-call(f32[256,256]{1,0:T(8,128)S(1)} %shard_map.263.refs_0_, f32[256,256]{1,0:T(8,128)S(1)} %collective-permute-done.7.refs_1_, bf16[384,1024]{1,0:T(8,128)(2,1)S(1)} %get-tuple-element.43.refs_2_, f32[64,256]{1,0:T(8,128)S(1)} %get-tuple-element.44.refs_3_, f32[256,512]{1,0:T(8,128)S(1)} %copy-done.12), custom_call_target="tpu_custom_call" | custom-call | flops 201326592 | bytes 2031616 | tf_op jit(solution)/shard_map/pallas_call | solution.py:370
  33.6 0.0 copy-start.14
  33.6 1.6 %collective-permute-start.8 = (f32[64,512]{1,0:T(8,128)S(1)}, f32[64,512]{1,0:T(8,128)S(1)}, u32[]{:S(2)}, u32[]{:S(2)}) collective-permute-start(f32[64,512]{1,0:T(8,128)S(1)} %shard_map.264.refs_9_.refs_0_), channel_id=1, source_target_pairs={{0,2},{2,0},{1,3},{3,1},{4,6},{6,4},{5,7},{7,5},{8,10},{10,8},{9,1... | collective-permute-start | bytes 393224 | tf_op jit(solution)/shard_map/ppermute | solution.py:387
  35.1 0.0 collective-permute-done.10.refs_8_
  35.1 0.0 collective-permute-done.9.refs_6_
  35.2 1.7 %shard_map.265 = (f32[512,512]{1,0:T(8,128)S(1)}, bf16[2,1536,256]{2,1,0:T(8,128)(2,1)S(1)}, bf16[1536,512]{1,0:T(8,128)(2,1)S(1)}) custom-call(f32[512,512]{1,0:T(8,128)S(1)} %copy-done, f32[512,256]{1,0:T(8,128)S(1)} %copy-done.1, f32[512,256]{1,0:T(8,128)S(1)} %copy-done.2, f32[3,256]{1,0:T(4,128)S(1)} %get-tuple-element.35.refs_4_.refs_3_.biases, ...), custom_call_target="tpu_custom_call" | custom-call | flops 805306368 | bytes 8555520 | tf_op jit(solution)/shard_map/pallas_call | solution.py:370
  36.8 2.3 %collective-permute-done.8.refs_1_ = f32[64,512]{1,0:T(8,128)S(1)} collective-permute-done((f32[64,512]{1,0:T(8,128)S(1)}, f32[64,512]{1,0:T(8,128)S(1)}, u32[]{:S(2)}, u32[]{:S(2)}) %collective-permute-start.8) | collective-permute-done | bytes 131104 | tf_op jit(solution)/shard_map/ppermute | solution.py:387
  39.2 1.9 %shard_map.266 = (f32[64,512]{1,0:T(8,128)}, bf16[128,512]{1,0:T(8,128)(2,1)S(1)}, f32[128,512]{1,0:T(8,128)S(1)}, f32[128,512]{1,0:T(8,128)S(1)}) custom-call(f32[64,512]{1,0:T(8,128)S(1)} %shard_map.264.refs_9_.refs_0_, f32[64,512]{1,0:T(8,128)S(1)} %collective-permute-done.8.refs_1_, f32[64,512]{1,0:T(8,128)S(1)} %get-tuple-element.45.refs_2_, ...), custom_call_target="tpu_custom_call" | custom-call | flops 402653184 | bytes 6436864 | tf_op jit(solution)/shard_map/pallas_call | solution.py:370
  41.1 1.4 %collective-permute-done.13.refs_2_ = f32[392,256]{1,0:T(8,128)S(1)} collective-permute-done((f32[392,256]{1,0:T(8,128)S(1)}, f32[392,256]{1,0:T(8,128)S(1)}, u32[]{:S(2)}, u32[]{:S(2)}) %collective-permute-start.13) | collective-permute-done | bytes 401440 | tf_op jit(solution)/shard_map/ppermute | solution.py:428
  42.4 0.0 collective-permute-start.14
  42.4 0.5 collective-permute-start.15
  42.9 2.8 %collective-permute-start.12 = (f32[128,512]{1,0:T(8,128)S(1)}, f32[128,512]{1,0:T(8,128)S(1)}, u32[]{:S(2)}, u32[]{:S(2)}) collective-permute-start(f32[128,512]{1,0:T(8,128)S(1)} %get-tuple-element.52.head), channel_id=1, source_target_pairs={{0,13},{1,0},{4,1},{5,4},{8,5},{9,8},{12,9},{13,12},{2,15},{3,2},{... | collective-permute-start | bytes 786440 | tf_op jit(solution)/shard_map/ppermute | solution.py:387
  45.7 0.0 collective-permute-start.11
  45.7 1.4 %shard_map.267.middle = f32[256,512]{1,0:T(8,128)S(1)} custom-call(f32[512,512]{1,0:T(8,128)S(1)} %copy-done, f32[512,512]{1,0:T(8,128)S(1)} %get-tuple-element.48.refs_5_.receivers, s32[3,512]{1,0:T(4,128)S(1)} %bitcast.13, bf16[128,512]{1,0:T(8,128)(2,1)S(1)} %get-tuple-element.53.senders, bf16[1536,512]{1,0:T(8,128)(2,1)S(1)} %get-tuple-element.50.refs_8_.wo, ...), custom_call_target="tpu_custom_call" | custom-call | flops 402653184 | bytes 4339712 | tf_op jit(solution)/shard_map/pallas_call | solution.py:370
  47.1 0.0 collective-permute-done.14.refs_1_
  47.1 0.0 collective-permute-done.15.refs_3_
  47.1 0.6 shard_map.268
  47.7 4.8 %shard_map.269 = (f32[512,512]{1,0:T(8,128)S(1)}, f32[256,512]{1,0:T(8,128)S(1)}, f32[1536,512]{1,0:T(8,128)S(1)}) custom-call(f32[128,512]{1,0:T(8,128)S(1)} %get-tuple-element.52.head, f32[256,512]{1,0:T(8,128)S(1)} %shard_map.267.middle, f32[128,512]{1,0:T(8,128)S(1)} %get-tuple-element.51.tail, bf16[3072,768]{1,0:T(8,128)(2,1)S(1)} %get-tuple-element.54.picks, ...), custom_call_target="tpu_custom_call" | custom-call | flops 3221225472 | bytes 15228928 | tf_op jit(solution)/shard_map/pallas_call | solution.py:370
  52.4 0.8 %collective-permute-done.11.before = f32[128,512]{1,0:T(8,128)S(1)} collective-permute-done((f32[128,512]{1,0:T(8,128)S(1)}, f32[128,512]{1,0:T(8,128)S(1)}, u32[]{:S(2)}, u32[]{:S(2)}) %collective-permute-start.11) | collective-permute-done | bytes 262176 | tf_op jit(solution)/shard_map/ppermute | solution.py:387
  53.3 0.0 collective-permute-done.12.after
  53.3 3.1 %shard_map.270 = f32[512,512]{1,0:T(8,128)} custom-call(f32[128,512]{1,0:T(8,128)S(1)} %collective-permute-done.11.before, f32[128,512]{1,0:T(8,128)S(1)} %collective-permute-done.12.after, f32[128,512]{1,0:T(8,128)S(1)} %get-tuple-element.52.head, f32[128,512]{1,0:T(8,128)S(1)} %get-tuple-element.51.tail, f32[256,512]{1,0:T(8,128)S(1)} %get-tuple-element.62.inner, ...), custom_call_target="tpu_custom_call" | custom-call | flops 805306368 | bytes 14688256 | tf_op jit(solution)/shard_map/pallas_call | solution.py:370
  (34 shorter events, 0.1 us)
Async XLA Ops:
  0.6 5.0 %copy-start = (f32[512,512]{1,0:T(8,128)S(1)}, f32[512,512]{1,0:T(8,128)}, u32[]{:S(2)}) copy-start(f32[512,512]{1,0:T(8,128)} %nodes.3) | copy-start | bytes 3145732
  0.6 5.0 %copy-start.7 = (f32[512,256]{1,0:T(8,128)S(1)}, f32[512,256]{1,0:T(8,128)}, u32[]{:S(2)}) copy-start(f32[512,256]{1,0:T(8,128)} %ws.2) | copy-start | bytes 1572868
  0.7 5.0 %copy-start.8 = (f32[512,256]{1,0:T(8,128)S(1)}, f32[512,256]{1,0:T(8,128)}, u32[]{:S(2)}) copy-start(f32[512,256]{1,0:T(8,128)} %wr.2) | copy-start | bytes 1572868
  0.7 5.0 %copy-start.9 = (f32[256,512]{1,0:T(8,128)S(1)}, f32[256,512]{1,0:T(8,128)}, u32[]{:S(2)}) copy-start(f32[256,512]{1,0:T(8,128)} %wo.2) | copy-start | bytes 1572868
  0.7 5.0 %copy-start.13 = (f32[64,512]{1,0:T(8,128)S(1)}, f32[64,512]{1,0:T(8,128)}, u32[]{:S(2)}) copy-start(f32[64,512]{1,0:T(8,128)} %refs_2_.4) | copy-start | bytes 393220
  0.7 5.0 %copy-start.16 = (s32[64,7]{0,1:T(8,128)S(1)}, s32[64,7]{0,1:T(8,128)}, u32[]{:S(2)}) copy-start(s32[64,7]{0,1:T(8,128)} %param.28) | copy-start | bytes 5380
  0.7 5.0 %copy-start.22 = (f32[256]{0:T(256)S(1)}, f32[256]{0:T(256)}, u32[]{:S(2)}) copy-start(f32[256]{0:T(256)} %param.34) | copy-start | bytes 3076
  2.7 16.1 %collective-permute-start.4 = (f32[392,256]{1,0:T(8,128)}, f32[392,256]{1,0:T(8,128)S(1)}, u32[]{:S(2)}, u32[]{:S(2)}) collective-permute-start(f32[392,256]{1,0:T(8,128)} %shard_map.261), channel_id=1, source_target_pairs={{0,2},{2,0},{1,3},{3,1},{4,6},{6,4},{5,7},{7,5},{8,10},{10,8},{9,1... | collective-permute-start | bytes 1204232 | tf_op jit(solution)/shard_map/ppermute | solution.py:387
  7.5 11.3 %collective-permute-start = (f32[64,512]{1,0:T(8,128)S(1)}, f32[64,512]{1,0:T(8,128)S(1)}, u32[]{:S(2)}, u32[]{:S(2)}) collective-permute-start(f32[64,512]{1,0:T(8,128)S(1)} %shard_map.257.refs_7_.refs_0_), channel_id=1, source_target_pairs={{0,2},{2,0},{1,3},{3,1},{4,6},{6,4},{5,7},{7,5},{8,10},{10,8},{9,1... | collective-permute-start | bytes 393224 | tf_op jit(solution)/shard_map/ppermute | solution.py:387
  7.6 13.3 %copy-start.18 = (f32[512]{0:T(512)S(1)}, f32[512]{0:T(512)}, u32[]{:S(2)}) copy-start(f32[512]{0:T(512)} %param.36) | copy-start | bytes 6148
  7.6 13.3 %copy-start.19 = (f32[512]{0:T(512)S(1)}, f32[512]{0:T(512)}, u32[]{:S(2)}) copy-start(f32[512]{0:T(512)} %param.41) | copy-start | bytes 6148
  7.6 13.3 %copy-start.20 = (f32[512]{0:T(512)S(1)}, f32[512]{0:T(512)}, u32[]{:S(2)}) copy-start(f32[512]{0:T(512)} %param.46) | copy-start | bytes 6148
  7.7 13.3 %copy-start.21 = (f32[512]{0:T(512)S(1)}, f32[512]{0:T(512)}, u32[]{:S(2)}) copy-start(f32[512]{0:T(512)} %param.51) | copy-start | bytes 6148
  7.7 13.2 %copy-start.23 = (f32[256]{0:T(256)S(1)}, f32[256]{0:T(256)}, u32[]{:S(2)}) copy-start(f32[256]{0:T(256)} %param.39) | copy-start | bytes 3076
  7.7 13.2 %copy-start.24 = (f32[256]{0:T(256)S(1)}, f32[256]{0:T(256)}, u32[]{:S(2)}) copy-start(f32[256]{0:T(256)} %param.44) | copy-start | bytes 3076
  7.7 13.2 %copy-start.25 = (f32[256]{0:T(256)S(1)}, f32[256]{0:T(256)}, u32[]{:S(2)}) copy-start(f32[256]{0:T(256)} %param.49) | copy-start | bytes 3076
  7.7 13.3 %copy-start.10 = (f32[512,256]{1,0:T(8,128)S(1)}, f32[512,256]{1,0:T(8,128)}, u32[]{:S(2)}) copy-start(f32[512,256]{1,0:T(8,128)} %refs_5_.1) | copy-start | bytes 1572868
  7.7 13.3 %copy-start.11 = (f32[512,256]{1,0:T(8,128)S(1)}, f32[512,256]{1,0:T(8,128)}, u32[]{:S(2)}) copy-start(f32[512,256]{1,0:T(8,128)} %refs_6_.1) | copy-start | bytes 1572868
  9.6 17.6 %copy-start.15 = (s32[512,6]{0,1:T(8,128)S(1)}, s32[512,6]{0,1:T(8,128)}, u32[]{:S(2)}) copy-start(s32[512,6]{0,1:T(8,128)} %param.30) | copy-start | bytes 36868
  9.6 17.5 %copy-start.17 = (s32[64,6]{0,1:T(8,128)S(1)}, s32[64,6]{0,1:T(8,128)}, u32[]{:S(2)}) copy-start(s32[64,6]{0,1:T(8,128)} %param.31) | copy-start | bytes 4612
  9.6 23.1 %copy-start.12 = (f32[256,512]{1,0:T(8,128)S(1)}, f32[256,512]{1,0:T(8,128)}, u32[]{:S(2)}) copy-start(f32[256,512]{1,0:T(8,128)} %refs_4_.3) | copy-start | bytes 1572868
  9.7 20.4 %collective-permute-start.6 = (f32[392,256]{1,0:T(8,128)}, f32[392,256]{1,0:T(8,128)S(1)}, u32[]{:S(2)}, u32[]{:S(2)}) collective-permute-start(f32[392,256]{1,0:T(8,128)} %shard_map.262), channel_id=1, source_target_pairs={{0,2},{2,0},{1,3},{3,1},{4,6},{6,4},{5,7},{7,5},{8,10},{10,8},{9,1... | collective-permute-start | bytes 1204232 | tf_op jit(solution)/shard_map/ppermute | solution.py:387
  18.8 11.3 %collective-permute-start.5 = (f32[392,256]{1,0:T(8,128)S(1)}, f32[392,256]{1,0:T(8,128)S(1)}, u32[]{:S(2)}, u32[]{:S(2)}) collective-permute-start(f32[392,256]{1,0:T(8,128)S(1)} %collective-permute-done.4.refs_5_), channel_id=1, source_target_pairs={{0,16},{16,0},{1,17},{17,1},{2,18},{18,2},{3,19},{19,3},{4,20},{20... | collective-permute-start | bytes 1204232 | tf_op jit(solution)/shard_map/ppermute | solution.py:428
  21.6 13.6 %copy-start.1 = (f32[512,256]{1,0:T(8,128)S(1)}, f32[512,256]{1,0:T(8,128)}, u32[]{:S(2)}) copy-start(f32[512,256]{1,0:T(8,128)} %refs_1_.5) | copy-start | bytes 1572868
  21.6 13.6 %copy-start.2 = (f32[512,256]{1,0:T(8,128)S(1)}, f32[512,256]{1,0:T(8,128)}, u32[]{:S(2)}) copy-start(f32[512,256]{1,0:T(8,128)} %refs_2_.7) | copy-start | bytes 1572868
  21.6 13.6 %copy-start.3 = (f32[256,512]{1,0:T(8,128)S(1)}, f32[256,512]{1,0:T(8,128)}, u32[]{:S(2)}) copy-start(f32[256,512]{1,0:T(8,128)} %refs_4_.4) | copy-start | bytes 1572868
  21.6 6.7 %collective-permute-start.1 = (f32[64,256]{1,0:T(8,128)S(1)}, f32[64,256]{1,0:T(8,128)S(1)}, u32[]{:S(2)}, u32[]{:S(2)}) collective-permute-start(f32[64,256]{1,0:T(8,128)S(1)} %get-tuple-element.36.refs_2_.refs_0_), channel_id=1, source_target_pairs={{0,4},{4,8},{8,12},{12,0},{1,5},{5,9},{9,13},{13,1},{2,6},{6,10},{... | collective-permute-start | bytes 196616 | tf_op jit(solution)/shard_map/ppermute | solution.py:387
  23.2 5.2 %collective-permute-start.2 = (f32[64,256]{1,0:T(8,128)S(1)}, f32[64,256]{1,0:T(8,128)S(1)}, u32[]{:S(2)}, u32[]{:S(2)}) collective-permute-start(f32[64,256]{1,0:T(8,128)S(1)} %get-tuple-element.36.refs_2_.refs_0_), channel_id=1, source_target_pairs={{0,8},{4,12},{8,0},{12,4},{1,9},{5,13},{9,1},{13,5},{2,10},{6,14},... | collective-permute-start | bytes 196616 | tf_op jit(solution)/shard_map/ppermute | solution.py:387
  25.8 4.3 %collective-permute-start.3 = (f32[64,256]{1,0:T(8,128)S(1)}, f32[64,256]{1,0:T(8,128)S(1)}, u32[]{:S(2)}, u32[]{:S(2)}) collective-permute-start(f32[64,256]{1,0:T(8,128)S(1)} %get-tuple-element.36.refs_2_.refs_0_), channel_id=1, source_target_pairs={{0,12},{4,0},{8,4},{12,8},{1,13},{5,1},{9,5},{13,9},{2,14},{6,2},{... | collective-permute-start | bytes 196616 | tf_op jit(solution)/shard_map/ppermute | solution.py:387
  30.1 5.0 %collective-permute-start.10 = (f32[392,256]{1,0:T(8,128)S(1)}, f32[392,256]{1,0:T(8,128)S(1)}, u32[]{:S(2)}, u32[]{:S(2)}) collective-permute-start(f32[392,256]{1,0:T(8,128)S(1)} %collective-permute-done.5.refs_7_), channel_id=1, source_target_pairs={{0,1},{1,0},{2,3},{3,2},{4,5},{5,4},{6,7},{7,6},{8,9},{9,8},{10,11... | collective-permute-start | bytes 1204232 | tf_op jit(solution)/shard_map/ppermute | solution.py:387
  30.1 5.0 %collective-permute-start.9 = (f32[392,256]{1,0:T(8,128)S(1)}, f32[392,256]{1,0:T(8,128)S(1)}, u32[]{:S(2)}, u32[]{:S(2)}) collective-permute-start(f32[392,256]{1,0:T(8,128)S(1)} %collective-permute-done.4.refs_5_), channel_id=1, source_target_pairs={{0,1},{1,0},{2,3},{3,2},{4,5},{5,4},{6,7},{7,6},{8,9},{9,8},{10,11... | collective-permute-start | bytes 1204232 | tf_op jit(solution)/shard_map/ppermute | solution.py:387
  30.6 2.2 %collective-permute-start.7 = (f32[256,256]{1,0:T(8,128)S(1)}, f32[256,256]{1,0:T(8,128)S(1)}, u32[]{:S(2)}, u32[]{:S(2)}) collective-permute-start(f32[256,256]{1,0:T(8,128)S(1)} %shard_map.263.refs_0_), channel_id=1, source_target_pairs={{0,1},{1,0},{2,3},{3,2},{4,5},{5,4},{6,7},{7,6},{8,9},{9,8},{10,11... | collective-permute-start | bytes 786440 | tf_op jit(solution)/shard_map/ppermute | solution.py:387
  30.8 11.6 %collective-permute-start.13 = (f32[392,256]{1,0:T(8,128)S(1)}, f32[392,256]{1,0:T(8,128)S(1)}, u32[]{:S(2)}, u32[]{:S(2)}) collective-permute-start(f32[392,256]{1,0:T(8,128)S(1)} %collective-permute-done.6.refs_0_), channel_id=1, source_target_pairs={{0,4},{4,0},{8,12},{12,8},{1,5},{5,1},{9,13},{13,9},{2,6},{6,2},{1... | collective-permute-start | bytes 1204232 | tf_op jit(solution)/shard_map/ppermute | solution.py:428
  33.6 5.6 %copy-start.14 = (s32[512,3]{0,1:T(4,128)S(1)}, s32[512,3]{0,1:T(4,128)}, u32[]{:S(2)}) copy-start(s32[512,3]{0,1:T(4,128)} %param.29) | copy-start | bytes 18436
  33.6 5.6 %collective-permute-start.8 = (f32[64,512]{1,0:T(8,128)S(1)}, f32[64,512]{1,0:T(8,128)S(1)}, u32[]{:S(2)}, u32[]{:S(2)}) collective-permute-start(f32[64,512]{1,0:T(8,128)S(1)} %shard_map.264.refs_9_.refs_0_), channel_id=1, source_target_pairs={{0,2},{2,0},{1,3},{3,1},{4,6},{6,4},{5,7},{7,5},{8,10},{10,8},{9,1... | collective-permute-start | bytes 393224 | tf_op jit(solution)/shard_map/ppermute | solution.py:387
  42.4 4.6 %collective-permute-start.14 = (f32[392,256]{1,0:T(8,128)S(1)}, f32[392,256]{1,0:T(8,128)S(1)}, u32[]{:S(2)}, u32[]{:S(2)}) collective-permute-start(f32[392,256]{1,0:T(8,128)S(1)} %collective-permute-done.6.refs_0_), channel_id=1, source_target_pairs={{0,1},{1,0},{2,3},{3,2},{4,5},{5,4},{6,7},{7,6},{8,9},{9,8},{10,11... | collective-permute-start | bytes 1204232 | tf_op jit(solution)/shard_map/ppermute | solution.py:387
  42.4 4.7 %collective-permute-start.15 = (f32[392,256]{1,0:T(8,128)S(1)}, f32[392,256]{1,0:T(8,128)S(1)}, u32[]{:S(2)}, u32[]{:S(2)}) collective-permute-start(f32[392,256]{1,0:T(8,128)S(1)} %collective-permute-done.13.refs_2_), channel_id=1, source_target_pairs={{0,1},{1,0},{2,3},{3,2},{4,5},{5,4},{6,7},{7,6},{8,9},{9,8},{10,11... | collective-permute-start | bytes 1204232 | tf_op jit(solution)/shard_map/ppermute | solution.py:387
  42.9 10.4 %collective-permute-start.12 = (f32[128,512]{1,0:T(8,128)S(1)}, f32[128,512]{1,0:T(8,128)S(1)}, u32[]{:S(2)}, u32[]{:S(2)}) collective-permute-start(f32[128,512]{1,0:T(8,128)S(1)} %get-tuple-element.52.head), channel_id=1, source_target_pairs={{0,13},{1,0},{4,1},{5,4},{8,5},{9,8},{12,9},{13,12},{2,15},{3,2},{... | collective-permute-start | bytes 786440 | tf_op jit(solution)/shard_map/ppermute | solution.py:387
  45.7 7.6 %collective-permute-start.11 = (f32[128,512]{1,0:T(8,128)S(1)}, f32[128,512]{1,0:T(8,128)S(1)}, u32[]{:S(2)}, u32[]{:S(2)}) collective-permute-start(f32[128,512]{1,0:T(8,128)S(1)} %get-tuple-element.51.tail), channel_id=1, source_target_pairs={{0,1},{1,4},{4,5},{5,8},{8,9},{9,12},{12,13},{13,0},{2,3},{3,6},{6... | collective-permute-start | bytes 786440 | tf_op jit(solution)/shard_map/ppermute | solution.py:387
  45.7 1.4 %copy-start.4 = (f32[512,256]{1,0:T(8,128)S(1)}, f32[512,256]{1,0:T(8,128)}, u32[]{:S(2)}) copy-start(f32[512,256]{1,0:T(8,128)} %ws.3) | copy-start | bytes 1572868
  45.7 1.4 %copy-start.5 = (f32[512,256]{1,0:T(8,128)S(1)}, f32[512,256]{1,0:T(8,128)}, u32[]{:S(2)}) copy-start(f32[512,256]{1,0:T(8,128)} %wr.3) | copy-start | bytes 1572868
  45.7 1.4 %copy-start.6 = (f32[256,512]{1,0:T(8,128)S(1)}, f32[256,512]{1,0:T(8,128)}, u32[]{:S(2)}) copy-start(f32[256,512]{1,0:T(8,128)} %wo.3) | copy-start | bytes 1572868
